TPU v7x, 32 devices: a whole 2x2x4 slice. The times are simulated.
32 devices in a mesh: groups: 2 (over y), tp: 4 (over z), sp: 4 (over x, core).
Axes of the slice: x: 2, y: 2, z: 4, core: 2. Of those that a mesh axis runs over, the one named last changes fastest.
Arguments:
- hidden_cont: bfloat16 [512, 5120], P(('groups', 'sp')), parts along dimension 0, may hold values from -6 to 6
- hidden_prompt: bfloat16 [1024, 5120], P(('groups', 'sp')), parts along dimension 0, may hold values from -6 to 6
- norm_gain: float32 [5120], replicated, may hold values from 0.1 to 1.9
- query_weight: bfloat16 [5120, 4096], P('sp', 'tp'), may hold values from -0.078125 to 0.078125
- keyval_weight: bfloat16 [5120, 1024], P('sp'), may hold values from -0.078125 to 0.078125
- out_weight: bfloat16 [4096, 5120], P('tp', 'sp'), may hold values from -0.125 to 0.125
- query_gain: float32 [128], replicated, may hold values from 0.5 to 5
- key_gain: float32 [128], replicated, may hold values from 0.5 to 5
- sample_lengths: int32 [16], P('groups'), parts along dimension 0, may hold values from 1 to 64, 256 in all
Outputs:
- mixed: bfloat16 [512, 5120], P(('groups', 'sp'), 'tp'), parts along dimension 0
There are 2 independent parts, one for each index of `groups`. A program takes and returns all parts, laid end to end along the dimension named above; an argument that names none is the same for every part. Nothing has to cross between parts.
Inputs may be any that keep to these rules, and one draw needn't show every extreme that they name: `sample_lengths`: the lengths sum to 256 and the longest has exactly 64 tokens.
All inputs are finite; a program needn't handle non-finite values.
Results may differ from a plain program's by a relative error of at most 0.012.
The roundings to bfloat16 on the way count: a program that leaves them out, or rounds other values in their place, can miss the bound.
Values may be sent and summed in bfloat16 or wider, within the bound.
No kernel may reach another device: no remote copies, remote signals or barrier semaphores. Data moves between devices by JAX's collectives and lax.ppermute only.
A program may use at most 128 MiB of HBM per device.

v0:
```python
import functools
import math

import jax
import jax.numpy as jnp
from jax import lax
from jax.experimental import pallas as pl
from jax.experimental.pallas import tpu as pltpu
from jax.sharding import PartitionSpec as P

QH = 32
KVH = 4
SP, TP, GROUP, HEAD = range(4)
BF16 = jnp.bfloat16
F32 = jnp.float32
ROOM = 24 * 1024 * 1024
ALL = 62 * 1024 * 1024


def call(kernel, place, grid, in_specs, out_specs, out_shape, args, cost, scratch=(), room=ROOM):
    flops, moved = cost
    return pl.pallas_call(
        kernel,
        out_shape=out_shape,
        grid_spec=pltpu.PrefetchScalarGridSpec(
            num_scalar_prefetch=1,
            grid=grid,
            in_specs=in_specs,
            out_specs=out_specs,
            scratch_shapes=scratch,
        ),
        compiler_params=pltpu.CompilerParams(vmem_limit_bytes=room),
        cost_estimate=pl.CostEstimate(flops=flops, bytes_accessed=moved, transcendentals=0),
    )(place, *args)


def whole(array):
    zeros = (0,) * array.ndim
    return pl.BlockSpec(array.shape, lambda i, place: zeros)


def shape_of(shape, dtype):
    return jax.ShapeDtypeStruct(shape, dtype)


def rms_rows(values, gain):
    return values * lax.rsqrt(jnp.mean(values * values, axis=-1, keepdims=True) + 1e-06) * gain


def split_normed(hidden, gain, out):
    count, _, depth = out.shape
    normed = rms_rows(hidden[...].astype(F32), gain[...]).astype(BF16)
    for j in range(count):
        out[j] = normed[:, j * depth : (j + 1) * depth]


def norm_kernel(place, hidden, gain, out):
    split_normed(hidden, gain, out)


def norm_split(place, hidden, gain, count):
    rows, width = hidden.shape
    step = min(rows, 64)
    out = (count, rows, width // count)
    return call(
        norm_kernel,
        place,
        (rows // step,),
        [pl.BlockSpec((step, width), lambda i, place: (i, 0)), whole(gain)],
        pl.BlockSpec((count, step, width // count), lambda i, place: (0, i, 0)),
        shape_of(out, BF16),
        (hidden, gain),
        (4 * rows * width, 4 * rows * width),
    )


def pick_kernel(place, first, key, value, half, both):
    size = half.shape[1]
    half[...] = first[...]
    both[:, :size] = key[...]
    both[:, size:] = value[...]


def pick_columns(place, weight, size):
    depth = weight.shape[0]
    block = (depth, size)
    outs = [shape_of(block, BF16), shape_of((depth, 2 * size), BF16)]
    return call(
        pick_kernel,
        place,
        (1,),
        [
            pl.BlockSpec(block, lambda i, place: (0, 2 * place[HEAD] + place[GROUP])),
            pl.BlockSpec(block, lambda i, place: (0, 2 * place[HEAD])),
            pl.BlockSpec(block, lambda i, place: (0, 2 * place[HEAD] + 1)),
        ],
        [whole(out) for out in outs],
        outs,
        (weight, weight, weight),
        (0, 12 * depth * size),
        room=ALL,
    )


def query_kernel(count, place, rows, weight, *outs):
    block = rows.shape[1]
    left = jnp.concatenate([rows[place[SP] ^ d] for d in range(count)], axis=0)
    part = jnp.dot(left, weight[...], preferred_element_type=F32)
    for d in range(count):
        outs[d][...] = part[d * block : (d + 1) * block]


def query_parts(place, rows, weight):
    count, block, depth = rows.shape
    width = weight.shape[1]
    step = min(width, 256)
    return call(
        functools.partial(query_kernel, count),
        place,
        (width // step,),
        [whole(rows), pl.BlockSpec((depth, step), lambda i, place: (0, i))],
        [pl.BlockSpec((block, step), lambda i, place: (0, i))] * count,
        [shape_of((block, width), F32)] * count,
        (rows, weight),
        (2 * count * block * depth * width, 2 * depth * width),
    )


def turn(values, cosine, sine):
    return values * cosine + pltpu.roll(values, values.shape[-1] // 2, 1) * sine


def near_kernel(place, hidden, norm_gain, cont, own, partner, prompt, out):
    split_normed(hidden, norm_gain, prompt)
    total = 0.0
    for d, weight in ((0, own), (1, partner)):
        left = jnp.concatenate([prompt[place[SP] ^ d], cont[place[SP] ^ d]], axis=0)
        total = total + jnp.dot(left, weight[...], preferred_element_type=F32)
    out[...] = total


def near_keyval(place, hidden, norm_gain, cont, own, partner):
    args = (hidden, norm_gain, cont, own, partner)
    count, cont_rows, depth = cont.shape
    prompt_rows = hidden.shape[0]
    rows = prompt_rows + cont_rows
    width = own.shape[1]
    outs = [shape_of((count, prompt_rows, depth), BF16), shape_of((rows, width), F32)]
    return call(
        near_kernel,
        place,
        (1,),
        [whole(a) for a in args],
        [whole(out) for out in outs],
        outs,
        args,
        (4 * rows * depth * width, 4 * depth * (rows * count + width)),
    )


def keyval_kernel(count, place, prompt, cont, cosine, sine, gain, near, *refs):
    weights, out = refs[:-1], refs[-1]
    size = gain.shape[1]
    total = 0.0
    for d in range(2, count):
        left = jnp.concatenate([prompt[place[SP] ^ d], cont[place[SP] ^ d]], axis=0)
        weight = jnp.concatenate([weights[2 * d - 4][...], weights[2 * d - 3][...]], axis=1)
        total = total + jnp.dot(left, weight, preferred_element_type=F32)
    swapped = place[GROUP] == 1
    first, second = total[:, :size], total[:, size:]
    key = near[:, :size] + jnp.where(swapped, second, first)
    value = near[:, size:] + jnp.where(swapped, first, second)
    out[:, :size] = turn(rms_rows(key, gain[...]), cosine[...], sine[...]).astype(BF16)
    out[:, size:] = value.astype(BF16)


def keyval_rows(place, prompt, cont, cosine, sine, gain, near, weights):
    count, prompt_rows, depth = prompt.shape
    rows = prompt_rows + cont.shape[1]
    size = gain.shape[1]
    args = (prompt, cont, cosine, sine, gain, near, *weights)
    out = shape_of((rows, 2 * size), BF16)
    return call(
        functools.partial(keyval_kernel, count),
        place,
        (1,),
        [whole(a) for a in args],
        whole(out),
        out,
        args,
        (2 * rows * count * depth * size, count * depth * (rows + 2 * size)),
    )


def attend_kernel(count, prompt_rows, place, lengths, mine, other, cosine, sine, gain, *refs):
    pairs, out = refs[:-1], refs[-1]
    rows, width = mine.shape
    size = gain.shape[1]
    heads = width // size
    queries = []
    for h in range(heads):
        part = slice(h * size, (h + 1) * size)
        value = rms_rows(mine[:, part] + other[:, part], gain[...])
        queries.append(turn(value, cosine[...], sine[...]).astype(BF16))
    queries = jnp.concatenate(queries, axis=0)
    prompt = jnp.concatenate([pair[:prompt_rows] for pair in pairs], axis=0)
    cont = jnp.concatenate([pair[prompt_rows:] for pair in pairs], axis=0)
    scale = 1.0 / math.sqrt(size)
    by_rows = (((1,), (1,)), ((), ()))
    to_prompt = (
        lax.dot_general(queries, prompt[:, :size], by_rows, preferred_element_type=F32) * scale
    )
    to_cont = (
        lax.dot_general(queries, cont[:, :size], by_rows, preferred_element_type=F32) * scale
    )
    shape = (rows, cont.shape[0])
    own = place[SP] * rows + lax.broadcasted_iota(jnp.int32, shape, 0)
    at = lax.broadcasted_iota(jnp.int32, shape, 1)
    key = jnp.zeros(shape, jnp.int32)
    for d in range(count):
        inside = (at >= d * rows) & (at < (d + 1) * rows)
        key = jnp.where(inside, (place[SP] ^ d) * rows + at - d * rows, key)
    start = jnp.zeros(shape, jnp.int32)
    total = jnp.int32(0)
    for c in range(lengths.shape[0]):
        start = jnp.where(own >= total, total, start)
        total = total + lengths[c]
    allowed = jnp.where((key >= start) & (key <= own), 0.0, -1e30)
    to_cont = to_cont + jnp.concatenate([allowed] * heads, axis=0)
    peak = jnp.maximum(
        jnp.max(to_prompt, axis=1, keepdims=True), jnp.max(to_cont, axis=1, keepdims=True)
    )
    to_prompt = jnp.exp(to_prompt - peak)
    to_cont = jnp.exp(to_cont - peak)
    divisor = jnp.sum(to_prompt, axis=1, keepdims=True) + jnp.sum(to_cont, axis=1, keepdims=True)
    result = jnp.dot(
        (to_prompt / divisor).astype(BF16), prompt[:, size:], preferred_element_type=F32
    ) + jnp.dot((to_cont / divisor).astype(BF16), cont[:, size:], preferred_element_type=F32)
    for h in range(heads):
        out[:, h * size : (h + 1) * size] = result[h * rows : (h + 1) * rows].astype(BF16)


def attend(place, lengths, mine, other, cosine, sine, gain, pairs, prompt_rows):
    rows, width = mine.shape
    args = (mine, other, cosine, sine, gain, *pairs)
    out = shape_of((rows, width), BF16)
    keys = len(pairs) * pairs[0].shape[0]
    return call(
        functools.partial(attend_kernel, len(pairs), prompt_rows),
        place,
        (1,),
        [pl.BlockSpec(memory_space=pltpu.SMEM)] + [whole(a) for a in args],
        whole(out),
        out,
        (lengths, *args),
        (4 * rows * width * keys, 10 * rows * width + 512 * keys),
    )


def out_kernel(count, place, *refs):
    heads, weights, outs, part = refs[: 2 * count], refs[-count - 3 : -count - 1], refs[-count - 1 : -1], refs[-1]
    rows = heads[0].shape[0]
    total = 0.0
    for side, weight in enumerate(weights):
        left = jnp.concatenate([h[...] for h in heads[side * count : (side + 1) * count]], axis=0)
        share = jnp.dot(left, weight[...], preferred_element_type=F32)
        total = total + share.astype(BF16).astype(F32)
    total = total.astype(BF16)
    for d in range(count):
        part[d] = total[d * rows : (d + 1) * rows]
    for e in range(count):
        outs[e][...] = part[place[TP] ^ e ^ place[SP]]


def out_parts(place, heads, weights):
    count = len(heads) // 2
    rows = heads[0].shape[0]
    depth, width = weights[0].shape
    args = (*heads, *weights)
    return call(
        functools.partial(out_kernel, count),
        place,
        (1,),
        [whole(a) for a in args],
        [pl.BlockSpec((rows, width), lambda i, place: (0, 0))] * count,
        [shape_of((rows, width), BF16)] * count,
        args,
        (4 * count * rows * depth * width, 4 * depth * width),
        [pltpu.VMEM((count, rows, width), BF16)],
    )


def final_kernel(count, place, hidden, *refs):
    parts, out = refs[:-1], refs[-1]
    width = parts[0].shape[1]
    sums = [0.0, 0.0]
    for e, part in enumerate(parts):
        sums[e % 2] = sums[e % 2] + part[...].astype(F32)
    odd = place[SP] % 2 == 1
    left = jnp.where(odd, sums[1], sums[0])
    right = jnp.where(odd, sums[0], sums[1])
    out[:, :width] = (hidden[:, :width].astype(F32) + left).astype(BF16)
    out[:, width:] = (hidden[:, width:].astype(F32) + right).astype(BF16)


def final_sum(place, parts, hidden):
    rows, width = hidden.shape
    count = len(parts)
    return call(
        functools.partial(final_kernel, count),
        place,
        (1,),
        [whole(a) for a in (hidden, *parts)],
        whole(hidden),
        shape_of((rows, width), BF16),
        (hidden, *parts),
        (count * rows * width, 12 * rows * width),
    )


def after(arrays, *others):
    return lax.optimization_barrier((arrays, others))[0]


def swap(array, axis, bits):
    return lax.ppermute(array, axis, [(i, i ^ bits) for i in range(lax.axis_size(axis))])


def swap_both(array, tp_bits, sp_bits, count):
    pairs = [
        (t * count + s, (t ^ tp_bits) * count + (s ^ sp_bits))
        for t in range(count)
        for s in range(count)
    ]
    return lax.ppermute(array, ("tp", "sp"), pairs)


def swap_bits(count):
    bits = []
    bit = 1
    while bit < count:
        bits.append(bit)
        bit *= 2
    return bits


def gather_blocks(block, axis, count):
    held = {0: block}
    bits = swap_bits(count)
    for bit in bits[1:] + bits[:1]:
        held.update({d ^ bit: swap(held[d], axis, bit) for d in sorted(held)})
    return [held[d] for d in range(count)]


def other_halves(half, axis, count):
    firsts = {0: half}
    for bit in swap_bits(count)[1:]:
        firsts.update({d ^ bit: swap(firsts[d], axis, bit) for d in sorted(firsts)})
    del firsts[0]
    return firsts


def both_cores(held, axis):
    return {**held, **{d ^ 1: swap(held[d], axis, 1) for d in sorted(held)}}


def sum_blocks(blocks, axis, count):
    held = dict(enumerate(blocks))
    bits = swap_bits(count)
    for bit in bits:
        sent = [d for d in sorted(held) if d & bit]
        got = {d ^ bit: swap(held[d], axis, bit) for d in sent}
        if bit == bits[-1]:
            return held[0], got[0]
        held = {d: held[d] + got[d] for d in got}


def tables(positions, size):
    half = size // 2
    frequency = jnp.exp(jnp.arange(half, dtype=F32) * (-2.0 * math.log(1000000.0) / size))
    angles = positions.astype(F32)[:, None] * frequency[None, :]
    cosine = jnp.cos(angles)
    sine = jnp.sin(angles)
    return (
        jnp.concatenate([cosine, cosine], axis=1),
        jnp.concatenate([-sine, sine], axis=1),
    )


def on_device(
    hidden_cont,
    hidden_prompt,
    norm_gain,
    query_weight,
    keyval_weight,
    out_weight,
    query_gain,
    key_gain,
    sample_lengths,
):
    size = query_gain.shape[0]
    heads_here = query_weight.shape[1] // size
    cont_rows = hidden_cont.shape[0]
    prompt_rows = hidden_prompt.shape[0]
    sp_index = lax.axis_index("sp")
    sp_count = lax.axis_size("sp")
    tp_index = lax.axis_index("tp")
    assert lax.axis_size("tp") == sp_count and lax.axis_size("groups") == 2
    place = jnp.stack(
        [
            sp_index,
            tp_index,
            lax.axis_index("groups"),
            tp_index * heads_here // (QH // KVH),
        ]
    ).astype(jnp.int32)
    norm_gain = norm_gain[None, :]
    query_gain = query_gain[None, :]
    key_gain = key_gain[None, :]

    cont = norm_split(place, hidden_cont, norm_gain, sp_count)
    half, both = pick_columns(place, keyval_weight, size)
    cont_all = lax.all_to_all(cont, "sp", 0, 0, tiled=True)
    halves = other_halves(half, "sp", sp_count)
    partner = swap(both, "sp", 1)
    width = out_weight.shape[1]
    side = tp_index % 2
    out_early = after(out_weight, cont)
    sent = lax.dynamic_slice_in_dim(out_early, (1 - side) * (width // 2), width // 2, 1)
    out_weights = [
        lax.dynamic_slice_in_dim(out_early, side * (width // 2), width // 2, 1),
        swap(sent, "tp", 1),
    ]
    others = {d: swap(half, "groups", 1) for d, half in halves.items()}
    halves = both_cores(halves, "sp")
    prompt, near_pair = near_keyval(
        place,
        hidden_prompt,
        norm_gain,
        cont,
        both,
        after(partner, halves, sent, out_weights[0]),
    )
    cont_all = after(cont_all, near_pair, others)
    others = both_cores(others, "sp")

    index = sp_index * cont_rows + jnp.arange(cont_rows, dtype=jnp.int32)
    starts = jnp.cumsum(sample_lengths, dtype=jnp.int32) - sample_lengths
    start = jnp.max(jnp.where(index[:, None] >= starts[None, :], starts[None, :], 0), axis=1)
    prompt_pos = sp_index * prompt_rows + jnp.arange(prompt_rows, dtype=jnp.int32)
    positions = jnp.concatenate([prompt_pos, prompt_rows * sp_count + index - start])
    cosine, sine = tables(positions, size)

    parts = query_parts(place, cont_all, query_weight)
    mine, other = sum_blocks(parts, "sp", sp_count)
    weights = [held[d] for d in range(2, sp_count) for held in (halves, others)]
    pair = keyval_rows(place, prompt, cont, cosine, sine, key_gain, near_pair, weights)
    pairs = gather_blocks(pair, "sp", sp_count)
    heads = attend(
        place,
        sample_lengths,
        mine,
        other,
        cosine[prompt_rows:],
        sine[prompt_rows:],
        query_gain,
        pairs,
        prompt_rows,
    )
    chips = range(0, sp_count, 2)
    near_heads = {d: swap(heads, "sp", d) if d else heads for d in chips}
    far_heads = {d: swap_both(heads, 1, d, sp_count) for d in chips}
    near_heads = both_cores(near_heads, "sp")
    far_heads = both_cores(far_heads, "sp")
    all_heads = [held[d] for held in (near_heads, far_heads) for d in range(sp_count)]
    parts = out_parts(place, all_heads, out_weights)
    parts = [
        lax.ppermute(
            part,
            ("tp", "sp"),
            [
                (t * sp_count + s, s * sp_count + (t ^ e))
                for t in range(sp_count)
                for s in range(sp_count)
            ],
        )
        for e, part in enumerate(parts)
    ]
    hidden = lax.dynamic_slice_in_dim(hidden_cont, tp_index * width, width, 1)
    return final_sum(place, parts, hidden)


def solution(mesh):
    placed = (
        P(("groups", "sp"), None),
        P(("groups", "sp"), None),
        P(),
        P("sp", "tp"),
        P("sp", None),
        P("tp", "sp"),
        P(),
        P(),
        P("groups"),
    )
    return jax.shard_map(
        on_device, mesh=mesh, in_specs=placed, out_specs=P(("groups", "sp"), "tp"), check_vma=False
    )
```

profile of v0, /device:TPU:1, one launch (start us, length us, event | category | flops | bytes accessed | tf_op | source)
XLA Modules:
  0.0 82.8 jit_solution(12605238363362674811)
XLA Ops:
  0.6 3.1 %shard_map.92 = (bf16[1280,128]{1,0:T(8,128)(2,1)}, bf16[1280,256]{1,0:T(8,128)(2,1)}) custom-call(s32[4]{0:T(128)} %pad_add_fusion.place, bf16[1280,1024]{1,0:T(8,128)(2,1)} %value.1, bf16[1280,1024]{1,0:T(8,128)(2,1)} %value.1, bf16[1280,1024]{1,0:T(8,128)(2,1)} %value.1), custom_call_target="tpu_custom_call" | custom-call | bytes 1966080 | tf_op jit(solution)/shard_map/pallas_call | solution.py:22
  3.7 2.0 %collective-permute-start.1 = (bf16[1280,128]{1,0:T(8,128)(2,1)}, bf16[1280,128]{1,0:T(8,128)(2,1)}, u32[]{:S(2)}, u32[]{:S(2)}) collective-permute-start(bf16[1280,128]{1,0:T(8,128)(2,1)} %get-tuple-element.21), channel_id=1, source_target_pairs={{0,2},{1,3},{2,0},{3,1},{4,6},{5,7},{6,4},{7,5},{8,10},{9,11},{10,... | collective-permute-start | bytes 983048 | tf_op jit(solution)/shard_map/ppermute | solution.py:326
  6.7 1.8 %shard_map.91.cont = bf16[4,64,1280]{2,1,0:T(8,128)(2,1)} custom-call(s32[4]{0:T(128)S(1)} %copy-done.7, bf16[64,5120]{1,0:T(8,128)(2,1)S(1)} %copy-done.4, f32[1,5120]{1,0:T(1,128)S(1)} %bitcast.10), custom_call_target="tpu_custom_call" | custom-call | flops 1310720 | bytes 1310720 | tf_op jit(solution)/shard_map/pallas_call | solution.py:22
  8.5 3.5 %all-to-all-start = ((bf16[4,64,1280]{2,1,0:T(8,128)(2,1)}), bf16[4,64,1280]{2,1,0:T(8,128)(2,1)S(1)}, u32[]{:S(2)}, u32[]{:S(2)}) async-start(bf16[4,64,1280]{2,1,0:T(8,128)(2,1)} %shard_map.91.cont), calls=%async_computation | async-start | bytes 1310720 | tf_op jit(solution)/shard_map/all_to_all | solution.py:423
  12.0 3.1 %constant_dynamic-slice_fusion = (bf16[1024,640]{1,0:T(8,128)(2,1)S(1)}, bf16[1024,640]{1,0:T(8,128)(2,1)}) fusion(bf16[1024,1280]{1,0:T(8,128)(2,1)} %param.14, s32[]{:T(128)S(6)} %select_n.28, s32[]{:T(128)S(6)} %select_n.27), kind=kLoop, calls=%fused_computation.13 | loop fusion | bytes 5242888 | tf_op jit(solution)/shard_map/dynamic_slice | solution.py:431
  15.1 1.3 %collective-permute-start.18 = (bf16[1024,640]{1,0:T(8,128)(2,1)}, bf16[1024,640]{1,0:T(8,128)(2,1)}, u32[]{:S(2)}, u32[]{:S(2)}) collective-permute-start(bf16[1024,640]{1,0:T(8,128)(2,1)} %get-tuple-element.36), channel_id=1, source_target_pairs={{0,4},{4,0},{8,12},{12,8},{1,5},{5,1},{9,13},{13,9},{2,6},{6,2},{1... | collective-permute-start | bytes 3932168 | tf_op jit(solution)/shard_map/ppermute | solution.py:326
  17.1 1.3 %collective-permute-start.3 = (bf16[1280,128]{1,0:T(8,128)(2,1)}, bf16[1280,128]{1,0:T(8,128)(2,1)}, u32[]{:S(2)}, u32[]{:S(2)}) collective-permute-start(bf16[1280,128]{1,0:T(8,128)(2,1)} %collective-permute-done.1.refs_0_), channel_id=1, source_target_pairs={{0,16},{16,0},{1,17},{17,1},{2,18},{18,2},{3,19},{19,3},{4,20},{20... | collective-permute-start | bytes 983048 | tf_op jit(solution)/shard_map/ppermute | solution.py:326
  19.8 2.9 %shard_map.93 = (bf16[4,128,1280]{2,1,0:T(8,128)(2,1)S(1)}, f32[192,256]{1,0:T(8,128)S(1)}) custom-call(s32[4]{0:T(128)S(1)} %copy-done.7, bf16[128,5120]{1,0:T(8,128)(2,1)S(1)} %copy-done.1, f32[1,5120]{1,0:T(1,128)S(1)} %bitcast.11, bf16[4,64,1280]{2,1,0:T(8,128)(2,1)} %shard_map.91.cont, bf16[1280,256]{1,0:T(8,128)(2,1)S(1)} %copy-done.5, ...), custom_call_target="tpu_custom_call" | custom-call | flops 251658240 | bytes 5242880 | tf_op jit(solution)/shard_map/pallas_call | solution.py:22
  23.8 2.7 %collective-permute-done.3.refs_1_ = bf16[1280,128]{1,0:T(8,128)(2,1)} collective-permute-done((bf16[1280,128]{1,0:T(8,128)(2,1)}, bf16[1280,128]{1,0:T(8,128)(2,1)}, u32[]{:S(2)}, u32[]{:S(2)}) %collective-permute-start.3) | collective-permute-done | bytes 327712 | tf_op jit(solution)/shard_map/ppermute | solution.py:326
  26.5 1.7 %copy-done = bf16[1280,1024]{1,0:T(8,128)(2,1)S(1)} copy-done((bf16[1280,1024]{1,0:T(8,128)(2,1)S(1)}, bf16[1280,1024]{1,0:T(8,128)(2,1)}, u32[]{:S(2)}) %copy-start) | copy-done | bytes 2621464
  28.2 2.4 %shard_map.94 = (f32[64,1024]{1,0:T(8,128)S(1)}, f32[64,1024]{1,0:T(8,128)S(1)}, f32[64,1024]{1,0:T(8,128)S(1)}, f32[64,1024]{1,0:T(8,128)S(1)}) custom-call(s32[4]{0:T(128)S(1)} %copy-done.7, bf16[4,64,1280]{2,1,0:T(8,128)(2,1)S(1)} %all-to-all-done.rows, bf16[1280,1024]{1,0:T(8,128)(2,1)S(1)} %copy-done), custom_call_target="tpu_custom_call" | custom-call | flops 671088640 | bytes 2621440 | tf_op jit(solution)/shard_map/pallas_call | solution.py:22
  33.0 1.7 %collective-permute-start.6 = (f32[64,1024]{1,0:T(8,128)S(1)}, f32[64,1024]{1,0:T(8,128)S(1)}, u32[]{:S(2)}, u32[]{:S(2)}) collective-permute-start(f32[64,1024]{1,0:T(8,128)S(1)} %add.53), channel_id=1, source_target_pairs={{0,2},{1,3},{2,0},{3,1},{4,6},{5,7},{6,4},{7,5},{8,10},{9,11},{10,... | collective-permute-start | bytes 786440 | tf_op jit(solution)/shard_map/ppermute | solution.py:326
  34.9 2.5 %shard_map.95.refs_0_ = bf16[192,256]{1,0:T(8,128)(2,1)S(1)} custom-call(s32[4]{0:T(128)S(1)} %copy-done.7, bf16[4,128,1280]{2,1,0:T(8,128)(2,1)S(1)} %copy-done.3, bf16[4,64,1280]{2,1,0:T(8,128)(2,1)} %shard_map.91.cont, f32[192,128]{1,0:T(8,128)S(1)} %get-tuple-element.40.cosine, f32[192,128]{1,0:T(8,128)S(1)} %get-tuple-element.41.sine, ...), custom_call_target="tpu_custom_call" | custom-call | flops 251658240 | bytes 2293760 | tf_op jit(solution)/shard_map/pallas_call | solution.py:22
  38.5 4.7 %collective-permute-done.9.refs_2_ = bf16[192,256]{1,0:T(8,128)(2,1)S(1)} collective-permute-done((bf16[192,256]{1,0:T(8,128)(2,1)S(1)}, bf16[192,256]{1,0:T(8,128)(2,1)S(1)}, u32[]{:S(2)}, u32[]{:S(2)}) %collective-permute-start.9) | collective-permute-done | bytes 98336 | tf_op jit(solution)/shard_map/ppermute | solution.py:326
  45.0 3.0 %shard_map.96.refs_0_ = bf16[64,1024]{1,0:T(8,128)(2,1)S(1)} custom-call(s32[4]{0:T(128)S(1)} %copy-done.7, s32[8]{0:T(128)S(1)} %copy-done.9, f32[64,1024]{1,0:T(8,128)S(1)} %add.52.mine, f32[64,1024]{1,0:T(8,128)S(1)} %collective-permute-done.6.other, f32[64,128]{1,0:T(8,128)S(1)} %get-tuple-element.43.cosine, f32[64,128]{1,0:T(8,128)S(1)} %get-tuple-element.42.sine, ...), custom_call_target="tpu_custom_call" | custom-call | flops 201326592 | bytes 1048576 | tf_op jit(solution)/shard_map/pallas_call | solution.py:22
  48.0 1.5 %collective-permute-start.12 = (bf16[64,1024]{1,0:T(8,128)(2,1)S(1)}, bf16[64,1024]{1,0:T(8,128)(2,1)S(1)}, u32[]{:S(2)}, u32[]{:S(2)}) collective-permute-start(bf16[64,1024]{1,0:T(8,128)(2,1)S(1)} %shard_map.96.refs_0_), channel_id=1, source_target_pairs={{0,2},{1,3},{2,0},{3,1},{4,6},{5,7},{6,4},{7,5},{8,10},{9,11},{10,... | collective-permute-start | bytes 393224 | tf_op jit(solution)/shard_map/ppermute | solution.py:326
  54.0 2.6 %collective-permute-start.15 = (bf16[64,1024]{1,0:T(8,128)(2,1)S(1)}, bf16[64,1024]{1,0:T(8,128)(2,1)S(1)}, u32[]{:S(2)}, u32[]{:S(2)}) collective-permute-start(bf16[64,1024]{1,0:T(8,128)(2,1)S(1)} %collective-permute-done.14.refs_4_), channel_id=1, source_target_pairs={{0,1},{1,0},{2,3},{3,2},{4,5},{5,4},{6,7},{7,6},{8,9},{9,8},{10,11... | collective-permute-start | bytes 393224 | tf_op jit(solution)/shard_map/ppermute | solution.py:326
  56.6 1.4 %collective-permute-start.17 = (bf16[64,1024]{1,0:T(8,128)(2,1)S(1)}, bf16[64,1024]{1,0:T(8,128)(2,1)S(1)}, u32[]{:S(2)}, u32[]{:S(2)}) collective-permute-start(bf16[64,1024]{1,0:T(8,128)(2,1)S(1)} %collective-permute-done.16.refs_6_), channel_id=1, source_target_pairs={{0,1},{1,0},{2,3},{3,2},{4,5},{5,4},{6,7},{7,6},{8,9},{9,8},{10,11... | collective-permute-start | bytes 393224 | tf_op jit(solution)/shard_map/ppermute | solution.py:326
  59.0 2.9 %shard_map.97 = (bf16[64,640]{1,0:T(8,128)(2,1)S(1)}, bf16[64,640]{1,0:T(8,128)(2,1)S(1)}, bf16[64,640]{1,0:T(8,128)(2,1)S(1)}, bf16[64,640]{1,0:T(8,128)(2,1)S(1)}) custom-call(s32[4]{0:T(128)S(1)} %copy-done.7, bf16[64,1024]{1,0:T(8,128)(2,1)S(1)} %shard_map.96.refs_0_, bf16[64,1024]{1,0:T(8,128)(2,1)S(1)} %collective-permute-done.11.refs_1_, ...), custom_call_target="tpu_custom_call" | custom-call | flops 671088640 | bytes 2621440 | tf_op jit(solution)/shard_map/pallas_call | solution.py:22
  61.9 2.3 %collective-permute-start.19 = (bf16[64,640]{1,0:T(8,128)(2,1)S(1)}, bf16[64,640]{1,0:T(8,128)(2,1)S(1)}, u32[]{:S(2)}, u32[]{:S(2)}) collective-permute-start(bf16[64,640]{1,0:T(8,128)(2,1)S(1)} %get-tuple-element.31), channel_id=1, source_target_pairs={{0,0},{1,4},{2,8},{3,12},{4,1},{5,5},{6,9},{7,13},{8,2},{9,6},{10,... | collective-permute-start | bytes 245768 | tf_op jit(solution)/shard_map/ppermute | solution.py:478
  64.3 5.0 %collective-permute-start.21 = (bf16[64,640]{1,0:T(8,128)(2,1)S(1)}, bf16[64,640]{1,0:T(8,128)(2,1)S(1)}, u32[]{:S(2)}, u32[]{:S(2)}) collective-permute-start(bf16[64,640]{1,0:T(8,128)(2,1)S(1)} %get-tuple-element.33), channel_id=1, source_target_pairs={{0,2},{1,6},{2,10},{3,14},{4,3},{5,7},{6,11},{7,15},{8,0},{9,4},{1... | collective-permute-start | bytes 245768 | tf_op jit(solution)/shard_map/ppermute | solution.py:478
  70.7 4.4 %collective-permute-done.21.refs_2_ = bf16[64,640]{1,0:T(8,128)(2,1)S(1)} collective-permute-done((bf16[64,640]{1,0:T(8,128)(2,1)S(1)}, bf16[64,640]{1,0:T(8,128)(2,1)S(1)}, u32[]{:S(2)}, u32[]{:S(2)}) %collective-permute-start.21) | collective-permute-done | bytes 81952 | tf_op jit(solution)/shard_map/ppermute | solution.py:478
  75.1 6.4 %collective-permute-done.22.refs_3_ = bf16[64,640]{1,0:T(8,128)(2,1)S(1)} collective-permute-done((bf16[64,640]{1,0:T(8,128)(2,1)S(1)}, bf16[64,640]{1,0:T(8,128)(2,1)S(1)}, u32[]{:S(2)}, u32[]{:S(2)}) %collective-permute-start.22) | collective-permute-done | bytes 81952 | tf_op jit(solution)/shard_map/ppermute | solution.py:478
  81.5 1.3 %shard_map.98 = bf16[64,1280]{1,0:T(8,128)(2,1)} custom-call(s32[4]{0:T(128)S(1)} %copy-done.7, bf16[64,1280]{1,0:T(8,128)(2,1)S(1)} %constant_dynamic-slice_fusion.2.hidden, bf16[64,640]{1,0:T(8,128)(2,1)S(1)} %collective-permute-done.19.refs_0_, bf16[64,640]{1,0:T(8,128)(2,1)S(1)} %collective-permute-done.20.refs_1_, ...), custom_call_target="tpu_custom_call" | custom-call | flops 327680 | bytes 983040 | tf_op jit(solution)/shard_map/pallas_call | solution.py:22
  (70 shorter events, 16.9 us)
Async XLA Ops:
  3.7 13.0 %collective-permute-start.1 = (bf16[1280,128]{1,0:T(8,128)(2,1)}, bf16[1280,128]{1,0:T(8,128)(2,1)}, u32[]{:S(2)}, u32[]{:S(2)}) collective-permute-start(bf16[1280,128]{1,0:T(8,128)(2,1)} %get-tuple-element.21), channel_id=1, source_target_pairs={{0,2},{1,3},{2,0},{3,1},{4,6},{5,7},{6,4},{7,5},{8,10},{9,11},{10,... | collective-permute-start | bytes 983048 | tf_op jit(solution)/shard_map/ppermute | solution.py:326
  5.7 13.0 %collective-permute-start = (bf16[1280,256]{1,0:T(8,128)(2,1)}, bf16[1280,256]{1,0:T(8,128)(2,1)}, u32[]{:S(2)}, u32[]{:S(2)}) collective-permute-start(bf16[1280,256]{1,0:T(8,128)(2,1)} %get-tuple-element.20.own), channel_id=1, source_target_pairs={{0,1},{1,0},{2,3},{3,2},{4,5},{5,4},{6,7},{7,6},{8,9},{9,8},{10,11... | collective-permute-start | bytes 1966088 | tf_op jit(solution)/shard_map/ppermute | solution.py:326
  8.5 15.3 %all-to-all-start = ((bf16[4,64,1280]{2,1,0:T(8,128)(2,1)}), bf16[4,64,1280]{2,1,0:T(8,128)(2,1)S(1)}, u32[]{:S(2)}, u32[]{:S(2)}) async-start(bf16[4,64,1280]{2,1,0:T(8,128)(2,1)} %shard_map.91.cont), calls=%async_computation | async-start | bytes 1310720 | tf_op jit(solution)/shard_map/all_to_all | solution.py:423
  15.1 42.9 %collective-permute-start.18 = (bf16[1024,640]{1,0:T(8,128)(2,1)}, bf16[1024,640]{1,0:T(8,128)(2,1)}, u32[]{:S(2)}, u32[]{:S(2)}) collective-permute-start(bf16[1024,640]{1,0:T(8,128)(2,1)} %get-tuple-element.36), channel_id=1, source_target_pairs={{0,4},{4,0},{8,12},{12,8},{1,5},{5,1},{9,13},{13,9},{2,6},{6,2},{1... | collective-permute-start | bytes 3932168 | tf_op jit(solution)/shard_map/ppermute | solution.py:326
  16.7 2.0 %collective-permute-start.2 = (bf16[1280,128]{1,0:T(8,128)(2,1)}, bf16[1280,128]{1,0:T(8,128)(2,1)}, u32[]{:S(2)}, u32[]{:S(2)}) collective-permute-start(bf16[1280,128]{1,0:T(8,128)(2,1)} %collective-permute-done.1.refs_0_), channel_id=1, source_target_pairs={{0,1},{1,0},{2,3},{3,2},{4,5},{5,4},{6,7},{7,6},{8,9},{9,8},{10,11... | collective-permute-start | bytes 983048 | tf_op jit(solution)/shard_map/ppermute | solution.py:326
  17.1 9.4 %collective-permute-start.3 = (bf16[1280,128]{1,0:T(8,128)(2,1)}, bf16[1280,128]{1,0:T(8,128)(2,1)}, u32[]{:S(2)}, u32[]{:S(2)}) collective-permute-start(bf16[1280,128]{1,0:T(8,128)(2,1)} %collective-permute-done.1.refs_0_), channel_id=1, source_target_pairs={{0,16},{16,0},{1,17},{17,1},{2,18},{18,2},{3,19},{19,3},{4,20},{20... | collective-permute-start | bytes 983048 | tf_op jit(solution)/shard_map/ppermute | solution.py:326
  30.7 2.2 %collective-permute-start.5 = (f32[64,1024]{1,0:T(8,128)S(1)}, f32[64,1024]{1,0:T(8,128)S(1)}, u32[]{:S(2)}, u32[]{:S(2)}) collective-permute-start(f32[64,1024]{1,0:T(8,128)S(1)} %get-tuple-element.29), channel_id=1, source_target_pairs={{0,1},{1,0},{2,3},{3,2},{4,5},{5,4},{6,7},{7,6},{8,9},{9,8},{10,11... | collective-permute-start | bytes 786440 | tf_op jit(solution)/shard_map/ppermute | solution.py:326
  31.8 3.1 %collective-permute-start.7 = (bf16[1280,128]{1,0:T(8,128)(2,1)}, bf16[1280,128]{1,0:T(8,128)(2,1)S(1)}, u32[]{:S(2)}, u32[]{:S(2)}) collective-permute-start(bf16[1280,128]{1,0:T(8,128)(2,1)} %collective-permute-done.3.refs_1_), channel_id=1, source_target_pairs={{0,1},{1,0},{2,3},{3,2},{4,5},{5,4},{6,7},{7,6},{8,9},{9,8},{10,11... | collective-permute-start | bytes 983048 | tf_op jit(solution)/shard_map/ppermute | solution.py:326
  32.3 11.9 %collective-permute-start.4 = (f32[64,1024]{1,0:T(8,128)S(1)}, f32[64,1024]{1,0:T(8,128)S(1)}, u32[]{:S(2)}, u32[]{:S(2)}) collective-permute-start(f32[64,1024]{1,0:T(8,128)S(1)} %get-tuple-element.27), channel_id=1, source_target_pairs={{0,1},{1,0},{2,3},{3,2},{4,5},{5,4},{6,7},{7,6},{8,9},{9,8},{10,11... | collective-permute-start | bytes 786440 | tf_op jit(solution)/shard_map/ppermute | solution.py:326
  33.0 11.3 %collective-permute-start.6 = (f32[64,1024]{1,0:T(8,128)S(1)}, f32[64,1024]{1,0:T(8,128)S(1)}, u32[]{:S(2)}, u32[]{:S(2)}) collective-permute-start(f32[64,1024]{1,0:T(8,128)S(1)} %add.53), channel_id=1, source_target_pairs={{0,2},{1,3},{2,0},{3,1},{4,6},{5,7},{6,4},{7,5},{8,10},{9,11},{10,... | collective-permute-start | bytes 786440 | tf_op jit(solution)/shard_map/ppermute | solution.py:326
  37.4 5.8 %collective-permute-start.9 = (bf16[192,256]{1,0:T(8,128)(2,1)S(1)}, bf16[192,256]{1,0:T(8,128)(2,1)S(1)}, u32[]{:S(2)}, u32[]{:S(2)}) collective-permute-start(bf16[192,256]{1,0:T(8,128)(2,1)S(1)} %shard_map.95.refs_0_), channel_id=1, source_target_pairs={{0,2},{1,3},{2,0},{3,1},{4,6},{5,7},{6,4},{7,5},{8,10},{9,11},{10,... | collective-permute-start | bytes 294920 | tf_op jit(solution)/shard_map/ppermute | solution.py:326
  37.9 6.3 %collective-permute-start.8 = (bf16[192,256]{1,0:T(8,128)(2,1)S(1)}, bf16[192,256]{1,0:T(8,128)(2,1)S(1)}, u32[]{:S(2)}, u32[]{:S(2)}) collective-permute-start(bf16[192,256]{1,0:T(8,128)(2,1)S(1)} %shard_map.95.refs_0_), channel_id=1, source_target_pairs={{0,1},{1,0},{2,3},{3,2},{4,5},{5,4},{6,7},{7,6},{8,9},{9,8},{10,11... | collective-permute-start | bytes 294920 | tf_op jit(solution)/shard_map/ppermute | solution.py:326
  43.2 1.8 %collective-permute-start.10 = (bf16[192,256]{1,0:T(8,128)(2,1)S(1)}, bf16[192,256]{1,0:T(8,128)(2,1)S(1)}, u32[]{:S(2)}, u32[]{:S(2)}) collective-permute-start(bf16[192,256]{1,0:T(8,128)(2,1)S(1)} %collective-permute-done.9.refs_2_), channel_id=1, source_target_pairs={{0,1},{1,0},{2,3},{3,2},{4,5},{5,4},{6,7},{7,6},{8,9},{9,8},{10,11... | collective-permute-start | bytes 294920 | tf_op jit(solution)/shard_map/ppermute | solution.py:326
  48.0 4.8 %collective-permute-start.12 = (bf16[64,1024]{1,0:T(8,128)(2,1)S(1)}, bf16[64,1024]{1,0:T(8,128)(2,1)S(1)}, u32[]{:S(2)}, u32[]{:S(2)}) collective-permute-start(bf16[64,1024]{1,0:T(8,128)(2,1)S(1)} %shard_map.96.refs_0_), channel_id=1, source_target_pairs={{0,2},{1,3},{2,0},{3,1},{4,6},{5,7},{6,4},{7,5},{8,10},{9,11},{10,... | collective-permute-start | bytes 393224 | tf_op jit(solution)/shard_map/ppermute | solution.py:326
  49.5 4.5 %collective-permute-start.14 = (bf16[64,1024]{1,0:T(8,128)(2,1)S(1)}, bf16[64,1024]{1,0:T(8,128)(2,1)S(1)}, u32[]{:S(2)}, u32[]{:S(2)}) collective-permute-start(bf16[64,1024]{1,0:T(8,128)(2,1)S(1)} %shard_map.96.refs_0_), channel_id=1, source_target_pairs={{0,4},{1,5},{2,6},{3,7},{4,0},{5,1},{6,2},{7,3},{8,12},{9,13},{10,... | collective-permute-start | bytes 393224 | tf_op jit(solution)/shard_map/ppermute | solution.py:335
  49.7 6.9 %collective-permute-start.16 = (bf16[64,1024]{1,0:T(8,128)(2,1)S(1)}, bf16[64,1024]{1,0:T(8,128)(2,1)S(1)}, u32[]{:S(2)}, u32[]{:S(2)}) collective-permute-start(bf16[64,1024]{1,0:T(8,128)(2,1)S(1)} %shard_map.96.refs_0_), channel_id=1, source_target_pairs={{0,6},{1,7},{2,4},{3,5},{4,2},{5,3},{6,0},{7,1},{8,14},{9,15},{10,... | collective-permute-start | bytes 393224 | tf_op jit(solution)/shard_map/ppermute | solution.py:335
  50.8 7.3 %collective-permute-start.11 = (bf16[64,1024]{1,0:T(8,128)(2,1)S(1)}, bf16[64,1024]{1,0:T(8,128)(2,1)S(1)}, u32[]{:S(2)}, u32[]{:S(2)}) collective-permute-start(bf16[64,1024]{1,0:T(8,128)(2,1)S(1)} %shard_map.96.refs_0_), channel_id=1, source_target_pairs={{0,1},{1,0},{2,3},{3,2},{4,5},{5,4},{6,7},{7,6},{8,9},{9,8},{10,11... | collective-permute-start | bytes 393224 | tf_op jit(solution)/shard_map/ppermute | solution.py:326
  52.8 5.3 %collective-permute-start.13 = (bf16[64,1024]{1,0:T(8,128)(2,1)S(1)}, bf16[64,1024]{1,0:T(8,128)(2,1)S(1)}, u32[]{:S(2)}, u32[]{:S(2)}) collective-permute-start(bf16[64,1024]{1,0:T(8,128)(2,1)S(1)} %collective-permute-done.12.refs_2_), channel_id=1, source_target_pairs={{0,1},{1,0},{2,3},{3,2},{4,5},{5,4},{6,7},{7,6},{8,9},{9,8},{10,11... | collective-permute-start | bytes 393224 | tf_op jit(solution)/shard_map/ppermute | solution.py:326
  54.0 4.1 %collective-permute-start.15 = (bf16[64,1024]{1,0:T(8,128)(2,1)S(1)}, bf16[64,1024]{1,0:T(8,128)(2,1)S(1)}, u32[]{:S(2)}, u32[]{:S(2)}) collective-permute-start(bf16[64,1024]{1,0:T(8,128)(2,1)S(1)} %collective-permute-done.14.refs_4_), channel_id=1, source_target_pairs={{0,1},{1,0},{2,3},{3,2},{4,5},{5,4},{6,7},{7,6},{8,9},{9,8},{10,11... | collective-permute-start | bytes 393224 | tf_op jit(solution)/shard_map/ppermute | solution.py:326
  56.6 2.4 %collective-permute-start.17 = (bf16[64,1024]{1,0:T(8,128)(2,1)S(1)}, bf16[64,1024]{1,0:T(8,128)(2,1)S(1)}, u32[]{:S(2)}, u32[]{:S(2)}) collective-permute-start(bf16[64,1024]{1,0:T(8,128)(2,1)S(1)} %collective-permute-done.16.refs_6_), channel_id=1, source_target_pairs={{0,1},{1,0},{2,3},{3,2},{4,5},{5,4},{6,7},{7,6},{8,9},{9,8},{10,11... | collective-permute-start | bytes 393224 | tf_op jit(solution)/shard_map/ppermute | solution.py:326
  61.9 8.8 %collective-permute-start.19 = (bf16[64,640]{1,0:T(8,128)(2,1)S(1)}, bf16[64,640]{1,0:T(8,128)(2,1)S(1)}, u32[]{:S(2)}, u32[]{:S(2)}) collective-permute-start(bf16[64,640]{1,0:T(8,128)(2,1)S(1)} %get-tuple-element.31), channel_id=1, source_target_pairs={{0,0},{1,4},{2,8},{3,12},{4,1},{5,5},{6,9},{7,13},{8,2},{9,6},{10,... | collective-permute-start | bytes 245768 | tf_op jit(solution)/shard_map/ppermute | solution.py:478
  64.2 6.4 %collective-permute-start.20 = (bf16[64,640]{1,0:T(8,128)(2,1)S(1)}, bf16[64,640]{1,0:T(8,128)(2,1)S(1)}, u32[]{:S(2)}, u32[]{:S(2)}) collective-permute-start(bf16[64,640]{1,0:T(8,128)(2,1)S(1)} %get-tuple-element.32), channel_id=1, source_target_pairs={{0,1},{1,5},{2,9},{3,13},{4,0},{5,4},{6,8},{7,12},{8,3},{9,7},{10,... | collective-permute-start | bytes 245768 | tf_op jit(solution)/shard_map/ppermute | solution.py:478
  64.3 10.8 %collective-permute-start.21 = (bf16[64,640]{1,0:T(8,128)(2,1)S(1)}, bf16[64,640]{1,0:T(8,128)(2,1)S(1)}, u32[]{:S(2)}, u32[]{:S(2)}) collective-permute-start(bf16[64,640]{1,0:T(8,128)(2,1)S(1)} %get-tuple-element.33), channel_id=1, source_target_pairs={{0,2},{1,6},{2,10},{3,14},{4,3},{5,7},{6,11},{7,15},{8,0},{9,4},{1... | collective-permute-start | bytes 245768 | tf_op jit(solution)/shard_map/ppermute | solution.py:478
  69.3 12.2 %collective-permute-start.22 = (bf16[64,640]{1,0:T(8,128)(2,1)S(1)}, bf16[64,640]{1,0:T(8,128)(2,1)S(1)}, u32[]{:S(2)}, u32[]{:S(2)}) collective-permute-start(bf16[64,640]{1,0:T(8,128)(2,1)S(1)} %get-tuple-element.34), channel_id=1, source_target_pairs={{0,3},{1,7},{2,11},{3,15},{4,2},{5,6},{6,10},{7,14},{8,1},{9,5},{1... | collective-permute-start | bytes 245768 | tf_op jit(solution)/shard_map/ppermute | solution.py:478
  (11 other events, 52.0 us)
where the time goes:
time: 83.2 us; the launch traced here: 82.8 us
  starting transfers between devices  31.7 us (38%)
  waiting for transfers between devices  21.4 us (26%)
  Pallas kernels  19.8 us (24%)
  local copies, waits for them, and re-layouts  7.96 us (10%)
  other arithmetic  1.58 us (2%)
    pallas_call x8, Pallas kernels, call(): pl.pallas_call(kernel, out_shape=out_shape, grid_spec=pltpu.PrefetchScala...  19.8 us
    ppermute x17, starting transfers between devices, swap(): lax.ppermute(array, axis, [(i, i ^ bits) for i in range(lax.axis_size(axi...  19.2 us
    ppermute x4, waiting for transfers between devices, on_device(): lax.ppermute(part, ('tp', 'sp'), [(t * sp_count + s, s * sp_count + (t ^...  10.8 us
    ppermute x17, waiting for transfers between devices, swap(): lax.ppermute(array, axis, [(i, i ^ bits) for i in range(lax.axis_size(axi...  10.5 us
    ppermute x4, starting transfers between devices, on_device(): lax.ppermute(part, ('tp', 'sp'), [(t * sp_count + s, s * sp_count + (t ^...  7.8 us
    unnamed x22, local copies, waits for them, and re-layouts  3.92 us
    all_to_all x1, starting transfers between devices, on_device(): cont_all = lax.all_to_all(cont, 'sp', 0, 0, tiled=True)  3.47 us
    dynamic_slice x1, local copies, waits for them, and re-layouts, on_device(): lax.dynamic_slice_in_dim(out_early, side * (width // 2), width // 2, 1)  3.11 us
  transfers between devices with their start and end apart: 24, of which 10 were waited for; matrix products, arithmetic and copies ran while one was open for 6% of the time, Pallas kernels for 15%

commit v1 on v0

--- a/solution.py
+++ b/solution.py
@@ -13,8 +13,7 @@
 SP, TP, GROUP, HEAD = range(4)
 BF16 = jnp.bfloat16
 F32 = jnp.float32
-ROOM = 24 * 1024 * 1024
-ALL = 62 * 1024 * 1024
+ROOM = 14 * 1024 * 1024
 
 
 def call(kernel, place, grid, in_specs, out_specs, out_shape, args, cost, scratch=(), room=ROOM):
@@ -98,7 +97,6 @@
         outs,
         (weight, weight, weight),
         (0, 12 * depth * size),
-        room=ALL,
     )
 
 
@@ -272,16 +270,21 @@
         outs[e][...] = part[place[TP] ^ e ^ place[SP]]
 
 
-def out_parts(place, heads, weights):
+def out_parts(place, heads, own, partner):
     count = len(heads) // 2
     rows = heads[0].shape[0]
-    depth, width = weights[0].shape
-    args = (*heads, *weights)
+    depth, width = partner.shape
+    if width % 128:
+        own = lax.dynamic_slice_in_dim(own, place[TP] % 2 * width, width, 1)
+        half = whole(own)
+    else:
+        half = pl.BlockSpec((depth, width), lambda i, place: (0, place[TP] % 2))
+    args = (*heads, own, partner)
     return call(
         functools.partial(out_kernel, count),
         place,
         (1,),
-        [whole(a) for a in args],
+        [whole(h) for h in heads] + [half, whole(partner)],
         [pl.BlockSpec((rows, width), lambda i, place: (0, 0))] * count,
         [shape_of((rows, width), BF16)] * count,
         args,
@@ -427,10 +430,7 @@
     side = tp_index % 2
     out_early = after(out_weight, cont)
     sent = lax.dynamic_slice_in_dim(out_early, (1 - side) * (width // 2), width // 2, 1)
-    out_weights = [
-        lax.dynamic_slice_in_dim(out_early, side * (width // 2), width // 2, 1),
-        swap(sent, "tp", 1),
-    ]
+    out_partner = swap(sent, "tp", 1)
     others = {d: swap(half, "groups", 1) for d, half in halves.items()}
     halves = both_cores(halves, "sp")
     prompt, near_pair = near_keyval(
@@ -439,7 +439,7 @@
         norm_gain,
         cont,
         both,
-        after(partner, halves, sent, out_weights[0]),
+        after(partner, halves, sent),
     )
     cont_all = after(cont_all, near_pair, others)
     others = both_cores(others, "sp")
@@ -473,7 +473,7 @@
     near_heads = both_cores(near_heads, "sp")
     far_heads = both_cores(far_heads, "sp")
     all_heads = [held[d] for held in (near_heads, far_heads) for d in range(sp_count)]
-    parts = out_parts(place, all_heads, out_weights)
+    parts = out_parts(place, all_heads, out_weight, out_partner)
     parts = [
         lax.ppermute(
             part,

time: 83.2 us -> 82.9 us (level)
  waiting for transfers between devices: 21.4 us -> 22.5 us
  Pallas kernels: 19.8 us -> 18.9 us
    unnamed x22, local copies, waits for them, and re-layouts: 3.92 us -> 5.89 us
    dynamic_slice x1, local copies, waits for them, and re-layouts: 3.11 us -> 1.19 us  [on_device(): lax.dynamic_slice_in_dim(out_early, (1 - side) * (width // 2), width // 2...]
    ppermute x4, waiting for transfers between devices: 10.8 us -> 12 us  [on_device(): lax.ppermute(part, ('tp', 'sp'), [(t * sp_count + s, s * sp_count + (t ^...]
    pallas_call x8, Pallas kernels: 19.8 us -> 18.9 us  [call(): pl.pallas_call(kernel, out_shape=out_shape, grid_spec=pltpu.PrefetchScala...]
  transfers between devices with their start and end apart: 24 -> 24, of which waited for: 10 -> 10; matrix products, arithmetic and copies ran while one was open for 6% -> 4% of each run, Pallas kernels for 15% -> 15%
where the time goes in v1:
time: 82.9 us; the launch traced here: 82.5 us
  starting transfers between devices  31.7 us (38%)
  waiting for transfers between devices  22.5 us (27%)
  Pallas kernels  18.9 us (23%)
  local copies, waits for them, and re-layouts  8.01 us (10%)
  other arithmetic  1.07 us (1%)
    ppermute x17, starting transfers between devices, swap(): lax.ppermute(array, axis, [(i, i ^ bits) for i in range(lax.axis_size(axi...  19.1 us
    pallas_call x8, Pallas kernels, call(): pl.pallas_call(kernel, out_shape=out_shape, grid_spec=pltpu.PrefetchScala...  18.9 us
    ppermute x4, waiting for transfers between devices, on_device(): lax.ppermute(part, ('tp', 'sp'), [(t * sp_count + s, s * sp_count + (t ^...  12 us
    ppermute x17, waiting for transfers between devices, swap(): lax.ppermute(array, axis, [(i, i ^ bits) for i in range(lax.axis_size(axi...  10.4 us
    ppermute x4, starting transfers between devices, on_device(): lax.ppermute(part, ('tp', 'sp'), [(t * sp_count + s, s * sp_count + (t ^...  7.8 us
    unnamed x22, local copies, waits for them, and re-layouts  5.89 us
    all_to_all x1, starting transfers between devices, on_device(): cont_all = lax.all_to_all(cont, 'sp', 0, 0, tiled=True)  3.47 us
  transfers between devices with their start and end apart: 24, of which 10 were waited for; matrix products, arithmetic and copies ran while one was open for 4% of the time, Pallas kernels for 15%

profile of v1, /device:TPU:1, one launch (start us, length us, event | category | flops | bytes accessed | tf_op | source)
XLA Modules:
  0.0 82.5 jit_solution(17208563927484389302)
XLA Ops:
  0.1 1.7 %copy-done = bf16[1280,1024]{1,0:T(8,128)(2,1)S(1)} copy-done((bf16[1280,1024]{1,0:T(8,128)(2,1)S(1)}, bf16[1280,1024]{1,0:T(8,128)(2,1)}, u32[]{:S(2)}) %copy-start) | copy-done | bytes 2621464
  1.8 1.9 %shard_map.92 = (bf16[1280,128]{1,0:T(8,128)(2,1)}, bf16[1280,256]{1,0:T(8,128)(2,1)}) custom-call(s32[4]{0:T(128)S(1)} %pad_add_fusion.place, bf16[1280,1024]{1,0:T(8,128)(2,1)S(1)} %copy-done, bf16[1280,1024]{1,0:T(8,128)(2,1)S(1)} %copy-done, bf16[1280,1024]{1,0:T(8,128)(2,1)S(1)} %copy-done), custom_call_target="tpu_custom_call" | custom-call | bytes 1966080 | tf_op jit(solution)/shard_map/pallas_call | solution.py:21
  3.7 2.0 %collective-permute-start.1 = (bf16[1280,128]{1,0:T(8,128)(2,1)}, bf16[1280,128]{1,0:T(8,128)(2,1)}, u32[]{:S(2)}, u32[]{:S(2)}) collective-permute-start(bf16[1280,128]{1,0:T(8,128)(2,1)} %get-tuple-element.21), channel_id=1, source_target_pairs={{0,2},{1,3},{2,0},{3,1},{4,6},{5,7},{6,4},{7,5},{8,10},{9,11},{10,... | collective-permute-start | bytes 983048 | tf_op jit(solution)/shard_map/ppermute | solution.py:329
  6.7 1.8 %shard_map.91.cont = bf16[4,64,1280]{2,1,0:T(8,128)(2,1)} custom-call(s32[4]{0:T(128)S(1)} %pad_add_fusion.place, bf16[64,5120]{1,0:T(8,128)(2,1)S(1)} %copy-done.6, f32[1,5120]{1,0:T(1,128)S(1)} %bitcast.10), custom_call_target="tpu_custom_call" | custom-call | flops 1310720 | bytes 1310720 | tf_op jit(solution)/shard_map/pallas_call | solution.py:21
  8.5 3.5 %all-to-all-start = ((bf16[4,64,1280]{2,1,0:T(8,128)(2,1)}), bf16[4,64,1280]{2,1,0:T(8,128)(2,1)S(1)}, u32[]{:S(2)}, u32[]{:S(2)}) async-start(bf16[4,64,1280]{2,1,0:T(8,128)(2,1)} %shard_map.91.cont), calls=%async_computation | async-start | bytes 1310720 | tf_op jit(solution)/shard_map/all_to_all | solution.py:426
  13.2 1.3 %collective-permute-start.18 = (bf16[1024,640]{1,0:T(8,128)(2,1)}, bf16[1024,640]{1,0:T(8,128)(2,1)}, u32[]{:S(2)}, u32[]{:S(2)}) collective-permute-start(bf16[1024,640]{1,0:T(8,128)(2,1)} %constant_dynamic-slice_fusion), channel_id=1, source_target_pairs={{0,4},{4,0},{8,12},{12,8},{1,5},{5,1},{9,13},{13,9},{2,6},{6,2},{1... | collective-permute-start | bytes 3932168 | tf_op jit(solution)/shard_map/ppermute | solution.py:329
  16.8 1.3 %copy-done.3 = bf16[128,5120]{1,0:T(8,128)(2,1)S(1)} copy-done((bf16[128,5120]{1,0:T(8,128)(2,1)S(1)}, bf16[128,5120]{1,0:T(8,128)(2,1)}, u32[]{:S(2)}) %copy-start.3) | copy-done | bytes 1310744
  18.1 3.1 %shard_map.93 = (bf16[4,128,1280]{2,1,0:T(8,128)(2,1)S(1)}, f32[192,256]{1,0:T(8,128)S(1)}) custom-call(s32[4]{0:T(128)S(1)} %pad_add_fusion.place, bf16[128,5120]{1,0:T(8,128)(2,1)S(1)} %copy-done.3, f32[1,5120]{1,0:T(1,128)S(1)} %bitcast.11, bf16[4,64,1280]{2,1,0:T(8,128)(2,1)} %shard_map.91.cont, bf16[1280,256]{1,0:T(8,128)(2,1)} %get-tuple-element.20.own, ...), custom_call_target="tpu_custom_call" | custom-call | flops 251658240 | bytes 5242880 | tf_op jit(solution)/shard_map/pallas_call | solution.py:21
  22.3 2.3 %collective-permute-done.3.refs_1_ = bf16[1280,128]{1,0:T(8,128)(2,1)} collective-permute-done((bf16[1280,128]{1,0:T(8,128)(2,1)}, bf16[1280,128]{1,0:T(8,128)(2,1)}, u32[]{:S(2)}, u32[]{:S(2)}) %collective-permute-start.3) | collective-permute-done | bytes 327712 | tf_op jit(solution)/shard_map/ppermute | solution.py:329
  24.6 1.7 %copy-done.2 = bf16[1280,1024]{1,0:T(8,128)(2,1)S(1)} copy-done((bf16[1280,1024]{1,0:T(8,128)(2,1)S(1)}, bf16[1280,1024]{1,0:T(8,128)(2,1)}, u32[]{:S(2)}) %copy-start.2) | copy-done | bytes 2621464
  26.3 2.4 %shard_map.94 = (f32[64,1024]{1,0:T(8,128)S(1)}, f32[64,1024]{1,0:T(8,128)S(1)}, f32[64,1024]{1,0:T(8,128)S(1)}, f32[64,1024]{1,0:T(8,128)S(1)}) custom-call(s32[4]{0:T(128)S(1)} %pad_add_fusion.place, bf16[4,64,1280]{2,1,0:T(8,128)(2,1)S(1)} %all-to-all-done.rows, bf16[1280,1024]{1,0:T(8,128)(2,1)S(1)} %copy-done.2), custom_call_target="tpu_custom_call" | custom-call | flops 671088640 | bytes 2621440 | tf_op jit(solution)/shard_map/pallas_call | solution.py:21
  31.0 1.9 %collective-permute-start.6 = (f32[64,1024]{1,0:T(8,128)S(1)}, f32[64,1024]{1,0:T(8,128)S(1)}, u32[]{:S(2)}, u32[]{:S(2)}) collective-permute-start(f32[64,1024]{1,0:T(8,128)S(1)} %add.49), channel_id=1, source_target_pairs={{0,2},{1,3},{2,0},{3,1},{4,6},{5,7},{6,4},{7,5},{8,10},{9,11},{10,... | collective-permute-start | bytes 786440 | tf_op jit(solution)/shard_map/ppermute | solution.py:329
  33.1 2.5 %shard_map.95.refs_0_ = bf16[192,256]{1,0:T(8,128)(2,1)S(1)} custom-call(s32[4]{0:T(128)S(1)} %pad_add_fusion.place, bf16[4,128,1280]{2,1,0:T(8,128)(2,1)S(1)} %copy-done.5, bf16[4,64,1280]{2,1,0:T(8,128)(2,1)} %shard_map.91.cont, f32[192,128]{1,0:T(8,128)S(1)} %get-tuple-element.38.cosine, f32[192,128]{1,0:T(8,128)S(1)} %get-tuple-element.39.sine, ...), custom_call_target="tpu_custom_call" | custom-call | flops 251658240 | bytes 2293760 | tf_op jit(solution)/shard_map/pallas_call | solution.py:21
  36.7 4.8 %collective-permute-done.9.refs_2_ = bf16[192,256]{1,0:T(8,128)(2,1)S(1)} collective-permute-done((bf16[192,256]{1,0:T(8,128)(2,1)S(1)}, bf16[192,256]{1,0:T(8,128)(2,1)S(1)}, u32[]{:S(2)}, u32[]{:S(2)}) %collective-permute-start.9) | collective-permute-done | bytes 98336 | tf_op jit(solution)/shard_map/ppermute | solution.py:329
  43.2 3.0 %shard_map.96.refs_0_ = bf16[64,1024]{1,0:T(8,128)(2,1)S(1)} custom-call(s32[4]{0:T(128)S(1)} %pad_add_fusion.place, s32[8]{0:T(128)S(1)} %copy-done.9, f32[64,1024]{1,0:T(8,128)S(1)} %add.48.mine, f32[64,1024]{1,0:T(8,128)S(1)} %collective-permute-done.6.other, f32[64,128]{1,0:T(8,128)S(1)} %get-tuple-element.41.cosine, ...), custom_call_target="tpu_custom_call" | custom-call | flops 201326592 | bytes 1048576 | tf_op jit(solution)/shard_map/pallas_call | solution.py:21
  46.2 1.5 %collective-permute-start.12 = (bf16[64,1024]{1,0:T(8,128)(2,1)S(1)}, bf16[64,1024]{1,0:T(8,128)(2,1)S(1)}, u32[]{:S(2)}, u32[]{:S(2)}) collective-permute-start(bf16[64,1024]{1,0:T(8,128)(2,1)S(1)} %shard_map.96.refs_0_), channel_id=1, source_target_pairs={{0,2},{1,3},{2,0},{3,1},{4,6},{5,7},{6,4},{7,5},{8,10},{9,11},{10,... | collective-permute-start | bytes 393224 | tf_op jit(solution)/shard_map/ppermute | solution.py:329
  47.7 1.3 %collective-permute-start.14 = (bf16[64,1024]{1,0:T(8,128)(2,1)S(1)}, bf16[64,1024]{1,0:T(8,128)(2,1)S(1)}, u32[]{:S(2)}, u32[]{:S(2)}) collective-permute-start(bf16[64,1024]{1,0:T(8,128)(2,1)S(1)} %shard_map.96.refs_0_), channel_id=1, source_target_pairs={{0,4},{1,5},{2,6},{3,7},{4,0},{5,1},{6,2},{7,3},{8,12},{9,13},{10,... | collective-permute-start | bytes 393224 | tf_op jit(solution)/shard_map/ppermute | solution.py:338
  52.2 2.6 %collective-permute-start.15 = (bf16[64,1024]{1,0:T(8,128)(2,1)S(1)}, bf16[64,1024]{1,0:T(8,128)(2,1)S(1)}, u32[]{:S(2)}, u32[]{:S(2)}) collective-permute-start(bf16[64,1024]{1,0:T(8,128)(2,1)S(1)} %collective-permute-done.14.refs_4_), channel_id=1, source_target_pairs={{0,1},{1,0},{2,3},{3,2},{4,5},{5,4},{6,7},{7,6},{8,9},{9,8},{10,11... | collective-permute-start | bytes 393224 | tf_op jit(solution)/shard_map/ppermute | solution.py:329
  54.8 1.4 %collective-permute-start.17 = (bf16[64,1024]{1,0:T(8,128)(2,1)S(1)}, bf16[64,1024]{1,0:T(8,128)(2,1)}, u32[]{:S(2)}, u32[]{:S(2)}) collective-permute-start(bf16[64,1024]{1,0:T(8,128)(2,1)S(1)} %collective-permute-done.16.refs_6_), channel_id=1, source_target_pairs={{0,1},{1,0},{2,3},{3,2},{4,5},{5,4},{6,7},{7,6},{8,9},{9,8},{10,11... | collective-permute-start | bytes 393224 | tf_op jit(solution)/shard_map/ppermute | solution.py:329
  57.4 3.0 %shard_map.97 = (bf16[64,640]{1,0:T(8,128)(2,1)S(1)}, bf16[64,640]{1,0:T(8,128)(2,1)S(1)}, bf16[64,640]{1,0:T(8,128)(2,1)S(1)}, bf16[64,640]{1,0:T(8,128)(2,1)S(1)}) custom-call(s32[4]{0:T(128)S(1)} %pad_add_fusion.place, bf16[64,1024]{1,0:T(8,128)(2,1)S(1)} %shard_map.96.refs_0_, bf16[64,1024]{1,0:T(8,128)(2,1)S(1)} %collective-permute-done.11.refs_1_, ...), custom_call_target="tpu_custom_call" | custom-call | flops 671088640 | bytes 2621440 | tf_op jit(solution)/shard_map/pallas_call | solution.py:21
  60.4 3.5 %collective-permute-start.19 = (bf16[64,640]{1,0:T(8,128)(2,1)S(1)}, bf16[64,640]{1,0:T(8,128)(2,1)S(1)}, u32[]{:S(2)}, u32[]{:S(2)}) collective-permute-start(bf16[64,640]{1,0:T(8,128)(2,1)S(1)} %get-tuple-element.31), channel_id=1, source_target_pairs={{0,0},{1,4},{2,8},{3,12},{4,1},{5,5},{6,9},{7,13},{8,2},{9,6},{10,... | collective-permute-start | bytes 245768 | tf_op jit(solution)/shard_map/ppermute | solution.py:478
  63.9 3.9 %collective-permute-start.21 = (bf16[64,640]{1,0:T(8,128)(2,1)S(1)}, bf16[64,640]{1,0:T(8,128)(2,1)S(1)}, u32[]{:S(2)}, u32[]{:S(2)}) collective-permute-start(bf16[64,640]{1,0:T(8,128)(2,1)S(1)} %get-tuple-element.33), channel_id=1, source_target_pairs={{0,2},{1,6},{2,10},{3,14},{4,3},{5,7},{6,11},{7,15},{8,0},{9,4},{1... | collective-permute-start | bytes 245768 | tf_op jit(solution)/shard_map/ppermute | solution.py:478
  69.1 4.5 %collective-permute-done.21.refs_2_ = bf16[64,640]{1,0:T(8,128)(2,1)S(1)} collective-permute-done((bf16[64,640]{1,0:T(8,128)(2,1)S(1)}, bf16[64,640]{1,0:T(8,128)(2,1)S(1)}, u32[]{:S(2)}, u32[]{:S(2)}) %collective-permute-start.21) | collective-permute-done | bytes 81952 | tf_op jit(solution)/shard_map/ppermute | solution.py:478
  73.6 7.6 %collective-permute-done.22.refs_3_ = bf16[64,640]{1,0:T(8,128)(2,1)S(1)} collective-permute-done((bf16[64,640]{1,0:T(8,128)(2,1)S(1)}, bf16[64,640]{1,0:T(8,128)(2,1)S(1)}, u32[]{:S(2)}, u32[]{:S(2)}) %collective-permute-start.22) | collective-permute-done | bytes 81952 | tf_op jit(solution)/shard_map/ppermute | solution.py:478
  (70 shorter events, 17.8 us)
Async XLA Ops:
  3.7 11.1 %collective-permute-start.1 = (bf16[1280,128]{1,0:T(8,128)(2,1)}, bf16[1280,128]{1,0:T(8,128)(2,1)}, u32[]{:S(2)}, u32[]{:S(2)}) collective-permute-start(bf16[1280,128]{1,0:T(8,128)(2,1)} %get-tuple-element.21), channel_id=1, source_target_pairs={{0,2},{1,3},{2,0},{3,1},{4,6},{5,7},{6,4},{7,5},{8,10},{9,11},{10,... | collective-permute-start | bytes 983048 | tf_op jit(solution)/shard_map/ppermute | solution.py:329
  5.8 11.1 %collective-permute-start = (bf16[1280,256]{1,0:T(8,128)(2,1)}, bf16[1280,256]{1,0:T(8,128)(2,1)}, u32[]{:S(2)}, u32[]{:S(2)}) collective-permute-start(bf16[1280,256]{1,0:T(8,128)(2,1)} %get-tuple-element.20.own), channel_id=1, source_target_pairs={{0,1},{1,0},{2,3},{3,2},{4,5},{5,4},{6,7},{7,6},{8,9},{9,8},{10,11... | collective-permute-start | bytes 1966088 | tf_op jit(solution)/shard_map/ppermute | solution.py:329
  8.5 13.8 %all-to-all-start = ((bf16[4,64,1280]{2,1,0:T(8,128)(2,1)}), bf16[4,64,1280]{2,1,0:T(8,128)(2,1)S(1)}, u32[]{:S(2)}, u32[]{:S(2)}) async-start(bf16[4,64,1280]{2,1,0:T(8,128)(2,1)} %shard_map.91.cont), calls=%async_computation | async-start | bytes 1310720 | tf_op jit(solution)/shard_map/all_to_all | solution.py:426
  13.2 43.1 %collective-permute-start.18 = (bf16[1024,640]{1,0:T(8,128)(2,1)}, bf16[1024,640]{1,0:T(8,128)(2,1)}, u32[]{:S(2)}, u32[]{:S(2)}) collective-permute-start(bf16[1024,640]{1,0:T(8,128)(2,1)} %constant_dynamic-slice_fusion), channel_id=1, source_target_pairs={{0,4},{4,0},{8,12},{12,8},{1,5},{5,1},{9,13},{13,9},{2,6},{6,2},{1... | collective-permute-start | bytes 3932168 | tf_op jit(solution)/shard_map/ppermute | solution.py:329
  14.8 2.0 %collective-permute-start.2 = (bf16[1280,128]{1,0:T(8,128)(2,1)}, bf16[1280,128]{1,0:T(8,128)(2,1)}, u32[]{:S(2)}, u32[]{:S(2)}) collective-permute-start(bf16[1280,128]{1,0:T(8,128)(2,1)} %collective-permute-done.1.refs_0_), channel_id=1, source_target_pairs={{0,1},{1,0},{2,3},{3,2},{4,5},{5,4},{6,7},{7,6},{8,9},{9,8},{10,11... | collective-permute-start | bytes 983048 | tf_op jit(solution)/shard_map/ppermute | solution.py:329
  15.2 9.4 %collective-permute-start.3 = (bf16[1280,128]{1,0:T(8,128)(2,1)}, bf16[1280,128]{1,0:T(8,128)(2,1)}, u32[]{:S(2)}, u32[]{:S(2)}) collective-permute-start(bf16[1280,128]{1,0:T(8,128)(2,1)} %collective-permute-done.1.refs_0_), channel_id=1, source_target_pairs={{0,16},{16,0},{1,17},{17,1},{2,18},{18,2},{3,19},{19,3},{4,20},{20... | collective-permute-start | bytes 983048 | tf_op jit(solution)/shard_map/ppermute | solution.py:329
  28.8 2.2 %collective-permute-start.5 = (f32[64,1024]{1,0:T(8,128)S(1)}, f32[64,1024]{1,0:T(8,128)S(1)}, u32[]{:S(2)}, u32[]{:S(2)}) collective-permute-start(f32[64,1024]{1,0:T(8,128)S(1)} %get-tuple-element.29), channel_id=1, source_target_pairs={{0,1},{1,0},{2,3},{3,2},{4,5},{5,4},{6,7},{7,6},{8,9},{9,8},{10,11... | collective-permute-start | bytes 786440 | tf_op jit(solution)/shard_map/ppermute | solution.py:329
  29.9 3.2 %collective-permute-start.7 = (bf16[1280,128]{1,0:T(8,128)(2,1)}, bf16[1280,128]{1,0:T(8,128)(2,1)S(1)}, u32[]{:S(2)}, u32[]{:S(2)}) collective-permute-start(bf16[1280,128]{1,0:T(8,128)(2,1)} %collective-permute-done.3.refs_1_), channel_id=1, source_target_pairs={{0,1},{1,0},{2,3},{3,2},{4,5},{5,4},{6,7},{7,6},{8,9},{9,8},{10,11... | collective-permute-start | bytes 983048 | tf_op jit(solution)/shard_map/ppermute | solution.py:329
  30.4 12.0 %collective-permute-start.4 = (f32[64,1024]{1,0:T(8,128)S(1)}, f32[64,1024]{1,0:T(8,128)S(1)}, u32[]{:S(2)}, u32[]{:S(2)}) collective-permute-start(f32[64,1024]{1,0:T(8,128)S(1)} %get-tuple-element.27), channel_id=1, source_target_pairs={{0,1},{1,0},{2,3},{3,2},{4,5},{5,4},{6,7},{7,6},{8,9},{9,8},{10,11... | collective-permute-start | bytes 786440 | tf_op jit(solution)/shard_map/ppermute | solution.py:329
  31.0 11.4 %collective-permute-start.6 = (f32[64,1024]{1,0:T(8,128)S(1)}, f32[64,1024]{1,0:T(8,128)S(1)}, u32[]{:S(2)}, u32[]{:S(2)}) collective-permute-start(f32[64,1024]{1,0:T(8,128)S(1)} %add.49), channel_id=1, source_target_pairs={{0,2},{1,3},{2,0},{3,1},{4,6},{5,7},{6,4},{7,5},{8,10},{9,11},{10,... | collective-permute-start | bytes 786440 | tf_op jit(solution)/shard_map/ppermute | solution.py:329
  35.6 5.9 %collective-permute-start.9 = (bf16[192,256]{1,0:T(8,128)(2,1)S(1)}, bf16[192,256]{1,0:T(8,128)(2,1)S(1)}, u32[]{:S(2)}, u32[]{:S(2)}) collective-permute-start(bf16[192,256]{1,0:T(8,128)(2,1)S(1)} %shard_map.95.refs_0_), channel_id=1, source_target_pairs={{0,2},{1,3},{2,0},{3,1},{4,6},{5,7},{6,4},{7,5},{8,10},{9,11},{10,... | collective-permute-start | bytes 294920 | tf_op jit(solution)/shard_map/ppermute | solution.py:329
  36.1 6.3 %collective-permute-start.8 = (bf16[192,256]{1,0:T(8,128)(2,1)S(1)}, bf16[192,256]{1,0:T(8,128)(2,1)S(1)}, u32[]{:S(2)}, u32[]{:S(2)}) collective-permute-start(bf16[192,256]{1,0:T(8,128)(2,1)S(1)} %shard_map.95.refs_0_), channel_id=1, source_target_pairs={{0,1},{1,0},{2,3},{3,2},{4,5},{5,4},{6,7},{7,6},{8,9},{9,8},{10,11... | collective-permute-start | bytes 294920 | tf_op jit(solution)/shard_map/ppermute | solution.py:329
  41.5 1.7 %collective-permute-start.10 = (bf16[192,256]{1,0:T(8,128)(2,1)S(1)}, bf16[192,256]{1,0:T(8,128)(2,1)S(1)}, u32[]{:S(2)}, u32[]{:S(2)}) collective-permute-start(bf16[192,256]{1,0:T(8,128)(2,1)S(1)} %collective-permute-done.9.refs_2_), channel_id=1, source_target_pairs={{0,1},{1,0},{2,3},{3,2},{4,5},{5,4},{6,7},{7,6},{8,9},{9,8},{10,11... | collective-permute-start | bytes 294920 | tf_op jit(solution)/shard_map/ppermute | solution.py:329
  46.2 4.8 %collective-permute-start.12 = (bf16[64,1024]{1,0:T(8,128)(2,1)S(1)}, bf16[64,1024]{1,0:T(8,128)(2,1)S(1)}, u32[]{:S(2)}, u32[]{:S(2)}) collective-permute-start(bf16[64,1024]{1,0:T(8,128)(2,1)S(1)} %shard_map.96.refs_0_), channel_id=1, source_target_pairs={{0,2},{1,3},{2,0},{3,1},{4,6},{5,7},{6,4},{7,5},{8,10},{9,11},{10,... | collective-permute-start | bytes 393224 | tf_op jit(solution)/shard_map/ppermute | solution.py:329
  47.7 4.5 %collective-permute-start.14 = (bf16[64,1024]{1,0:T(8,128)(2,1)S(1)}, bf16[64,1024]{1,0:T(8,128)(2,1)S(1)}, u32[]{:S(2)}, u32[]{:S(2)}) collective-permute-start(bf16[64,1024]{1,0:T(8,128)(2,1)S(1)} %shard_map.96.refs_0_), channel_id=1, source_target_pairs={{0,4},{1,5},{2,6},{3,7},{4,0},{5,1},{6,2},{7,3},{8,12},{9,13},{10,... | collective-permute-start | bytes 393224 | tf_op jit(solution)/shard_map/ppermute | solution.py:338
  49.0 5.8 %collective-permute-start.16 = (bf16[64,1024]{1,0:T(8,128)(2,1)S(1)}, bf16[64,1024]{1,0:T(8,128)(2,1)S(1)}, u32[]{:S(2)}, u32[]{:S(2)}) collective-permute-start(bf16[64,1024]{1,0:T(8,128)(2,1)S(1)} %shard_map.96.refs_0_), channel_id=1, source_target_pairs={{0,6},{1,7},{2,4},{3,5},{4,2},{5,3},{6,0},{7,1},{8,14},{9,15},{10,... | collective-permute-start | bytes 393224 | tf_op jit(solution)/shard_map/ppermute | solution.py:338
  49.0 7.2 %collective-permute-start.11 = (bf16[64,1024]{1,0:T(8,128)(2,1)S(1)}, bf16[64,1024]{1,0:T(8,128)(2,1)S(1)}, u32[]{:S(2)}, u32[]{:S(2)}) collective-permute-start(bf16[64,1024]{1,0:T(8,128)(2,1)S(1)} %shard_map.96.refs_0_), channel_id=1, source_target_pairs={{0,1},{1,0},{2,3},{3,2},{4,5},{5,4},{6,7},{7,6},{8,9},{9,8},{10,11... | collective-permute-start | bytes 393224 | tf_op jit(solution)/shard_map/ppermute | solution.py:329
  51.0 5.3 %collective-permute-start.13 = (bf16[64,1024]{1,0:T(8,128)(2,1)S(1)}, bf16[64,1024]{1,0:T(8,128)(2,1)S(1)}, u32[]{:S(2)}, u32[]{:S(2)}) collective-permute-start(bf16[64,1024]{1,0:T(8,128)(2,1)S(1)} %collective-permute-done.12.refs_2_), channel_id=1, source_target_pairs={{0,1},{1,0},{2,3},{3,2},{4,5},{5,4},{6,7},{7,6},{8,9},{9,8},{10,11... | collective-permute-start | bytes 393224 | tf_op jit(solution)/shard_map/ppermute | solution.py:329
  52.2 4.1 %collective-permute-start.15 = (bf16[64,1024]{1,0:T(8,128)(2,1)S(1)}, bf16[64,1024]{1,0:T(8,128)(2,1)S(1)}, u32[]{:S(2)}, u32[]{:S(2)}) collective-permute-start(bf16[64,1024]{1,0:T(8,128)(2,1)S(1)} %collective-permute-done.14.refs_4_), channel_id=1, source_target_pairs={{0,1},{1,0},{2,3},{3,2},{4,5},{5,4},{6,7},{7,6},{8,9},{9,8},{10,11... | collective-permute-start | bytes 393224 | tf_op jit(solution)/shard_map/ppermute | solution.py:329
  54.8 2.5 %collective-permute-start.17 = (bf16[64,1024]{1,0:T(8,128)(2,1)S(1)}, bf16[64,1024]{1,0:T(8,128)(2,1)}, u32[]{:S(2)}, u32[]{:S(2)}) collective-permute-start(bf16[64,1024]{1,0:T(8,128)(2,1)S(1)} %collective-permute-done.16.refs_6_), channel_id=1, source_target_pairs={{0,1},{1,0},{2,3},{3,2},{4,5},{5,4},{6,7},{7,6},{8,9},{9,8},{10,11... | collective-permute-start | bytes 393224 | tf_op jit(solution)/shard_map/ppermute | solution.py:329
  60.4 8.7 %collective-permute-start.19 = (bf16[64,640]{1,0:T(8,128)(2,1)S(1)}, bf16[64,640]{1,0:T(8,128)(2,1)S(1)}, u32[]{:S(2)}, u32[]{:S(2)}) collective-permute-start(bf16[64,640]{1,0:T(8,128)(2,1)S(1)} %get-tuple-element.31), channel_id=1, source_target_pairs={{0,0},{1,4},{2,8},{3,12},{4,1},{5,5},{6,9},{7,13},{8,2},{9,6},{10,... | collective-permute-start | bytes 245768 | tf_op jit(solution)/shard_map/ppermute | solution.py:478
  63.8 5.3 %collective-permute-start.20 = (bf16[64,640]{1,0:T(8,128)(2,1)S(1)}, bf16[64,640]{1,0:T(8,128)(2,1)S(1)}, u32[]{:S(2)}, u32[]{:S(2)}) collective-permute-start(bf16[64,640]{1,0:T(8,128)(2,1)S(1)} %get-tuple-element.32), channel_id=1, source_target_pairs={{0,1},{1,5},{2,9},{3,13},{4,0},{5,4},{6,8},{7,12},{8,3},{9,7},{10,... | collective-permute-start | bytes 245768 | tf_op jit(solution)/shard_map/ppermute | solution.py:478
  63.9 9.7 %collective-permute-start.21 = (bf16[64,640]{1,0:T(8,128)(2,1)S(1)}, bf16[64,640]{1,0:T(8,128)(2,1)S(1)}, u32[]{:S(2)}, u32[]{:S(2)}) collective-permute-start(bf16[64,640]{1,0:T(8,128)(2,1)S(1)} %get-tuple-element.33), channel_id=1, source_target_pairs={{0,2},{1,6},{2,10},{3,14},{4,3},{5,7},{6,11},{7,15},{8,0},{9,4},{1... | collective-permute-start | bytes 245768 | tf_op jit(solution)/shard_map/ppermute | solution.py:478
  67.8 13.4 %collective-permute-start.22 = (bf16[64,640]{1,0:T(8,128)(2,1)S(1)}, bf16[64,640]{1,0:T(8,128)(2,1)S(1)}, u32[]{:S(2)}, u32[]{:S(2)}) collective-permute-start(bf16[64,640]{1,0:T(8,128)(2,1)S(1)} %get-tuple-element.34), channel_id=1, source_target_pairs={{0,3},{1,7},{2,11},{3,15},{4,2},{5,6},{6,10},{7,14},{8,1},{9,5},{1... | collective-permute-start | bytes 245768 | tf_op jit(solution)/shard_map/ppermute | solution.py:478
  (11 other events, 42.3 us)

commit v2 on v1

--- a/solution.py
+++ b/solution.py
@@ -10,7 +10,7 @@
 
 QH = 32
 KVH = 4
-SP, TP, GROUP, HEAD = range(4)
+SP, TP, HEAD = range(3)
 BF16 = jnp.bfloat16
 F32 = jnp.float32
 ROOM = 14 * 1024 * 1024
@@ -73,30 +73,21 @@
     )
 
 
-def pick_kernel(place, first, key, value, half, both):
-    size = half.shape[1]
-    half[...] = first[...]
-    both[:, :size] = key[...]
-    both[:, size:] = value[...]
+def pick_kernel(place, columns, out):
+    out[...] = columns[...]
 
 
 def pick_columns(place, weight, size):
-    depth = weight.shape[0]
-    block = (depth, size)
-    outs = [shape_of(block, BF16), shape_of((depth, 2 * size), BF16)]
+    block = (weight.shape[0], 2 * size)
     return call(
         pick_kernel,
         place,
         (1,),
-        [
-            pl.BlockSpec(block, lambda i, place: (0, 2 * place[HEAD] + place[GROUP])),
-            pl.BlockSpec(block, lambda i, place: (0, 2 * place[HEAD])),
-            pl.BlockSpec(block, lambda i, place: (0, 2 * place[HEAD] + 1)),
-        ],
-        [whole(out) for out in outs],
-        outs,
-        (weight, weight, weight),
-        (0, 12 * depth * size),
+        [pl.BlockSpec(block, lambda i, place: (0, place[HEAD]))],
+        pl.BlockSpec(block, lambda i, place: (0, 0)),
+        shape_of(block, BF16),
+        (weight,),
+        (0, 8 * block[0] * size),
     )
 
 
@@ -159,17 +150,13 @@
 def keyval_kernel(count, place, prompt, cont, cosine, sine, gain, near, *refs):
     weights, out = refs[:-1], refs[-1]
     size = gain.shape[1]
-    total = 0.0
+    total = near[...]
     for d in range(2, count):
         left = jnp.concatenate([prompt[place[SP] ^ d], cont[place[SP] ^ d]], axis=0)
-        weight = jnp.concatenate([weights[2 * d - 4][...], weights[2 * d - 3][...]], axis=1)
-        total = total + jnp.dot(left, weight, preferred_element_type=F32)
-    swapped = place[GROUP] == 1
-    first, second = total[:, :size], total[:, size:]
-    key = near[:, :size] + jnp.where(swapped, second, first)
-    value = near[:, size:] + jnp.where(swapped, first, second)
-    out[:, :size] = turn(rms_rows(key, gain[...]), cosine[...], sine[...]).astype(BF16)
-    out[:, size:] = value.astype(BF16)
+        total = total + jnp.dot(left, weights[d - 2][...], preferred_element_type=F32)
+    key = rms_rows(total[:, :size], gain[...])
+    out[:, :size] = turn(key, cosine[...], sine[...]).astype(BF16)
+    out[:, size:] = total[:, size:].astype(BF16)
 
 
 def keyval_rows(place, prompt, cont, cosine, sine, gain, near, weights):
@@ -355,12 +342,12 @@
     return [held[d] for d in range(count)]
 
 
-def other_halves(half, axis, count):
-    firsts = {0: half}
+def from_chips(block, axis, count):
+    held = {0: block}
     for bit in swap_bits(count)[1:]:
-        firsts.update({d ^ bit: swap(firsts[d], axis, bit) for d in sorted(firsts)})
-    del firsts[0]
-    return firsts
+        held.update({d ^ bit: swap(held[d], axis, bit) for d in sorted(held)})
+    del held[0]
+    return held
 
 
 def both_cores(held, axis):
@@ -408,12 +395,11 @@
     sp_index = lax.axis_index("sp")
     sp_count = lax.axis_size("sp")
     tp_index = lax.axis_index("tp")
-    assert lax.axis_size("tp") == sp_count and lax.axis_size("groups") == 2
+    assert lax.axis_size("tp") == sp_count
     place = jnp.stack(
         [
             sp_index,
             tp_index,
-            lax.axis_index("groups"),
             tp_index * heads_here // (QH // KVH),
         ]
     ).astype(jnp.int32)
@@ -421,28 +407,20 @@
     query_gain = query_gain[None, :]
     key_gain = key_gain[None, :]
 
+    own = pick_columns(place, keyval_weight, size)
+    weights = from_chips(own, "sp", sp_count)
     cont = norm_split(place, hidden_cont, norm_gain, sp_count)
-    half, both = pick_columns(place, keyval_weight, size)
     cont_all = lax.all_to_all(cont, "sp", 0, 0, tiled=True)
-    halves = other_halves(half, "sp", sp_count)
-    partner = swap(both, "sp", 1)
+    partner = swap(own, "sp", 1)
     width = out_weight.shape[1]
     side = tp_index % 2
     out_early = after(out_weight, cont)
     sent = lax.dynamic_slice_in_dim(out_early, (1 - side) * (width // 2), width // 2, 1)
     out_partner = swap(sent, "tp", 1)
-    others = {d: swap(half, "groups", 1) for d, half in halves.items()}
-    halves = both_cores(halves, "sp")
     prompt, near_pair = near_keyval(
-        place,
-        hidden_prompt,
-        norm_gain,
-        cont,
-        both,
-        after(partner, halves, sent),
-    )
-    cont_all = after(cont_all, near_pair, others)
-    others = both_cores(others, "sp")
+        place, hidden_prompt, norm_gain, cont, own, after(partner, sent)
+    )
+    cont_all = after(cont_all, near_pair)
 
     index = sp_index * cont_rows + jnp.arange(cont_rows, dtype=jnp.int32)
     starts = jnp.cumsum(sample_lengths, dtype=jnp.int32) - sample_lengths
@@ -453,7 +431,8 @@
 
     parts = query_parts(place, cont_all, query_weight)
     mine, other = sum_blocks(parts, "sp", sp_count)
-    weights = [held[d] for d in range(2, sp_count) for held in (halves, others)]
+    weights = both_cores(after(weights, parts), "sp")
+    weights = [weights[d] for d in range(2, sp_count)]
     pair = keyval_rows(place, prompt, cont, cosine, sine, key_gain, near_pair, weights)
     pairs = gather_blocks(pair, "sp", sp_count)
     heads = attend(

time: 82.9 us -> 86.8 us (1.047)
  waiting for transfers between devices: 22.5 us -> 29.1 us
  starting transfers between devices: 31.7 us -> 29.5 us
    all_to_all x1, waiting for transfers between devices: 0.01 us -> 8.63 us  [on_device(): cont_all = lax.all_to_all(cont, 'sp', 0, 0, tiled=True)]
    ppermute x17 -> x15, starting transfers between devices: 19.1 us -> 16.7 us  [swap(): lax.ppermute(array, axis, [(i, i ^ bits) for i in range(lax.axis_size(axi...]
    ppermute x17 -> x15, waiting for transfers between devices: 10.4 us -> 8.36 us  [swap(): lax.ppermute(array, axis, [(i, i ^ bits) for i in range(lax.axis_size(axi...]
  transfers between devices with their start and end apart: 24 -> 22, of which waited for: 10 -> 9; matrix products, arithmetic and copies ran while one was open for 4% -> 4% of each run, Pallas kernels for 15% -> 15%
where the time goes in v2:
time: 86.8 us; the launch traced here: 86.4 us
  starting transfers between devices  29.5 us (34%)
  waiting for transfers between devices  29.1 us (34%)
  Pallas kernels  18.4 us (21%)
  local copies, waits for them, and re-layouts  8.02 us (9%)
  other arithmetic  1.08 us (1%)
    pallas_call x8, Pallas kernels, call(): pl.pallas_call(kernel, out_shape=out_shape, grid_spec=pltpu.PrefetchScala...  18.4 us
    ppermute x15, starting transfers between devices, swap(): lax.ppermute(array, axis, [(i, i ^ bits) for i in range(lax.axis_size(axi...  16.7 us
    ppermute x4, waiting for transfers between devices, on_device(): lax.ppermute(part, ('tp', 'sp'), [(t * sp_count + s, s * sp_count + (t ^...  12 us
    all_to_all x1, waiting for transfers between devices, on_device(): cont_all = lax.all_to_all(cont, 'sp', 0, 0, tiled=True)  8.63 us
    ppermute x15, waiting for transfers between devices, swap(): lax.ppermute(array, axis, [(i, i ^ bits) for i in range(lax.axis_size(axi...  8.36 us
    ppermute x4, starting transfers between devices, on_device(): lax.ppermute(part, ('tp', 'sp'), [(t * sp_count + s, s * sp_count + (t ^...  7.78 us
    unnamed x22, local copies, waits for them, and re-layouts  5.9 us
    all_to_all x1, starting transfers between devices, on_device(): cont_all = lax.all_to_all(cont, 'sp', 0, 0, tiled=True)  3.73 us
  transfers between devices with their start and end apart: 22, of which 9 were waited for; matrix products, arithmetic and copies ran while one was open for 4% of the time, Pallas kernels for 15%

profile of v2, /device:TPU:1, one launch (start us, length us, event | category | flops | bytes accessed | tf_op | source)
XLA Modules:
  0.0 86.4 jit_solution(2242295346001328808)
XLA Ops:
  0.1 1.7 %copy-done.1 = bf16[1280,1024]{1,0:T(8,128)(2,1)S(1)} copy-done((bf16[1280,1024]{1,0:T(8,128)(2,1)S(1)}, bf16[1280,1024]{1,0:T(8,128)(2,1)}, u32[]{:S(2)}) %copy-start.1) | copy-done | bytes 2621464
  1.8 1.5 %shard_map.92.own = bf16[1280,256]{1,0:T(8,128)(2,1)} custom-call(s32[3]{0:T(128)S(1)} %pad_add_fusion.place, bf16[1280,1024]{1,0:T(8,128)(2,1)S(1)} %copy-done.1), custom_call_target="tpu_custom_call" | custom-call | bytes 1310720 | tf_op jit(solution)/shard_map/pallas_call | solution.py:21
  3.4 2.7 %collective-permute-start.4 = (bf16[1280,256]{1,0:T(8,128)(2,1)}, bf16[1280,256]{1,0:T(8,128)(2,1)}, u32[]{:S(2)}, u32[]{:S(2)}) collective-permute-start(bf16[1280,256]{1,0:T(8,128)(2,1)} %shard_map.92.own), channel_id=1, source_target_pairs={{0,2},{1,3},{2,0},{3,1},{4,6},{5,7},{6,4},{7,5},{8,10},{9,11},{10,... | collective-permute-start | bytes 1966088 | tf_op jit(solution)/shard_map/ppermute | solution.py:316
  6.0 1.8 %shard_map.91.cont = bf16[4,64,1280]{2,1,0:T(8,128)(2,1)} custom-call(s32[3]{0:T(128)S(1)} %pad_add_fusion.place, bf16[64,5120]{1,0:T(8,128)(2,1)S(1)} %copy-done.6, f32[1,5120]{1,0:T(1,128)S(1)} %bitcast.9), custom_call_target="tpu_custom_call" | custom-call | flops 1310720 | bytes 1310720 | tf_op jit(solution)/shard_map/pallas_call | solution.py:21
  7.8 3.7 %all-to-all-start = ((bf16[4,64,1280]{2,1,0:T(8,128)(2,1)}), bf16[4,64,1280]{2,1,0:T(8,128)(2,1)S(1)}, u32[]{:S(2)}, u32[]{:S(2)}) async-start(bf16[4,64,1280]{2,1,0:T(8,128)(2,1)} %shard_map.91.cont), calls=%async_computation | async-start | bytes 1310720 | tf_op jit(solution)/shard_map/all_to_all | solution.py:413
  12.7 1.3 %collective-permute-start.16 = (bf16[1024,640]{1,0:T(8,128)(2,1)}, bf16[1024,640]{1,0:T(8,128)(2,1)}, u32[]{:S(2)}, u32[]{:S(2)}) collective-permute-start(bf16[1024,640]{1,0:T(8,128)(2,1)} %constant_dynamic-slice_fusion), channel_id=1, source_target_pairs={{0,4},{4,0},{8,12},{12,8},{1,5},{5,1},{9,13},{13,9},{2,6},{6,2},{1... | collective-permute-start | bytes 3932168 | tf_op jit(solution)/shard_map/ppermute | solution.py:316
  14.3 1.3 %copy-done.3 = bf16[128,5120]{1,0:T(8,128)(2,1)S(1)} copy-done((bf16[128,5120]{1,0:T(8,128)(2,1)S(1)}, bf16[128,5120]{1,0:T(8,128)(2,1)}, u32[]{:S(2)}) %copy-start.3) | copy-done | bytes 1310744
  15.7 3.1 %shard_map.93 = (bf16[4,128,1280]{2,1,0:T(8,128)(2,1)S(1)}, f32[192,256]{1,0:T(8,128)S(1)}) custom-call(s32[3]{0:T(128)S(1)} %pad_add_fusion.place, bf16[128,5120]{1,0:T(8,128)(2,1)S(1)} %copy-done.3, f32[1,5120]{1,0:T(1,128)S(1)} %bitcast.10, bf16[4,64,1280]{2,1,0:T(8,128)(2,1)} %shard_map.91.cont, bf16[1280,256]{1,0:T(8,128)(2,1)} %shard_map.92.own, ...), custom_call_target="tpu_custom_call" | custom-call | flops 251658240 | bytes 5242880 | tf_op jit(solution)/shard_map/pallas_call | solution.py:21
  19.8 8.6 %all-to-all-done.rows = bf16[4,64,1280]{2,1,0:T(8,128)(2,1)S(1)} async-done(((bf16[4,64,1280]{2,1,0:T(8,128)(2,1)}), bf16[4,64,1280]{2,1,0:T(8,128)(2,1)S(1)}, u32[]{:S(2)}, u32[]{:S(2)}) %all-to-all-start) | async-done | bytes 655392 | tf_op jit(solution)/shard_map/all_to_all | solution.py:413
  28.5 1.7 %copy-done.2 = bf16[1280,1024]{1,0:T(8,128)(2,1)S(1)} copy-done((bf16[1280,1024]{1,0:T(8,128)(2,1)S(1)}, bf16[1280,1024]{1,0:T(8,128)(2,1)}, u32[]{:S(2)}) %copy-start.2) | copy-done | bytes 2621464
  30.2 2.4 %shard_map.94 = (f32[64,1024]{1,0:T(8,128)S(1)}, f32[64,1024]{1,0:T(8,128)S(1)}, f32[64,1024]{1,0:T(8,128)S(1)}, f32[64,1024]{1,0:T(8,128)S(1)}) custom-call(s32[3]{0:T(128)S(1)} %pad_add_fusion.place, bf16[4,64,1280]{2,1,0:T(8,128)(2,1)S(1)} %all-to-all-done.rows, bf16[1280,1024]{1,0:T(8,128)(2,1)S(1)} %copy-done.2), custom_call_target="tpu_custom_call" | custom-call | flops 671088640 | bytes 2621440 | tf_op jit(solution)/shard_map/pallas_call | solution.py:21
  35.3 1.5 %collective-permute-start.3 = (f32[64,1024]{1,0:T(8,128)S(1)}, f32[64,1024]{1,0:T(8,128)S(1)}, u32[]{:S(2)}, u32[]{:S(2)}) collective-permute-start(f32[64,1024]{1,0:T(8,128)S(1)} %add.49), channel_id=1, source_target_pairs={{0,2},{1,3},{2,0},{3,1},{4,6},{5,7},{6,4},{7,5},{8,10},{9,11},{10,... | collective-permute-start | bytes 786440 | tf_op jit(solution)/shard_map/ppermute | solution.py:316
  37.0 2.4 %shard_map.95.refs_0_ = bf16[192,256]{1,0:T(8,128)(2,1)S(1)} custom-call(s32[3]{0:T(128)S(1)} %pad_add_fusion.place, bf16[4,128,1280]{2,1,0:T(8,128)(2,1)S(1)} %copy-done.5, bf16[4,64,1280]{2,1,0:T(8,128)(2,1)} %shard_map.91.cont, f32[192,128]{1,0:T(8,128)S(1)} %get-tuple-element.36.cosine, f32[192,128]{1,0:T(8,128)S(1)} %get-tuple-element.37.sine, ...), custom_call_target="tpu_custom_call" | custom-call | flops 251658240 | bytes 2293760 | tf_op jit(solution)/shard_map/pallas_call | solution.py:21
  40.5 4.6 %collective-permute-done.7.refs_2_ = bf16[192,256]{1,0:T(8,128)(2,1)S(1)} collective-permute-done((bf16[192,256]{1,0:T(8,128)(2,1)S(1)}, bf16[192,256]{1,0:T(8,128)(2,1)S(1)}, u32[]{:S(2)}, u32[]{:S(2)}) %collective-permute-start.7) | collective-permute-done | bytes 98336 | tf_op jit(solution)/shard_map/ppermute | solution.py:316
  47.2 3.0 %shard_map.96.refs_0_ = bf16[64,1024]{1,0:T(8,128)(2,1)S(1)} custom-call(s32[3]{0:T(128)S(1)} %pad_add_fusion.place, s32[8]{0:T(128)S(1)} %copy-done.9, f32[64,1024]{1,0:T(8,128)S(1)} %add.48.mine, f32[64,1024]{1,0:T(8,128)S(1)} %collective-permute-done.3.other, f32[64,128]{1,0:T(8,128)S(1)} %get-tuple-element.39.cosine, ...), custom_call_target="tpu_custom_call" | custom-call | flops 201326592 | bytes 1048576 | tf_op jit(solution)/shard_map/pallas_call | solution.py:21
  50.2 1.5 %collective-permute-start.10 = (bf16[64,1024]{1,0:T(8,128)(2,1)S(1)}, bf16[64,1024]{1,0:T(8,128)(2,1)S(1)}, u32[]{:S(2)}, u32[]{:S(2)}) collective-permute-start(bf16[64,1024]{1,0:T(8,128)(2,1)S(1)} %shard_map.96.refs_0_), channel_id=1, source_target_pairs={{0,2},{1,3},{2,0},{3,1},{4,6},{5,7},{6,4},{7,5},{8,10},{9,11},{10,... | collective-permute-start | bytes 393224 | tf_op jit(solution)/shard_map/ppermute | solution.py:316
  51.7 1.3 %collective-permute-start.12 = (bf16[64,1024]{1,0:T(8,128)(2,1)S(1)}, bf16[64,1024]{1,0:T(8,128)(2,1)S(1)}, u32[]{:S(2)}, u32[]{:S(2)}) collective-permute-start(bf16[64,1024]{1,0:T(8,128)(2,1)S(1)} %shard_map.96.refs_0_), channel_id=1, source_target_pairs={{0,4},{1,5},{2,6},{3,7},{4,0},{5,1},{6,2},{7,3},{8,12},{9,13},{10,... | collective-permute-start | bytes 393224 | tf_op jit(solution)/shard_map/ppermute | solution.py:325
  56.1 2.6 %collective-permute-start.13 = (bf16[64,1024]{1,0:T(8,128)(2,1)S(1)}, bf16[64,1024]{1,0:T(8,128)(2,1)S(1)}, u32[]{:S(2)}, u32[]{:S(2)}) collective-permute-start(bf16[64,1024]{1,0:T(8,128)(2,1)S(1)} %collective-permute-done.12.refs_4_), channel_id=1, source_target_pairs={{0,1},{1,0},{2,3},{3,2},{4,5},{5,4},{6,7},{7,6},{8,9},{9,8},{10,11... | collective-permute-start | bytes 393224 | tf_op jit(solution)/shard_map/ppermute | solution.py:316
  58.8 1.4 %collective-permute-start.15 = (bf16[64,1024]{1,0:T(8,128)(2,1)S(1)}, bf16[64,1024]{1,0:T(8,128)(2,1)}, u32[]{:S(2)}, u32[]{:S(2)}) collective-permute-start(bf16[64,1024]{1,0:T(8,128)(2,1)S(1)} %collective-permute-done.14.refs_6_), channel_id=1, source_target_pairs={{0,1},{1,0},{2,3},{3,2},{4,5},{5,4},{6,7},{7,6},{8,9},{9,8},{10,11... | collective-permute-start | bytes 393224 | tf_op jit(solution)/shard_map/ppermute | solution.py:316
  61.3 3.0 %shard_map.97 = (bf16[64,640]{1,0:T(8,128)(2,1)S(1)}, bf16[64,640]{1,0:T(8,128)(2,1)S(1)}, bf16[64,640]{1,0:T(8,128)(2,1)S(1)}, bf16[64,640]{1,0:T(8,128)(2,1)S(1)}) custom-call(s32[3]{0:T(128)S(1)} %pad_add_fusion.place, bf16[64,1024]{1,0:T(8,128)(2,1)S(1)} %shard_map.96.refs_0_, bf16[64,1024]{1,0:T(8,128)(2,1)S(1)} %collective-permute-done.9.refs_1_, ...), custom_call_target="tpu_custom_call" | custom-call | flops 671088640 | bytes 2621440 | tf_op jit(solution)/shard_map/pallas_call | solution.py:21
  64.3 3.6 %collective-permute-start.17 = (bf16[64,640]{1,0:T(8,128)(2,1)S(1)}, bf16[64,640]{1,0:T(8,128)(2,1)S(1)}, u32[]{:S(2)}, u32[]{:S(2)}) collective-permute-start(bf16[64,640]{1,0:T(8,128)(2,1)S(1)} %get-tuple-element.29), channel_id=1, source_target_pairs={{0,0},{1,4},{2,8},{3,12},{4,1},{5,5},{6,9},{7,13},{8,2},{9,6},{10,... | collective-permute-start | bytes 245768 | tf_op jit(solution)/shard_map/ppermute | solution.py:457
  68.0 3.7 %collective-permute-start.19 = (bf16[64,640]{1,0:T(8,128)(2,1)S(1)}, bf16[64,640]{1,0:T(8,128)(2,1)S(1)}, u32[]{:S(2)}, u32[]{:S(2)}) collective-permute-start(bf16[64,640]{1,0:T(8,128)(2,1)S(1)} %get-tuple-element.31), channel_id=1, source_target_pairs={{0,2},{1,6},{2,10},{3,14},{4,3},{5,7},{6,11},{7,15},{8,0},{9,4},{1... | collective-permute-start | bytes 245768 | tf_op jit(solution)/shard_map/ppermute | solution.py:457
  73.1 4.5 %collective-permute-done.19.refs_2_ = bf16[64,640]{1,0:T(8,128)(2,1)S(1)} collective-permute-done((bf16[64,640]{1,0:T(8,128)(2,1)S(1)}, bf16[64,640]{1,0:T(8,128)(2,1)S(1)}, u32[]{:S(2)}, u32[]{:S(2)}) %collective-permute-start.19) | collective-permute-done | bytes 81952 | tf_op jit(solution)/shard_map/ppermute | solution.py:457
  77.5 7.6 %collective-permute-done.20.refs_3_ = bf16[64,640]{1,0:T(8,128)(2,1)S(1)} collective-permute-done((bf16[64,640]{1,0:T(8,128)(2,1)S(1)}, bf16[64,640]{1,0:T(8,128)(2,1)S(1)}, u32[]{:S(2)}, u32[]{:S(2)}) %collective-permute-start.20) | collective-permute-done | bytes 81952 | tf_op jit(solution)/shard_map/ppermute | solution.py:457
  (66 shorter events, 15.7 us)
Async XLA Ops:
  3.3 11.0 %collective-permute-start = (bf16[1280,256]{1,0:T(8,128)(2,1)}, bf16[1280,256]{1,0:T(8,128)(2,1)}, u32[]{:S(2)}, u32[]{:S(2)}) collective-permute-start(bf16[1280,256]{1,0:T(8,128)(2,1)} %shard_map.92.own), channel_id=1, source_target_pairs={{0,1},{1,0},{2,3},{3,2},{4,5},{5,4},{6,7},{7,6},{8,9},{9,8},{10,11... | collective-permute-start | bytes 1966088 | tf_op jit(solution)/shard_map/ppermute | solution.py:316
  3.4 29.3 %collective-permute-start.4 = (bf16[1280,256]{1,0:T(8,128)(2,1)}, bf16[1280,256]{1,0:T(8,128)(2,1)}, u32[]{:S(2)}, u32[]{:S(2)}) collective-permute-start(bf16[1280,256]{1,0:T(8,128)(2,1)} %shard_map.92.own), channel_id=1, source_target_pairs={{0,2},{1,3},{2,0},{3,1},{4,6},{5,7},{6,4},{7,5},{8,10},{9,11},{10,... | collective-permute-start | bytes 1966088 | tf_op jit(solution)/shard_map/ppermute | solution.py:316
  6.0 5.5 %copy-start = (bf16[1024,1280]{1,0:T(8,128)(2,1)S(1)}, bf16[1024,1280]{1,0:T(8,128)(2,1)}, u32[]{:S(2)}) copy-start(bf16[1024,1280]{1,0:T(8,128)(2,1)} %refs_8_.1) | copy-start | bytes 7864324
  7.8 20.7 %all-to-all-start = ((bf16[4,64,1280]{2,1,0:T(8,128)(2,1)}), bf16[4,64,1280]{2,1,0:T(8,128)(2,1)S(1)}, u32[]{:S(2)}, u32[]{:S(2)}) async-start(bf16[4,64,1280]{2,1,0:T(8,128)(2,1)} %shard_map.91.cont), calls=%async_computation | async-start | bytes 1310720 | tf_op jit(solution)/shard_map/all_to_all | solution.py:413
  12.7 47.5 %collective-permute-start.16 = (bf16[1024,640]{1,0:T(8,128)(2,1)}, bf16[1024,640]{1,0:T(8,128)(2,1)}, u32[]{:S(2)}, u32[]{:S(2)}) collective-permute-start(bf16[1024,640]{1,0:T(8,128)(2,1)} %constant_dynamic-slice_fusion), channel_id=1, source_target_pairs={{0,4},{4,0},{8,12},{12,8},{1,5},{5,1},{9,13},{13,9},{2,6},{6,2},{1... | collective-permute-start | bytes 3932168 | tf_op jit(solution)/shard_map/ppermute | solution.py:316
  32.7 4.3 %collective-permute-start.5 = (bf16[1280,256]{1,0:T(8,128)(2,1)}, bf16[1280,256]{1,0:T(8,128)(2,1)S(1)}, u32[]{:S(2)}, u32[]{:S(2)}) collective-permute-start(bf16[1280,256]{1,0:T(8,128)(2,1)} %collective-permute-done.4.refs_0_), channel_id=1, source_target_pairs={{0,1},{1,0},{2,3},{3,2},{4,5},{5,4},{6,7},{7,6},{8,9},{9,8},{10,11... | collective-permute-start | bytes 1966088 | tf_op jit(solution)/shard_map/ppermute | solution.py:316
  33.2 2.1 %collective-permute-start.2 = (f32[64,1024]{1,0:T(8,128)S(1)}, f32[64,1024]{1,0:T(8,128)S(1)}, u32[]{:S(2)}, u32[]{:S(2)}) collective-permute-start(f32[64,1024]{1,0:T(8,128)S(1)} %get-tuple-element.26), channel_id=1, source_target_pairs={{0,1},{1,0},{2,3},{3,2},{4,5},{5,4},{6,7},{7,6},{8,9},{9,8},{10,11... | collective-permute-start | bytes 786440 | tf_op jit(solution)/shard_map/ppermute | solution.py:316
  33.8 12.6 %collective-permute-start.1 = (f32[64,1024]{1,0:T(8,128)S(1)}, f32[64,1024]{1,0:T(8,128)S(1)}, u32[]{:S(2)}, u32[]{:S(2)}) collective-permute-start(f32[64,1024]{1,0:T(8,128)S(1)} %get-tuple-element.24), channel_id=1, source_target_pairs={{0,1},{1,0},{2,3},{3,2},{4,5},{5,4},{6,7},{7,6},{8,9},{9,8},{10,11... | collective-permute-start | bytes 786440 | tf_op jit(solution)/shard_map/ppermute | solution.py:316
  35.3 11.0 %collective-permute-start.3 = (f32[64,1024]{1,0:T(8,128)S(1)}, f32[64,1024]{1,0:T(8,128)S(1)}, u32[]{:S(2)}, u32[]{:S(2)}) collective-permute-start(f32[64,1024]{1,0:T(8,128)S(1)} %add.49), channel_id=1, source_target_pairs={{0,2},{1,3},{2,0},{3,1},{4,6},{5,7},{6,4},{7,5},{8,10},{9,11},{10,... | collective-permute-start | bytes 786440 | tf_op jit(solution)/shard_map/ppermute | solution.py:316
  37.0 10.2 %copy-start.10 = (f32[128]{0:T(128)S(1)}, f32[128]{0:T(128)}, u32[]{:S(2)}) copy-start(f32[128]{0:T(128)} %param.15) | copy-start | bytes 1540
  39.5 5.6 %collective-permute-start.7 = (bf16[192,256]{1,0:T(8,128)(2,1)S(1)}, bf16[192,256]{1,0:T(8,128)(2,1)S(1)}, u32[]{:S(2)}, u32[]{:S(2)}) collective-permute-start(bf16[192,256]{1,0:T(8,128)(2,1)S(1)} %shard_map.95.refs_0_), channel_id=1, source_target_pairs={{0,2},{1,3},{2,0},{3,1},{4,6},{5,7},{6,4},{7,5},{8,10},{9,11},{10,... | collective-permute-start | bytes 294920 | tf_op jit(solution)/shard_map/ppermute | solution.py:316
  39.5 6.8 %collective-permute-start.6 = (bf16[192,256]{1,0:T(8,128)(2,1)S(1)}, bf16[192,256]{1,0:T(8,128)(2,1)S(1)}, u32[]{:S(2)}, u32[]{:S(2)}) collective-permute-start(bf16[192,256]{1,0:T(8,128)(2,1)S(1)} %shard_map.95.refs_0_), channel_id=1, source_target_pairs={{0,1},{1,0},{2,3},{3,2},{4,5},{5,4},{6,7},{7,6},{8,9},{9,8},{10,11... | collective-permute-start | bytes 294920 | tf_op jit(solution)/shard_map/ppermute | solution.py:316
  45.0 2.1 %collective-permute-start.8 = (bf16[192,256]{1,0:T(8,128)(2,1)S(1)}, bf16[192,256]{1,0:T(8,128)(2,1)S(1)}, u32[]{:S(2)}, u32[]{:S(2)}) collective-permute-start(bf16[192,256]{1,0:T(8,128)(2,1)S(1)} %collective-permute-done.7.refs_2_), channel_id=1, source_target_pairs={{0,1},{1,0},{2,3},{3,2},{4,5},{5,4},{6,7},{7,6},{8,9},{9,8},{10,11... | collective-permute-start | bytes 294920 | tf_op jit(solution)/shard_map/ppermute | solution.py:316
  50.2 4.8 %collective-permute-start.10 = (bf16[64,1024]{1,0:T(8,128)(2,1)S(1)}, bf16[64,1024]{1,0:T(8,128)(2,1)S(1)}, u32[]{:S(2)}, u32[]{:S(2)}) collective-permute-start(bf16[64,1024]{1,0:T(8,128)(2,1)S(1)} %shard_map.96.refs_0_), channel_id=1, source_target_pairs={{0,2},{1,3},{2,0},{3,1},{4,6},{5,7},{6,4},{7,5},{8,10},{9,11},{10,... | collective-permute-start | bytes 393224 | tf_op jit(solution)/shard_map/ppermute | solution.py:316
  51.7 4.5 %collective-permute-start.12 = (bf16[64,1024]{1,0:T(8,128)(2,1)S(1)}, bf16[64,1024]{1,0:T(8,128)(2,1)S(1)}, u32[]{:S(2)}, u32[]{:S(2)}) collective-permute-start(bf16[64,1024]{1,0:T(8,128)(2,1)S(1)} %shard_map.96.refs_0_), channel_id=1, source_target_pairs={{0,4},{1,5},{2,6},{3,7},{4,0},{5,1},{6,2},{7,3},{8,12},{9,13},{10,... | collective-permute-start | bytes 393224 | tf_op jit(solution)/shard_map/ppermute | solution.py:325
  53.0 5.8 %collective-permute-start.14 = (bf16[64,1024]{1,0:T(8,128)(2,1)S(1)}, bf16[64,1024]{1,0:T(8,128)(2,1)S(1)}, u32[]{:S(2)}, u32[]{:S(2)}) collective-permute-start(bf16[64,1024]{1,0:T(8,128)(2,1)S(1)} %shard_map.96.refs_0_), channel_id=1, source_target_pairs={{0,6},{1,7},{2,4},{3,5},{4,2},{5,3},{6,0},{7,1},{8,14},{9,15},{10,... | collective-permute-start | bytes 393224 | tf_op jit(solution)/shard_map/ppermute | solution.py:325
  53.0 7.2 %collective-permute-start.9 = (bf16[64,1024]{1,0:T(8,128)(2,1)S(1)}, bf16[64,1024]{1,0:T(8,128)(2,1)S(1)}, u32[]{:S(2)}, u32[]{:S(2)}) collective-permute-start(bf16[64,1024]{1,0:T(8,128)(2,1)S(1)} %shard_map.96.refs_0_), channel_id=1, source_target_pairs={{0,1},{1,0},{2,3},{3,2},{4,5},{5,4},{6,7},{7,6},{8,9},{9,8},{10,11... | collective-permute-start | bytes 393224 | tf_op jit(solution)/shard_map/ppermute | solution.py:316
  54.9 5.3 %collective-permute-start.11 = (bf16[64,1024]{1,0:T(8,128)(2,1)S(1)}, bf16[64,1024]{1,0:T(8,128)(2,1)S(1)}, u32[]{:S(2)}, u32[]{:S(2)}) collective-permute-start(bf16[64,1024]{1,0:T(8,128)(2,1)S(1)} %collective-permute-done.10.refs_2_), channel_id=1, source_target_pairs={{0,1},{1,0},{2,3},{3,2},{4,5},{5,4},{6,7},{7,6},{8,9},{9,8},{10,11... | collective-permute-start | bytes 393224 | tf_op jit(solution)/shard_map/ppermute | solution.py:316
  56.1 4.1 %collective-permute-start.13 = (bf16[64,1024]{1,0:T(8,128)(2,1)S(1)}, bf16[64,1024]{1,0:T(8,128)(2,1)S(1)}, u32[]{:S(2)}, u32[]{:S(2)}) collective-permute-start(bf16[64,1024]{1,0:T(8,128)(2,1)S(1)} %collective-permute-done.12.refs_4_), channel_id=1, source_target_pairs={{0,1},{1,0},{2,3},{3,2},{4,5},{5,4},{6,7},{7,6},{8,9},{9,8},{10,11... | collective-permute-start | bytes 393224 | tf_op jit(solution)/shard_map/ppermute | solution.py:316
  58.8 2.5 %collective-permute-start.15 = (bf16[64,1024]{1,0:T(8,128)(2,1)S(1)}, bf16[64,1024]{1,0:T(8,128)(2,1)}, u32[]{:S(2)}, u32[]{:S(2)}) collective-permute-start(bf16[64,1024]{1,0:T(8,128)(2,1)S(1)} %collective-permute-done.14.refs_6_), channel_id=1, source_target_pairs={{0,1},{1,0},{2,3},{3,2},{4,5},{5,4},{6,7},{7,6},{8,9},{9,8},{10,11... | collective-permute-start | bytes 393224 | tf_op jit(solution)/shard_map/ppermute | solution.py:316
  64.3 8.7 %collective-permute-start.17 = (bf16[64,640]{1,0:T(8,128)(2,1)S(1)}, bf16[64,640]{1,0:T(8,128)(2,1)S(1)}, u32[]{:S(2)}, u32[]{:S(2)}) collective-permute-start(bf16[64,640]{1,0:T(8,128)(2,1)S(1)} %get-tuple-element.29), channel_id=1, source_target_pairs={{0,0},{1,4},{2,8},{3,12},{4,1},{5,5},{6,9},{7,13},{8,2},{9,6},{10,... | collective-permute-start | bytes 245768 | tf_op jit(solution)/shard_map/ppermute | solution.py:457
  68.0 5.1 %collective-permute-start.18 = (bf16[64,640]{1,0:T(8,128)(2,1)S(1)}, bf16[64,640]{1,0:T(8,128)(2,1)S(1)}, u32[]{:S(2)}, u32[]{:S(2)}) collective-permute-start(bf16[64,640]{1,0:T(8,128)(2,1)S(1)} %get-tuple-element.30), channel_id=1, source_target_pairs={{0,1},{1,5},{2,9},{3,13},{4,0},{5,4},{6,8},{7,12},{8,3},{9,7},{10,... | collective-permute-start | bytes 245768 | tf_op jit(solution)/shard_map/ppermute | solution.py:457
  68.0 9.5 %collective-permute-start.19 = (bf16[64,640]{1,0:T(8,128)(2,1)S(1)}, bf16[64,640]{1,0:T(8,128)(2,1)S(1)}, u32[]{:S(2)}, u32[]{:S(2)}) collective-permute-start(bf16[64,640]{1,0:T(8,128)(2,1)S(1)} %get-tuple-element.31), channel_id=1, source_target_pairs={{0,2},{1,6},{2,10},{3,14},{4,3},{5,7},{6,11},{7,15},{8,0},{9,4},{1... | collective-permute-start | bytes 245768 | tf_op jit(solution)/shard_map/ppermute | solution.py:457
  71.8 13.4 %collective-permute-start.20 = (bf16[64,640]{1,0:T(8,128)(2,1)S(1)}, bf16[64,640]{1,0:T(8,128)(2,1)S(1)}, u32[]{:S(2)}, u32[]{:S(2)}) collective-permute-start(bf16[64,640]{1,0:T(8,128)(2,1)S(1)} %get-tuple-element.32), channel_id=1, source_target_pairs={{0,3},{1,7},{2,11},{3,15},{4,2},{5,6},{6,10},{7,14},{8,1},{9,5},{1... | collective-permute-start | bytes 245768 | tf_op jit(solution)/shard_map/ppermute | solution.py:457
  (9 other events, 25.6 us)

commit v3 on v1

--- a/solution.py
+++ b/solution.py
@@ -14,6 +14,7 @@
 BF16 = jnp.bfloat16
 F32 = jnp.float32
 ROOM = 14 * 1024 * 1024
+ALL = 62 * 1024 * 1024
 
 
 def call(kernel, place, grid, in_specs, out_specs, out_shape, args, cost, scratch=(), room=ROOM):
@@ -73,30 +74,35 @@
     )
 
 
-def pick_kernel(place, first, key, value, half, both):
-    size = half.shape[1]
-    half[...] = first[...]
-    both[:, :size] = key[...]
-    both[:, size:] = value[...]
+def pick_kernel(place, weight, upper, lower, both, sems):
+    rows, size = upper.shape
+    half = pl.multiple_of((2 * place[HEAD] + place[GROUP]) * size, size)
+    head = pl.multiple_of(2 * place[HEAD] * size, size)
+    copies = [
+        pltpu.make_async_copy(weight.at[0:rows, pl.ds(half, size)], upper, sems.at[0]),
+        pltpu.make_async_copy(weight.at[rows : 2 * rows, pl.ds(half, size)], lower, sems.at[1]),
+        pltpu.make_async_copy(weight.at[:, pl.ds(head, 2 * size)], both, sems.at[2]),
+    ]
+    for copy in copies:
+        copy.start()
+    for copy in copies:
+        copy.wait()
 
 
 def pick_columns(place, weight, size):
     depth = weight.shape[0]
-    block = (depth, size)
-    outs = [shape_of(block, BF16), shape_of((depth, 2 * size), BF16)]
+    outs = [shape_of((depth // 2, size), BF16)] * 2 + [shape_of((depth, 2 * size), BF16)]
     return call(
         pick_kernel,
         place,
         (1,),
-        [
-            pl.BlockSpec(block, lambda i, place: (0, 2 * place[HEAD] + place[GROUP])),
-            pl.BlockSpec(block, lambda i, place: (0, 2 * place[HEAD])),
-            pl.BlockSpec(block, lambda i, place: (0, 2 * place[HEAD] + 1)),
-        ],
-        [whole(out) for out in outs],
+        [pl.BlockSpec(memory_space=pl.ANY)],
+        [pl.BlockSpec(memory_space=pl.ANY)] * 3,
         outs,
-        (weight, weight, weight),
+        (weight,),
         (0, 12 * depth * size),
+        [pltpu.SemaphoreType.DMA((3,))],
+        ALL,
     )
 
 
@@ -162,7 +168,10 @@
     total = 0.0
     for d in range(2, count):
         left = jnp.concatenate([prompt[place[SP] ^ d], cont[place[SP] ^ d]], axis=0)
-        weight = jnp.concatenate([weights[2 * d - 4][...], weights[2 * d - 3][...]], axis=1)
+        four = [weight[...] for weight in weights[4 * d - 8 : 4 * d - 4]]
+        weight = jnp.concatenate(
+            [jnp.concatenate(four[i : i + 2], axis=0) for i in (0, 2)], axis=1
+        )
         total = total + jnp.dot(left, weight, preferred_element_type=F32)
     swapped = place[GROUP] == 1
     first, second = total[:, :size], total[:, size:]
@@ -421,28 +430,25 @@
     query_gain = query_gain[None, :]
     key_gain = key_gain[None, :]
 
+    upper, lower, both = pick_columns(place, keyval_weight, size)
+    upper = other_halves(upper, "sp", sp_count)
+    lower = other_halves(lower, "sp", sp_count)
     cont = norm_split(place, hidden_cont, norm_gain, sp_count)
-    half, both = pick_columns(place, keyval_weight, size)
     cont_all = lax.all_to_all(cont, "sp", 0, 0, tiled=True)
-    halves = other_halves(half, "sp", sp_count)
     partner = swap(both, "sp", 1)
+    others = [{d: swap(a, "groups", 1) for d, a in held.items()} for held in (upper, lower)]
+    upper = both_cores(upper, "sp")
+    lower = both_cores(lower, "sp")
     width = out_weight.shape[1]
     side = tp_index % 2
-    out_early = after(out_weight, cont)
+    out_early = after(out_weight, others[0], lower)
     sent = lax.dynamic_slice_in_dim(out_early, (1 - side) * (width // 2), width // 2, 1)
     out_partner = swap(sent, "tp", 1)
-    others = {d: swap(half, "groups", 1) for d, half in halves.items()}
-    halves = both_cores(halves, "sp")
     prompt, near_pair = near_keyval(
-        place,
-        hidden_prompt,
-        norm_gain,
-        cont,
-        both,
-        after(partner, halves, sent),
-    )
-    cont_all = after(cont_all, near_pair, others)
-    others = both_cores(others, "sp")
+        place, hidden_prompt, norm_gain, cont, both, after(partner, lower)
+    )
+    cont_all = after(cont_all, near_pair, others, sent)
+    others = [both_cores(held, "sp") for held in others]
 
     index = sp_index * cont_rows + jnp.arange(cont_rows, dtype=jnp.int32)
     starts = jnp.cumsum(sample_lengths, dtype=jnp.int32) - sample_lengths
@@ -453,7 +459,7 @@
 
     parts = query_parts(place, cont_all, query_weight)
     mine, other = sum_blocks(parts, "sp", sp_count)
-    weights = [held[d] for d in range(2, sp_count) for held in (halves, others)]
+    weights = [held[d] for d in range(2, sp_count) for held in (upper, lower, *others)]
     pair = keyval_rows(place, prompt, cont, cosine, sine, key_gain, near_pair, weights)
     pairs = gather_blocks(pair, "sp", sp_count)
     heads = attend(

time: 82.9 us -> 117 us (1.41)
  Pallas kernels: 18.9 us -> 48.5 us
  waiting for transfers between devices: 22.5 us -> 25.1 us
  starting transfers between devices: 31.7 us -> 33.5 us
    pallas_call x8, Pallas kernels: 18.9 us -> 48.5 us  [call(): pl.pallas_call(kernel, out_shape=out_shape, grid_spec=pltpu.PrefetchScala...]
    ppermute x17 -> x21, waiting for transfers between devices: 10.4 us -> 14.1 us  [swap(): lax.ppermute(array, axis, [(i, i ^ bits) for i in range(lax.axis_size(axi...]
    ppermute x17 -> x21, starting transfers between devices: 19.1 us -> 20.6 us  [swap(): lax.ppermute(array, axis, [(i, i ^ bits) for i in range(lax.axis_size(axi...]
    ppermute x4, waiting for transfers between devices: 12 us -> 10.8 us  [on_device(): lax.ppermute(part, ('tp', 'sp'), [(t * sp_count + s, s * sp_count + (t ^...]
    unnamed x22 -> x28, local copies, waits for them, and re-layouts: 5.89 us -> 5.25 us
  transfers between devices with their start and end apart: 24 -> 28, of which waited for: 10 -> 10; matrix products, arithmetic and copies ran while one was open for 4% -> 3% of each run, Pallas kernels for 15% -> 11%
where the time goes in v3:
time: 117 us; the launch traced here: 116 us
  Pallas kernels  48.5 us (41%)
  starting transfers between devices  33.5 us (29%)
  waiting for transfers between devices  25.1 us (21%)
  local copies, waits for them, and re-layouts  7.38 us (6%)
  other arithmetic  1.65 us (1%)
    pallas_call x8, Pallas kernels, call(): pl.pallas_call(kernel, out_shape=out_shape, grid_spec=pltpu.PrefetchScala...  48.5 us
    ppermute x21, starting transfers between devices, swap(): lax.ppermute(array, axis, [(i, i ^ bits) for i in range(lax.axis_size(axi...  20.6 us
    ppermute x21, waiting for transfers between devices, swap(): lax.ppermute(array, axis, [(i, i ^ bits) for i in range(lax.axis_size(axi...  14.1 us
    ppermute x4, waiting for transfers between devices, on_device(): lax.ppermute(part, ('tp', 'sp'), [(t * sp_count + s, s * sp_count + (t ^...  10.8 us
    ppermute x4, starting transfers between devices, on_device(): lax.ppermute(part, ('tp', 'sp'), [(t * sp_count + s, s * sp_count + (t ^...  7.62 us
    unnamed x28, local copies, waits for them, and re-layouts  5.25 us
    all_to_all x1, starting transfers between devices, on_device(): cont_all = lax.all_to_all(cont, 'sp', 0, 0, tiled=True)  3.87 us
  transfers between devices with their start and end apart: 28, of which 10 were waited for; matrix products, arithmetic and copies ran while one was open for 3% of the time, Pallas kernels for 11%

profile of v3, /device:TPU:1, one launch (start us, length us, event | category | flops | bytes accessed | tf_op | source)
XLA Modules:
  0.0 116.4 jit_solution(9900716157460535188)
XLA Ops:
  0.7 31.7 %shard_map.92 = (bf16[640,128]{1,0:T(8,128)(2,1)}, bf16[640,128]{1,0:T(8,128)(2,1)}, bf16[1280,256]{1,0:T(8,128)(2,1)}) custom-call(s32[4]{0:T(128)} %pad_add_fusion.place, bf16[1280,1024]{1,0:T(8,128)(2,1)} %weight.2), custom_call_target="tpu_custom_call" | custom-call | bytes 1966080 | tf_op jit(solution)/shard_map/pallas_call | solution.py:22
  32.5 2.7 %collective-permute-start.1 = (bf16[640,128]{1,0:T(8,128)(2,1)}, bf16[640,128]{1,0:T(8,128)(2,1)}, u32[]{:S(2)}, u32[]{:S(2)}) collective-permute-start(bf16[640,128]{1,0:T(8,128)(2,1)} %get-tuple-element.22), channel_id=1, source_target_pairs={{0,2},{1,3},{2,0},{3,1},{4,6},{5,7},{6,4},{7,5},{8,10},{9,11},{10,... | collective-permute-start | bytes 491528 | tf_op jit(solution)/shard_map/ppermute | solution.py:338
  35.2 1.8 %shard_map.91.cont = bf16[4,64,1280]{2,1,0:T(8,128)(2,1)} custom-call(s32[4]{0:T(128)S(1)} %copy-done.10, bf16[64,5120]{1,0:T(8,128)(2,1)S(1)} %copy-done.5, f32[1,5120]{1,0:T(1,128)S(1)} %bitcast.10), custom_call_target="tpu_custom_call" | custom-call | flops 1310720 | bytes 1310720 | tf_op jit(solution)/shard_map/pallas_call | solution.py:22
  37.0 3.9 %all-to-all-start = ((bf16[4,64,1280]{2,1,0:T(8,128)(2,1)}), bf16[4,64,1280]{2,1,0:T(8,128)(2,1)S(1)}, u32[]{:S(2)}, u32[]{:S(2)}) async-start(bf16[4,64,1280]{2,1,0:T(8,128)(2,1)} %shard_map.91.cont), calls=%async_computation | async-start | bytes 1310720 | tf_op jit(solution)/shard_map/all_to_all | solution.py:437
  41.1 2.2 %collective-permute-done.3.refs_0_ = bf16[640,128]{1,0:T(8,128)(2,1)S(1)} collective-permute-done((bf16[640,128]{1,0:T(8,128)(2,1)}, bf16[640,128]{1,0:T(8,128)(2,1)S(1)}, u32[]{:S(2)}, u32[]{:S(2)}) %collective-permute-start.3) | collective-permute-done | bytes 163872 | tf_op jit(solution)/shard_map/ppermute | solution.py:338
  43.4 1.3 %collective-permute-start.4 = (bf16[640,128]{1,0:T(8,128)(2,1)S(1)}, bf16[640,128]{1,0:T(8,128)(2,1)}, u32[]{:S(2)}, u32[]{:S(2)}) collective-permute-start(bf16[640,128]{1,0:T(8,128)(2,1)S(1)} %collective-permute-done.3.refs_0_), channel_id=1, source_target_pairs={{0,16},{16,0},{1,17},{17,1},{2,18},{18,2},{3,19},{19,3},{4,20},{20... | collective-permute-start | bytes 491528 | tf_op jit(solution)/shard_map/ppermute | solution.py:338
  44.8 3.8 %collective-permute-done.4.refs_2_ = bf16[640,128]{1,0:T(8,128)(2,1)} collective-permute-done((bf16[640,128]{1,0:T(8,128)(2,1)S(1)}, bf16[640,128]{1,0:T(8,128)(2,1)}, u32[]{:S(2)}, u32[]{:S(2)}) %collective-permute-start.4) | collective-permute-done | bytes 163872 | tf_op jit(solution)/shard_map/ppermute | solution.py:338
  52.2 1.3 %copy-done.2 = bf16[128,5120]{1,0:T(8,128)(2,1)S(1)} copy-done((bf16[128,5120]{1,0:T(8,128)(2,1)S(1)}, bf16[128,5120]{1,0:T(8,128)(2,1)}, u32[]{:S(2)}) %copy-start.2) | copy-done | bytes 1310744
  54.6 2.9 %shard_map.93 = (bf16[4,128,1280]{2,1,0:T(8,128)(2,1)S(1)}, f32[192,256]{1,0:T(8,128)S(1)}) custom-call(s32[4]{0:T(128)S(1)} %copy-done.10, bf16[128,5120]{1,0:T(8,128)(2,1)S(1)} %copy-done.2, f32[1,5120]{1,0:T(1,128)S(1)} %bitcast.11, bf16[4,64,1280]{2,1,0:T(8,128)(2,1)} %shard_map.91.cont, bf16[1280,256]{1,0:T(8,128)(2,1)S(1)} %copy-done.6, ...), custom_call_target="tpu_custom_call" | custom-call | flops 251658240 | bytes 5242880 | tf_op jit(solution)/shard_map/pallas_call | solution.py:22
  58.6 1.7 %copy-done.1 = bf16[1280,1024]{1,0:T(8,128)(2,1)S(1)} copy-done((bf16[1280,1024]{1,0:T(8,128)(2,1)S(1)}, bf16[1280,1024]{1,0:T(8,128)(2,1)}, u32[]{:S(2)}) %copy-start.1) | copy-done | bytes 2621464
  60.4 2.4 %shard_map.94 = (f32[64,1024]{1,0:T(8,128)S(1)}, f32[64,1024]{1,0:T(8,128)S(1)}, f32[64,1024]{1,0:T(8,128)S(1)}, f32[64,1024]{1,0:T(8,128)S(1)}) custom-call(s32[4]{0:T(128)S(1)} %copy-done.10, bf16[4,64,1280]{2,1,0:T(8,128)(2,1)S(1)} %all-to-all-done.rows, bf16[1280,1024]{1,0:T(8,128)(2,1)S(1)} %copy-done.1), custom_call_target="tpu_custom_call" | custom-call | flops 671088640 | bytes 2621440 | tf_op jit(solution)/shard_map/pallas_call | solution.py:22
  62.8 2.4 %collective-permute-start.7 = (f32[64,1024]{1,0:T(8,128)S(1)}, f32[64,1024]{1,0:T(8,128)S(1)}, u32[]{:S(2)}, u32[]{:S(2)}) collective-permute-start(f32[64,1024]{1,0:T(8,128)S(1)} %get-tuple-element.31), channel_id=1, source_target_pairs={{0,1},{1,0},{2,3},{3,2},{4,5},{5,4},{6,7},{7,6},{8,9},{9,8},{10,11... | collective-permute-start | bytes 786440 | tf_op jit(solution)/shard_map/ppermute | solution.py:338
  66.8 1.3 %collective-permute-start.8 = (f32[64,1024]{1,0:T(8,128)S(1)}, f32[64,1024]{1,0:T(8,128)S(1)}, u32[]{:S(2)}, u32[]{:S(2)}) collective-permute-start(f32[64,1024]{1,0:T(8,128)S(1)} %add.49), channel_id=1, source_target_pairs={{0,2},{1,3},{2,0},{3,1},{4,6},{5,7},{6,4},{7,5},{8,10},{9,11},{10,... | collective-permute-start | bytes 786440 | tf_op jit(solution)/shard_map/ppermute | solution.py:338
  68.3 2.5 %shard_map.95.refs_0_ = bf16[192,256]{1,0:T(8,128)(2,1)S(1)} custom-call(s32[4]{0:T(128)S(1)} %copy-done.10, bf16[4,128,1280]{2,1,0:T(8,128)(2,1)S(1)} %copy-done.4, bf16[4,64,1280]{2,1,0:T(8,128)(2,1)} %shard_map.91.cont, f32[192,128]{1,0:T(8,128)S(1)} %get-tuple-element.40.cosine, f32[192,128]{1,0:T(8,128)S(1)} %get-tuple-element.41.sine, ...), custom_call_target="tpu_custom_call" | custom-call | flops 251658240 | bytes 2293760 | tf_op jit(solution)/shard_map/pallas_call | solution.py:22
  71.7 5.3 %collective-permute-done.13.refs_2_ = bf16[192,256]{1,0:T(8,128)(2,1)S(1)} collective-permute-done((bf16[192,256]{1,0:T(8,128)(2,1)S(1)}, bf16[192,256]{1,0:T(8,128)(2,1)S(1)}, u32[]{:S(2)}, u32[]{:S(2)}) %collective-permute-start.13) | collective-permute-done | bytes 98336 | tf_op jit(solution)/shard_map/ppermute | solution.py:338
  78.7 3.0 %shard_map.96.refs_0_ = bf16[64,1024]{1,0:T(8,128)(2,1)S(1)} custom-call(s32[4]{0:T(128)S(1)} %copy-done.10, s32[8]{0:T(128)S(1)} %copy-done.12, f32[64,1024]{1,0:T(8,128)S(1)} %add.48.mine, f32[64,1024]{1,0:T(8,128)S(1)} %collective-permute-done.8.other, f32[64,128]{1,0:T(8,128)S(1)} %get-tuple-element.43.cosine, f32[64,128]{1,0:T(8,128)S(1)} %get-tuple-element.42.sine, ...), custom_call_target="tpu_custom_call" | custom-call | flops 201326592 | bytes 1048576 | tf_op jit(solution)/shard_map/pallas_call | solution.py:22
  87.6 2.3 %collective-permute-start.19 = (bf16[64,1024]{1,0:T(8,128)(2,1)S(1)}, bf16[64,1024]{1,0:T(8,128)(2,1)S(1)}, u32[]{:S(2)}, u32[]{:S(2)}) collective-permute-start(bf16[64,1024]{1,0:T(8,128)(2,1)S(1)} %collective-permute-done.18.refs_4_), channel_id=1, source_target_pairs={{0,1},{1,0},{2,3},{3,2},{4,5},{5,4},{6,7},{7,6},{8,9},{9,8},{10,11... | collective-permute-start | bytes 393224 | tf_op jit(solution)/shard_map/ppermute | solution.py:338
  90.1 1.5 %collective-permute-start.21 = (bf16[64,1024]{1,0:T(8,128)(2,1)S(1)}, bf16[64,1024]{1,0:T(8,128)(2,1)}, u32[]{:S(2)}, u32[]{:S(2)}) collective-permute-start(bf16[64,1024]{1,0:T(8,128)(2,1)S(1)} %collective-permute-done.20.refs_6_), channel_id=1, source_target_pairs={{0,1},{1,0},{2,3},{3,2},{4,5},{5,4},{6,7},{7,6},{8,9},{9,8},{10,11... | collective-permute-start | bytes 393224 | tf_op jit(solution)/shard_map/ppermute | solution.py:338
  92.7 3.0 %shard_map.97 = (bf16[64,640]{1,0:T(8,128)(2,1)S(1)}, bf16[64,640]{1,0:T(8,128)(2,1)S(1)}, bf16[64,640]{1,0:T(8,128)(2,1)S(1)}, bf16[64,640]{1,0:T(8,128)(2,1)S(1)}) custom-call(s32[4]{0:T(128)S(1)} %copy-done.10, bf16[64,1024]{1,0:T(8,128)(2,1)S(1)} %shard_map.96.refs_0_, bf16[64,1024]{1,0:T(8,128)(2,1)S(1)} %collective-permute-done.15.refs_1_, ...), custom_call_target="tpu_custom_call" | custom-call | flops 671088640 | bytes 2621440 | tf_op jit(solution)/shard_map/pallas_call | solution.py:22
  95.7 2.3 %collective-permute-start.23 = (bf16[64,640]{1,0:T(8,128)(2,1)S(1)}, bf16[64,640]{1,0:T(8,128)(2,1)S(1)}, u32[]{:S(2)}, u32[]{:S(2)}) collective-permute-start(bf16[64,640]{1,0:T(8,128)(2,1)S(1)} %get-tuple-element.33), channel_id=1, source_target_pairs={{0,0},{1,4},{2,8},{3,12},{4,1},{5,5},{6,9},{7,13},{8,2},{9,6},{10,... | collective-permute-start | bytes 245768 | tf_op jit(solution)/shard_map/ppermute | solution.py:484
  98.1 4.9 %collective-permute-start.25 = (bf16[64,640]{1,0:T(8,128)(2,1)S(1)}, bf16[64,640]{1,0:T(8,128)(2,1)S(1)}, u32[]{:S(2)}, u32[]{:S(2)}) collective-permute-start(bf16[64,640]{1,0:T(8,128)(2,1)S(1)} %get-tuple-element.35), channel_id=1, source_target_pairs={{0,2},{1,6},{2,10},{3,14},{4,3},{5,7},{6,11},{7,15},{8,0},{9,4},{1... | collective-permute-start | bytes 245768 | tf_op jit(solution)/shard_map/ppermute | solution.py:484
  104.3 4.6 %collective-permute-done.25.refs_2_ = bf16[64,640]{1,0:T(8,128)(2,1)S(1)} collective-permute-done((bf16[64,640]{1,0:T(8,128)(2,1)S(1)}, bf16[64,640]{1,0:T(8,128)(2,1)S(1)}, u32[]{:S(2)}, u32[]{:S(2)}) %collective-permute-start.25) | collective-permute-done | bytes 81952 | tf_op jit(solution)/shard_map/ppermute | solution.py:484
  108.9 6.2 %collective-permute-done.26.refs_3_ = bf16[64,640]{1,0:T(8,128)(2,1)S(1)} collective-permute-done((bf16[64,640]{1,0:T(8,128)(2,1)S(1)}, bf16[64,640]{1,0:T(8,128)(2,1)S(1)}, u32[]{:S(2)}, u32[]{:S(2)}) %collective-permute-start.26) | collective-permute-done | bytes 81952 | tf_op jit(solution)/shard_map/ppermute | solution.py:484
  115.2 1.3 %shard_map.98 = bf16[64,1280]{1,0:T(8,128)(2,1)} custom-call(s32[4]{0:T(128)S(1)} %copy-done.10, bf16[64,1280]{1,0:T(8,128)(2,1)S(1)} %constant_dynamic-slice_fusion.1.hidden, bf16[64,640]{1,0:T(8,128)(2,1)S(1)} %collective-permute-done.23.refs_0_, bf16[64,640]{1,0:T(8,128)(2,1)S(1)} %collective-permute-done.24.refs_1_, ...), custom_call_target="tpu_custom_call" | custom-call | flops 327680 | bytes 983040 | tf_op jit(solution)/shard_map/pallas_call | solution.py:22
  (84 shorter events, 20.0 us)
Async XLA Ops:
  32.4 19.8 %collective-permute-start = (bf16[1280,256]{1,0:T(8,128)(2,1)}, bf16[1280,256]{1,0:T(8,128)(2,1)}, u32[]{:S(2)}, u32[]{:S(2)}) collective-permute-start(bf16[1280,256]{1,0:T(8,128)(2,1)} %get-tuple-element.21.own), channel_id=1, source_target_pairs={{0,1},{1,0},{2,3},{3,2},{4,5},{5,4},{6,7},{7,6},{8,9},{9,8},{10,11... | collective-permute-start | bytes 1966088 | tf_op jit(solution)/shard_map/ppermute | solution.py:338
  32.5 8.6 %collective-permute-start.1 = (bf16[640,128]{1,0:T(8,128)(2,1)}, bf16[640,128]{1,0:T(8,128)(2,1)}, u32[]{:S(2)}, u32[]{:S(2)}) collective-permute-start(bf16[640,128]{1,0:T(8,128)(2,1)} %get-tuple-element.22), channel_id=1, source_target_pairs={{0,2},{1,3},{2,0},{3,1},{4,6},{5,7},{6,4},{7,5},{8,10},{9,11},{10,... | collective-permute-start | bytes 491528 | tf_op jit(solution)/shard_map/ppermute | solution.py:338
  35.2 8.2 %collective-permute-start.3 = (bf16[640,128]{1,0:T(8,128)(2,1)}, bf16[640,128]{1,0:T(8,128)(2,1)S(1)}, u32[]{:S(2)}, u32[]{:S(2)}) collective-permute-start(bf16[640,128]{1,0:T(8,128)(2,1)} %get-tuple-element.25), channel_id=1, source_target_pairs={{0,2},{1,3},{2,0},{3,1},{4,6},{5,7},{6,4},{7,5},{8,10},{9,11},{10,... | collective-permute-start | bytes 491528 | tf_op jit(solution)/shard_map/ppermute | solution.py:338
  37.0 21.6 %all-to-all-start = ((bf16[4,64,1280]{2,1,0:T(8,128)(2,1)}), bf16[4,64,1280]{2,1,0:T(8,128)(2,1)S(1)}, u32[]{:S(2)}, u32[]{:S(2)}) async-start(bf16[4,64,1280]{2,1,0:T(8,128)(2,1)} %shard_map.91.cont), calls=%async_computation | async-start | bytes 1310720 | tf_op jit(solution)/shard_map/all_to_all | solution.py:437
  41.0 3.7 %collective-permute-start.2 = (bf16[640,128]{1,0:T(8,128)(2,1)}, bf16[640,128]{1,0:T(8,128)(2,1)}, u32[]{:S(2)}, u32[]{:S(2)}) collective-permute-start(bf16[640,128]{1,0:T(8,128)(2,1)} %collective-permute-done.1.refs_1_), channel_id=1, source_target_pairs={{0,1},{1,0},{2,3},{3,2},{4,5},{5,4},{6,7},{7,6},{8,9},{9,8},{10,11... | collective-permute-start | bytes 491528 | tf_op jit(solution)/shard_map/ppermute | solution.py:338
  43.4 5.2 %collective-permute-start.4 = (bf16[640,128]{1,0:T(8,128)(2,1)S(1)}, bf16[640,128]{1,0:T(8,128)(2,1)}, u32[]{:S(2)}, u32[]{:S(2)}) collective-permute-start(bf16[640,128]{1,0:T(8,128)(2,1)S(1)} %collective-permute-done.3.refs_0_), channel_id=1, source_target_pairs={{0,16},{16,0},{1,17},{17,1},{2,18},{18,2},{3,19},{19,3},{4,20},{20... | collective-permute-start | bytes 491528 | tf_op jit(solution)/shard_map/ppermute | solution.py:338
  49.8 43.0 %collective-permute-start.22 = (bf16[1024,640]{1,0:T(8,128)(2,1)}, bf16[1024,640]{1,0:T(8,128)(2,1)}, u32[]{:S(2)}, u32[]{:S(2)}) collective-permute-start(bf16[1024,640]{1,0:T(8,128)(2,1)} %constant_dynamic-slice_fusion), channel_id=1, source_target_pairs={{0,4},{4,0},{8,12},{12,8},{1,5},{5,1},{9,13},{13,9},{2,6},{6,2},{1... | collective-permute-start | bytes 3932168 | tf_op jit(solution)/shard_map/ppermute | solution.py:338
  50.9 7.7 %collective-permute-start.5 = (bf16[640,128]{1,0:T(8,128)(2,1)}, bf16[640,128]{1,0:T(8,128)(2,1)}, u32[]{:S(2)}, u32[]{:S(2)}) collective-permute-start(bf16[640,128]{1,0:T(8,128)(2,1)} %collective-permute-done.1.refs_1_), channel_id=1, source_target_pairs={{0,16},{16,0},{1,17},{17,1},{2,18},{18,2},{3,19},{19,3},{4,20},{20... | collective-permute-start | bytes 491528 | tf_op jit(solution)/shard_map/ppermute | solution.py:338
  62.8 3.5 %collective-permute-start.7 = (f32[64,1024]{1,0:T(8,128)S(1)}, f32[64,1024]{1,0:T(8,128)S(1)}, u32[]{:S(2)}, u32[]{:S(2)}) collective-permute-start(f32[64,1024]{1,0:T(8,128)S(1)} %get-tuple-element.31), channel_id=1, source_target_pairs={{0,1},{1,0},{2,3},{3,2},{4,5},{5,4},{6,7},{7,6},{8,9},{9,8},{10,11... | collective-permute-start | bytes 786440 | tf_op jit(solution)/shard_map/ppermute | solution.py:338
  65.3 3.0 %collective-permute-start.10 = (bf16[640,128]{1,0:T(8,128)(2,1)}, bf16[640,128]{1,0:T(8,128)(2,1)S(1)}, u32[]{:S(2)}, u32[]{:S(2)}) collective-permute-start(bf16[640,128]{1,0:T(8,128)(2,1)} %collective-permute-done.4.refs_2_), channel_id=1, source_target_pairs={{0,1},{1,0},{2,3},{3,2},{4,5},{5,4},{6,7},{7,6},{8,9},{9,8},{10,11... | collective-permute-start | bytes 491528 | tf_op jit(solution)/shard_map/ppermute | solution.py:338
  66.3 11.5 %collective-permute-start.6 = (f32[64,1024]{1,0:T(8,128)S(1)}, f32[64,1024]{1,0:T(8,128)S(1)}, u32[]{:S(2)}, u32[]{:S(2)}) collective-permute-start(f32[64,1024]{1,0:T(8,128)S(1)} %get-tuple-element.29), channel_id=1, source_target_pairs={{0,1},{1,0},{2,3},{3,2},{4,5},{5,4},{6,7},{7,6},{8,9},{9,8},{10,11... | collective-permute-start | bytes 786440 | tf_op jit(solution)/shard_map/ppermute | solution.py:338
  66.8 11.9 %collective-permute-start.8 = (f32[64,1024]{1,0:T(8,128)S(1)}, f32[64,1024]{1,0:T(8,128)S(1)}, u32[]{:S(2)}, u32[]{:S(2)}) collective-permute-start(f32[64,1024]{1,0:T(8,128)S(1)} %add.49), channel_id=1, source_target_pairs={{0,2},{1,3},{2,0},{3,1},{4,6},{5,7},{6,4},{7,5},{8,10},{9,11},{10,... | collective-permute-start | bytes 786440 | tf_op jit(solution)/shard_map/ppermute | solution.py:338
  70.7 6.2 %collective-permute-start.13 = (bf16[192,256]{1,0:T(8,128)(2,1)S(1)}, bf16[192,256]{1,0:T(8,128)(2,1)S(1)}, u32[]{:S(2)}, u32[]{:S(2)}) collective-permute-start(bf16[192,256]{1,0:T(8,128)(2,1)S(1)} %shard_map.95.refs_0_), channel_id=1, source_target_pairs={{0,2},{1,3},{2,0},{3,1},{4,6},{5,7},{6,4},{7,5},{8,10},{9,11},{10,... | collective-permute-start | bytes 294920 | tf_op jit(solution)/shard_map/ppermute | solution.py:338
  71.1 6.7 %collective-permute-start.12 = (bf16[192,256]{1,0:T(8,128)(2,1)S(1)}, bf16[192,256]{1,0:T(8,128)(2,1)S(1)}, u32[]{:S(2)}, u32[]{:S(2)}) collective-permute-start(bf16[192,256]{1,0:T(8,128)(2,1)S(1)} %shard_map.95.refs_0_), channel_id=1, source_target_pairs={{0,1},{1,0},{2,3},{3,2},{4,5},{5,4},{6,7},{7,6},{8,9},{9,8},{10,11... | collective-permute-start | bytes 294920 | tf_op jit(solution)/shard_map/ppermute | solution.py:338
  81.6 4.8 %collective-permute-start.16 = (bf16[64,1024]{1,0:T(8,128)(2,1)S(1)}, bf16[64,1024]{1,0:T(8,128)(2,1)S(1)}, u32[]{:S(2)}, u32[]{:S(2)}) collective-permute-start(bf16[64,1024]{1,0:T(8,128)(2,1)S(1)} %shard_map.96.refs_0_), channel_id=1, source_target_pairs={{0,2},{1,3},{2,0},{3,1},{4,6},{5,7},{6,4},{7,5},{8,10},{9,11},{10,... | collective-permute-start | bytes 393224 | tf_op jit(solution)/shard_map/ppermute | solution.py:338
  82.9 4.7 %collective-permute-start.18 = (bf16[64,1024]{1,0:T(8,128)(2,1)S(1)}, bf16[64,1024]{1,0:T(8,128)(2,1)S(1)}, u32[]{:S(2)}, u32[]{:S(2)}) collective-permute-start(bf16[64,1024]{1,0:T(8,128)(2,1)S(1)} %shard_map.96.refs_0_), channel_id=1, source_target_pairs={{0,4},{1,5},{2,6},{3,7},{4,0},{5,1},{6,2},{7,3},{8,12},{9,13},{10,... | collective-permute-start | bytes 393224 | tf_op jit(solution)/shard_map/ppermute | solution.py:347
  83.1 7.0 %collective-permute-start.20 = (bf16[64,1024]{1,0:T(8,128)(2,1)S(1)}, bf16[64,1024]{1,0:T(8,128)(2,1)S(1)}, u32[]{:S(2)}, u32[]{:S(2)}) collective-permute-start(bf16[64,1024]{1,0:T(8,128)(2,1)S(1)} %shard_map.96.refs_0_), channel_id=1, source_target_pairs={{0,6},{1,7},{2,4},{3,5},{4,2},{5,3},{6,0},{7,1},{8,14},{9,15},{10,... | collective-permute-start | bytes 393224 | tf_op jit(solution)/shard_map/ppermute | solution.py:347
  84.4 7.3 %collective-permute-start.15 = (bf16[64,1024]{1,0:T(8,128)(2,1)S(1)}, bf16[64,1024]{1,0:T(8,128)(2,1)S(1)}, u32[]{:S(2)}, u32[]{:S(2)}) collective-permute-start(bf16[64,1024]{1,0:T(8,128)(2,1)S(1)} %shard_map.96.refs_0_), channel_id=1, source_target_pairs={{0,1},{1,0},{2,3},{3,2},{4,5},{5,4},{6,7},{7,6},{8,9},{9,8},{10,11... | collective-permute-start | bytes 393224 | tf_op jit(solution)/shard_map/ppermute | solution.py:338
  86.4 5.2 %collective-permute-start.17 = (bf16[64,1024]{1,0:T(8,128)(2,1)S(1)}, bf16[64,1024]{1,0:T(8,128)(2,1)S(1)}, u32[]{:S(2)}, u32[]{:S(2)}) collective-permute-start(bf16[64,1024]{1,0:T(8,128)(2,1)S(1)} %collective-permute-done.16.refs_2_), channel_id=1, source_target_pairs={{0,1},{1,0},{2,3},{3,2},{4,5},{5,4},{6,7},{7,6},{8,9},{9,8},{10,11... | collective-permute-start | bytes 393224 | tf_op jit(solution)/shard_map/ppermute | solution.py:338
  87.6 4.0 %collective-permute-start.19 = (bf16[64,1024]{1,0:T(8,128)(2,1)S(1)}, bf16[64,1024]{1,0:T(8,128)(2,1)S(1)}, u32[]{:S(2)}, u32[]{:S(2)}) collective-permute-start(bf16[64,1024]{1,0:T(8,128)(2,1)S(1)} %collective-permute-done.18.refs_4_), channel_id=1, source_target_pairs={{0,1},{1,0},{2,3},{3,2},{4,5},{5,4},{6,7},{7,6},{8,9},{9,8},{10,11... | collective-permute-start | bytes 393224 | tf_op jit(solution)/shard_map/ppermute | solution.py:338
  95.7 8.6 %collective-permute-start.23 = (bf16[64,640]{1,0:T(8,128)(2,1)S(1)}, bf16[64,640]{1,0:T(8,128)(2,1)S(1)}, u32[]{:S(2)}, u32[]{:S(2)}) collective-permute-start(bf16[64,640]{1,0:T(8,128)(2,1)S(1)} %get-tuple-element.33), channel_id=1, source_target_pairs={{0,0},{1,4},{2,8},{3,12},{4,1},{5,5},{6,9},{7,13},{8,2},{9,6},{10,... | collective-permute-start | bytes 245768 | tf_op jit(solution)/shard_map/ppermute | solution.py:484
  98.1 6.2 %collective-permute-start.24 = (bf16[64,640]{1,0:T(8,128)(2,1)S(1)}, bf16[64,640]{1,0:T(8,128)(2,1)S(1)}, u32[]{:S(2)}, u32[]{:S(2)}) collective-permute-start(bf16[64,640]{1,0:T(8,128)(2,1)S(1)} %get-tuple-element.34), channel_id=1, source_target_pairs={{0,1},{1,5},{2,9},{3,13},{4,0},{5,4},{6,8},{7,12},{8,3},{9,7},{10,... | collective-permute-start | bytes 245768 | tf_op jit(solution)/shard_map/ppermute | solution.py:484
  98.1 10.8 %collective-permute-start.25 = (bf16[64,640]{1,0:T(8,128)(2,1)S(1)}, bf16[64,640]{1,0:T(8,128)(2,1)S(1)}, u32[]{:S(2)}, u32[]{:S(2)}) collective-permute-start(bf16[64,640]{1,0:T(8,128)(2,1)S(1)} %get-tuple-element.35), channel_id=1, source_target_pairs={{0,2},{1,6},{2,10},{3,14},{4,3},{5,7},{6,11},{7,15},{8,0},{9,4},{1... | collective-permute-start | bytes 245768 | tf_op jit(solution)/shard_map/ppermute | solution.py:484
  103.0 12.2 %collective-permute-start.26 = (bf16[64,640]{1,0:T(8,128)(2,1)S(1)}, bf16[64,640]{1,0:T(8,128)(2,1)S(1)}, u32[]{:S(2)}, u32[]{:S(2)}) collective-permute-start(bf16[64,640]{1,0:T(8,128)(2,1)S(1)} %get-tuple-element.36), channel_id=1, source_target_pairs={{0,3},{1,7},{2,11},{3,15},{4,2},{5,6},{6,10},{7,14},{8,1},{9,5},{1... | collective-permute-start | bytes 245768 | tf_op jit(solution)/shard_map/ppermute | solution.py:484
  (18 other events, 168.8 us)

commit v4 on v1

--- a/solution.py
+++ b/solution.py
@@ -100,25 +100,27 @@
     )
 
 
-def query_kernel(count, place, rows, weight, *outs):
+def query_kernel(count, place, rows, weight, keep, send):
     block = rows.shape[1]
     left = jnp.concatenate([rows[place[SP] ^ d] for d in range(count)], axis=0)
     part = jnp.dot(left, weight[...], preferred_element_type=F32)
     for d in range(count):
-        outs[d][...] = part[d * block : (d + 1) * block]
+        at = d // 2 * block
+        (keep, send)[d % 2][at : at + block, :] = part[d * block : (d + 1) * block]
 
 
 def query_parts(place, rows, weight):
     count, block, depth = rows.shape
     width = weight.shape[1]
     step = min(width, 256)
+    half = count // 2 * block
     return call(
         functools.partial(query_kernel, count),
         place,
         (width // step,),
         [whole(rows), pl.BlockSpec((depth, step), lambda i, place: (0, i))],
-        [pl.BlockSpec((block, step), lambda i, place: (0, i))] * count,
-        [shape_of((block, width), F32)] * count,
+        [pl.BlockSpec((half, step), lambda i, place: (0, i))] * 2,
+        [shape_of((half, width), F32)] * 2,
         (rows, weight),
         (2 * count * block * depth * width, 2 * depth * width),
     )
@@ -190,16 +192,26 @@
     )
 
 
-def attend_kernel(count, prompt_rows, place, lengths, mine, other, cosine, sine, gain, *refs):
+def starts_of(lengths, index):
+    start = jnp.zeros(index.shape, jnp.int32)
+    total = jnp.int32(0)
+    for c in range(lengths.shape[0]):
+        start = jnp.where(index >= total, total, start)
+        total = total + lengths[c]
+    return start
+
+
+def attend_kernel(count, prompt_rows, place, lengths, mine, near, far, cosine, sine, gain, *refs):
     pairs, out = refs[:-1], refs[-1]
-    rows, width = mine.shape
+    rows, width = far.shape
     size = gain.shape[1]
     heads = width // size
+    cosine, sine = cosine[prompt_rows:, :], sine[prompt_rows:, :]
     queries = []
     for h in range(heads):
         part = slice(h * size, (h + 1) * size)
-        value = rms_rows(mine[:, part] + other[:, part], gain[...])
-        queries.append(turn(value, cosine[...], sine[...]).astype(BF16))
+        value = rms_rows(mine[:rows, part] + near[:rows, part] + far[:, part], gain[...])
+        queries.append(turn(value, cosine, sine).astype(BF16))
     queries = jnp.concatenate(queries, axis=0)
     prompt = jnp.concatenate([pair[:prompt_rows] for pair in pairs], axis=0)
     cont = jnp.concatenate([pair[prompt_rows:] for pair in pairs], axis=0)
@@ -218,12 +230,7 @@
     for d in range(count):
         inside = (at >= d * rows) & (at < (d + 1) * rows)
         key = jnp.where(inside, (place[SP] ^ d) * rows + at - d * rows, key)
-    start = jnp.zeros(shape, jnp.int32)
-    total = jnp.int32(0)
-    for c in range(lengths.shape[0]):
-        start = jnp.where(own >= total, total, start)
-        total = total + lengths[c]
-    allowed = jnp.where((key >= start) & (key <= own), 0.0, -1e30)
+    allowed = jnp.where((key >= starts_of(lengths, own)) & (key <= own), 0.0, -1e30)
     to_cont = to_cont + jnp.concatenate([allowed] * heads, axis=0)
     peak = jnp.maximum(
         jnp.max(to_prompt, axis=1, keepdims=True), jnp.max(to_cont, axis=1, keepdims=True)
@@ -238,9 +245,9 @@
         out[:, h * size : (h + 1) * size] = result[h * rows : (h + 1) * rows].astype(BF16)
 
 
-def attend(place, lengths, mine, other, cosine, sine, gain, pairs, prompt_rows):
-    rows, width = mine.shape
-    args = (mine, other, cosine, sine, gain, *pairs)
+def attend(place, lengths, mine, near, far, cosine, sine, gain, pairs, prompt_rows):
+    rows, width = far.shape
+    args = (mine, near, far, cosine, sine, gain, *pairs)
     out = shape_of((rows, width), BF16)
     keys = len(pairs) * pairs[0].shape[0]
     return call(
@@ -275,7 +282,7 @@
     rows = heads[0].shape[0]
     depth, width = partner.shape
     if width % 128:
-        own = lax.dynamic_slice_in_dim(own, place[TP] % 2 * width, width, 1)
+        own = column_half(place, own, False)
         half = whole(own)
     else:
         half = pl.BlockSpec((depth, width), lambda i, place: (0, place[TP] % 2))
@@ -307,14 +314,20 @@
 
 
 def final_sum(place, parts, hidden):
-    rows, width = hidden.shape
+    rows, width = parts[0].shape
+    width *= 2
     count = len(parts)
+    if width % 128:
+        hidden = lax.dynamic_slice_in_dim(hidden, place[TP] * width, width, 1)
+        residual = whole(hidden)
+    else:
+        residual = pl.BlockSpec((rows, width), lambda i, place: (0, place[TP]))
     return call(
         functools.partial(final_kernel, count),
         place,
         (1,),
-        [whole(a) for a in (hidden, *parts)],
-        whole(hidden),
+        [residual] + [whole(a) for a in parts],
+        pl.BlockSpec((rows, width), lambda i, place: (0, 0)),
         shape_of((rows, width), BF16),
         (hidden, *parts),
         (count * rows * width, 12 * rows * width),
@@ -367,26 +380,91 @@
     return {**held, **{d ^ 1: swap(held[d], axis, 1) for d in sorted(held)}}
 
 
-def sum_blocks(blocks, axis, count):
-    held = dict(enumerate(blocks))
-    bits = swap_bits(count)
-    for bit in bits:
+def sum_blocks(place, keep, send, axis, count):
+    near = swap(send, axis, 1)
+    rows = keep.shape[0] // (count // 2)
+    held = {d: add_rows(place, keep, near, d // 2 * rows, rows) for d in range(2, count, 2)}
+    far = 0.0
+    for bit in swap_bits(count)[1:]:
         sent = [d for d in sorted(held) if d & bit]
         got = {d ^ bit: swap(held[d], axis, bit) for d in sent}
-        if bit == bits[-1]:
-            return held[0], got[0]
+        far = far + got.pop(0)
         held = {d: held[d] + got[d] for d in got}
-
-
-def tables(positions, size):
+    return keep, near, far
+
+
+def table_kernel(prompt_rows, prompt_total, place, lengths, cosine, sine):
+    rows, size = cosine.shape
+    shape = cosine.shape
+    row = lax.broadcasted_iota(jnp.int32, shape, 0)
+    lane = lax.broadcasted_iota(jnp.int32, shape, 1)
+    index = place[SP] * (rows - prompt_rows) + row - prompt_rows
+    position = jnp.where(
+        row < prompt_rows,
+        place[SP] * prompt_rows + row,
+        prompt_total + index - starts_of(lengths, index),
+    )
     half = size // 2
-    frequency = jnp.exp(jnp.arange(half, dtype=F32) * (-2.0 * math.log(1000000.0) / size))
-    angles = positions.astype(F32)[:, None] * frequency[None, :]
-    cosine = jnp.cos(angles)
-    sine = jnp.sin(angles)
-    return (
-        jnp.concatenate([cosine, cosine], axis=1),
-        jnp.concatenate([-sine, sine], axis=1),
+    step = jnp.where(lane < half, lane, lane - half).astype(F32)
+    angle = position.astype(F32) * jnp.exp(step * (-2.0 * math.log(1000000.0) / size))
+    cosine[...] = jnp.cos(angle)
+    angle = jnp.sin(angle)
+    sine[...] = jnp.where(lane < half, -angle, angle)
+
+
+def tables(place, lengths, prompt_rows, prompt_total, cont_rows, size):
+    out = shape_of((prompt_rows + cont_rows, size), F32)
+    return call(
+        functools.partial(table_kernel, prompt_rows, prompt_total),
+        place,
+        (1,),
+        [pl.BlockSpec(memory_space=pltpu.SMEM)],
+        [whole(out)] * 2,
+        [out] * 2,
+        (lengths,),
+        (100 * out.size, 8 * out.size),
+    )
+
+
+def slice_kernel(place, array, out):
+    out[...] = array[...]
+
+
+def column_half(place, array, other):
+    rows, width = array.shape
+    width //= 2
+    side = 1 if other else 0
+    if width % 128:
+        at = (place[TP] + side) % 2 * width
+        return lax.dynamic_slice_in_dim(array, at, width, 1)
+    return call(
+        slice_kernel,
+        place,
+        (4,),
+        [pl.BlockSpec((rows // 4, width), lambda i, place: (i, (place[TP] + side) % 2))],
+        pl.BlockSpec((rows // 4, width), lambda i, place: (i, 0)),
+        shape_of((rows, width), BF16),
+        (array,),
+        (0, 4 * rows * width),
+    )
+
+
+def add_kernel(place, left, right, out):
+    out[...] = left[...] + right[...]
+
+
+def add_rows(place, left, right, at, rows):
+    width = left.shape[1]
+    spec = pl.BlockSpec((rows, width), lambda i, place: (at // rows, 0))
+    return call(
+        add_kernel,
+        place,
+        (1,),
+        [spec, spec],
+        pl.BlockSpec((rows, width), lambda i, place: (0, 0)),
+        shape_of((rows, width), F32),
+        (left, right),
+        (rows * width, 12 * rows * width),
     )
 
 
@@ -426,33 +504,22 @@
     cont_all = lax.all_to_all(cont, "sp", 0, 0, tiled=True)
     halves = other_halves(half, "sp", sp_count)
     partner = swap(both, "sp", 1)
-    width = out_weight.shape[1]
-    side = tp_index % 2
-    out_early = after(out_weight, cont)
-    sent = lax.dynamic_slice_in_dim(out_early, (1 - side) * (width // 2), width // 2, 1)
-    out_partner = swap(sent, "tp", 1)
+    halves = after(halves, cont)
     others = {d: swap(half, "groups", 1) for d, half in halves.items()}
     halves = both_cores(halves, "sp")
+    sent = column_half(place, after(out_weight, halves), True)
+    out_partner = swap(sent, "tp", 1)
     prompt, near_pair = near_keyval(
-        place,
-        hidden_prompt,
-        norm_gain,
-        cont,
-        both,
-        after(partner, halves, sent),
-    )
-    cont_all = after(cont_all, near_pair, others)
+        place, hidden_prompt, norm_gain, cont, both, after(partner, halves)
+    )
+    cosine, sine = tables(
+        place, sample_lengths, prompt_rows, prompt_rows * sp_count, cont_rows, size
+    )
+    cont_all = after(cont_all, near_pair, others, sent, cosine)
     others = both_cores(others, "sp")
 
-    index = sp_index * cont_rows + jnp.arange(cont_rows, dtype=jnp.int32)
-    starts = jnp.cumsum(sample_lengths, dtype=jnp.int32) - sample_lengths
-    start = jnp.max(jnp.where(index[:, None] >= starts[None, :], starts[None, :], 0), axis=1)
-    prompt_pos = sp_index * prompt_rows + jnp.arange(prompt_rows, dtype=jnp.int32)
-    positions = jnp.concatenate([prompt_pos, prompt_rows * sp_count + index - start])
-    cosine, sine = tables(positions, size)
-
-    parts = query_parts(place, cont_all, query_weight)
-    mine, other = sum_blocks(parts, "sp", sp_count)
+    keep, send = query_parts(place, cont_all, query_weight)
+    mine, near, far = sum_blocks(place, keep, send, "sp", sp_count)
     weights = [held[d] for d in range(2, sp_count) for held in (halves, others)]
     pair = keyval_rows(place, prompt, cont, cosine, sine, key_gain, near_pair, weights)
     pairs = gather_blocks(pair, "sp", sp_count)
@@ -460,9 +527,10 @@
         place,
         sample_lengths,
         mine,
-        other,
-        cosine[prompt_rows:],
-        sine[prompt_rows:],
+        near,
+        far,
+        cosine,
+        sine,
         query_gain,
         pairs,
         prompt_rows,
@@ -486,8 +554,7 @@
         )
         for e, part in enumerate(parts)
     ]
-    hidden = lax.dynamic_slice_in_dim(hidden_cont, tp_index * width, width, 1)
-    return final_sum(place, parts, hidden)
+    return final_sum(place, parts, hidden_cont)
 
 
 def solution(mesh):

time: 82.9 us -> 88.3 us (1.065)
  Pallas kernels: 18.9 us -> 24.2 us
  waiting for transfers between devices: 22.5 us -> 26 us
  local copies, waits for them, and re-layouts: 8.01 us -> 5.29 us
  other arithmetic: 1.07 us -> 0.08 us
    pallas_call x8 -> x11, Pallas kernels: 18.9 us -> 24.2 us  [call(): pl.pallas_call(kernel, out_shape=out_shape, grid_spec=pltpu.PrefetchScala...]
    ppermute x17 -> x16, waiting for transfers between devices: 10.4 us -> 14.1 us  [swap(): lax.ppermute(array, axis, [(i, i ^ bits) for i in range(lax.axis_size(axi...]
    dynamic_slice x2 -> x0, local copies, waits for them, and re-layouts: 2.12 us -> none  [the longest x1 1.19 us: on_device(): lax.dynamic_slice_in_dim(out_early, (1 - side) * (width // 2), width // 2...]
    unnamed x22 -> x26, local copies, waits for them, and re-layouts: 5.89 us -> 5.29 us
    ppermute x17 -> x16, starting transfers between devices: 19.1 us -> 19.1 us  [swap(): lax.ppermute(array, axis, [(i, i ^ bits) for i in range(lax.axis_size(axi...]
  transfers between devices with their start and end apart: 24 -> 23, of which waited for: 10 -> 9; matrix products, arithmetic and copies ran while one was open for 4% -> 0% of each run, Pallas kernels for 15% -> 21%
where the time goes in v4:
time: 88.3 us; the launch traced here: 88 us
  starting transfers between devices  32.3 us (37%)
  waiting for transfers between devices  26 us (29%)
  Pallas kernels  24.2 us (27%)
  local copies, waits for them, and re-layouts  5.29 us (6%)
    pallas_call x11, Pallas kernels, call(): pl.pallas_call(kernel, out_shape=out_shape, grid_spec=pltpu.PrefetchScala...  24.2 us
    ppermute x16, starting transfers between devices, swap(): lax.ppermute(array, axis, [(i, i ^ bits) for i in range(lax.axis_size(axi...  19.1 us
    ppermute x16, waiting for transfers between devices, swap(): lax.ppermute(array, axis, [(i, i ^ bits) for i in range(lax.axis_size(axi...  14.1 us
    ppermute x4, waiting for transfers between devices, on_device(): lax.ppermute(part, ('tp', 'sp'), [(t * sp_count + s, s * sp_count + (t ^...  11.8 us
    ppermute x4, starting transfers between devices, on_device(): lax.ppermute(part, ('tp', 'sp'), [(t * sp_count + s, s * sp_count + (t ^...  7.8 us
    unnamed x26, local copies, waits for them, and re-layouts  5.29 us
    all_to_all x1, starting transfers between devices, on_device(): cont_all = lax.all_to_all(cont, 'sp', 0, 0, tiled=True)  4.16 us
  transfers between devices with their start and end apart: 23, of which 9 were waited for; matrix products, arithmetic and copies ran while one was open for 0% of the time, Pallas kernels for 21%

profile of v4, /device:TPU:1, one launch (start us, length us, event | category | flops | bytes accessed | tf_op | source)
XLA Modules:
  0.0 88.0 jit_solution(4510197480079391845)
XLA Ops:
  0.1 1.7 %copy-done = bf16[1280,1024]{1,0:T(8,128)(2,1)S(1)} copy-done((bf16[1280,1024]{1,0:T(8,128)(2,1)S(1)}, bf16[1280,1024]{1,0:T(8,128)(2,1)}, u32[]{:S(2)}) %copy-start) | copy-done | bytes 2621464
  1.8 1.7 %shard_map.92 = (bf16[1280,128]{1,0:T(8,128)(2,1)S(1)}, bf16[1280,256]{1,0:T(8,128)(2,1)}) custom-call(s32[4]{0:T(128)S(1)} %pad_add_fusion.place, bf16[1280,1024]{1,0:T(8,128)(2,1)S(1)} %copy-done, bf16[1280,1024]{1,0:T(8,128)(2,1)S(1)} %copy-done, bf16[1280,1024]{1,0:T(8,128)(2,1)S(1)} %copy-done), custom_call_target="tpu_custom_call" | custom-call | bytes 1966080 | tf_op jit(solution)/shard_map/pallas_call | solution.py:21
  3.6 2.0 %collective-permute-start.1 = (bf16[1280,128]{1,0:T(8,128)(2,1)S(1)}, bf16[1280,128]{1,0:T(8,128)(2,1)}, u32[]{:S(2)}, u32[]{:S(2)}) collective-permute-start(bf16[1280,128]{1,0:T(8,128)(2,1)S(1)} %get-tuple-element.22), channel_id=1, source_target_pairs={{0,2},{1,3},{2,0},{3,1},{4,6},{5,7},{6,4},{7,5},{8,10},{9,11},{10,... | collective-permute-start | bytes 983048 | tf_op jit(solution)/shard_map/ppermute | solution.py:342
  6.6 1.8 %shard_map.91.cont = bf16[4,64,1280]{2,1,0:T(8,128)(2,1)} custom-call(s32[4]{0:T(128)S(1)} %pad_add_fusion.place, bf16[64,5120]{1,0:T(8,128)(2,1)S(1)} %copy-done.3, f32[1,5120]{1,0:T(1,128)S(1)} %bitcast.7), custom_call_target="tpu_custom_call" | custom-call | flops 1310720 | bytes 1310720 | tf_op jit(solution)/shard_map/pallas_call | solution.py:21
  8.3 4.8 %collective-permute-done.1.refs_0_ = bf16[1280,128]{1,0:T(8,128)(2,1)} collective-permute-done((bf16[1280,128]{1,0:T(8,128)(2,1)S(1)}, bf16[1280,128]{1,0:T(8,128)(2,1)}, u32[]{:S(2)}, u32[]{:S(2)}) %collective-permute-start.1) | collective-permute-done | bytes 327712 | tf_op jit(solution)/shard_map/ppermute | solution.py:342
  14.4 4.2 %all-to-all-start = ((bf16[4,64,1280]{2,1,0:T(8,128)(2,1)}), bf16[4,64,1280]{2,1,0:T(8,128)(2,1)}, u32[]{:S(2)}, u32[]{:S(2)}) async-start(bf16[4,64,1280]{2,1,0:T(8,128)(2,1)} %shard_map.91.cont), calls=%async_computation | async-start | bytes 1310720 | tf_op jit(solution)/shard_map/all_to_all | solution.py:504
  18.6 1.6 %collective-permute-start.3 = (bf16[1280,128]{1,0:T(8,128)(2,1)}, bf16[1280,128]{1,0:T(8,128)(2,1)}, u32[]{:S(2)}, u32[]{:S(2)}) collective-permute-start(bf16[1280,128]{1,0:T(8,128)(2,1)} %collective-permute-done.1.refs_0_), channel_id=1, source_target_pairs={{0,16},{16,0},{1,17},{17,1},{2,18},{18,2},{3,19},{19,3},{4,20},{20... | collective-permute-start | bytes 983048 | tf_op jit(solution)/shard_map/ppermute | solution.py:342
  20.1 2.3 %shard_map.94 = bf16[1024,640]{1,0:T(8,128)(2,1)} custom-call(s32[4]{0:T(128)S(1)} %pad_add_fusion.place, bf16[1024,1280]{1,0:T(8,128)(2,1)S(1)} %copy-done.1), custom_call_target="tpu_custom_call" | custom-call | bytes 2621440 | tf_op jit(solution)/shard_map/pallas_call | solution.py:21
  23.8 1.5 %shard_map.95 = (f32[192,128]{1,0:T(8,128)S(1)}, f32[192,128]{1,0:T(8,128)S(1)}) custom-call(s32[4]{0:T(128)S(1)} %pad_add_fusion.place, s32[8]{0:T(128)S(1)} %copy-done.11), custom_call_target="tpu_custom_call" | custom-call | flops 2457600 | bytes 196608 | tf_op jit(solution)/shard_map/pallas_call | solution.py:21
  25.3 3.1 %shard_map.93 = (bf16[4,128,1280]{2,1,0:T(8,128)(2,1)S(1)}, f32[192,256]{1,0:T(8,128)S(1)}) custom-call(s32[4]{0:T(128)S(1)} %pad_add_fusion.place, bf16[128,5120]{1,0:T(8,128)(2,1)S(1)} %copy-done.4, f32[1,5120]{1,0:T(1,128)S(1)} %bitcast.8, bf16[4,64,1280]{2,1,0:T(8,128)(2,1)} %shard_map.91.cont, bf16[1280,256]{1,0:T(8,128)(2,1)} %get-tuple-element.21.own, ...), custom_call_target="tpu_custom_call" | custom-call | flops 251658240 | bytes 5242880 | tf_op jit(solution)/shard_map/pallas_call | solution.py:21
  30.2 1.7 %copy-done.2 = bf16[1280,1024]{1,0:T(8,128)(2,1)S(1)} copy-done((bf16[1280,1024]{1,0:T(8,128)(2,1)S(1)}, bf16[1280,1024]{1,0:T(8,128)(2,1)}, u32[]{:S(2)}) %copy-start.2) | copy-done | bytes 2621464
  31.9 3.4 %shard_map.96 = (f32[128,1024]{1,0:T(8,128)S(1)}, f32[128,1024]{1,0:T(8,128)S(1)}) custom-call(s32[4]{0:T(128)S(1)} %pad_add_fusion.place, bf16[4,64,1280]{2,1,0:T(8,128)(2,1)} %all-to-all-done.rows, bf16[1280,1024]{1,0:T(8,128)(2,1)S(1)} %copy-done.2), custom_call_target="tpu_custom_call" | custom-call | flops 671088640 | bytes 2621440 | tf_op jit(solution)/shard_map/pallas_call | solution.py:21
  36.0 1.5 %collective-permute-done.4.right.near = f32[128,1024]{1,0:T(8,128)S(1)} collective-permute-done((f32[128,1024]{1,0:T(8,128)S(1)}, f32[128,1024]{1,0:T(8,128)S(1)}, u32[]{:S(2)}, u32[]{:S(2)}) %collective-permute-start.4) | collective-permute-done | bytes 524320 | tf_op jit(solution)/shard_map/ppermute | solution.py:342
  38.1 1.7 %collective-permute-start.5 = (f32[64,1024]{1,0:T(8,128)S(1)}, f32[64,1024]{1,0:T(8,128)S(1)}, u32[]{:S(2)}, u32[]{:S(2)}) collective-permute-start(f32[64,1024]{1,0:T(8,128)S(1)} %shard_map.97), channel_id=1, source_target_pairs={{0,2},{1,3},{2,0},{3,1},{4,6},{5,7},{6,4},{7,5},{8,10},{9,11},{10,... | collective-permute-start | bytes 786440 | tf_op jit(solution)/shard_map/ppermute | solution.py:342
  39.8 2.5 %shard_map.98.refs_0_ = bf16[192,256]{1,0:T(8,128)(2,1)S(1)} custom-call(s32[4]{0:T(128)S(1)} %pad_add_fusion.place, bf16[4,128,1280]{2,1,0:T(8,128)(2,1)S(1)} %copy-done.6, bf16[4,64,1280]{2,1,0:T(8,128)(2,1)} %shard_map.91.cont, f32[192,128]{1,0:T(8,128)S(1)} %get-tuple-element.27.cosine, f32[192,128]{1,0:T(8,128)S(1)} %get-tuple-element.31.sine, ...), custom_call_target="tpu_custom_call" | custom-call | flops 251658240 | bytes 2293760 | tf_op jit(solution)/shard_map/pallas_call | solution.py:21
  43.1 5.0 %collective-permute-done.8.refs_2_ = bf16[192,256]{1,0:T(8,128)(2,1)S(1)} collective-permute-done((bf16[192,256]{1,0:T(8,128)(2,1)S(1)}, bf16[192,256]{1,0:T(8,128)(2,1)S(1)}, u32[]{:S(2)}, u32[]{:S(2)}) %collective-permute-start.8) | collective-permute-done | bytes 98336 | tf_op jit(solution)/shard_map/ppermute | solution.py:342
  50.1 3.0 %shard_map.99.refs_0_ = bf16[64,1024]{1,0:T(8,128)(2,1)S(1)} custom-call(s32[4]{0:T(128)S(1)} %pad_add_fusion.place, s32[8]{0:T(128)S(1)} %copy-done.11, f32[128,1024]{1,0:T(8,128)S(1)} %get-tuple-element.29.left.mine, f32[128,1024]{1,0:T(8,128)S(1)} %collective-permute-done.4.right.near, f32[64,1024]{1,0:T(8,128)S(1)} %collective-permute-done.5.far, ...), custom_call_target="tpu_custom_call" | custom-call | flops 201326592 | bytes 1048576 | tf_op jit(solution)/shard_map/pallas_call | solution.py:21
  53.0 1.5 %collective-permute-start.11 = (bf16[64,1024]{1,0:T(8,128)(2,1)S(1)}, bf16[64,1024]{1,0:T(8,128)(2,1)S(1)}, u32[]{:S(2)}, u32[]{:S(2)}) collective-permute-start(bf16[64,1024]{1,0:T(8,128)(2,1)S(1)} %shard_map.99.refs_0_), channel_id=1, source_target_pairs={{0,2},{1,3},{2,0},{3,1},{4,6},{5,7},{6,4},{7,5},{8,10},{9,11},{10,... | collective-permute-start | bytes 393224 | tf_op jit(solution)/shard_map/ppermute | solution.py:342
  59.0 2.6 %collective-permute-start.14 = (bf16[64,1024]{1,0:T(8,128)(2,1)S(1)}, bf16[64,1024]{1,0:T(8,128)(2,1)S(1)}, u32[]{:S(2)}, u32[]{:S(2)}) collective-permute-start(bf16[64,1024]{1,0:T(8,128)(2,1)S(1)} %collective-permute-done.13.refs_4_), channel_id=1, source_target_pairs={{0,1},{1,0},{2,3},{3,2},{4,5},{5,4},{6,7},{7,6},{8,9},{9,8},{10,11... | collective-permute-start | bytes 393224 | tf_op jit(solution)/shard_map/ppermute | solution.py:342
  64.1 3.0 %shard_map.100 = (bf16[64,640]{1,0:T(8,128)(2,1)S(1)}, bf16[64,640]{1,0:T(8,128)(2,1)S(1)}, bf16[64,640]{1,0:T(8,128)(2,1)S(1)}, bf16[64,640]{1,0:T(8,128)(2,1)S(1)}) custom-call(s32[4]{0:T(128)S(1)} %pad_add_fusion.place, bf16[64,1024]{1,0:T(8,128)(2,1)S(1)} %shard_map.99.refs_0_, bf16[64,1024]{1,0:T(8,128)(2,1)S(1)} %collective-permute-done.10.refs_1_, ...), custom_call_target="tpu_custom_call" | custom-call | flops 671088640 | bytes 2621440 | tf_op jit(solution)/shard_map/pallas_call | solution.py:21
  67.1 2.3 %collective-permute-start.18 = (bf16[64,640]{1,0:T(8,128)(2,1)S(1)}, bf16[64,640]{1,0:T(8,128)(2,1)S(1)}, u32[]{:S(2)}, u32[]{:S(2)}) collective-permute-start(bf16[64,640]{1,0:T(8,128)(2,1)S(1)} %get-tuple-element.33), channel_id=1, source_target_pairs={{0,0},{1,4},{2,8},{3,12},{4,1},{5,5},{6,9},{7,13},{8,2},{9,6},{10,... | collective-permute-start | bytes 245768 | tf_op jit(solution)/shard_map/ppermute | solution.py:546
  69.5 5.0 %collective-permute-start.20 = (bf16[64,640]{1,0:T(8,128)(2,1)S(1)}, bf16[64,640]{1,0:T(8,128)(2,1)S(1)}, u32[]{:S(2)}, u32[]{:S(2)}) collective-permute-start(bf16[64,640]{1,0:T(8,128)(2,1)S(1)} %get-tuple-element.35), channel_id=1, source_target_pairs={{0,2},{1,6},{2,10},{3,14},{4,3},{5,7},{6,11},{7,15},{8,0},{9,4},{1... | collective-permute-start | bytes 245768 | tf_op jit(solution)/shard_map/ppermute | solution.py:546
  74.9 5.3 %collective-permute-done.20.refs_2_ = bf16[64,640]{1,0:T(8,128)(2,1)S(1)} collective-permute-done((bf16[64,640]{1,0:T(8,128)(2,1)S(1)}, bf16[64,640]{1,0:T(8,128)(2,1)S(1)}, u32[]{:S(2)}, u32[]{:S(2)}) %collective-permute-start.20) | collective-permute-done | bytes 81952 | tf_op jit(solution)/shard_map/ppermute | solution.py:546
  80.2 6.4 %collective-permute-done.21.refs_3_ = bf16[64,640]{1,0:T(8,128)(2,1)S(1)} collective-permute-done((bf16[64,640]{1,0:T(8,128)(2,1)S(1)}, bf16[64,640]{1,0:T(8,128)(2,1)S(1)}, u32[]{:S(2)}, u32[]{:S(2)}) %collective-permute-start.21) | collective-permute-done | bytes 81952 | tf_op jit(solution)/shard_map/ppermute | solution.py:546
  (60 shorter events, 18.1 us)
Async XLA Ops:
  3.6 9.6 %collective-permute-start.1 = (bf16[1280,128]{1,0:T(8,128)(2,1)S(1)}, bf16[1280,128]{1,0:T(8,128)(2,1)}, u32[]{:S(2)}, u32[]{:S(2)}) collective-permute-start(bf16[1280,128]{1,0:T(8,128)(2,1)S(1)} %get-tuple-element.22), channel_id=1, source_target_pairs={{0,2},{1,3},{2,0},{3,1},{4,6},{5,7},{6,4},{7,5},{8,10},{9,11},{10,... | collective-permute-start | bytes 983048 | tf_op jit(solution)/shard_map/ppermute | solution.py:342
  5.6 19.6 %collective-permute-start = (bf16[1280,256]{1,0:T(8,128)(2,1)}, bf16[1280,256]{1,0:T(8,128)(2,1)}, u32[]{:S(2)}, u32[]{:S(2)}) collective-permute-start(bf16[1280,256]{1,0:T(8,128)(2,1)} %get-tuple-element.21.own), channel_id=1, source_target_pairs={{0,1},{1,0},{2,3},{3,2},{4,5},{5,4},{6,7},{7,6},{8,9},{9,8},{10,11... | collective-permute-start | bytes 1966088 | tf_op jit(solution)/shard_map/ppermute | solution.py:342
  6.6 13.6 %copy-start.1 = (bf16[1024,1280]{1,0:T(8,128)(2,1)S(1)}, bf16[1024,1280]{1,0:T(8,128)(2,1)}, u32[]{:S(2)}) copy-start(bf16[1024,1280]{1,0:T(8,128)(2,1)} %refs_8_.1) | copy-start | bytes 7864324
  13.1 7.0 %collective-permute-start.2 = (bf16[1280,128]{1,0:T(8,128)(2,1)}, bf16[1280,128]{1,0:T(8,128)(2,1)}, u32[]{:S(2)}, u32[]{:S(2)}) collective-permute-start(bf16[1280,128]{1,0:T(8,128)(2,1)} %collective-permute-done.1.refs_0_), channel_id=1, source_target_pairs={{0,1},{1,0},{2,3},{3,2},{4,5},{5,4},{6,7},{7,6},{8,9},{9,8},{10,11... | collective-permute-start | bytes 983048 | tf_op jit(solution)/shard_map/ppermute | solution.py:342
  14.4 15.8 %all-to-all-start = ((bf16[4,64,1280]{2,1,0:T(8,128)(2,1)}), bf16[4,64,1280]{2,1,0:T(8,128)(2,1)}, u32[]{:S(2)}, u32[]{:S(2)}) async-start(bf16[4,64,1280]{2,1,0:T(8,128)(2,1)} %shard_map.91.cont), calls=%async_computation | async-start | bytes 1310720 | tf_op jit(solution)/shard_map/all_to_all | solution.py:504
  18.6 11.6 %collective-permute-start.3 = (bf16[1280,128]{1,0:T(8,128)(2,1)}, bf16[1280,128]{1,0:T(8,128)(2,1)}, u32[]{:S(2)}, u32[]{:S(2)}) collective-permute-start(bf16[1280,128]{1,0:T(8,128)(2,1)} %collective-permute-done.1.refs_0_), channel_id=1, source_target_pairs={{0,16},{16,0},{1,17},{17,1},{2,18},{18,2},{3,19},{19,3},{4,20},{20... | collective-permute-start | bytes 983048 | tf_op jit(solution)/shard_map/ppermute | solution.py:342
  22.5 41.6 %collective-permute-start.17 = (bf16[1024,640]{1,0:T(8,128)(2,1)}, bf16[1024,640]{1,0:T(8,128)(2,1)}, u32[]{:S(2)}, u32[]{:S(2)}) collective-permute-start(bf16[1024,640]{1,0:T(8,128)(2,1)} %shard_map.94), channel_id=1, source_target_pairs={{0,4},{4,0},{8,12},{12,8},{1,5},{5,1},{9,13},{13,9},{2,6},{6,2},{1... | collective-permute-start | bytes 3932168 | tf_op jit(solution)/shard_map/ppermute | solution.py:342
  35.3 2.2 %collective-permute-start.4 = (f32[128,1024]{1,0:T(8,128)S(1)}, f32[128,1024]{1,0:T(8,128)S(1)}, u32[]{:S(2)}, u32[]{:S(2)}) collective-permute-start(f32[128,1024]{1,0:T(8,128)S(1)} %get-tuple-element.30), channel_id=1, source_target_pairs={{0,1},{1,0},{2,3},{3,2},{4,5},{5,4},{6,7},{7,6},{8,9},{9,8},{10,11... | collective-permute-start | bytes 1572872 | tf_op jit(solution)/shard_map/ppermute | solution.py:342
  35.9 3.8 %collective-permute-start.6 = (bf16[1280,128]{1,0:T(8,128)(2,1)}, bf16[1280,128]{1,0:T(8,128)(2,1)S(1)}, u32[]{:S(2)}, u32[]{:S(2)}) collective-permute-start(bf16[1280,128]{1,0:T(8,128)(2,1)} %collective-permute-done.3.refs_1_), channel_id=1, source_target_pairs={{0,1},{1,0},{2,3},{3,2},{4,5},{5,4},{6,7},{7,6},{8,9},{9,8},{10,11... | collective-permute-start | bytes 983048 | tf_op jit(solution)/shard_map/ppermute | solution.py:342
  38.1 12.0 %collective-permute-start.5 = (f32[64,1024]{1,0:T(8,128)S(1)}, f32[64,1024]{1,0:T(8,128)S(1)}, u32[]{:S(2)}, u32[]{:S(2)}) collective-permute-start(f32[64,1024]{1,0:T(8,128)S(1)} %shard_map.97), channel_id=1, source_target_pairs={{0,2},{1,3},{2,0},{3,1},{4,6},{5,7},{6,4},{7,5},{8,10},{9,11},{10,... | collective-permute-start | bytes 786440 | tf_op jit(solution)/shard_map/ppermute | solution.py:342
  42.3 5.9 %collective-permute-start.8 = (bf16[192,256]{1,0:T(8,128)(2,1)S(1)}, bf16[192,256]{1,0:T(8,128)(2,1)S(1)}, u32[]{:S(2)}, u32[]{:S(2)}) collective-permute-start(bf16[192,256]{1,0:T(8,128)(2,1)S(1)} %shard_map.98.refs_0_), channel_id=1, source_target_pairs={{0,2},{1,3},{2,0},{3,1},{4,6},{5,7},{6,4},{7,5},{8,10},{9,11},{10,... | collective-permute-start | bytes 294920 | tf_op jit(solution)/shard_map/ppermute | solution.py:342
  42.4 6.7 %collective-permute-start.7 = (bf16[192,256]{1,0:T(8,128)(2,1)S(1)}, bf16[192,256]{1,0:T(8,128)(2,1)S(1)}, u32[]{:S(2)}, u32[]{:S(2)}) collective-permute-start(bf16[192,256]{1,0:T(8,128)(2,1)S(1)} %shard_map.98.refs_0_), channel_id=1, source_target_pairs={{0,1},{1,0},{2,3},{3,2},{4,5},{5,4},{6,7},{7,6},{8,9},{9,8},{10,11... | collective-permute-start | bytes 294920 | tf_op jit(solution)/shard_map/ppermute | solution.py:342
  48.2 1.9 %collective-permute-start.9 = (bf16[192,256]{1,0:T(8,128)(2,1)S(1)}, bf16[192,256]{1,0:T(8,128)(2,1)S(1)}, u32[]{:S(2)}, u32[]{:S(2)}) collective-permute-start(bf16[192,256]{1,0:T(8,128)(2,1)S(1)} %collective-permute-done.8.refs_2_), channel_id=1, source_target_pairs={{0,1},{1,0},{2,3},{3,2},{4,5},{5,4},{6,7},{7,6},{8,9},{9,8},{10,11... | collective-permute-start | bytes 294920 | tf_op jit(solution)/shard_map/ppermute | solution.py:342
  53.0 4.8 %collective-permute-start.11 = (bf16[64,1024]{1,0:T(8,128)(2,1)S(1)}, bf16[64,1024]{1,0:T(8,128)(2,1)S(1)}, u32[]{:S(2)}, u32[]{:S(2)}) collective-permute-start(bf16[64,1024]{1,0:T(8,128)(2,1)S(1)} %shard_map.99.refs_0_), channel_id=1, source_target_pairs={{0,2},{1,3},{2,0},{3,1},{4,6},{5,7},{6,4},{7,5},{8,10},{9,11},{10,... | collective-permute-start | bytes 393224 | tf_op jit(solution)/shard_map/ppermute | solution.py:342
  54.6 4.5 %collective-permute-start.13 = (bf16[64,1024]{1,0:T(8,128)(2,1)S(1)}, bf16[64,1024]{1,0:T(8,128)(2,1)S(1)}, u32[]{:S(2)}, u32[]{:S(2)}) collective-permute-start(bf16[64,1024]{1,0:T(8,128)(2,1)S(1)} %shard_map.99.refs_0_), channel_id=1, source_target_pairs={{0,4},{1,5},{2,6},{3,7},{4,0},{5,1},{6,2},{7,3},{8,12},{9,13},{10,... | collective-permute-start | bytes 393224 | tf_op jit(solution)/shard_map/ppermute | solution.py:351
  54.7 6.9 %collective-permute-start.15 = (bf16[64,1024]{1,0:T(8,128)(2,1)S(1)}, bf16[64,1024]{1,0:T(8,128)(2,1)S(1)}, u32[]{:S(2)}, u32[]{:S(2)}) collective-permute-start(bf16[64,1024]{1,0:T(8,128)(2,1)S(1)} %shard_map.99.refs_0_), channel_id=1, source_target_pairs={{0,6},{1,7},{2,4},{3,5},{4,2},{5,3},{6,0},{7,1},{8,14},{9,15},{10,... | collective-permute-start | bytes 393224 | tf_op jit(solution)/shard_map/ppermute | solution.py:351
  55.8 7.3 %collective-permute-start.10 = (bf16[64,1024]{1,0:T(8,128)(2,1)S(1)}, bf16[64,1024]{1,0:T(8,128)(2,1)S(1)}, u32[]{:S(2)}, u32[]{:S(2)}) collective-permute-start(bf16[64,1024]{1,0:T(8,128)(2,1)S(1)} %shard_map.99.refs_0_), channel_id=1, source_target_pairs={{0,1},{1,0},{2,3},{3,2},{4,5},{5,4},{6,7},{7,6},{8,9},{9,8},{10,11... | collective-permute-start | bytes 393224 | tf_op jit(solution)/shard_map/ppermute | solution.py:342
  57.8 5.3 %collective-permute-start.12 = (bf16[64,1024]{1,0:T(8,128)(2,1)S(1)}, bf16[64,1024]{1,0:T(8,128)(2,1)S(1)}, u32[]{:S(2)}, u32[]{:S(2)}) collective-permute-start(bf16[64,1024]{1,0:T(8,128)(2,1)S(1)} %collective-permute-done.11.refs_2_), channel_id=1, source_target_pairs={{0,1},{1,0},{2,3},{3,2},{4,5},{5,4},{6,7},{7,6},{8,9},{9,8},{10,11... | collective-permute-start | bytes 393224 | tf_op jit(solution)/shard_map/ppermute | solution.py:342
  59.0 4.1 %collective-permute-start.14 = (bf16[64,1024]{1,0:T(8,128)(2,1)S(1)}, bf16[64,1024]{1,0:T(8,128)(2,1)S(1)}, u32[]{:S(2)}, u32[]{:S(2)}) collective-permute-start(bf16[64,1024]{1,0:T(8,128)(2,1)S(1)} %collective-permute-done.13.refs_4_), channel_id=1, source_target_pairs={{0,1},{1,0},{2,3},{3,2},{4,5},{5,4},{6,7},{7,6},{8,9},{9,8},{10,11... | collective-permute-start | bytes 393224 | tf_op jit(solution)/shard_map/ppermute | solution.py:342
  61.7 2.4 %collective-permute-start.16 = (bf16[64,1024]{1,0:T(8,128)(2,1)S(1)}, bf16[64,1024]{1,0:T(8,128)(2,1)S(1)}, u32[]{:S(2)}, u32[]{:S(2)}) collective-permute-start(bf16[64,1024]{1,0:T(8,128)(2,1)S(1)} %collective-permute-done.15.refs_6_), channel_id=1, source_target_pairs={{0,1},{1,0},{2,3},{3,2},{4,5},{5,4},{6,7},{7,6},{8,9},{9,8},{10,11... | collective-permute-start | bytes 393224 | tf_op jit(solution)/shard_map/ppermute | solution.py:342
  67.1 7.8 %collective-permute-start.18 = (bf16[64,640]{1,0:T(8,128)(2,1)S(1)}, bf16[64,640]{1,0:T(8,128)(2,1)S(1)}, u32[]{:S(2)}, u32[]{:S(2)}) collective-permute-start(bf16[64,640]{1,0:T(8,128)(2,1)S(1)} %get-tuple-element.33), channel_id=1, source_target_pairs={{0,0},{1,4},{2,8},{3,12},{4,1},{5,5},{6,9},{7,13},{8,2},{9,6},{10,... | collective-permute-start | bytes 245768 | tf_op jit(solution)/shard_map/ppermute | solution.py:546
  69.4 5.5 %collective-permute-start.19 = (bf16[64,640]{1,0:T(8,128)(2,1)S(1)}, bf16[64,640]{1,0:T(8,128)(2,1)S(1)}, u32[]{:S(2)}, u32[]{:S(2)}) collective-permute-start(bf16[64,640]{1,0:T(8,128)(2,1)S(1)} %get-tuple-element.34), channel_id=1, source_target_pairs={{0,1},{1,5},{2,9},{3,13},{4,0},{5,4},{6,8},{7,12},{8,3},{9,7},{10,... | collective-permute-start | bytes 245768 | tf_op jit(solution)/shard_map/ppermute | solution.py:546
  69.5 10.7 %collective-permute-start.20 = (bf16[64,640]{1,0:T(8,128)(2,1)S(1)}, bf16[64,640]{1,0:T(8,128)(2,1)S(1)}, u32[]{:S(2)}, u32[]{:S(2)}) collective-permute-start(bf16[64,640]{1,0:T(8,128)(2,1)S(1)} %get-tuple-element.35), channel_id=1, source_target_pairs={{0,2},{1,6},{2,10},{3,14},{4,3},{5,7},{6,11},{7,15},{8,0},{9,4},{1... | collective-permute-start | bytes 245768 | tf_op jit(solution)/shard_map/ppermute | solution.py:546
  74.5 12.2 %collective-permute-start.21 = (bf16[64,640]{1,0:T(8,128)(2,1)S(1)}, bf16[64,640]{1,0:T(8,128)(2,1)S(1)}, u32[]{:S(2)}, u32[]{:S(2)}) collective-permute-start(bf16[64,640]{1,0:T(8,128)(2,1)S(1)} %get-tuple-element.36), channel_id=1, source_target_pairs={{0,3},{1,7},{2,11},{3,15},{4,2},{5,6},{6,10},{7,14},{8,1},{9,5},{1... | collective-permute-start | bytes 245768 | tf_op jit(solution)/shard_map/ppermute | solution.py:546
  (12 other events, 53.7 us)

commit v5 on v4

--- a/solution.py
+++ b/solution.py
@@ -53,23 +53,50 @@
         out[j] = normed[:, j * depth : (j + 1) * depth]
 
 
-def norm_kernel(place, hidden, gain, out):
-    split_normed(hidden, gain, out)
+def norm_kernel(place, hidden, gain, out, split):
+    split_normed(hidden, gain, split)
+    for d in range(out.shape[0]):
+        out[d] = split[place[SP] ^ 1 ^ 2 * d]
 
 
 def norm_split(place, hidden, gain, count):
     rows, width = hidden.shape
-    step = min(rows, 64)
-    out = (count, rows, width // count)
+    step = rows if rows % 32 else 32
+    depth = width // count
     return call(
         norm_kernel,
         place,
         (rows // step,),
         [pl.BlockSpec((step, width), lambda i, place: (i, 0)), whole(gain)],
-        pl.BlockSpec((count, step, width // count), lambda i, place: (0, i, 0)),
-        shape_of(out, BF16),
+        [
+            pl.BlockSpec((n, step, depth), lambda i, place: (0, i, 0))
+            for n in (count // 2, count)
+        ],
+        [shape_of((n, rows, depth), BF16) for n in (count // 2, count)],
         (hidden, gain),
         (4 * rows * width, 4 * rows * width),
+    )
+
+
+def pack_kernel(place, cont, other, *outs):
+    for d, out in enumerate(outs, 1):
+        out[0] = cont[place[SP] ^ 2 * d]
+        out[1] = other[d]
+
+
+def pack(place, cont, other):
+    count, rows, depth = cont.shape
+    block = (2, rows, depth)
+    sent = count // 2 - 1
+    return call(
+        pack_kernel,
+        place,
+        (1,),
+        [whole(cont), whole(other)],
+        [pl.BlockSpec(block, lambda i, place: (0, 0, 0))] * sent,
+        [shape_of(block, BF16)] * sent,
+        (cont, other),
+        (0, 8 * sent * rows * depth),
     )
 
 
@@ -100,17 +127,20 @@
     )
 
 
-def query_kernel(count, place, rows, weight, keep, send):
-    block = rows.shape[1]
-    left = jnp.concatenate([rows[place[SP] ^ d] for d in range(count)], axis=0)
-    part = jnp.dot(left, weight[...], preferred_element_type=F32)
+def query_kernel(count, place, *refs):
+    cont, other, chips, (weight, keep, send) = refs[0], refs[1], refs[2:-3], refs[-3:]
+    block = cont.shape[1]
+    rows = [cont[place[SP]], other[0]]
+    for chip in chips:
+        rows += [chip[0], chip[1]]
+    part = jnp.dot(jnp.concatenate(rows, axis=0), weight[...], preferred_element_type=F32)
     for d in range(count):
         at = d // 2 * block
         (keep, send)[d % 2][at : at + block, :] = part[d * block : (d + 1) * block]
 
 
-def query_parts(place, rows, weight):
-    count, block, depth = rows.shape
+def query_parts(place, cont, got, weight):
+    count, block, depth = cont.shape
     width = weight.shape[1]
     step = min(width, 256)
     half = count // 2 * block
@@ -118,10 +148,11 @@
         functools.partial(query_kernel, count),
         place,
         (width // step,),
-        [whole(rows), pl.BlockSpec((depth, step), lambda i, place: (0, i))],
+        [whole(a) for a in (cont, *got)]
+        + [pl.BlockSpec((depth, step), lambda i, place: (0, i))],
         [pl.BlockSpec((half, step), lambda i, place: (0, i))] * 2,
         [shape_of((half, width), F32)] * 2,
-        (rows, weight),
+        (cont, *got, weight),
         (2 * count * block * depth * width, 2 * depth * width),
     )
 
@@ -499,12 +530,14 @@
     query_gain = query_gain[None, :]
     key_gain = key_gain[None, :]
 
-    cont = norm_split(place, hidden_cont, norm_gain, sp_count)
     half, both = pick_columns(place, keyval_weight, size)
-    cont_all = lax.all_to_all(cont, "sp", 0, 0, tiled=True)
     halves = other_halves(half, "sp", sp_count)
+    block, cont = norm_split(after(place, half), hidden_cont, norm_gain, sp_count)
+    other = swap(block, "sp", 1)
+    packed = pack(place, cont, other)
+    got = [swap(block, "sp", 2 * d) for d, block in enumerate(packed, 1)]
     partner = swap(both, "sp", 1)
-    halves = after(halves, cont)
+    halves = after(halves, packed)
     others = {d: swap(half, "groups", 1) for d, half in halves.items()}
     halves = both_cores(halves, "sp")
     sent = column_half(place, after(out_weight, halves), True)
@@ -515,10 +548,10 @@
     cosine, sine = tables(
         place, sample_lengths, prompt_rows, prompt_rows * sp_count, cont_rows, size
     )
-    cont_all = after(cont_all, near_pair, others, sent, cosine)
+    got = after(got, near_pair, others, sent, cosine)
     others = both_cores(others, "sp")
 
-    keep, send = query_parts(place, cont_all, query_weight)
+    keep, send = query_parts(place, cont, [other] + got, query_weight)
     mine, near, far = sum_blocks(place, keep, send, "sp", sp_count)
     weights = [held[d] for d in range(2, sp_count) for held in (halves, others)]
     pair = keyval_rows(place, prompt, cont, cosine, sine, key_gain, near_pair, weights)

time: 88.3 us -> 81.1 us (0.918)
  Pallas kernels: 24.2 us -> 16.5 us
  waiting for transfers between devices: 26 us -> 33.1 us
  local copies, waits for them, and re-layouts: 5.29 us -> 1.93 us
  starting transfers between devices: 32.3 us -> 29.2 us
    pallas_call x11 -> x12, Pallas kernels: 24.2 us -> 16.5 us  [call(): pl.pallas_call(kernel, out_shape=out_shape, grid_spec=pltpu.PrefetchScala...]
    ppermute x16 -> x18, waiting for transfers between devices: 14.1 us -> 19.7 us  [swap(): lax.ppermute(array, axis, [(i, i ^ bits) for i in range(lax.axis_size(axi...]
    all_to_all x1 -> x0, starting transfers between devices: 4.16 us -> none  [on_device(): cont_all = lax.all_to_all(cont, 'sp', 0, 0, tiled=True)]
    unnamed x26 -> x18, local copies, waits for them, and re-layouts: 5.29 us -> 1.93 us
    ppermute x4, waiting for transfers between devices: 11.8 us -> 13 us  [on_device(): lax.ppermute(part, ('tp', 'sp'), [(t * sp_count + s, s * sp_count + (t ^...]
    ppermute x16 -> x18, starting transfers between devices: 19.1 us -> 20.1 us  [swap(): lax.ppermute(array, axis, [(i, i ^ bits) for i in range(lax.axis_size(axi...]
  transfers between devices with their start and end apart: 23 -> 24, of which waited for: 9 -> 11; matrix products, arithmetic and copies ran while one was open for 0% -> 0% of each run, Pallas kernels for 21% -> 14%
where the time goes in v5:
time: 81.1 us; the launch traced here: 81 us
  waiting for transfers between devices  33.1 us (41%)
  starting transfers between devices  29.2 us (36%)
  Pallas kernels  16.5 us (20%)
  local copies, waits for them, and re-layouts  1.93 us (2%)
    ppermute x18, starting transfers between devices, swap(): lax.ppermute(array, axis, [(i, i ^ bits) for i in range(lax.axis_size(axi...  20.1 us
    ppermute x18, waiting for transfers between devices, swap(): lax.ppermute(array, axis, [(i, i ^ bits) for i in range(lax.axis_size(axi...  19.7 us
    pallas_call x12, Pallas kernels, call(): pl.pallas_call(kernel, out_shape=out_shape, grid_spec=pltpu.PrefetchScala...  16.5 us
    ppermute x4, waiting for transfers between devices, on_device(): lax.ppermute(part, ('tp', 'sp'), [(t * sp_count + s, s * sp_count + (t ^...  13 us
    ppermute x4, starting transfers between devices, on_device(): lax.ppermute(part, ('tp', 'sp'), [(t * sp_count + s, s * sp_count + (t ^...  7.63 us
    unnamed x18, local copies, waits for them, and re-layouts  1.93 us
  transfers between devices with their start and end apart: 24, of which 11 were waited for; matrix products, arithmetic and copies ran while one was open for 0% of the time, Pallas kernels for 14%

profile of v5, /device:TPU:1, one launch (start us, length us, event | category | flops | bytes accessed | tf_op | source)
XLA Modules:
  0.0 81.0 jit_solution(15515587580866551468)
XLA Ops:
  0.1 1.7 %copy-done = bf16[1280,1024]{1,0:T(8,128)(2,1)S(1)} copy-done((bf16[1280,1024]{1,0:T(8,128)(2,1)S(1)}, bf16[1280,1024]{1,0:T(8,128)(2,1)}, u32[]{:S(2)}) %copy-start) | copy-done | bytes 2621464
  4.1 2.7 %collective-permute-start.3 = (bf16[1280,128]{1,0:T(8,128)(2,1)S(1)}, bf16[1280,128]{1,0:T(8,128)(2,1)S(1)}, u32[]{:S(2)}, u32[]{:S(2)}) collective-permute-start(bf16[1280,128]{1,0:T(8,128)(2,1)S(1)} %get-tuple-element.24), channel_id=1, source_target_pairs={{0,2},{1,3},{2,0},{3,1},{4,6},{5,7},{6,4},{7,5},{8,10},{9,11},{10,... | collective-permute-start | bytes 983048 | tf_op jit(solution)/shard_map/ppermute | solution.py:373
  7.7 7.0 %collective-permute-done.3.refs_0_ = bf16[1280,128]{1,0:T(8,128)(2,1)S(1)} collective-permute-done((bf16[1280,128]{1,0:T(8,128)(2,1)S(1)}, bf16[1280,128]{1,0:T(8,128)(2,1)S(1)}, u32[]{:S(2)}, u32[]{:S(2)}) %collective-permute-start.3) | collective-permute-done | bytes 327712 | tf_op jit(solution)/shard_map/ppermute | solution.py:373
  15.4 1.5 %collective-permute-start.5 = (bf16[1280,128]{1,0:T(8,128)(2,1)S(1)}, bf16[1280,128]{1,0:T(8,128)(2,1)S(1)}, u32[]{:S(2)}, u32[]{:S(2)}) collective-permute-start(bf16[1280,128]{1,0:T(8,128)(2,1)S(1)} %collective-permute-done.3.refs_0_), channel_id=1, source_target_pairs={{0,16},{16,0},{1,17},{17,1},{2,18},{18,2},{3,19},{19,3},{4,20},{20... | collective-permute-start | bytes 983048 | tf_op jit(solution)/shard_map/ppermute | solution.py:373
  16.9 1.2 %collective-permute-start.1 = (bf16[2,64,1280]{2,1,0:T(8,128)(2,1)S(1)}, bf16[2,64,1280]{2,1,0:T(8,128)(2,1)S(1)}, u32[]{:S(2)}, u32[]{:S(2)}) collective-permute-start(bf16[2,64,1280]{2,1,0:T(8,128)(2,1)S(1)} %shard_map.93), channel_id=1, source_target_pairs={{0,2},{1,3},{2,0},{3,1},{4,6},{5,7},{6,4},{7,5},{8,10},{9,11},{10,... | collective-permute-start | bytes 983048 | tf_op jit(solution)/shard_map/ppermute | solution.py:373
  19.1 1.4 %collective-permute-start.19 = (bf16[1024,640]{1,0:T(8,128)(2,1)S(1)}, bf16[1024,640]{1,0:T(8,128)(2,1)S(1)}, u32[]{:S(2)}, u32[]{:S(2)}) collective-permute-start(bf16[1024,640]{1,0:T(8,128)(2,1)S(1)} %shard_map.95), channel_id=1, source_target_pairs={{0,4},{4,0},{8,12},{12,8},{1,5},{5,1},{9,13},{13,9},{2,6},{6,2},{1... | collective-permute-start | bytes 3932168 | tf_op jit(solution)/shard_map/ppermute | solution.py:373
  20.4 1.5 %shard_map.96 = (f32[192,128]{1,0:T(8,128)S(1)}, f32[192,128]{1,0:T(8,128)S(1)}) custom-call(s32[4]{0:T(128)S(1)} %pad_add_fusion.place, s32[8]{0:T(128)S(1)} %copy-done.7), custom_call_target="tpu_custom_call" | custom-call | flops 2457600 | bytes 196608 | tf_op jit(solution)/shard_map/pallas_call | solution.py:21
  22.0 1.6 %shard_map.94 = (bf16[4,128,1280]{2,1,0:T(8,128)(2,1)S(1)}, f32[192,256]{1,0:T(8,128)S(1)}) custom-call(s32[4]{0:T(128)S(1)} %pad_add_fusion.place, bf16[128,5120]{1,0:T(8,128)(2,1)S(1)} %copy-done.4, f32[1,5120]{1,0:T(1,128)S(1)} %bitcast.8, bf16[4,64,1280]{2,1,0:T(8,128)(2,1)S(1)} %get-tuple-element.26.cont.refs_0_, ...), custom_call_target="tpu_custom_call" | custom-call | flops 251658240 | bytes 5242880 | tf_op jit(solution)/shard_map/pallas_call | solution.py:21
  23.6 1.3 %collective-permute-done.5.refs_1_ = bf16[1280,128]{1,0:T(8,128)(2,1)S(1)} collective-permute-done((bf16[1280,128]{1,0:T(8,128)(2,1)S(1)}, bf16[1280,128]{1,0:T(8,128)(2,1)S(1)}, u32[]{:S(2)}, u32[]{:S(2)}) %collective-permute-start.5) | collective-permute-done | bytes 327712 | tf_op jit(solution)/shard_map/ppermute | solution.py:373
  26.0 2.4 %shard_map.97 = (f32[128,1024]{1,0:T(8,128)S(1)}, f32[128,1024]{1,0:T(8,128)S(1)}) custom-call(s32[4]{0:T(128)S(1)} %pad_add_fusion.place, bf16[4,64,1280]{2,1,0:T(8,128)(2,1)S(1)} %get-tuple-element.26.cont.refs_0_, bf16[2,64,1280]{2,1,0:T(8,128)(2,1)S(1)} %collective-permute-done.other.refs_1_, bf16[2,64,1280]{2,1,0:T(8,128)(2,1)S(1)} %collective-permute-done.1.refs_2_, ...), custom_call_target="tpu_custom_call" | custom-call | flops 671088640 | bytes 2621440 | tf_op jit(solution)/shard_map/pallas_call | solution.py:21
  29.6 1.5 %collective-permute-done.6.right.near = f32[128,1024]{1,0:T(8,128)S(1)} collective-permute-done((f32[128,1024]{1,0:T(8,128)S(1)}, f32[128,1024]{1,0:T(8,128)S(1)}, u32[]{:S(2)}, u32[]{:S(2)}) %collective-permute-start.6) | collective-permute-done | bytes 524320 | tf_op jit(solution)/shard_map/ppermute | solution.py:373
  31.7 1.3 %collective-permute-start.7 = (f32[64,1024]{1,0:T(8,128)S(1)}, f32[64,1024]{1,0:T(8,128)S(1)}, u32[]{:S(2)}, u32[]{:S(2)}) collective-permute-start(f32[64,1024]{1,0:T(8,128)S(1)} %shard_map.98), channel_id=1, source_target_pairs={{0,2},{1,3},{2,0},{3,1},{4,6},{5,7},{6,4},{7,5},{8,10},{9,11},{10,... | collective-permute-start | bytes 786440 | tf_op jit(solution)/shard_map/ppermute | solution.py:373
  35.3 6.0 %collective-permute-done.10.refs_2_ = bf16[192,256]{1,0:T(8,128)(2,1)S(1)} collective-permute-done((bf16[192,256]{1,0:T(8,128)(2,1)S(1)}, bf16[192,256]{1,0:T(8,128)(2,1)S(1)}, u32[]{:S(2)}, u32[]{:S(2)}) %collective-permute-start.10) | collective-permute-done | bytes 98336 | tf_op jit(solution)/shard_map/ppermute | solution.py:373
  43.5 3.0 %shard_map.100.refs_0_ = bf16[64,1024]{1,0:T(8,128)(2,1)S(1)} custom-call(s32[4]{0:T(128)S(1)} %pad_add_fusion.place, s32[8]{0:T(128)S(1)} %copy-done.7, f32[128,1024]{1,0:T(8,128)S(1)} %get-tuple-element.35.left.mine, f32[128,1024]{1,0:T(8,128)S(1)} %collective-permute-done.6.right.near, f32[64,1024]{1,0:T(8,128)S(1)} %collective-permute-done.7.far, ...), custom_call_target="tpu_custom_call" | custom-call | flops 201326592 | bytes 1048576 | tf_op jit(solution)/shard_map/pallas_call | solution.py:21
  46.5 1.3 %collective-permute-start.13 = (bf16[64,1024]{1,0:T(8,128)(2,1)S(1)}, bf16[64,1024]{1,0:T(8,128)(2,1)S(1)}, u32[]{:S(2)}, u32[]{:S(2)}) collective-permute-start(bf16[64,1024]{1,0:T(8,128)(2,1)S(1)} %shard_map.100.refs_0_), channel_id=1, source_target_pairs={{0,2},{1,3},{2,0},{3,1},{4,6},{5,7},{6,4},{7,5},{8,10},{9,11},{10,... | collective-permute-start | bytes 393224 | tf_op jit(solution)/shard_map/ppermute | solution.py:373
  47.8 1.3 %collective-permute-start.15 = (bf16[64,1024]{1,0:T(8,128)(2,1)S(1)}, bf16[64,1024]{1,0:T(8,128)(2,1)S(1)}, u32[]{:S(2)}, u32[]{:S(2)}) collective-permute-start(bf16[64,1024]{1,0:T(8,128)(2,1)S(1)} %shard_map.100.refs_0_), channel_id=1, source_target_pairs={{0,4},{1,5},{2,6},{3,7},{4,0},{5,1},{6,2},{7,3},{8,12},{9,13},{10,... | collective-permute-start | bytes 393224 | tf_op jit(solution)/shard_map/ppermute | solution.py:382
  52.5 2.3 %collective-permute-start.16 = (bf16[64,1024]{1,0:T(8,128)(2,1)S(1)}, bf16[64,1024]{1,0:T(8,128)(2,1)S(1)}, u32[]{:S(2)}, u32[]{:S(2)}) collective-permute-start(bf16[64,1024]{1,0:T(8,128)(2,1)S(1)} %collective-permute-done.15.refs_4_), channel_id=1, source_target_pairs={{0,1},{1,0},{2,3},{3,2},{4,5},{5,4},{6,7},{7,6},{8,9},{9,8},{10,11... | collective-permute-start | bytes 393224 | tf_op jit(solution)/shard_map/ppermute | solution.py:373
  55.2 1.2 %collective-permute-start.18 = (bf16[64,1024]{1,0:T(8,128)(2,1)S(1)}, bf16[64,1024]{1,0:T(8,128)(2,1)S(1)}, u32[]{:S(2)}, u32[]{:S(2)}) collective-permute-start(bf16[64,1024]{1,0:T(8,128)(2,1)S(1)} %collective-permute-done.17.refs_6_), channel_id=1, source_target_pairs={{0,1},{1,0},{2,3},{3,2},{4,5},{5,4},{6,7},{7,6},{8,9},{9,8},{10,11... | collective-permute-start | bytes 393224 | tf_op jit(solution)/shard_map/ppermute | solution.py:373
  57.5 1.6 %shard_map.101 = (bf16[64,640]{1,0:T(8,128)(2,1)S(1)}, bf16[64,640]{1,0:T(8,128)(2,1)S(1)}, bf16[64,640]{1,0:T(8,128)(2,1)S(1)}, bf16[64,640]{1,0:T(8,128)(2,1)S(1)}) custom-call(s32[4]{0:T(128)S(1)} %pad_add_fusion.place, bf16[64,1024]{1,0:T(8,128)(2,1)S(1)} %shard_map.100.refs_0_, bf16[64,1024]{1,0:T(8,128)(2,1)S(1)} %collective-permute-done.12.refs_1_, ...), custom_call_target="tpu_custom_call" | custom-call | flops 671088640 | bytes 2621440 | tf_op jit(solution)/shard_map/pallas_call | solution.py:21
  59.0 3.5 %collective-permute-start.20 = (bf16[64,640]{1,0:T(8,128)(2,1)S(1)}, bf16[64,640]{1,0:T(8,128)(2,1)S(1)}, u32[]{:S(2)}, u32[]{:S(2)}) collective-permute-start(bf16[64,640]{1,0:T(8,128)(2,1)S(1)} %get-tuple-element.39), channel_id=1, source_target_pairs={{0,0},{1,4},{2,8},{3,12},{4,1},{5,5},{6,9},{7,13},{8,2},{9,6},{10,... | collective-permute-start | bytes 245768 | tf_op jit(solution)/shard_map/ppermute | solution.py:579
  62.6 3.7 %collective-permute-start.22 = (bf16[64,640]{1,0:T(8,128)(2,1)S(1)}, bf16[64,640]{1,0:T(8,128)(2,1)S(1)}, u32[]{:S(2)}, u32[]{:S(2)}) collective-permute-start(bf16[64,640]{1,0:T(8,128)(2,1)S(1)} %get-tuple-element.41), channel_id=1, source_target_pairs={{0,2},{1,6},{2,10},{3,14},{4,3},{5,7},{6,11},{7,15},{8,0},{9,4},{1... | collective-permute-start | bytes 245768 | tf_op jit(solution)/shard_map/ppermute | solution.py:579
  66.7 5.4 %collective-permute-done.22.refs_2_ = bf16[64,640]{1,0:T(8,128)(2,1)S(1)} collective-permute-done((bf16[64,640]{1,0:T(8,128)(2,1)S(1)}, bf16[64,640]{1,0:T(8,128)(2,1)S(1)}, u32[]{:S(2)}, u32[]{:S(2)}) %collective-permute-start.22) | collective-permute-done | bytes 81952 | tf_op jit(solution)/shard_map/ppermute | solution.py:579
  72.1 7.6 %collective-permute-done.23.refs_3_ = bf16[64,640]{1,0:T(8,128)(2,1)S(1)} collective-permute-done((bf16[64,640]{1,0:T(8,128)(2,1)S(1)}, bf16[64,640]{1,0:T(8,128)(2,1)S(1)}, u32[]{:S(2)}, u32[]{:S(2)}) %collective-permute-start.23) | collective-permute-done | bytes 81952 | tf_op jit(solution)/shard_map/ppermute | solution.py:579
  79.7 1.3 %shard_map.102 = bf16[64,1280]{1,0:T(8,128)(2,1)} custom-call(s32[4]{0:T(128)S(1)} %pad_add_fusion.place, bf16[64,5120]{1,0:T(8,128)(2,1)S(1)} %copy-done.2, bf16[64,640]{1,0:T(8,128)(2,1)S(1)} %collective-permute-done.20.refs_0_, bf16[64,640]{1,0:T(8,128)(2,1)S(1)} %collective-permute-done.21.refs_1_, bf16[64,640]{1,0:T(8,128)(2,1)S(1)} %collective-permute-done.22.refs_2_, ...), custom_call_target="tpu_custom_call" | custom-call | flops 327680 | bytes 983040 | tf_op jit(solution)/shard_map/pallas_call | solution.py:21
  (55 shorter events, 17.6 us)
Async XLA Ops:
  4.0 3.1 %collective-permute-start = (bf16[2,64,1280]{2,1,0:T(8,128)(2,1)S(1)}, bf16[2,64,1280]{2,1,0:T(8,128)(2,1)S(1)}, u32[]{:S(2)}, u32[]{:S(2)}) collective-permute-start(bf16[2,64,1280]{2,1,0:T(8,128)(2,1)S(1)} %get-tuple-element.27), channel_id=1, source_target_pairs={{0,1},{1,0},{2,3},{3,2},{4,5},{5,4},{6,7},{7,6},{8,9},{9,8},{10,11... | collective-permute-start | bytes 983048 | tf_op jit(solution)/shard_map/ppermute | solution.py:373
  4.1 10.7 %collective-permute-start.3 = (bf16[1280,128]{1,0:T(8,128)(2,1)S(1)}, bf16[1280,128]{1,0:T(8,128)(2,1)S(1)}, u32[]{:S(2)}, u32[]{:S(2)}) collective-permute-start(bf16[1280,128]{1,0:T(8,128)(2,1)S(1)} %get-tuple-element.24), channel_id=1, source_target_pairs={{0,2},{1,3},{2,0},{3,1},{4,6},{5,7},{6,4},{7,5},{8,10},{9,11},{10,... | collective-permute-start | bytes 983048 | tf_op jit(solution)/shard_map/ppermute | solution.py:373
  6.8 15.1 %collective-permute-start.2 = (bf16[1280,256]{1,0:T(8,128)(2,1)S(1)}, bf16[1280,256]{1,0:T(8,128)(2,1)S(1)}, u32[]{:S(2)}, u32[]{:S(2)}) collective-permute-start(bf16[1280,256]{1,0:T(8,128)(2,1)S(1)} %get-tuple-element.28.own), channel_id=1, source_target_pairs={{0,1},{1,0},{2,3},{3,2},{4,5},{5,4},{6,7},{7,6},{8,9},{9,8},{10,11... | collective-permute-start | bytes 1966088 | tf_op jit(solution)/shard_map/ppermute | solution.py:373
  14.8 3.4 %collective-permute-start.4 = (bf16[1280,128]{1,0:T(8,128)(2,1)S(1)}, bf16[1280,128]{1,0:T(8,128)(2,1)S(1)}, u32[]{:S(2)}, u32[]{:S(2)}) collective-permute-start(bf16[1280,128]{1,0:T(8,128)(2,1)S(1)} %collective-permute-done.3.refs_0_), channel_id=1, source_target_pairs={{0,1},{1,0},{2,3},{3,2},{4,5},{5,4},{6,7},{7,6},{8,9},{9,8},{10,11... | collective-permute-start | bytes 983048 | tf_op jit(solution)/shard_map/ppermute | solution.py:373
  15.4 9.4 %collective-permute-start.5 = (bf16[1280,128]{1,0:T(8,128)(2,1)S(1)}, bf16[1280,128]{1,0:T(8,128)(2,1)S(1)}, u32[]{:S(2)}, u32[]{:S(2)}) collective-permute-start(bf16[1280,128]{1,0:T(8,128)(2,1)S(1)} %collective-permute-done.3.refs_0_), channel_id=1, source_target_pairs={{0,16},{16,0},{1,17},{17,1},{2,18},{18,2},{3,19},{19,3},{4,20},{20... | collective-permute-start | bytes 983048 | tf_op jit(solution)/shard_map/ppermute | solution.py:373
  16.9 9.0 %collective-permute-start.1 = (bf16[2,64,1280]{2,1,0:T(8,128)(2,1)S(1)}, bf16[2,64,1280]{2,1,0:T(8,128)(2,1)S(1)}, u32[]{:S(2)}, u32[]{:S(2)}) collective-permute-start(bf16[2,64,1280]{2,1,0:T(8,128)(2,1)S(1)} %shard_map.93), channel_id=1, source_target_pairs={{0,2},{1,3},{2,0},{3,1},{4,6},{5,7},{6,4},{7,5},{8,10},{9,11},{10,... | collective-permute-start | bytes 983048 | tf_op jit(solution)/shard_map/ppermute | solution.py:373
  19.1 38.4 %collective-permute-start.19 = (bf16[1024,640]{1,0:T(8,128)(2,1)S(1)}, bf16[1024,640]{1,0:T(8,128)(2,1)S(1)}, u32[]{:S(2)}, u32[]{:S(2)}) collective-permute-start(bf16[1024,640]{1,0:T(8,128)(2,1)S(1)} %shard_map.95), channel_id=1, source_target_pairs={{0,4},{4,0},{8,12},{12,8},{1,5},{5,1},{9,13},{13,9},{2,6},{6,2},{1... | collective-permute-start | bytes 3932168 | tf_op jit(solution)/shard_map/ppermute | solution.py:373
  28.4 2.7 %collective-permute-start.6 = (f32[128,1024]{1,0:T(8,128)S(1)}, f32[128,1024]{1,0:T(8,128)S(1)}, u32[]{:S(2)}, u32[]{:S(2)}) collective-permute-start(f32[128,1024]{1,0:T(8,128)S(1)} %get-tuple-element.36), channel_id=1, source_target_pairs={{0,1},{1,0},{2,3},{3,2},{4,5},{5,4},{6,7},{7,6},{8,9},{9,8},{10,11... | collective-permute-start | bytes 1572872 | tf_op jit(solution)/shard_map/ppermute | solution.py:373
  29.6 3.4 %collective-permute-start.8 = (bf16[1280,128]{1,0:T(8,128)(2,1)S(1)}, bf16[1280,128]{1,0:T(8,128)(2,1)S(1)}, u32[]{:S(2)}, u32[]{:S(2)}) collective-permute-start(bf16[1280,128]{1,0:T(8,128)(2,1)S(1)} %collective-permute-done.5.refs_1_), channel_id=1, source_target_pairs={{0,1},{1,0},{2,3},{3,2},{4,5},{5,4},{6,7},{7,6},{8,9},{9,8},{10,11... | collective-permute-start | bytes 983048 | tf_op jit(solution)/shard_map/ppermute | solution.py:373
  31.7 11.8 %collective-permute-start.7 = (f32[64,1024]{1,0:T(8,128)S(1)}, f32[64,1024]{1,0:T(8,128)S(1)}, u32[]{:S(2)}, u32[]{:S(2)}) collective-permute-start(f32[64,1024]{1,0:T(8,128)S(1)} %shard_map.98), channel_id=1, source_target_pairs={{0,2},{1,3},{2,0},{3,1},{4,6},{5,7},{6,4},{7,5},{8,10},{9,11},{10,... | collective-permute-start | bytes 786440 | tf_op jit(solution)/shard_map/ppermute | solution.py:373
  34.1 7.3 %collective-permute-start.10 = (bf16[192,256]{1,0:T(8,128)(2,1)S(1)}, bf16[192,256]{1,0:T(8,128)(2,1)S(1)}, u32[]{:S(2)}, u32[]{:S(2)}) collective-permute-start(bf16[192,256]{1,0:T(8,128)(2,1)S(1)} %shard_map.99.refs_0_), channel_id=1, source_target_pairs={{0,2},{1,3},{2,0},{3,1},{4,6},{5,7},{6,4},{7,5},{8,10},{9,11},{10,... | collective-permute-start | bytes 294920 | tf_op jit(solution)/shard_map/ppermute | solution.py:373
  34.4 8.2 %collective-permute-start.9 = (bf16[192,256]{1,0:T(8,128)(2,1)S(1)}, bf16[192,256]{1,0:T(8,128)(2,1)S(1)}, u32[]{:S(2)}, u32[]{:S(2)}) collective-permute-start(bf16[192,256]{1,0:T(8,128)(2,1)S(1)} %shard_map.99.refs_0_), channel_id=1, source_target_pairs={{0,1},{1,0},{2,3},{3,2},{4,5},{5,4},{6,7},{7,6},{8,9},{9,8},{10,11... | collective-permute-start | bytes 294920 | tf_op jit(solution)/shard_map/ppermute | solution.py:373
  41.4 2.1 %collective-permute-start.11 = (bf16[192,256]{1,0:T(8,128)(2,1)S(1)}, bf16[192,256]{1,0:T(8,128)(2,1)S(1)}, u32[]{:S(2)}, u32[]{:S(2)}) collective-permute-start(bf16[192,256]{1,0:T(8,128)(2,1)S(1)} %collective-permute-done.10.refs_2_), channel_id=1, source_target_pairs={{0,1},{1,0},{2,3},{3,2},{4,5},{5,4},{6,7},{7,6},{8,9},{9,8},{10,11... | collective-permute-start | bytes 294920 | tf_op jit(solution)/shard_map/ppermute | solution.py:373
  46.5 4.8 %collective-permute-start.13 = (bf16[64,1024]{1,0:T(8,128)(2,1)S(1)}, bf16[64,1024]{1,0:T(8,128)(2,1)S(1)}, u32[]{:S(2)}, u32[]{:S(2)}) collective-permute-start(bf16[64,1024]{1,0:T(8,128)(2,1)S(1)} %shard_map.100.refs_0_), channel_id=1, source_target_pairs={{0,2},{1,3},{2,0},{3,1},{4,6},{5,7},{6,4},{7,5},{8,10},{9,11},{10,... | collective-permute-start | bytes 393224 | tf_op jit(solution)/shard_map/ppermute | solution.py:373
  47.8 4.7 %collective-permute-start.15 = (bf16[64,1024]{1,0:T(8,128)(2,1)S(1)}, bf16[64,1024]{1,0:T(8,128)(2,1)S(1)}, u32[]{:S(2)}, u32[]{:S(2)}) collective-permute-start(bf16[64,1024]{1,0:T(8,128)(2,1)S(1)} %shard_map.100.refs_0_), channel_id=1, source_target_pairs={{0,4},{1,5},{2,6},{3,7},{4,0},{5,1},{6,2},{7,3},{8,12},{9,13},{10,... | collective-permute-start | bytes 393224 | tf_op jit(solution)/shard_map/ppermute | solution.py:382
  49.1 6.2 %collective-permute-start.17 = (bf16[64,1024]{1,0:T(8,128)(2,1)S(1)}, bf16[64,1024]{1,0:T(8,128)(2,1)S(1)}, u32[]{:S(2)}, u32[]{:S(2)}) collective-permute-start(bf16[64,1024]{1,0:T(8,128)(2,1)S(1)} %shard_map.100.refs_0_), channel_id=1, source_target_pairs={{0,6},{1,7},{2,4},{3,5},{4,2},{5,3},{6,0},{7,1},{8,14},{9,15},{10,... | collective-permute-start | bytes 393224 | tf_op jit(solution)/shard_map/ppermute | solution.py:382
  49.2 7.3 %collective-permute-start.12 = (bf16[64,1024]{1,0:T(8,128)(2,1)S(1)}, bf16[64,1024]{1,0:T(8,128)(2,1)S(1)}, u32[]{:S(2)}, u32[]{:S(2)}) collective-permute-start(bf16[64,1024]{1,0:T(8,128)(2,1)S(1)} %shard_map.100.refs_0_), channel_id=1, source_target_pairs={{0,1},{1,0},{2,3},{3,2},{4,5},{5,4},{6,7},{7,6},{8,9},{9,8},{10,11... | collective-permute-start | bytes 393224 | tf_op jit(solution)/shard_map/ppermute | solution.py:373
  51.3 5.2 %collective-permute-start.14 = (bf16[64,1024]{1,0:T(8,128)(2,1)S(1)}, bf16[64,1024]{1,0:T(8,128)(2,1)S(1)}, u32[]{:S(2)}, u32[]{:S(2)}) collective-permute-start(bf16[64,1024]{1,0:T(8,128)(2,1)S(1)} %collective-permute-done.13.refs_2_), channel_id=1, source_target_pairs={{0,1},{1,0},{2,3},{3,2},{4,5},{5,4},{6,7},{7,6},{8,9},{9,8},{10,11... | collective-permute-start | bytes 393224 | tf_op jit(solution)/shard_map/ppermute | solution.py:373
  52.5 4.0 %collective-permute-start.16 = (bf16[64,1024]{1,0:T(8,128)(2,1)S(1)}, bf16[64,1024]{1,0:T(8,128)(2,1)S(1)}, u32[]{:S(2)}, u32[]{:S(2)}) collective-permute-start(bf16[64,1024]{1,0:T(8,128)(2,1)S(1)} %collective-permute-done.15.refs_4_), channel_id=1, source_target_pairs={{0,1},{1,0},{2,3},{3,2},{4,5},{5,4},{6,7},{7,6},{8,9},{9,8},{10,11... | collective-permute-start | bytes 393224 | tf_op jit(solution)/shard_map/ppermute | solution.py:373
  55.2 2.2 %collective-permute-start.18 = (bf16[64,1024]{1,0:T(8,128)(2,1)S(1)}, bf16[64,1024]{1,0:T(8,128)(2,1)S(1)}, u32[]{:S(2)}, u32[]{:S(2)}) collective-permute-start(bf16[64,1024]{1,0:T(8,128)(2,1)S(1)} %collective-permute-done.17.refs_6_), channel_id=1, source_target_pairs={{0,1},{1,0},{2,3},{3,2},{4,5},{5,4},{6,7},{7,6},{8,9},{9,8},{10,11... | collective-permute-start | bytes 393224 | tf_op jit(solution)/shard_map/ppermute | solution.py:373
  59.0 7.6 %collective-permute-start.20 = (bf16[64,640]{1,0:T(8,128)(2,1)S(1)}, bf16[64,640]{1,0:T(8,128)(2,1)S(1)}, u32[]{:S(2)}, u32[]{:S(2)}) collective-permute-start(bf16[64,640]{1,0:T(8,128)(2,1)S(1)} %get-tuple-element.39), channel_id=1, source_target_pairs={{0,0},{1,4},{2,8},{3,12},{4,1},{5,5},{6,9},{7,13},{8,2},{9,6},{10,... | collective-permute-start | bytes 245768 | tf_op jit(solution)/shard_map/ppermute | solution.py:579
  62.5 4.2 %collective-permute-start.21 = (bf16[64,640]{1,0:T(8,128)(2,1)S(1)}, bf16[64,640]{1,0:T(8,128)(2,1)S(1)}, u32[]{:S(2)}, u32[]{:S(2)}) collective-permute-start(bf16[64,640]{1,0:T(8,128)(2,1)S(1)} %get-tuple-element.40), channel_id=1, source_target_pairs={{0,1},{1,5},{2,9},{3,13},{4,0},{5,4},{6,8},{7,12},{8,3},{9,7},{10,... | collective-permute-start | bytes 245768 | tf_op jit(solution)/shard_map/ppermute | solution.py:579
  62.6 9.5 %collective-permute-start.22 = (bf16[64,640]{1,0:T(8,128)(2,1)S(1)}, bf16[64,640]{1,0:T(8,128)(2,1)S(1)}, u32[]{:S(2)}, u32[]{:S(2)}) collective-permute-start(bf16[64,640]{1,0:T(8,128)(2,1)S(1)} %get-tuple-element.41), channel_id=1, source_target_pairs={{0,2},{1,6},{2,10},{3,14},{4,3},{5,7},{6,11},{7,15},{8,0},{9,4},{1... | collective-permute-start | bytes 245768 | tf_op jit(solution)/shard_map/ppermute | solution.py:579
  66.3 13.4 %collective-permute-start.23 = (bf16[64,640]{1,0:T(8,128)(2,1)S(1)}, bf16[64,640]{1,0:T(8,128)(2,1)S(1)}, u32[]{:S(2)}, u32[]{:S(2)}) collective-permute-start(bf16[64,640]{1,0:T(8,128)(2,1)S(1)} %get-tuple-element.42), channel_id=1, source_target_pairs={{0,3},{1,7},{2,11},{3,15},{4,2},{5,6},{6,10},{7,14},{8,1},{9,5},{1... | collective-permute-start | bytes 245768 | tf_op jit(solution)/shard_map/ppermute | solution.py:579
  (9 other events, 66.4 us)

commit v6 on v5

--- a/solution.py
+++ b/solution.py
@@ -232,16 +232,19 @@
     return start
 
 
-def attend_kernel(count, prompt_rows, place, lengths, mine, near, far, cosine, sine, gain, *refs):
-    pairs, out = refs[:-1], refs[-1]
-    rows, width = far.shape
+def attend_kernel(count, prompt_rows, place, lengths, mine, near, cosine, sine, gain, *refs):
+    pairs, far, out = refs[:count], refs[count:-1], refs[-1]
+    rows, width = out.shape
     size = gain.shape[1]
     heads = width // size
     cosine, sine = cosine[prompt_rows:, :], sine[prompt_rows:, :]
     queries = []
     for h in range(heads):
         part = slice(h * size, (h + 1) * size)
-        value = rms_rows(mine[:rows, part] + near[:rows, part] + far[:, part], gain[...])
+        value = mine[:rows, part] + near[:rows, part]
+        for block in far:
+            value = value + block[:, part].astype(F32)
+        value = rms_rows(value, gain[...])
         queries.append(turn(value, cosine, sine).astype(BF16))
     queries = jnp.concatenate(queries, axis=0)
     prompt = jnp.concatenate([pair[:prompt_rows] for pair in pairs], axis=0)
@@ -277,8 +280,8 @@
 
 
 def attend(place, lengths, mine, near, far, cosine, sine, gain, pairs, prompt_rows):
-    rows, width = far.shape
-    args = (mine, near, far, cosine, sine, gain, *pairs)
+    rows, width = far[0].shape
+    args = (mine, near, cosine, sine, gain, *pairs, *far)
     out = shape_of((rows, width), BF16)
     keys = len(pairs) * pairs[0].shape[0]
     return call(
@@ -415,12 +418,12 @@
     near = swap(send, axis, 1)
     rows = keep.shape[0] // (count // 2)
     held = {d: add_rows(place, keep, near, d // 2 * rows, rows) for d in range(2, count, 2)}
-    far = 0.0
+    far = []
     for bit in swap_bits(count)[1:]:
         sent = [d for d in sorted(held) if d & bit]
         got = {d ^ bit: swap(held[d], axis, bit) for d in sent}
-        far = far + got.pop(0)
-        held = {d: held[d] + got[d] for d in got}
+        far.append(got.pop(0))
+        held = {d: (held[d].astype(F32) + got[d].astype(F32)).astype(BF16) for d in got}
     return keep, near, far
 
 
@@ -481,7 +484,7 @@
 
 
 def add_kernel(place, left, right, out):
-    out[...] = left[...] + right[...]
+    out[...] = (left[...] + right[...]).astype(BF16)
 
 
 def add_rows(place, left, right, at, rows):
@@ -493,9 +496,9 @@
         (1,),
         [spec, spec],
         pl.BlockSpec((rows, width), lambda i, place: (0, 0)),
-        shape_of((rows, width), F32),
+        shape_of((rows, width), BF16),
         (left, right),
-        (rows * width, 12 * rows * width),
+        (rows * width, 10 * rows * width),
     )
 
 

time: 81.1 us -> 79.9 us (0.985)
    ppermute x18, waiting for transfers between devices: 19.7 us -> 14.9 us  [swap(): lax.ppermute(array, axis, [(i, i ^ bits) for i in range(lax.axis_size(axi...]
    ppermute x2, waiting for transfers between devices: 0.43 us -> 4.78 us  [swap_both(): return lax.ppermute(array, ('tp', 'sp'), pairs)]
    ppermute x2, starting transfers between devices: 1.43 us -> 2.7 us  [swap_both(): return lax.ppermute(array, ('tp', 'sp'), pairs)]
    ppermute x18, starting transfers between devices: 20.1 us -> 19.1 us  [swap(): lax.ppermute(array, axis, [(i, i ^ bits) for i in range(lax.axis_size(axi...]
    ppermute x4, starting transfers between devices: 7.63 us -> 6.66 us  [on_device(): lax.ppermute(part, ('tp', 'sp'), [(t * sp_count + s, s * sp_count + (t ^...]
  transfers between devices with their start and end apart: 24 -> 24, of which waited for: 11 -> 13; matrix products, arithmetic and copies ran while one was open for 0% -> 0% of each run, Pallas kernels for 14% -> 15%
where the time goes in v6:
time: 79.9 us; the launch traced here: 79.7 us
  waiting for transfers between devices  32.5 us (41%)
  starting transfers between devices  28.5 us (36%)
  Pallas kernels  16.5 us (21%)
  local copies, waits for them, and re-layouts  1.93 us (2%)
    ppermute x18, starting transfers between devices, swap(): lax.ppermute(array, axis, [(i, i ^ bits) for i in range(lax.axis_size(axi...  19.1 us
    pallas_call x12, Pallas kernels, call(): pl.pallas_call(kernel, out_shape=out_shape, grid_spec=pltpu.PrefetchScala...  16.5 us
    ppermute x18, waiting for transfers between devices, swap(): lax.ppermute(array, axis, [(i, i ^ bits) for i in range(lax.axis_size(axi...  14.9 us
    ppermute x4, waiting for transfers between devices, on_device(): lax.ppermute(part, ('tp', 'sp'), [(t * sp_count + s, s * sp_count + (t ^...  12.8 us
    ppermute x4, starting transfers between devices, on_device(): lax.ppermute(part, ('tp', 'sp'), [(t * sp_count + s, s * sp_count + (t ^...  6.66 us
    ppermute x2, waiting for transfers between devices, swap_both(): return lax.ppermute(array, ('tp', 'sp'), pairs)  4.78 us
    ppermute x2, starting transfers between devices, swap_both(): return lax.ppermute(array, ('tp', 'sp'), pairs)  2.7 us
    unnamed x18, local copies, waits for them, and re-layouts  1.93 us
  transfers between devices with their start and end apart: 24, of which 13 were waited for; matrix products, arithmetic and copies ran while one was open for 0% of the time, Pallas kernels for 15%

profile of v6, /device:TPU:1, one launch (start us, length us, event | category | flops | bytes accessed | tf_op | source)
XLA Modules:
  0.0 79.7 jit_solution(3098980374889061106)
XLA Ops:
  0.1 1.7 %copy-done = bf16[1280,1024]{1,0:T(8,128)(2,1)S(1)} copy-done((bf16[1280,1024]{1,0:T(8,128)(2,1)S(1)}, bf16[1280,1024]{1,0:T(8,128)(2,1)}, u32[]{:S(2)}) %copy-start) | copy-done | bytes 2621464
  4.1 2.7 %collective-permute-start.3 = (bf16[1280,128]{1,0:T(8,128)(2,1)S(1)}, bf16[1280,128]{1,0:T(8,128)(2,1)S(1)}, u32[]{:S(2)}, u32[]{:S(2)}) collective-permute-start(bf16[1280,128]{1,0:T(8,128)(2,1)S(1)} %get-tuple-element.24), channel_id=1, source_target_pairs={{0,2},{1,3},{2,0},{3,1},{4,6},{5,7},{6,4},{7,5},{8,10},{9,11},{10,... | collective-permute-start | bytes 983048 | tf_op jit(solution)/shard_map/ppermute | solution.py:376
  7.7 7.0 %collective-permute-done.3.refs_0_ = bf16[1280,128]{1,0:T(8,128)(2,1)S(1)} collective-permute-done((bf16[1280,128]{1,0:T(8,128)(2,1)S(1)}, bf16[1280,128]{1,0:T(8,128)(2,1)S(1)}, u32[]{:S(2)}, u32[]{:S(2)}) %collective-permute-start.3) | collective-permute-done | bytes 327712 | tf_op jit(solution)/shard_map/ppermute | solution.py:376
  15.4 1.5 %collective-permute-start.5 = (bf16[1280,128]{1,0:T(8,128)(2,1)S(1)}, bf16[1280,128]{1,0:T(8,128)(2,1)S(1)}, u32[]{:S(2)}, u32[]{:S(2)}) collective-permute-start(bf16[1280,128]{1,0:T(8,128)(2,1)S(1)} %collective-permute-done.3.refs_0_), channel_id=1, source_target_pairs={{0,16},{16,0},{1,17},{17,1},{2,18},{18,2},{3,19},{19,3},{4,20},{20... | collective-permute-start | bytes 983048 | tf_op jit(solution)/shard_map/ppermute | solution.py:376
  19.1 1.4 %collective-permute-start.19 = (bf16[1024,640]{1,0:T(8,128)(2,1)S(1)}, bf16[1024,640]{1,0:T(8,128)(2,1)S(1)}, u32[]{:S(2)}, u32[]{:S(2)}) collective-permute-start(bf16[1024,640]{1,0:T(8,128)(2,1)S(1)} %shard_map.95), channel_id=1, source_target_pairs={{0,4},{4,0},{8,12},{12,8},{1,5},{5,1},{9,13},{13,9},{2,6},{6,2},{1... | collective-permute-start | bytes 3932168 | tf_op jit(solution)/shard_map/ppermute | solution.py:376
  20.4 1.5 %shard_map.96 = (f32[192,128]{1,0:T(8,128)S(1)}, f32[192,128]{1,0:T(8,128)S(1)}) custom-call(s32[4]{0:T(128)S(1)} %pad_add_fusion.place, s32[8]{0:T(128)S(1)} %copy-done.7), custom_call_target="tpu_custom_call" | custom-call | flops 2457600 | bytes 196608 | tf_op jit(solution)/shard_map/pallas_call | solution.py:21
  22.0 1.6 %shard_map.94 = (bf16[4,128,1280]{2,1,0:T(8,128)(2,1)S(1)}, f32[192,256]{1,0:T(8,128)S(1)}) custom-call(s32[4]{0:T(128)S(1)} %pad_add_fusion.place, bf16[128,5120]{1,0:T(8,128)(2,1)S(1)} %copy-done.4, f32[1,5120]{1,0:T(1,128)S(1)} %bitcast.8, bf16[4,64,1280]{2,1,0:T(8,128)(2,1)S(1)} %get-tuple-element.26.cont.refs_0_, ...), custom_call_target="tpu_custom_call" | custom-call | flops 251658240 | bytes 5242880 | tf_op jit(solution)/shard_map/pallas_call | solution.py:21
  23.6 1.3 %collective-permute-done.5.refs_1_ = bf16[1280,128]{1,0:T(8,128)(2,1)S(1)} collective-permute-done((bf16[1280,128]{1,0:T(8,128)(2,1)S(1)}, bf16[1280,128]{1,0:T(8,128)(2,1)S(1)}, u32[]{:S(2)}, u32[]{:S(2)}) %collective-permute-start.5) | collective-permute-done | bytes 327712 | tf_op jit(solution)/shard_map/ppermute | solution.py:376
  26.0 2.4 %shard_map.97 = (f32[128,1024]{1,0:T(8,128)S(1)}, f32[128,1024]{1,0:T(8,128)S(1)}) custom-call(s32[4]{0:T(128)S(1)} %pad_add_fusion.place, bf16[4,64,1280]{2,1,0:T(8,128)(2,1)S(1)} %get-tuple-element.26.cont.refs_0_, bf16[2,64,1280]{2,1,0:T(8,128)(2,1)S(1)} %collective-permute-done.other.refs_1_, bf16[2,64,1280]{2,1,0:T(8,128)(2,1)S(1)} %collective-permute-done.1.refs_2_, ...), custom_call_target="tpu_custom_call" | custom-call | flops 671088640 | bytes 2621440 | tf_op jit(solution)/shard_map/pallas_call | solution.py:21
  29.6 1.9 %collective-permute-done.7.refs_3_ = bf16[1280,128]{1,0:T(8,128)(2,1)S(1)} collective-permute-done((bf16[1280,128]{1,0:T(8,128)(2,1)S(1)}, bf16[1280,128]{1,0:T(8,128)(2,1)S(1)}, u32[]{:S(2)}, u32[]{:S(2)}) %collective-permute-start.7) | collective-permute-done | bytes 327712 | tf_op jit(solution)/shard_map/ppermute | solution.py:376
  32.7 1.3 %collective-permute-start.9 = (bf16[192,256]{1,0:T(8,128)(2,1)S(1)}, bf16[192,256]{1,0:T(8,128)(2,1)S(1)}, u32[]{:S(2)}, u32[]{:S(2)}) collective-permute-start(bf16[192,256]{1,0:T(8,128)(2,1)S(1)} %shard_map.98.refs_0_), channel_id=1, source_target_pairs={{0,2},{1,3},{2,0},{3,1},{4,6},{5,7},{6,4},{7,5},{8,10},{9,11},{10,... | collective-permute-start | bytes 294920 | tf_op jit(solution)/shard_map/ppermute | solution.py:376
  36.8 1.5 %collective-permute-start.10 = (bf16[192,256]{1,0:T(8,128)(2,1)S(1)}, bf16[192,256]{1,0:T(8,128)(2,1)S(1)}, u32[]{:S(2)}, u32[]{:S(2)}) collective-permute-start(bf16[192,256]{1,0:T(8,128)(2,1)S(1)} %collective-permute-done.9.refs_2_), channel_id=1, source_target_pairs={{0,1},{1,0},{2,3},{3,2},{4,5},{5,4},{6,7},{7,6},{8,9},{9,8},{10,11... | collective-permute-start | bytes 294920 | tf_op jit(solution)/shard_map/ppermute | solution.py:376
  39.5 3.0 %shard_map.100.refs_0_ = bf16[64,1024]{1,0:T(8,128)(2,1)S(1)} custom-call(s32[4]{0:T(128)S(1)} %pad_add_fusion.place, s32[8]{0:T(128)S(1)} %copy-done.7, f32[128,1024]{1,0:T(8,128)S(1)} %get-tuple-element.35.left.mine, f32[128,1024]{1,0:T(8,128)S(1)} %collective-permute-done.6.right.near, f32[192,128]{1,0:T(8,128)S(1)} %get-tuple-element.33.cosine, ...), custom_call_target="tpu_custom_call" | custom-call | flops 201326592 | bytes 1048576 | tf_op jit(solution)/shard_map/pallas_call | solution.py:21
  42.5 2.5 %collective-permute-start.17 = (bf16[64,1024]{1,0:T(8,128)(2,1)S(1)}, bf16[64,1024]{1,0:T(8,128)(2,1)S(1)}, u32[]{:S(2)}, u32[]{:S(2)}) collective-permute-start(bf16[64,1024]{1,0:T(8,128)(2,1)S(1)} %shard_map.100.refs_0_), channel_id=1, source_target_pairs={{0,6},{1,7},{2,4},{3,5},{4,2},{5,3},{6,0},{7,1},{8,14},{9,15},{10,... | collective-permute-start | bytes 393224 | tf_op jit(solution)/shard_map/ppermute | solution.py:385
  45.3 2.0 %collective-permute-start.12 = (bf16[64,1024]{1,0:T(8,128)(2,1)S(1)}, bf16[64,1024]{1,0:T(8,128)(2,1)S(1)}, u32[]{:S(2)}, u32[]{:S(2)}) collective-permute-start(bf16[64,1024]{1,0:T(8,128)(2,1)S(1)} %shard_map.100.refs_0_), channel_id=1, source_target_pairs={{0,1},{1,0},{2,3},{3,2},{4,5},{5,4},{6,7},{7,6},{8,9},{9,8},{10,11... | collective-permute-start | bytes 393224 | tf_op jit(solution)/shard_map/ppermute | solution.py:376
  47.3 4.4 %collective-permute-done.17.refs_6_ = bf16[64,1024]{1,0:T(8,128)(2,1)S(1)} collective-permute-done((bf16[64,1024]{1,0:T(8,128)(2,1)S(1)}, bf16[64,1024]{1,0:T(8,128)(2,1)S(1)}, u32[]{:S(2)}, u32[]{:S(2)}) %collective-permute-start.17) | collective-permute-done | bytes 131104 | tf_op jit(solution)/shard_map/ppermute | solution.py:385
  51.7 2.4 %collective-permute-start.18 = (bf16[64,1024]{1,0:T(8,128)(2,1)S(1)}, bf16[64,1024]{1,0:T(8,128)(2,1)S(1)}, u32[]{:S(2)}, u32[]{:S(2)}) collective-permute-start(bf16[64,1024]{1,0:T(8,128)(2,1)S(1)} %collective-permute-done.17.refs_6_), channel_id=1, source_target_pairs={{0,1},{1,0},{2,3},{3,2},{4,5},{5,4},{6,7},{7,6},{8,9},{9,8},{10,11... | collective-permute-start | bytes 393224 | tf_op jit(solution)/shard_map/ppermute | solution.py:376
  54.5 1.4 %collective-permute-start.16 = (bf16[64,1024]{1,0:T(8,128)(2,1)S(1)}, bf16[64,1024]{1,0:T(8,128)(2,1)S(1)}, u32[]{:S(2)}, u32[]{:S(2)}) collective-permute-start(bf16[64,1024]{1,0:T(8,128)(2,1)S(1)} %collective-permute-done.15.refs_4_), channel_id=1, source_target_pairs={{0,1},{1,0},{2,3},{3,2},{4,5},{5,4},{6,7},{7,6},{8,9},{9,8},{10,11... | collective-permute-start | bytes 393224 | tf_op jit(solution)/shard_map/ppermute | solution.py:376
  57.3 1.6 %shard_map.101 = (bf16[64,640]{1,0:T(8,128)(2,1)S(1)}, bf16[64,640]{1,0:T(8,128)(2,1)S(1)}, bf16[64,640]{1,0:T(8,128)(2,1)S(1)}, bf16[64,640]{1,0:T(8,128)(2,1)S(1)}) custom-call(s32[4]{0:T(128)S(1)} %pad_add_fusion.place, bf16[64,1024]{1,0:T(8,128)(2,1)S(1)} %shard_map.100.refs_0_, bf16[64,1024]{1,0:T(8,128)(2,1)S(1)} %collective-permute-done.12.refs_1_, ...), custom_call_target="tpu_custom_call" | custom-call | flops 671088640 | bytes 2621440 | tf_op jit(solution)/shard_map/pallas_call | solution.py:21
  58.9 3.3 %collective-permute-start.20 = (bf16[64,640]{1,0:T(8,128)(2,1)S(1)}, bf16[64,640]{1,0:T(8,128)(2,1)S(1)}, u32[]{:S(2)}, u32[]{:S(2)}) collective-permute-start(bf16[64,640]{1,0:T(8,128)(2,1)S(1)} %get-tuple-element.39), channel_id=1, source_target_pairs={{0,0},{1,4},{2,8},{3,12},{4,1},{5,5},{6,9},{7,13},{8,2},{9,6},{10,... | collective-permute-start | bytes 245768 | tf_op jit(solution)/shard_map/ppermute | solution.py:582
  62.3 2.8 %collective-permute-start.22 = (bf16[64,640]{1,0:T(8,128)(2,1)S(1)}, bf16[64,640]{1,0:T(8,128)(2,1)S(1)}, u32[]{:S(2)}, u32[]{:S(2)}) collective-permute-start(bf16[64,640]{1,0:T(8,128)(2,1)S(1)} %get-tuple-element.41), channel_id=1, source_target_pairs={{0,2},{1,6},{2,10},{3,14},{4,3},{5,7},{6,11},{7,15},{8,0},{9,4},{1... | collective-permute-start | bytes 245768 | tf_op jit(solution)/shard_map/ppermute | solution.py:582
  65.6 6.7 %collective-permute-done.22.refs_2_ = bf16[64,640]{1,0:T(8,128)(2,1)S(1)} collective-permute-done((bf16[64,640]{1,0:T(8,128)(2,1)S(1)}, bf16[64,640]{1,0:T(8,128)(2,1)S(1)}, u32[]{:S(2)}, u32[]{:S(2)}) %collective-permute-start.22) | collective-permute-done | bytes 81952 | tf_op jit(solution)/shard_map/ppermute | solution.py:582
  72.3 6.1 %collective-permute-done.23.refs_3_ = bf16[64,640]{1,0:T(8,128)(2,1)S(1)} collective-permute-done((bf16[64,640]{1,0:T(8,128)(2,1)S(1)}, bf16[64,640]{1,0:T(8,128)(2,1)S(1)}, u32[]{:S(2)}, u32[]{:S(2)}) %collective-permute-start.23) | collective-permute-done | bytes 81952 | tf_op jit(solution)/shard_map/ppermute | solution.py:582
  78.4 1.3 %shard_map.102 = bf16[64,1280]{1,0:T(8,128)(2,1)} custom-call(s32[4]{0:T(128)S(1)} %pad_add_fusion.place, bf16[64,5120]{1,0:T(8,128)(2,1)S(1)} %copy-done.2, bf16[64,640]{1,0:T(8,128)(2,1)S(1)} %collective-permute-done.20.refs_0_, bf16[64,640]{1,0:T(8,128)(2,1)S(1)} %collective-permute-done.21.refs_1_, bf16[64,640]{1,0:T(8,128)(2,1)S(1)} %collective-permute-done.22.refs_2_, ...), custom_call_target="tpu_custom_call" | custom-call | flops 327680 | bytes 983040 | tf_op jit(solution)/shard_map/pallas_call | solution.py:21
  (55 shorter events, 16.3 us)
Async XLA Ops:
  4.0 3.1 %collective-permute-start = (bf16[2,64,1280]{2,1,0:T(8,128)(2,1)S(1)}, bf16[2,64,1280]{2,1,0:T(8,128)(2,1)S(1)}, u32[]{:S(2)}, u32[]{:S(2)}) collective-permute-start(bf16[2,64,1280]{2,1,0:T(8,128)(2,1)S(1)} %get-tuple-element.27), channel_id=1, source_target_pairs={{0,1},{1,0},{2,3},{3,2},{4,5},{5,4},{6,7},{7,6},{8,9},{9,8},{10,11... | collective-permute-start | bytes 983048 | tf_op jit(solution)/shard_map/ppermute | solution.py:376
  4.1 10.7 %collective-permute-start.3 = (bf16[1280,128]{1,0:T(8,128)(2,1)S(1)}, bf16[1280,128]{1,0:T(8,128)(2,1)S(1)}, u32[]{:S(2)}, u32[]{:S(2)}) collective-permute-start(bf16[1280,128]{1,0:T(8,128)(2,1)S(1)} %get-tuple-element.24), channel_id=1, source_target_pairs={{0,2},{1,3},{2,0},{3,1},{4,6},{5,7},{6,4},{7,5},{8,10},{9,11},{10,... | collective-permute-start | bytes 983048 | tf_op jit(solution)/shard_map/ppermute | solution.py:376
  6.8 15.1 %collective-permute-start.2 = (bf16[1280,256]{1,0:T(8,128)(2,1)S(1)}, bf16[1280,256]{1,0:T(8,128)(2,1)S(1)}, u32[]{:S(2)}, u32[]{:S(2)}) collective-permute-start(bf16[1280,256]{1,0:T(8,128)(2,1)S(1)} %get-tuple-element.28.own), channel_id=1, source_target_pairs={{0,1},{1,0},{2,3},{3,2},{4,5},{5,4},{6,7},{7,6},{8,9},{9,8},{10,11... | collective-permute-start | bytes 1966088 | tf_op jit(solution)/shard_map/ppermute | solution.py:376
  14.8 3.4 %collective-permute-start.4 = (bf16[1280,128]{1,0:T(8,128)(2,1)S(1)}, bf16[1280,128]{1,0:T(8,128)(2,1)S(1)}, u32[]{:S(2)}, u32[]{:S(2)}) collective-permute-start(bf16[1280,128]{1,0:T(8,128)(2,1)S(1)} %collective-permute-done.3.refs_0_), channel_id=1, source_target_pairs={{0,1},{1,0},{2,3},{3,2},{4,5},{5,4},{6,7},{7,6},{8,9},{9,8},{10,11... | collective-permute-start | bytes 983048 | tf_op jit(solution)/shard_map/ppermute | solution.py:376
  15.4 9.4 %collective-permute-start.5 = (bf16[1280,128]{1,0:T(8,128)(2,1)S(1)}, bf16[1280,128]{1,0:T(8,128)(2,1)S(1)}, u32[]{:S(2)}, u32[]{:S(2)}) collective-permute-start(bf16[1280,128]{1,0:T(8,128)(2,1)S(1)} %collective-permute-done.3.refs_0_), channel_id=1, source_target_pairs={{0,16},{16,0},{1,17},{17,1},{2,18},{18,2},{3,19},{19,3},{4,20},{20... | collective-permute-start | bytes 983048 | tf_op jit(solution)/shard_map/ppermute | solution.py:376
  16.9 9.0 %collective-permute-start.1 = (bf16[2,64,1280]{2,1,0:T(8,128)(2,1)S(1)}, bf16[2,64,1280]{2,1,0:T(8,128)(2,1)S(1)}, u32[]{:S(2)}, u32[]{:S(2)}) collective-permute-start(bf16[2,64,1280]{2,1,0:T(8,128)(2,1)S(1)} %shard_map.93), channel_id=1, source_target_pairs={{0,2},{1,3},{2,0},{3,1},{4,6},{5,7},{6,4},{7,5},{8,10},{9,11},{10,... | collective-permute-start | bytes 983048 | tf_op jit(solution)/shard_map/ppermute | solution.py:376
  19.1 38.2 %collective-permute-start.19 = (bf16[1024,640]{1,0:T(8,128)(2,1)S(1)}, bf16[1024,640]{1,0:T(8,128)(2,1)S(1)}, u32[]{:S(2)}, u32[]{:S(2)}) collective-permute-start(bf16[1024,640]{1,0:T(8,128)(2,1)S(1)} %shard_map.95), channel_id=1, source_target_pairs={{0,4},{4,0},{8,12},{12,8},{1,5},{5,1},{9,13},{13,9},{2,6},{6,2},{1... | collective-permute-start | bytes 3932168 | tf_op jit(solution)/shard_map/ppermute | solution.py:376
  28.4 5.6 %collective-permute-start.6 = (f32[128,1024]{1,0:T(8,128)S(1)}, f32[128,1024]{1,0:T(8,128)S(1)}, u32[]{:S(2)}, u32[]{:S(2)}) collective-permute-start(f32[128,1024]{1,0:T(8,128)S(1)} %get-tuple-element.36), channel_id=1, source_target_pairs={{0,1},{1,0},{2,3},{3,2},{4,5},{5,4},{6,7},{7,6},{8,9},{9,8},{10,11... | collective-permute-start | bytes 1572872 | tf_op jit(solution)/shard_map/ppermute | solution.py:376
  29.5 2.0 %collective-permute-start.7 = (bf16[1280,128]{1,0:T(8,128)(2,1)S(1)}, bf16[1280,128]{1,0:T(8,128)(2,1)S(1)}, u32[]{:S(2)}, u32[]{:S(2)}) collective-permute-start(bf16[1280,128]{1,0:T(8,128)(2,1)S(1)} %collective-permute-done.5.refs_1_), channel_id=1, source_target_pairs={{0,1},{1,0},{2,3},{3,2},{4,5},{5,4},{6,7},{7,6},{8,9},{9,8},{10,11... | collective-permute-start | bytes 983048 | tf_op jit(solution)/shard_map/ppermute | solution.py:376
  32.7 4.1 %collective-permute-start.9 = (bf16[192,256]{1,0:T(8,128)(2,1)S(1)}, bf16[192,256]{1,0:T(8,128)(2,1)S(1)}, u32[]{:S(2)}, u32[]{:S(2)}) collective-permute-start(bf16[192,256]{1,0:T(8,128)(2,1)S(1)} %shard_map.98.refs_0_), channel_id=1, source_target_pairs={{0,2},{1,3},{2,0},{3,1},{4,6},{5,7},{6,4},{7,5},{8,10},{9,11},{10,... | collective-permute-start | bytes 294920 | tf_op jit(solution)/shard_map/ppermute | solution.py:376
  34.5 4.9 %collective-permute-start.11 = (bf16[64,1024]{1,0:T(8,128)(2,1)S(1)}, bf16[64,1024]{1,0:T(8,128)(2,1)S(1)}, u32[]{:S(2)}, u32[]{:S(2)}) collective-permute-start(bf16[64,1024]{1,0:T(8,128)(2,1)S(1)} %shard_map.99), channel_id=1, source_target_pairs={{0,2},{1,3},{2,0},{3,1},{4,6},{5,7},{6,4},{7,5},{8,10},{9,11},{10,... | collective-permute-start | bytes 393224 | tf_op jit(solution)/shard_map/ppermute | solution.py:376
  34.9 3.4 %collective-permute-start.8 = (bf16[192,256]{1,0:T(8,128)(2,1)S(1)}, bf16[192,256]{1,0:T(8,128)(2,1)S(1)}, u32[]{:S(2)}, u32[]{:S(2)}) collective-permute-start(bf16[192,256]{1,0:T(8,128)(2,1)S(1)} %shard_map.98.refs_0_), channel_id=1, source_target_pairs={{0,1},{1,0},{2,3},{3,2},{4,5},{5,4},{6,7},{7,6},{8,9},{9,8},{10,11... | collective-permute-start | bytes 294920 | tf_op jit(solution)/shard_map/ppermute | solution.py:376
  36.8 2.4 %collective-permute-start.10 = (bf16[192,256]{1,0:T(8,128)(2,1)S(1)}, bf16[192,256]{1,0:T(8,128)(2,1)S(1)}, u32[]{:S(2)}, u32[]{:S(2)}) collective-permute-start(bf16[192,256]{1,0:T(8,128)(2,1)S(1)} %collective-permute-done.9.refs_2_), channel_id=1, source_target_pairs={{0,1},{1,0},{2,3},{3,2},{4,5},{5,4},{6,7},{7,6},{8,9},{9,8},{10,11... | collective-permute-start | bytes 294920 | tf_op jit(solution)/shard_map/ppermute | solution.py:376
  42.5 9.2 %collective-permute-start.17 = (bf16[64,1024]{1,0:T(8,128)(2,1)S(1)}, bf16[64,1024]{1,0:T(8,128)(2,1)S(1)}, u32[]{:S(2)}, u32[]{:S(2)}) collective-permute-start(bf16[64,1024]{1,0:T(8,128)(2,1)S(1)} %shard_map.100.refs_0_), channel_id=1, source_target_pairs={{0,6},{1,7},{2,4},{3,5},{4,2},{5,3},{6,0},{7,1},{8,14},{9,15},{10,... | collective-permute-start | bytes 393224 | tf_op jit(solution)/shard_map/ppermute | solution.py:385
  45.0 9.6 %collective-permute-start.15 = (bf16[64,1024]{1,0:T(8,128)(2,1)S(1)}, bf16[64,1024]{1,0:T(8,128)(2,1)S(1)}, u32[]{:S(2)}, u32[]{:S(2)}) collective-permute-start(bf16[64,1024]{1,0:T(8,128)(2,1)S(1)} %shard_map.100.refs_0_), channel_id=1, source_target_pairs={{0,4},{1,5},{2,6},{3,7},{4,0},{5,1},{6,2},{7,3},{8,12},{9,13},{10,... | collective-permute-start | bytes 393224 | tf_op jit(solution)/shard_map/ppermute | solution.py:385
  45.2 10.8 %collective-permute-start.13 = (bf16[64,1024]{1,0:T(8,128)(2,1)S(1)}, bf16[64,1024]{1,0:T(8,128)(2,1)S(1)}, u32[]{:S(2)}, u32[]{:S(2)}) collective-permute-start(bf16[64,1024]{1,0:T(8,128)(2,1)S(1)} %shard_map.100.refs_0_), channel_id=1, source_target_pairs={{0,2},{1,3},{2,0},{3,1},{4,6},{5,7},{6,4},{7,5},{8,10},{9,11},{10,... | collective-permute-start | bytes 393224 | tf_op jit(solution)/shard_map/ppermute | solution.py:376
  45.3 10.6 %collective-permute-start.12 = (bf16[64,1024]{1,0:T(8,128)(2,1)S(1)}, bf16[64,1024]{1,0:T(8,128)(2,1)S(1)}, u32[]{:S(2)}, u32[]{:S(2)}) collective-permute-start(bf16[64,1024]{1,0:T(8,128)(2,1)S(1)} %shard_map.100.refs_0_), channel_id=1, source_target_pairs={{0,1},{1,0},{2,3},{3,2},{4,5},{5,4},{6,7},{7,6},{8,9},{9,8},{10,11... | collective-permute-start | bytes 393224 | tf_op jit(solution)/shard_map/ppermute | solution.py:376
  51.7 4.3 %collective-permute-start.18 = (bf16[64,1024]{1,0:T(8,128)(2,1)S(1)}, bf16[64,1024]{1,0:T(8,128)(2,1)S(1)}, u32[]{:S(2)}, u32[]{:S(2)}) collective-permute-start(bf16[64,1024]{1,0:T(8,128)(2,1)S(1)} %collective-permute-done.17.refs_6_), channel_id=1, source_target_pairs={{0,1},{1,0},{2,3},{3,2},{4,5},{5,4},{6,7},{7,6},{8,9},{9,8},{10,11... | collective-permute-start | bytes 393224 | tf_op jit(solution)/shard_map/ppermute | solution.py:376
  54.5 2.4 %collective-permute-start.16 = (bf16[64,1024]{1,0:T(8,128)(2,1)S(1)}, bf16[64,1024]{1,0:T(8,128)(2,1)S(1)}, u32[]{:S(2)}, u32[]{:S(2)}) collective-permute-start(bf16[64,1024]{1,0:T(8,128)(2,1)S(1)} %collective-permute-done.15.refs_4_), channel_id=1, source_target_pairs={{0,1},{1,0},{2,3},{3,2},{4,5},{5,4},{6,7},{7,6},{8,9},{9,8},{10,11... | collective-permute-start | bytes 393224 | tf_op jit(solution)/shard_map/ppermute | solution.py:376
  56.0 1.3 %collective-permute-start.14 = (bf16[64,1024]{1,0:T(8,128)(2,1)S(1)}, bf16[64,1024]{1,0:T(8,128)(2,1)S(1)}, u32[]{:S(2)}, u32[]{:S(2)}) collective-permute-start(bf16[64,1024]{1,0:T(8,128)(2,1)S(1)} %collective-permute-done.13.refs_2_), channel_id=1, source_target_pairs={{0,1},{1,0},{2,3},{3,2},{4,5},{5,4},{6,7},{7,6},{8,9},{9,8},{10,11... | collective-permute-start | bytes 393224 | tf_op jit(solution)/shard_map/ppermute | solution.py:376
  58.9 6.7 %collective-permute-start.20 = (bf16[64,640]{1,0:T(8,128)(2,1)S(1)}, bf16[64,640]{1,0:T(8,128)(2,1)S(1)}, u32[]{:S(2)}, u32[]{:S(2)}) collective-permute-start(bf16[64,640]{1,0:T(8,128)(2,1)S(1)} %get-tuple-element.39), channel_id=1, source_target_pairs={{0,0},{1,4},{2,8},{3,12},{4,1},{5,5},{6,9},{7,13},{8,2},{9,6},{10,... | collective-permute-start | bytes 245768 | tf_op jit(solution)/shard_map/ppermute | solution.py:582
  62.2 3.4 %collective-permute-start.21 = (bf16[64,640]{1,0:T(8,128)(2,1)S(1)}, bf16[64,640]{1,0:T(8,128)(2,1)S(1)}, u32[]{:S(2)}, u32[]{:S(2)}) collective-permute-start(bf16[64,640]{1,0:T(8,128)(2,1)S(1)} %get-tuple-element.40), channel_id=1, source_target_pairs={{0,1},{1,5},{2,9},{3,13},{4,0},{5,4},{6,8},{7,12},{8,3},{9,7},{10,... | collective-permute-start | bytes 245768 | tf_op jit(solution)/shard_map/ppermute | solution.py:582
  62.3 10.0 %collective-permute-start.22 = (bf16[64,640]{1,0:T(8,128)(2,1)S(1)}, bf16[64,640]{1,0:T(8,128)(2,1)S(1)}, u32[]{:S(2)}, u32[]{:S(2)}) collective-permute-start(bf16[64,640]{1,0:T(8,128)(2,1)S(1)} %get-tuple-element.41), channel_id=1, source_target_pairs={{0,2},{1,6},{2,10},{3,14},{4,3},{5,7},{6,11},{7,15},{8,0},{9,4},{1... | collective-permute-start | bytes 245768 | tf_op jit(solution)/shard_map/ppermute | solution.py:582
  65.0 13.4 %collective-permute-start.23 = (bf16[64,640]{1,0:T(8,128)(2,1)S(1)}, bf16[64,640]{1,0:T(8,128)(2,1)S(1)}, u32[]{:S(2)}, u32[]{:S(2)}) collective-permute-start(bf16[64,640]{1,0:T(8,128)(2,1)S(1)} %get-tuple-element.42), channel_id=1, source_target_pairs={{0,3},{1,7},{2,11},{3,15},{4,2},{5,6},{6,10},{7,14},{8,1},{9,5},{1... | collective-permute-start | bytes 245768 | tf_op jit(solution)/shard_map/ppermute | solution.py:582
  (9 other events, 64.8 us)

commit v7 on v5

--- a/solution.py
+++ b/solution.py
@@ -53,31 +53,6 @@
         out[j] = normed[:, j * depth : (j + 1) * depth]
 
 
-def norm_kernel(place, hidden, gain, out, split):
-    split_normed(hidden, gain, split)
-    for d in range(out.shape[0]):
-        out[d] = split[place[SP] ^ 1 ^ 2 * d]
-
-
-def norm_split(place, hidden, gain, count):
-    rows, width = hidden.shape
-    step = rows if rows % 32 else 32
-    depth = width // count
-    return call(
-        norm_kernel,
-        place,
-        (rows // step,),
-        [pl.BlockSpec((step, width), lambda i, place: (i, 0)), whole(gain)],
-        [
-            pl.BlockSpec((n, step, depth), lambda i, place: (0, i, 0))
-            for n in (count // 2, count)
-        ],
-        [shape_of((n, rows, depth), BF16) for n in (count // 2, count)],
-        (hidden, gain),
-        (4 * rows * width, 4 * rows * width),
-    )
-
-
 def pack_kernel(place, cont, other, *outs):
     for d, out in enumerate(outs, 1):
         out[0] = cont[place[SP] ^ 2 * d]
@@ -100,30 +75,37 @@
     )
 
 
-def pick_kernel(place, first, key, value, half, both):
+def first_kernel(place, first, key, value, hidden, gain, half, both, out, split):
     size = half.shape[1]
     half[...] = first[...]
     both[:, :size] = key[...]
     both[:, size:] = value[...]
-
-
-def pick_columns(place, weight, size):
+    split_normed(hidden, gain, split)
+    for d in range(out.shape[0]):
+        out[d] = split[place[SP] ^ 1 ^ 2 * d]
+
+
+def first_step(place, weight, hidden, gain, size, count):
     depth = weight.shape[0]
+    rows = hidden.shape[0]
     block = (depth, size)
     outs = [shape_of(block, BF16), shape_of((depth, 2 * size), BF16)]
-    return call(
-        pick_kernel,
+    outs += [shape_of((n, rows, depth), BF16) for n in (count // 2, count)]
+    return call(
+        first_kernel,
         place,
         (1,),
         [
             pl.BlockSpec(block, lambda i, place: (0, 2 * place[HEAD] + place[GROUP])),
             pl.BlockSpec(block, lambda i, place: (0, 2 * place[HEAD])),
             pl.BlockSpec(block, lambda i, place: (0, 2 * place[HEAD] + 1)),
+            whole(hidden),
+            whole(gain),
         ],
         [whole(out) for out in outs],
         outs,
-        (weight, weight, weight),
-        (0, 12 * depth * size),
+        (weight, weight, weight, hidden, gain),
+        (4 * rows * depth * count, 12 * depth * size + 6 * rows * depth * count),
     )
 
 
@@ -268,10 +250,12 @@
     )
     to_prompt = jnp.exp(to_prompt - peak)
     to_cont = jnp.exp(to_cont - peak)
-    divisor = jnp.sum(to_prompt, axis=1, keepdims=True) + jnp.sum(to_cont, axis=1, keepdims=True)
+    factor = 1.0 / (
+        jnp.sum(to_prompt, axis=1, keepdims=True) + jnp.sum(to_cont, axis=1, keepdims=True)
+    )
     result = jnp.dot(
-        (to_prompt / divisor).astype(BF16), prompt[:, size:], preferred_element_type=F32
-    ) + jnp.dot((to_cont / divisor).astype(BF16), cont[:, size:], preferred_element_type=F32)
+        (to_prompt * factor).astype(BF16), prompt[:, size:], preferred_element_type=F32
+    ) + jnp.dot((to_cont * factor).astype(BF16), cont[:, size:], preferred_element_type=F32)
     for h in range(heads):
         out[:, h * size : (h + 1) * size] = result[h * rows : (h + 1) * rows].astype(BF16)
 
@@ -345,20 +329,14 @@
 
 
 def final_sum(place, parts, hidden):
-    rows, width = parts[0].shape
-    width *= 2
+    rows, width = hidden.shape
     count = len(parts)
-    if width % 128:
-        hidden = lax.dynamic_slice_in_dim(hidden, place[TP] * width, width, 1)
-        residual = whole(hidden)
-    else:
-        residual = pl.BlockSpec((rows, width), lambda i, place: (0, place[TP]))
     return call(
         functools.partial(final_kernel, count),
         place,
         (1,),
-        [residual] + [whole(a) for a in parts],
-        pl.BlockSpec((rows, width), lambda i, place: (0, 0)),
+        [whole(a) for a in (hidden, *parts)],
+        whole(hidden),
         shape_of((rows, width), BF16),
         (hidden, *parts),
         (count * rows * width, 12 * rows * width),
@@ -474,6 +452,22 @@
         (4,),
         [pl.BlockSpec((rows // 4, width), lambda i, place: (i, (place[TP] + side) % 2))],
         pl.BlockSpec((rows // 4, width), lambda i, place: (i, 0)),
+        shape_of((rows, width), BF16),
+        (array,),
+        (0, 4 * rows * width),
+    )
+
+
+def own_columns(place, array, width):
+    rows = array.shape[0]
+    if width % 128:
+        return lax.dynamic_slice_in_dim(array, place[TP] * width, width, 1)
+    return call(
+        slice_kernel,
+        place,
+        (1,),
+        [pl.BlockSpec((rows, width), lambda i, place: (0, place[TP]))],
+        pl.BlockSpec((rows, width), lambda i, place: (0, 0)),
         shape_of((rows, width), BF16),
         (array,),
         (0, 4 * rows * width),
@@ -530,13 +524,14 @@
     query_gain = query_gain[None, :]
     key_gain = key_gain[None, :]
 
-    half, both = pick_columns(place, keyval_weight, size)
+    half, both, block, cont = first_step(
+        place, keyval_weight, hidden_cont, norm_gain, size, sp_count
+    )
     halves = other_halves(half, "sp", sp_count)
-    block, cont = norm_split(after(place, half), hidden_cont, norm_gain, sp_count)
+    partner = swap(both, "sp", 1)
     other = swap(block, "sp", 1)
     packed = pack(place, cont, other)
     got = [swap(block, "sp", 2 * d) for d, block in enumerate(packed, 1)]
-    partner = swap(both, "sp", 1)
     halves = after(halves, packed)
     others = {d: swap(half, "groups", 1) for d, half in halves.items()}
     halves = both_cores(halves, "sp")
@@ -548,7 +543,8 @@
     cosine, sine = tables(
         place, sample_lengths, prompt_rows, prompt_rows * sp_count, cont_rows, size
     )
-    got = after(got, near_pair, others, sent, cosine)
+    hidden = own_columns(place, after(hidden_cont, cosine), out_weight.shape[1])
+    got = after(got, near_pair, others, sent, cosine, hidden)
     others = both_cores(others, "sp")
 
     keep, send = query_parts(place, cont, [other] + got, query_weight)
@@ -587,7 +583,7 @@
         )
         for e, part in enumerate(parts)
     ]
-    return final_sum(place, parts, hidden_cont)
+    return final_sum(place, parts, hidden)
 
 
 def solution(mesh):

time: 81.1 us -> 82.2 us (1.014)
  local copies, waits for them, and re-layouts: 1.93 us -> 3.6 us
    unnamed x18 -> x22, local copies, waits for them, and re-layouts: 1.93 us -> 3.6 us
  transfers between devices with their start and end apart: 24 -> 24, of which waited for: 11 -> 11; matrix products, arithmetic and copies ran while one was open for 0% -> 0% of each run, Pallas kernels for 14% -> 15%
where the time goes in v7:
time: 82.2 us; the launch traced here: 81.9 us
  waiting for transfers between devices  32.6 us (40%)
  starting transfers between devices  29.1 us (35%)
  Pallas kernels  16.4 us (20%)
  local copies, waits for them, and re-layouts  3.6 us (4%)
    ppermute x18, starting transfers between devices, swap(): lax.ppermute(array, axis, [(i, i ^ bits) for i in range(lax.axis_size(axi...  20.1 us
    ppermute x18, waiting for transfers between devices, swap(): lax.ppermute(array, axis, [(i, i ^ bits) for i in range(lax.axis_size(axi...  19.1 us
    pallas_call x12, Pallas kernels, call(): pl.pallas_call(kernel, out_shape=out_shape, grid_spec=pltpu.PrefetchScala...  16.4 us
    ppermute x4, waiting for transfers between devices, on_device(): lax.ppermute(part, ('tp', 'sp'), [(t * sp_count + s, s * sp_count + (t ^...  13 us
    ppermute x4, starting transfers between devices, on_device(): lax.ppermute(part, ('tp', 'sp'), [(t * sp_count + s, s * sp_count + (t ^...  7.62 us
    unnamed x22, local copies, waits for them, and re-layouts  3.6 us
  transfers between devices with their start and end apart: 24, of which 11 were waited for; matrix products, arithmetic and copies ran while one was open for 0% of the time, Pallas kernels for 15%

profile of v7, /device:TPU:1, one launch (start us, length us, event | category | flops | bytes accessed | tf_op | source)
XLA Modules:
  0.0 81.9 jit_solution(1918008186501470465)
XLA Ops:
  0.1 1.7 %copy-done = bf16[1280,1024]{1,0:T(8,128)(2,1)S(1)} copy-done((bf16[1280,1024]{1,0:T(8,128)(2,1)S(1)}, bf16[1280,1024]{1,0:T(8,128)(2,1)}, u32[]{:S(2)}) %copy-start) | copy-done | bytes 2621464
  3.6 1.3 %shard_map.93 = (bf16[1280,128]{1,0:T(8,128)(2,1)S(1)}, bf16[1280,256]{1,0:T(8,128)(2,1)S(1)}, bf16[2,64,1280]{2,1,0:T(8,128)(2,1)S(1)}, bf16[4,64,1280]{2,1,0:T(8,128)(2,1)S(1)}) custom-call(s32[4]{0:T(128)S(1)} %pad_add_fusion.place, bf16[1280,1024]{1,0:T(8,128)(2,1)S(1)} %copy-done, bf16[1280,1024]{1,0:T(8,128)(2,1)S(1)} %copy-done, ...), custom_call_target="tpu_custom_call" | custom-call | flops 1310720 | bytes 3932160 | tf_op jit(solution)/shard_map/pallas_call | solution.py:21
  5.1 2.7 %collective-permute-start.3 = (bf16[1280,128]{1,0:T(8,128)(2,1)S(1)}, bf16[1280,128]{1,0:T(8,128)(2,1)S(1)}, u32[]{:S(2)}, u32[]{:S(2)}) collective-permute-start(bf16[1280,128]{1,0:T(8,128)(2,1)S(1)} %get-tuple-element.29), channel_id=1, source_target_pairs={{0,2},{1,3},{2,0},{3,1},{4,6},{5,7},{6,4},{7,5},{8,10},{9,11},{10,... | collective-permute-start | bytes 983048 | tf_op jit(solution)/shard_map/ppermute | solution.py:351
  8.7 7.0 %collective-permute-done.3.refs_0_ = bf16[1280,128]{1,0:T(8,128)(2,1)S(1)} collective-permute-done((bf16[1280,128]{1,0:T(8,128)(2,1)S(1)}, bf16[1280,128]{1,0:T(8,128)(2,1)S(1)}, u32[]{:S(2)}, u32[]{:S(2)}) %collective-permute-start.3) | collective-permute-done | bytes 327712 | tf_op jit(solution)/shard_map/ppermute | solution.py:351
  16.4 1.5 %collective-permute-start.5 = (bf16[1280,128]{1,0:T(8,128)(2,1)S(1)}, bf16[1280,128]{1,0:T(8,128)(2,1)S(1)}, u32[]{:S(2)}, u32[]{:S(2)}) collective-permute-start(bf16[1280,128]{1,0:T(8,128)(2,1)S(1)} %collective-permute-done.3.refs_0_), channel_id=1, source_target_pairs={{0,16},{16,0},{1,17},{17,1},{2,18},{18,2},{3,19},{19,3},{4,20},{20... | collective-permute-start | bytes 983048 | tf_op jit(solution)/shard_map/ppermute | solution.py:351
  17.9 1.2 %collective-permute-start.1 = (bf16[2,64,1280]{2,1,0:T(8,128)(2,1)S(1)}, bf16[2,64,1280]{2,1,0:T(8,128)(2,1)S(1)}, u32[]{:S(2)}, u32[]{:S(2)}) collective-permute-start(bf16[2,64,1280]{2,1,0:T(8,128)(2,1)S(1)} %shard_map.94), channel_id=1, source_target_pairs={{0,2},{1,3},{2,0},{3,1},{4,6},{5,7},{6,4},{7,5},{8,10},{9,11},{10,... | collective-permute-start | bytes 983048 | tf_op jit(solution)/shard_map/ppermute | solution.py:351
  20.0 1.4 %collective-permute-start.19 = (bf16[1024,640]{1,0:T(8,128)(2,1)S(1)}, bf16[1024,640]{1,0:T(8,128)(2,1)S(1)}, u32[]{:S(2)}, u32[]{:S(2)}) collective-permute-start(bf16[1024,640]{1,0:T(8,128)(2,1)S(1)} %shard_map.96), channel_id=1, source_target_pairs={{0,4},{4,0},{8,12},{12,8},{1,5},{5,1},{9,13},{13,9},{2,6},{6,2},{1... | collective-permute-start | bytes 3932168 | tf_op jit(solution)/shard_map/ppermute | solution.py:351
  21.4 1.5 %shard_map.91 = (f32[192,128]{1,0:T(8,128)S(1)}, f32[192,128]{1,0:T(8,128)S(1)}) custom-call(s32[4]{0:T(128)S(1)} %pad_add_fusion.place, s32[8]{0:T(128)S(1)} %copy-done.9), custom_call_target="tpu_custom_call" | custom-call | flops 2457600 | bytes 196608 | tf_op jit(solution)/shard_map/pallas_call | solution.py:21
  23.5 1.6 %shard_map.95 = (bf16[4,128,1280]{2,1,0:T(8,128)(2,1)S(1)}, f32[192,256]{1,0:T(8,128)S(1)}) custom-call(s32[4]{0:T(128)S(1)} %pad_add_fusion.place, bf16[128,5120]{1,0:T(8,128)(2,1)S(1)} %copy-done.5, f32[1,5120]{1,0:T(1,128)S(1)} %bitcast.8, bf16[4,64,1280]{2,1,0:T(8,128)(2,1)S(1)} %get-tuple-element.26.cont.refs_0_, ...), custom_call_target="tpu_custom_call" | custom-call | flops 251658240 | bytes 5242880 | tf_op jit(solution)/shard_map/pallas_call | solution.py:21
  26.9 2.4 %shard_map.97 = (f32[128,1024]{1,0:T(8,128)S(1)}, f32[128,1024]{1,0:T(8,128)S(1)}) custom-call(s32[4]{0:T(128)S(1)} %pad_add_fusion.place, bf16[4,64,1280]{2,1,0:T(8,128)(2,1)S(1)} %get-tuple-element.26.cont.refs_0_, bf16[2,64,1280]{2,1,0:T(8,128)(2,1)S(1)} %collective-permute-done.other.refs_1_, bf16[2,64,1280]{2,1,0:T(8,128)(2,1)S(1)} %collective-permute-done.1.refs_2_, ...), custom_call_target="tpu_custom_call" | custom-call | flops 671088640 | bytes 2621440 | tf_op jit(solution)/shard_map/pallas_call | solution.py:21
  30.6 1.5 %collective-permute-done.6.right.near = f32[128,1024]{1,0:T(8,128)S(1)} collective-permute-done((f32[128,1024]{1,0:T(8,128)S(1)}, f32[128,1024]{1,0:T(8,128)S(1)}, u32[]{:S(2)}, u32[]{:S(2)}) %collective-permute-start.6) | collective-permute-done | bytes 524320 | tf_op jit(solution)/shard_map/ppermute | solution.py:351
  32.6 1.3 %collective-permute-start.7 = (f32[64,1024]{1,0:T(8,128)S(1)}, f32[64,1024]{1,0:T(8,128)S(1)}, u32[]{:S(2)}, u32[]{:S(2)}) collective-permute-start(f32[64,1024]{1,0:T(8,128)S(1)} %shard_map.98), channel_id=1, source_target_pairs={{0,2},{1,3},{2,0},{3,1},{4,6},{5,7},{6,4},{7,5},{8,10},{9,11},{10,... | collective-permute-start | bytes 786440 | tf_op jit(solution)/shard_map/ppermute | solution.py:351
  36.3 6.0 %collective-permute-done.10.refs_2_ = bf16[192,256]{1,0:T(8,128)(2,1)S(1)} collective-permute-done((bf16[192,256]{1,0:T(8,128)(2,1)S(1)}, bf16[192,256]{1,0:T(8,128)(2,1)S(1)}, u32[]{:S(2)}, u32[]{:S(2)}) %collective-permute-start.10) | collective-permute-done | bytes 98336 | tf_op jit(solution)/shard_map/ppermute | solution.py:351
  44.5 3.0 %shard_map.100.refs_0_ = bf16[64,1024]{1,0:T(8,128)(2,1)S(1)} custom-call(s32[4]{0:T(128)S(1)} %pad_add_fusion.place, s32[8]{0:T(128)S(1)} %copy-done.9, f32[128,1024]{1,0:T(8,128)S(1)} %get-tuple-element.35.left.mine, f32[128,1024]{1,0:T(8,128)S(1)} %collective-permute-done.6.right.near, f32[64,1024]{1,0:T(8,128)S(1)} %collective-permute-done.7.far, ...), custom_call_target="tpu_custom_call" | custom-call | flops 201326592 | bytes 1048576 | tf_op jit(solution)/shard_map/pallas_call | solution.py:21
  47.4 1.3 %collective-permute-start.13 = (bf16[64,1024]{1,0:T(8,128)(2,1)S(1)}, bf16[64,1024]{1,0:T(8,128)(2,1)S(1)}, u32[]{:S(2)}, u32[]{:S(2)}) collective-permute-start(bf16[64,1024]{1,0:T(8,128)(2,1)S(1)} %shard_map.100.refs_0_), channel_id=1, source_target_pairs={{0,2},{1,3},{2,0},{3,1},{4,6},{5,7},{6,4},{7,5},{8,10},{9,11},{10,... | collective-permute-start | bytes 393224 | tf_op jit(solution)/shard_map/ppermute | solution.py:351
  48.7 1.3 %collective-permute-start.15 = (bf16[64,1024]{1,0:T(8,128)(2,1)S(1)}, bf16[64,1024]{1,0:T(8,128)(2,1)S(1)}, u32[]{:S(2)}, u32[]{:S(2)}) collective-permute-start(bf16[64,1024]{1,0:T(8,128)(2,1)S(1)} %shard_map.100.refs_0_), channel_id=1, source_target_pairs={{0,4},{1,5},{2,6},{3,7},{4,0},{5,1},{6,2},{7,3},{8,12},{9,13},{10,... | collective-permute-start | bytes 393224 | tf_op jit(solution)/shard_map/ppermute | solution.py:360
  53.4 2.3 %collective-permute-start.16 = (bf16[64,1024]{1,0:T(8,128)(2,1)S(1)}, bf16[64,1024]{1,0:T(8,128)(2,1)S(1)}, u32[]{:S(2)}, u32[]{:S(2)}) collective-permute-start(bf16[64,1024]{1,0:T(8,128)(2,1)S(1)} %collective-permute-done.15.refs_4_), channel_id=1, source_target_pairs={{0,1},{1,0},{2,3},{3,2},{4,5},{5,4},{6,7},{7,6},{8,9},{9,8},{10,11... | collective-permute-start | bytes 393224 | tf_op jit(solution)/shard_map/ppermute | solution.py:351
  56.2 1.2 %collective-permute-start.18 = (bf16[64,1024]{1,0:T(8,128)(2,1)S(1)}, bf16[64,1024]{1,0:T(8,128)(2,1)S(1)}, u32[]{:S(2)}, u32[]{:S(2)}) collective-permute-start(bf16[64,1024]{1,0:T(8,128)(2,1)S(1)} %collective-permute-done.17.refs_6_), channel_id=1, source_target_pairs={{0,1},{1,0},{2,3},{3,2},{4,5},{5,4},{6,7},{7,6},{8,9},{9,8},{10,11... | collective-permute-start | bytes 393224 | tf_op jit(solution)/shard_map/ppermute | solution.py:351
  58.4 1.6 %shard_map.101 = (bf16[64,640]{1,0:T(8,128)(2,1)S(1)}, bf16[64,640]{1,0:T(8,128)(2,1)S(1)}, bf16[64,640]{1,0:T(8,128)(2,1)S(1)}, bf16[64,640]{1,0:T(8,128)(2,1)S(1)}) custom-call(s32[4]{0:T(128)S(1)} %pad_add_fusion.place, bf16[64,1024]{1,0:T(8,128)(2,1)S(1)} %shard_map.100.refs_0_, bf16[64,1024]{1,0:T(8,128)(2,1)S(1)} %collective-permute-done.12.refs_1_, ...), custom_call_target="tpu_custom_call" | custom-call | flops 671088640 | bytes 2621440 | tf_op jit(solution)/shard_map/pallas_call | solution.py:21
  60.0 3.5 %collective-permute-start.20 = (bf16[64,640]{1,0:T(8,128)(2,1)S(1)}, bf16[64,640]{1,0:T(8,128)(2,1)S(1)}, u32[]{:S(2)}, u32[]{:S(2)}) collective-permute-start(bf16[64,640]{1,0:T(8,128)(2,1)S(1)} %get-tuple-element.39), channel_id=1, source_target_pairs={{0,0},{1,4},{2,8},{3,12},{4,1},{5,5},{6,9},{7,13},{8,2},{9,6},{10,... | collective-permute-start | bytes 245768 | tf_op jit(solution)/shard_map/ppermute | solution.py:575
  63.5 3.7 %collective-permute-start.22 = (bf16[64,640]{1,0:T(8,128)(2,1)S(1)}, bf16[64,640]{1,0:T(8,128)(2,1)S(1)}, u32[]{:S(2)}, u32[]{:S(2)}) collective-permute-start(bf16[64,640]{1,0:T(8,128)(2,1)S(1)} %get-tuple-element.41), channel_id=1, source_target_pairs={{0,2},{1,6},{2,10},{3,14},{4,3},{5,7},{6,11},{7,15},{8,0},{9,4},{1... | collective-permute-start | bytes 245768 | tf_op jit(solution)/shard_map/ppermute | solution.py:575
  67.6 5.4 %collective-permute-done.22.refs_2_ = bf16[64,640]{1,0:T(8,128)(2,1)S(1)} collective-permute-done((bf16[64,640]{1,0:T(8,128)(2,1)S(1)}, bf16[64,640]{1,0:T(8,128)(2,1)S(1)}, u32[]{:S(2)}, u32[]{:S(2)}) %collective-permute-start.22) | collective-permute-done | bytes 81952 | tf_op jit(solution)/shard_map/ppermute | solution.py:575
  73.0 7.6 %collective-permute-done.23.refs_3_ = bf16[64,640]{1,0:T(8,128)(2,1)S(1)} collective-permute-done((bf16[64,640]{1,0:T(8,128)(2,1)S(1)}, bf16[64,640]{1,0:T(8,128)(2,1)S(1)}, u32[]{:S(2)}, u32[]{:S(2)}) %collective-permute-start.23) | collective-permute-done | bytes 81952 | tf_op jit(solution)/shard_map/ppermute | solution.py:575
  80.6 1.3 %shard_map.102 = bf16[64,1280]{1,0:T(8,128)(2,1)} custom-call(s32[4]{0:T(128)S(1)} %pad_add_fusion.place, bf16[64,1280]{1,0:T(8,128)(2,1)S(1)} %shard_map.92.hidden, bf16[64,640]{1,0:T(8,128)(2,1)S(1)} %collective-permute-done.20.refs_0_, bf16[64,640]{1,0:T(8,128)(2,1)S(1)} %collective-permute-done.21.refs_1_, ...), custom_call_target="tpu_custom_call" | custom-call | flops 327680 | bytes 983040 | tf_op jit(solution)/shard_map/pallas_call | solution.py:21
  (59 shorter events, 18.5 us)
Async XLA Ops:
  4.9 3.1 %collective-permute-start = (bf16[2,64,1280]{2,1,0:T(8,128)(2,1)S(1)}, bf16[2,64,1280]{2,1,0:T(8,128)(2,1)S(1)}, u32[]{:S(2)}, u32[]{:S(2)}) collective-permute-start(bf16[2,64,1280]{2,1,0:T(8,128)(2,1)S(1)} %get-tuple-element.27), channel_id=1, source_target_pairs={{0,1},{1,0},{2,3},{3,2},{4,5},{5,4},{6,7},{7,6},{8,9},{9,8},{10,11... | collective-permute-start | bytes 983048 | tf_op jit(solution)/shard_map/ppermute | solution.py:351
  5.1 10.7 %collective-permute-start.3 = (bf16[1280,128]{1,0:T(8,128)(2,1)S(1)}, bf16[1280,128]{1,0:T(8,128)(2,1)S(1)}, u32[]{:S(2)}, u32[]{:S(2)}) collective-permute-start(bf16[1280,128]{1,0:T(8,128)(2,1)S(1)} %get-tuple-element.29), channel_id=1, source_target_pairs={{0,2},{1,3},{2,0},{3,1},{4,6},{5,7},{6,4},{7,5},{8,10},{9,11},{10,... | collective-permute-start | bytes 983048 | tf_op jit(solution)/shard_map/ppermute | solution.py:351
  7.7 15.7 %collective-permute-start.2 = (bf16[1280,256]{1,0:T(8,128)(2,1)S(1)}, bf16[1280,256]{1,0:T(8,128)(2,1)S(1)}, u32[]{:S(2)}, u32[]{:S(2)}) collective-permute-start(bf16[1280,256]{1,0:T(8,128)(2,1)S(1)} %get-tuple-element.28.own), channel_id=1, source_target_pairs={{0,1},{1,0},{2,3},{3,2},{4,5},{5,4},{6,7},{7,6},{8,9},{9,8},{10,11... | collective-permute-start | bytes 1966088 | tf_op jit(solution)/shard_map/ppermute | solution.py:351
  15.7 3.4 %collective-permute-start.4 = (bf16[1280,128]{1,0:T(8,128)(2,1)S(1)}, bf16[1280,128]{1,0:T(8,128)(2,1)S(1)}, u32[]{:S(2)}, u32[]{:S(2)}) collective-permute-start(bf16[1280,128]{1,0:T(8,128)(2,1)S(1)} %collective-permute-done.3.refs_0_), channel_id=1, source_target_pairs={{0,1},{1,0},{2,3},{3,2},{4,5},{5,4},{6,7},{7,6},{8,9},{9,8},{10,11... | collective-permute-start | bytes 983048 | tf_op jit(solution)/shard_map/ppermute | solution.py:351
  16.4 9.4 %collective-permute-start.5 = (bf16[1280,128]{1,0:T(8,128)(2,1)S(1)}, bf16[1280,128]{1,0:T(8,128)(2,1)S(1)}, u32[]{:S(2)}, u32[]{:S(2)}) collective-permute-start(bf16[1280,128]{1,0:T(8,128)(2,1)S(1)} %collective-permute-done.3.refs_0_), channel_id=1, source_target_pairs={{0,16},{16,0},{1,17},{17,1},{2,18},{18,2},{3,19},{19,3},{4,20},{20... | collective-permute-start | bytes 983048 | tf_op jit(solution)/shard_map/ppermute | solution.py:351
  17.9 9.0 %collective-permute-start.1 = (bf16[2,64,1280]{2,1,0:T(8,128)(2,1)S(1)}, bf16[2,64,1280]{2,1,0:T(8,128)(2,1)S(1)}, u32[]{:S(2)}, u32[]{:S(2)}) collective-permute-start(bf16[2,64,1280]{2,1,0:T(8,128)(2,1)S(1)} %shard_map.94), channel_id=1, source_target_pairs={{0,2},{1,3},{2,0},{3,1},{4,6},{5,7},{6,4},{7,5},{8,10},{9,11},{10,... | collective-permute-start | bytes 983048 | tf_op jit(solution)/shard_map/ppermute | solution.py:351
  20.0 38.4 %collective-permute-start.19 = (bf16[1024,640]{1,0:T(8,128)(2,1)S(1)}, bf16[1024,640]{1,0:T(8,128)(2,1)S(1)}, u32[]{:S(2)}, u32[]{:S(2)}) collective-permute-start(bf16[1024,640]{1,0:T(8,128)(2,1)S(1)} %shard_map.96), channel_id=1, source_target_pairs={{0,4},{4,0},{8,12},{12,8},{1,5},{5,1},{9,13},{13,9},{2,6},{6,2},{1... | collective-permute-start | bytes 3932168 | tf_op jit(solution)/shard_map/ppermute | solution.py:351
  29.3 2.7 %collective-permute-start.6 = (f32[128,1024]{1,0:T(8,128)S(1)}, f32[128,1024]{1,0:T(8,128)S(1)}, u32[]{:S(2)}, u32[]{:S(2)}) collective-permute-start(f32[128,1024]{1,0:T(8,128)S(1)} %get-tuple-element.36), channel_id=1, source_target_pairs={{0,1},{1,0},{2,3},{3,2},{4,5},{5,4},{6,7},{7,6},{8,9},{9,8},{10,11... | collective-permute-start | bytes 1572872 | tf_op jit(solution)/shard_map/ppermute | solution.py:351
  30.5 3.4 %collective-permute-start.8 = (bf16[1280,128]{1,0:T(8,128)(2,1)S(1)}, bf16[1280,128]{1,0:T(8,128)(2,1)S(1)}, u32[]{:S(2)}, u32[]{:S(2)}) collective-permute-start(bf16[1280,128]{1,0:T(8,128)(2,1)S(1)} %collective-permute-done.5.refs_1_), channel_id=1, source_target_pairs={{0,1},{1,0},{2,3},{3,2},{4,5},{5,4},{6,7},{7,6},{8,9},{9,8},{10,11... | collective-permute-start | bytes 983048 | tf_op jit(solution)/shard_map/ppermute | solution.py:351
  32.6 11.8 %collective-permute-start.7 = (f32[64,1024]{1,0:T(8,128)S(1)}, f32[64,1024]{1,0:T(8,128)S(1)}, u32[]{:S(2)}, u32[]{:S(2)}) collective-permute-start(f32[64,1024]{1,0:T(8,128)S(1)} %shard_map.98), channel_id=1, source_target_pairs={{0,2},{1,3},{2,0},{3,1},{4,6},{5,7},{6,4},{7,5},{8,10},{9,11},{10,... | collective-permute-start | bytes 786440 | tf_op jit(solution)/shard_map/ppermute | solution.py:351
  35.0 7.3 %collective-permute-start.10 = (bf16[192,256]{1,0:T(8,128)(2,1)S(1)}, bf16[192,256]{1,0:T(8,128)(2,1)S(1)}, u32[]{:S(2)}, u32[]{:S(2)}) collective-permute-start(bf16[192,256]{1,0:T(8,128)(2,1)S(1)} %shard_map.99.refs_0_), channel_id=1, source_target_pairs={{0,2},{1,3},{2,0},{3,1},{4,6},{5,7},{6,4},{7,5},{8,10},{9,11},{10,... | collective-permute-start | bytes 294920 | tf_op jit(solution)/shard_map/ppermute | solution.py:351
  35.4 8.2 %collective-permute-start.9 = (bf16[192,256]{1,0:T(8,128)(2,1)S(1)}, bf16[192,256]{1,0:T(8,128)(2,1)S(1)}, u32[]{:S(2)}, u32[]{:S(2)}) collective-permute-start(bf16[192,256]{1,0:T(8,128)(2,1)S(1)} %shard_map.99.refs_0_), channel_id=1, source_target_pairs={{0,1},{1,0},{2,3},{3,2},{4,5},{5,4},{6,7},{7,6},{8,9},{9,8},{10,11... | collective-permute-start | bytes 294920 | tf_op jit(solution)/shard_map/ppermute | solution.py:351
  42.3 2.1 %collective-permute-start.11 = (bf16[192,256]{1,0:T(8,128)(2,1)S(1)}, bf16[192,256]{1,0:T(8,128)(2,1)S(1)}, u32[]{:S(2)}, u32[]{:S(2)}) collective-permute-start(bf16[192,256]{1,0:T(8,128)(2,1)S(1)} %collective-permute-done.10.refs_2_), channel_id=1, source_target_pairs={{0,1},{1,0},{2,3},{3,2},{4,5},{5,4},{6,7},{7,6},{8,9},{9,8},{10,11... | collective-permute-start | bytes 294920 | tf_op jit(solution)/shard_map/ppermute | solution.py:351
  47.4 4.8 %collective-permute-start.13 = (bf16[64,1024]{1,0:T(8,128)(2,1)S(1)}, bf16[64,1024]{1,0:T(8,128)(2,1)S(1)}, u32[]{:S(2)}, u32[]{:S(2)}) collective-permute-start(bf16[64,1024]{1,0:T(8,128)(2,1)S(1)} %shard_map.100.refs_0_), channel_id=1, source_target_pairs={{0,2},{1,3},{2,0},{3,1},{4,6},{5,7},{6,4},{7,5},{8,10},{9,11},{10,... | collective-permute-start | bytes 393224 | tf_op jit(solution)/shard_map/ppermute | solution.py:351
  48.7 4.7 %collective-permute-start.15 = (bf16[64,1024]{1,0:T(8,128)(2,1)S(1)}, bf16[64,1024]{1,0:T(8,128)(2,1)S(1)}, u32[]{:S(2)}, u32[]{:S(2)}) collective-permute-start(bf16[64,1024]{1,0:T(8,128)(2,1)S(1)} %shard_map.100.refs_0_), channel_id=1, source_target_pairs={{0,4},{1,5},{2,6},{3,7},{4,0},{5,1},{6,2},{7,3},{8,12},{9,13},{10,... | collective-permute-start | bytes 393224 | tf_op jit(solution)/shard_map/ppermute | solution.py:360
  50.0 6.2 %collective-permute-start.17 = (bf16[64,1024]{1,0:T(8,128)(2,1)S(1)}, bf16[64,1024]{1,0:T(8,128)(2,1)S(1)}, u32[]{:S(2)}, u32[]{:S(2)}) collective-permute-start(bf16[64,1024]{1,0:T(8,128)(2,1)S(1)} %shard_map.100.refs_0_), channel_id=1, source_target_pairs={{0,6},{1,7},{2,4},{3,5},{4,2},{5,3},{6,0},{7,1},{8,14},{9,15},{10,... | collective-permute-start | bytes 393224 | tf_op jit(solution)/shard_map/ppermute | solution.py:360
  50.2 7.3 %collective-permute-start.12 = (bf16[64,1024]{1,0:T(8,128)(2,1)S(1)}, bf16[64,1024]{1,0:T(8,128)(2,1)S(1)}, u32[]{:S(2)}, u32[]{:S(2)}) collective-permute-start(bf16[64,1024]{1,0:T(8,128)(2,1)S(1)} %shard_map.100.refs_0_), channel_id=1, source_target_pairs={{0,1},{1,0},{2,3},{3,2},{4,5},{5,4},{6,7},{7,6},{8,9},{9,8},{10,11... | collective-permute-start | bytes 393224 | tf_op jit(solution)/shard_map/ppermute | solution.py:351
  52.2 5.2 %collective-permute-start.14 = (bf16[64,1024]{1,0:T(8,128)(2,1)S(1)}, bf16[64,1024]{1,0:T(8,128)(2,1)S(1)}, u32[]{:S(2)}, u32[]{:S(2)}) collective-permute-start(bf16[64,1024]{1,0:T(8,128)(2,1)S(1)} %collective-permute-done.13.refs_2_), channel_id=1, source_target_pairs={{0,1},{1,0},{2,3},{3,2},{4,5},{5,4},{6,7},{7,6},{8,9},{9,8},{10,11... | collective-permute-start | bytes 393224 | tf_op jit(solution)/shard_map/ppermute | solution.py:351
  53.4 4.0 %collective-permute-start.16 = (bf16[64,1024]{1,0:T(8,128)(2,1)S(1)}, bf16[64,1024]{1,0:T(8,128)(2,1)S(1)}, u32[]{:S(2)}, u32[]{:S(2)}) collective-permute-start(bf16[64,1024]{1,0:T(8,128)(2,1)S(1)} %collective-permute-done.15.refs_4_), channel_id=1, source_target_pairs={{0,1},{1,0},{2,3},{3,2},{4,5},{5,4},{6,7},{7,6},{8,9},{9,8},{10,11... | collective-permute-start | bytes 393224 | tf_op jit(solution)/shard_map/ppermute | solution.py:351
  56.2 2.2 %collective-permute-start.18 = (bf16[64,1024]{1,0:T(8,128)(2,1)S(1)}, bf16[64,1024]{1,0:T(8,128)(2,1)S(1)}, u32[]{:S(2)}, u32[]{:S(2)}) collective-permute-start(bf16[64,1024]{1,0:T(8,128)(2,1)S(1)} %collective-permute-done.17.refs_6_), channel_id=1, source_target_pairs={{0,1},{1,0},{2,3},{3,2},{4,5},{5,4},{6,7},{7,6},{8,9},{9,8},{10,11... | collective-permute-start | bytes 393224 | tf_op jit(solution)/shard_map/ppermute | solution.py:351
  60.0 7.6 %collective-permute-start.20 = (bf16[64,640]{1,0:T(8,128)(2,1)S(1)}, bf16[64,640]{1,0:T(8,128)(2,1)S(1)}, u32[]{:S(2)}, u32[]{:S(2)}) collective-permute-start(bf16[64,640]{1,0:T(8,128)(2,1)S(1)} %get-tuple-element.39), channel_id=1, source_target_pairs={{0,0},{1,4},{2,8},{3,12},{4,1},{5,5},{6,9},{7,13},{8,2},{9,6},{10,... | collective-permute-start | bytes 245768 | tf_op jit(solution)/shard_map/ppermute | solution.py:575
  63.5 4.2 %collective-permute-start.21 = (bf16[64,640]{1,0:T(8,128)(2,1)S(1)}, bf16[64,640]{1,0:T(8,128)(2,1)S(1)}, u32[]{:S(2)}, u32[]{:S(2)}) collective-permute-start(bf16[64,640]{1,0:T(8,128)(2,1)S(1)} %get-tuple-element.40), channel_id=1, source_target_pairs={{0,1},{1,5},{2,9},{3,13},{4,0},{5,4},{6,8},{7,12},{8,3},{9,7},{10,... | collective-permute-start | bytes 245768 | tf_op jit(solution)/shard_map/ppermute | solution.py:575
  63.5 9.5 %collective-permute-start.22 = (bf16[64,640]{1,0:T(8,128)(2,1)S(1)}, bf16[64,640]{1,0:T(8,128)(2,1)S(1)}, u32[]{:S(2)}, u32[]{:S(2)}) collective-permute-start(bf16[64,640]{1,0:T(8,128)(2,1)S(1)} %get-tuple-element.41), channel_id=1, source_target_pairs={{0,2},{1,6},{2,10},{3,14},{4,3},{5,7},{6,11},{7,15},{8,0},{9,4},{1... | collective-permute-start | bytes 245768 | tf_op jit(solution)/shard_map/ppermute | solution.py:575
  67.3 13.4 %collective-permute-start.23 = (bf16[64,640]{1,0:T(8,128)(2,1)S(1)}, bf16[64,640]{1,0:T(8,128)(2,1)S(1)}, u32[]{:S(2)}, u32[]{:S(2)}) collective-permute-start(bf16[64,640]{1,0:T(8,128)(2,1)S(1)} %get-tuple-element.42), channel_id=1, source_target_pairs={{0,3},{1,7},{2,11},{3,15},{4,2},{5,6},{6,10},{7,14},{8,1},{9,5},{1... | collective-permute-start | bytes 245768 | tf_op jit(solution)/shard_map/ppermute | solution.py:575
  (11 other events, 83.7 us)

commit v8 on v5

--- a/solution.py
+++ b/solution.py
@@ -537,18 +537,18 @@
     packed = pack(place, cont, other)
     got = [swap(block, "sp", 2 * d) for d, block in enumerate(packed, 1)]
     partner = swap(both, "sp", 1)
-    halves = after(halves, packed)
+    sent = column_half(place, after(out_weight, packed), True)
+    out_partner = swap(sent, "tp", 1)
+    cosine, sine = tables(
+        place, sample_lengths, prompt_rows, prompt_rows * sp_count, cont_rows, size
+    )
+    halves = after(halves, packed, sent, cosine)
     others = {d: swap(half, "groups", 1) for d, half in halves.items()}
     halves = both_cores(halves, "sp")
-    sent = column_half(place, after(out_weight, halves), True)
-    out_partner = swap(sent, "tp", 1)
     prompt, near_pair = near_keyval(
         place, hidden_prompt, norm_gain, cont, both, after(partner, halves)
     )
-    cosine, sine = tables(
-        place, sample_lengths, prompt_rows, prompt_rows * sp_count, cont_rows, size
-    )
-    got = after(got, near_pair, others, sent, cosine)
+    got = after(got, near_pair, sent, cosine)
     others = both_cores(others, "sp")
 
     keep, send = query_parts(place, cont, [other] + got, query_weight)

time: 81.1 us -> 79.9 us (0.985)
  waiting for transfers between devices: 33.1 us -> 31.5 us
    ppermute x18, waiting for transfers between devices: 19.7 us -> 18.4 us  [swap(): lax.ppermute(array, axis, [(i, i ^ bits) for i in range(lax.axis_size(axi...]
  transfers between devices with their start and end apart: 24 -> 24, of which waited for: 11 -> 10; matrix products, arithmetic and copies ran while one was open for 0% -> 0% of each run, Pallas kernels for 14% -> 15%
where the time goes in v8:
time: 79.9 us; the launch traced here: 79.7 us
  waiting for transfers between devices  31.5 us (39%)
  starting transfers between devices  29.5 us (37%)
  Pallas kernels  16.5 us (21%)
  local copies, waits for them, and re-layouts  1.92 us (2%)
    ppermute x18, starting transfers between devices, swap(): lax.ppermute(array, axis, [(i, i ^ bits) for i in range(lax.axis_size(axi...  20.4 us
    ppermute x18, waiting for transfers between devices, swap(): lax.ppermute(array, axis, [(i, i ^ bits) for i in range(lax.axis_size(axi...  18.4 us
    pallas_call x12, Pallas kernels, call(): pl.pallas_call(kernel, out_shape=out_shape, grid_spec=pltpu.PrefetchScala...  16.5 us
    ppermute x4, waiting for transfers between devices, on_device(): lax.ppermute(part, ('tp', 'sp'), [(t * sp_count + s, s * sp_count + (t ^...  13 us
    ppermute x4, starting transfers between devices, on_device(): lax.ppermute(part, ('tp', 'sp'), [(t * sp_count + s, s * sp_count + (t ^...  7.79 us
    unnamed x18, local copies, waits for them, and re-layouts  1.92 us
  transfers between devices with their start and end apart: 24, of which 10 were waited for; matrix products, arithmetic and copies ran while one was open for 0% of the time, Pallas kernels for 15%

profile of v8, /device:TPU:1, one launch (start us, length us, event | category | flops | bytes accessed | tf_op | source)
XLA Modules:
  0.0 79.7 jit_solution(17873726911906450195)
XLA Ops:
  0.1 1.7 %copy-done = bf16[1280,1024]{1,0:T(8,128)(2,1)S(1)} copy-done((bf16[1280,1024]{1,0:T(8,128)(2,1)S(1)}, bf16[1280,1024]{1,0:T(8,128)(2,1)}, u32[]{:S(2)}) %copy-start) | copy-done | bytes 2621464
  4.1 2.7 %collective-permute-start.3 = (bf16[1280,128]{1,0:T(8,128)(2,1)S(1)}, bf16[1280,128]{1,0:T(8,128)(2,1)S(1)}, u32[]{:S(2)}, u32[]{:S(2)}) collective-permute-start(bf16[1280,128]{1,0:T(8,128)(2,1)S(1)} %get-tuple-element.24), channel_id=1, source_target_pairs={{0,2},{1,3},{2,0},{3,1},{4,6},{5,7},{6,4},{7,5},{8,10},{9,11},{10,... | collective-permute-start | bytes 983048 | tf_op jit(solution)/shard_map/ppermute | solution.py:373
  7.1 1.5 %shard_map.95 = (f32[192,128]{1,0:T(8,128)S(1)}, f32[192,128]{1,0:T(8,128)S(1)}) custom-call(s32[4]{0:T(128)S(1)} %pad_add_fusion.place, s32[8]{0:T(128)S(1)} %copy-done.7), custom_call_target="tpu_custom_call" | custom-call | flops 2457600 | bytes 196608 | tf_op jit(solution)/shard_map/pallas_call | solution.py:21
  10.1 4.6 %collective-permute-done.3.refs_0_ = bf16[1280,128]{1,0:T(8,128)(2,1)S(1)} collective-permute-done((bf16[1280,128]{1,0:T(8,128)(2,1)S(1)}, bf16[1280,128]{1,0:T(8,128)(2,1)S(1)}, u32[]{:S(2)}, u32[]{:S(2)}) %collective-permute-start.3) | collective-permute-done | bytes 327712 | tf_op jit(solution)/shard_map/ppermute | solution.py:373
  15.4 1.5 %collective-permute-start.1 = (bf16[2,64,1280]{2,1,0:T(8,128)(2,1)S(1)}, bf16[2,64,1280]{2,1,0:T(8,128)(2,1)S(1)}, u32[]{:S(2)}, u32[]{:S(2)}) collective-permute-start(bf16[2,64,1280]{2,1,0:T(8,128)(2,1)S(1)} %shard_map.93), channel_id=1, source_target_pairs={{0,2},{1,3},{2,0},{3,1},{4,6},{5,7},{6,4},{7,5},{8,10},{9,11},{10,... | collective-permute-start | bytes 983048 | tf_op jit(solution)/shard_map/ppermute | solution.py:373
  16.9 1.3 %collective-permute-start.19 = (bf16[1024,640]{1,0:T(8,128)(2,1)S(1)}, bf16[1024,640]{1,0:T(8,128)(2,1)S(1)}, u32[]{:S(2)}, u32[]{:S(2)}) collective-permute-start(bf16[1024,640]{1,0:T(8,128)(2,1)S(1)} %shard_map.94), channel_id=1, source_target_pairs={{0,4},{4,0},{8,12},{12,8},{1,5},{5,1},{9,13},{13,9},{2,6},{6,2},{1... | collective-permute-start | bytes 3932168 | tf_op jit(solution)/shard_map/ppermute | solution.py:373
  18.2 1.2 %collective-permute-start.7 = (bf16[1280,128]{1,0:T(8,128)(2,1)S(1)}, bf16[1280,128]{1,0:T(8,128)(2,1)S(1)}, u32[]{:S(2)}, u32[]{:S(2)}) collective-permute-start(bf16[1280,128]{1,0:T(8,128)(2,1)S(1)} %collective-permute-done.3.refs_0_), channel_id=1, source_target_pairs={{0,16},{16,0},{1,17},{17,1},{2,18},{18,2},{3,19},{19,3},{4,20},{20... | collective-permute-start | bytes 983048 | tf_op jit(solution)/shard_map/ppermute | solution.py:373
  19.5 1.6 %shard_map.96 = (bf16[4,128,1280]{2,1,0:T(8,128)(2,1)S(1)}, f32[192,256]{1,0:T(8,128)S(1)}) custom-call(s32[4]{0:T(128)S(1)} %pad_add_fusion.place, bf16[128,5120]{1,0:T(8,128)(2,1)S(1)} %copy-done.4, f32[1,5120]{1,0:T(1,128)S(1)} %bitcast.8, bf16[4,64,1280]{2,1,0:T(8,128)(2,1)S(1)} %get-tuple-element.26.cont.refs_0_, ...), custom_call_target="tpu_custom_call" | custom-call | flops 251658240 | bytes 5242880 | tf_op jit(solution)/shard_map/pallas_call | solution.py:21
  21.1 3.7 %collective-permute-done.1.refs_2_ = bf16[2,64,1280]{2,1,0:T(8,128)(2,1)S(1)} collective-permute-done((bf16[2,64,1280]{2,1,0:T(8,128)(2,1)S(1)}, bf16[2,64,1280]{2,1,0:T(8,128)(2,1)S(1)}, u32[]{:S(2)}, u32[]{:S(2)}) %collective-permute-start.1) | collective-permute-done | bytes 327712 | tf_op jit(solution)/shard_map/ppermute | solution.py:373
  24.8 2.4 %shard_map.97 = (f32[128,1024]{1,0:T(8,128)S(1)}, f32[128,1024]{1,0:T(8,128)S(1)}) custom-call(s32[4]{0:T(128)S(1)} %pad_add_fusion.place, bf16[4,64,1280]{2,1,0:T(8,128)(2,1)S(1)} %get-tuple-element.26.cont.refs_0_, bf16[2,64,1280]{2,1,0:T(8,128)(2,1)S(1)} %collective-permute-done.other.refs_1_, bf16[2,64,1280]{2,1,0:T(8,128)(2,1)S(1)} %collective-permute-done.1.refs_2_, ...), custom_call_target="tpu_custom_call" | custom-call | flops 671088640 | bytes 2621440 | tf_op jit(solution)/shard_map/pallas_call | solution.py:21
  28.3 1.3 %collective-permute-done.5.right.near = f32[128,1024]{1,0:T(8,128)S(1)} collective-permute-done((f32[128,1024]{1,0:T(8,128)S(1)}, f32[128,1024]{1,0:T(8,128)S(1)}, u32[]{:S(2)}, u32[]{:S(2)}) %collective-permute-start.5) | collective-permute-done | bytes 524320 | tf_op jit(solution)/shard_map/ppermute | solution.py:373
  30.2 1.5 %collective-permute-start.6 = (f32[64,1024]{1,0:T(8,128)S(1)}, f32[64,1024]{1,0:T(8,128)S(1)}, u32[]{:S(2)}, u32[]{:S(2)}) collective-permute-start(f32[64,1024]{1,0:T(8,128)S(1)} %shard_map.98), channel_id=1, source_target_pairs={{0,2},{1,3},{2,0},{3,1},{4,6},{5,7},{6,4},{7,5},{8,10},{9,11},{10,... | collective-permute-start | bytes 786440 | tf_op jit(solution)/shard_map/ppermute | solution.py:373
  33.9 6.0 %collective-permute-done.10.refs_2_ = bf16[192,256]{1,0:T(8,128)(2,1)S(1)} collective-permute-done((bf16[192,256]{1,0:T(8,128)(2,1)S(1)}, bf16[192,256]{1,0:T(8,128)(2,1)S(1)}, u32[]{:S(2)}, u32[]{:S(2)}) %collective-permute-start.10) | collective-permute-done | bytes 98336 | tf_op jit(solution)/shard_map/ppermute | solution.py:373
  42.0 3.0 %shard_map.100.refs_0_ = bf16[64,1024]{1,0:T(8,128)(2,1)S(1)} custom-call(s32[4]{0:T(128)S(1)} %pad_add_fusion.place, s32[8]{0:T(128)S(1)} %copy-done.7, f32[128,1024]{1,0:T(8,128)S(1)} %get-tuple-element.35.left.mine, f32[128,1024]{1,0:T(8,128)S(1)} %collective-permute-done.5.right.near, f32[64,1024]{1,0:T(8,128)S(1)} %collective-permute-done.6.far, ...), custom_call_target="tpu_custom_call" | custom-call | flops 201326592 | bytes 1048576 | tf_op jit(solution)/shard_map/pallas_call | solution.py:21
  45.0 1.5 %collective-permute-start.13 = (bf16[64,1024]{1,0:T(8,128)(2,1)S(1)}, bf16[64,1024]{1,0:T(8,128)(2,1)S(1)}, u32[]{:S(2)}, u32[]{:S(2)}) collective-permute-start(bf16[64,1024]{1,0:T(8,128)(2,1)S(1)} %shard_map.100.refs_0_), channel_id=1, source_target_pairs={{0,2},{1,3},{2,0},{3,1},{4,6},{5,7},{6,4},{7,5},{8,10},{9,11},{10,... | collective-permute-start | bytes 393224 | tf_op jit(solution)/shard_map/ppermute | solution.py:373
  46.5 1.3 %collective-permute-start.15 = (bf16[64,1024]{1,0:T(8,128)(2,1)S(1)}, bf16[64,1024]{1,0:T(8,128)(2,1)S(1)}, u32[]{:S(2)}, u32[]{:S(2)}) collective-permute-start(bf16[64,1024]{1,0:T(8,128)(2,1)S(1)} %shard_map.100.refs_0_), channel_id=1, source_target_pairs={{0,4},{1,5},{2,6},{3,7},{4,0},{5,1},{6,2},{7,3},{8,12},{9,13},{10,... | collective-permute-start | bytes 393224 | tf_op jit(solution)/shard_map/ppermute | solution.py:382
  51.0 2.6 %collective-permute-start.16 = (bf16[64,1024]{1,0:T(8,128)(2,1)S(1)}, bf16[64,1024]{1,0:T(8,128)(2,1)S(1)}, u32[]{:S(2)}, u32[]{:S(2)}) collective-permute-start(bf16[64,1024]{1,0:T(8,128)(2,1)S(1)} %collective-permute-done.15.refs_4_), channel_id=1, source_target_pairs={{0,1},{1,0},{2,3},{3,2},{4,5},{5,4},{6,7},{7,6},{8,9},{9,8},{10,11... | collective-permute-start | bytes 393224 | tf_op jit(solution)/shard_map/ppermute | solution.py:373
  53.6 1.4 %collective-permute-start.18 = (bf16[64,1024]{1,0:T(8,128)(2,1)S(1)}, bf16[64,1024]{1,0:T(8,128)(2,1)S(1)}, u32[]{:S(2)}, u32[]{:S(2)}) collective-permute-start(bf16[64,1024]{1,0:T(8,128)(2,1)S(1)} %collective-permute-done.17.refs_6_), channel_id=1, source_target_pairs={{0,1},{1,0},{2,3},{3,2},{4,5},{5,4},{6,7},{7,6},{8,9},{9,8},{10,11... | collective-permute-start | bytes 393224 | tf_op jit(solution)/shard_map/ppermute | solution.py:373
  56.0 1.6 %shard_map.101 = (bf16[64,640]{1,0:T(8,128)(2,1)S(1)}, bf16[64,640]{1,0:T(8,128)(2,1)S(1)}, bf16[64,640]{1,0:T(8,128)(2,1)S(1)}, bf16[64,640]{1,0:T(8,128)(2,1)S(1)}) custom-call(s32[4]{0:T(128)S(1)} %pad_add_fusion.place, bf16[64,1024]{1,0:T(8,128)(2,1)S(1)} %shard_map.100.refs_0_, bf16[64,1024]{1,0:T(8,128)(2,1)S(1)} %collective-permute-done.12.refs_1_, ...), custom_call_target="tpu_custom_call" | custom-call | flops 671088640 | bytes 2621440 | tf_op jit(solution)/shard_map/pallas_call | solution.py:21
  57.6 3.6 %collective-permute-start.20 = (bf16[64,640]{1,0:T(8,128)(2,1)S(1)}, bf16[64,640]{1,0:T(8,128)(2,1)S(1)}, u32[]{:S(2)}, u32[]{:S(2)}) collective-permute-start(bf16[64,640]{1,0:T(8,128)(2,1)S(1)} %get-tuple-element.39), channel_id=1, source_target_pairs={{0,0},{1,4},{2,8},{3,12},{4,1},{5,5},{6,9},{7,13},{8,2},{9,6},{10,... | collective-permute-start | bytes 245768 | tf_op jit(solution)/shard_map/ppermute | solution.py:579
  61.4 3.7 %collective-permute-start.22 = (bf16[64,640]{1,0:T(8,128)(2,1)S(1)}, bf16[64,640]{1,0:T(8,128)(2,1)S(1)}, u32[]{:S(2)}, u32[]{:S(2)}) collective-permute-start(bf16[64,640]{1,0:T(8,128)(2,1)S(1)} %get-tuple-element.41), channel_id=1, source_target_pairs={{0,2},{1,6},{2,10},{3,14},{4,3},{5,7},{6,11},{7,15},{8,0},{9,4},{1... | collective-permute-start | bytes 245768 | tf_op jit(solution)/shard_map/ppermute | solution.py:579
  65.5 5.4 %collective-permute-done.22.refs_2_ = bf16[64,640]{1,0:T(8,128)(2,1)S(1)} collective-permute-done((bf16[64,640]{1,0:T(8,128)(2,1)S(1)}, bf16[64,640]{1,0:T(8,128)(2,1)S(1)}, u32[]{:S(2)}, u32[]{:S(2)}) %collective-permute-start.22) | collective-permute-done | bytes 81952 | tf_op jit(solution)/shard_map/ppermute | solution.py:579
  70.9 7.6 %collective-permute-done.23.refs_3_ = bf16[64,640]{1,0:T(8,128)(2,1)S(1)} collective-permute-done((bf16[64,640]{1,0:T(8,128)(2,1)S(1)}, bf16[64,640]{1,0:T(8,128)(2,1)S(1)}, u32[]{:S(2)}, u32[]{:S(2)}) %collective-permute-start.23) | collective-permute-done | bytes 81952 | tf_op jit(solution)/shard_map/ppermute | solution.py:579
  78.4 1.3 %shard_map.102 = bf16[64,1280]{1,0:T(8,128)(2,1)} custom-call(s32[4]{0:T(128)S(1)} %pad_add_fusion.place, bf16[64,5120]{1,0:T(8,128)(2,1)S(1)} %copy-done.2, bf16[64,640]{1,0:T(8,128)(2,1)S(1)} %collective-permute-done.20.refs_0_, bf16[64,640]{1,0:T(8,128)(2,1)S(1)} %collective-permute-done.21.refs_1_, bf16[64,640]{1,0:T(8,128)(2,1)S(1)} %collective-permute-done.22.refs_2_, ...), custom_call_target="tpu_custom_call" | custom-call | flops 327680 | bytes 983040 | tf_op jit(solution)/shard_map/pallas_call | solution.py:21
  (55 shorter events, 15.5 us)
Async XLA Ops:
  4.0 4.6 %collective-permute-start = (bf16[2,64,1280]{2,1,0:T(8,128)(2,1)S(1)}, bf16[2,64,1280]{2,1,0:T(8,128)(2,1)S(1)}, u32[]{:S(2)}, u32[]{:S(2)}) collective-permute-start(bf16[2,64,1280]{2,1,0:T(8,128)(2,1)S(1)} %get-tuple-element.27), channel_id=1, source_target_pairs={{0,1},{1,0},{2,3},{3,2},{4,5},{5,4},{6,7},{7,6},{8,9},{9,8},{10,11... | collective-permute-start | bytes 983048 | tf_op jit(solution)/shard_map/ppermute | solution.py:373
  4.1 10.7 %collective-permute-start.3 = (bf16[1280,128]{1,0:T(8,128)(2,1)S(1)}, bf16[1280,128]{1,0:T(8,128)(2,1)S(1)}, u32[]{:S(2)}, u32[]{:S(2)}) collective-permute-start(bf16[1280,128]{1,0:T(8,128)(2,1)S(1)} %get-tuple-element.24), channel_id=1, source_target_pairs={{0,2},{1,3},{2,0},{3,1},{4,6},{5,7},{6,4},{7,5},{8,10},{9,11},{10,... | collective-permute-start | bytes 983048 | tf_op jit(solution)/shard_map/ppermute | solution.py:373
  6.8 12.7 %collective-permute-start.2 = (bf16[1280,256]{1,0:T(8,128)(2,1)S(1)}, bf16[1280,256]{1,0:T(8,128)(2,1)S(1)}, u32[]{:S(2)}, u32[]{:S(2)}) collective-permute-start(bf16[1280,256]{1,0:T(8,128)(2,1)S(1)} %get-tuple-element.28.own), channel_id=1, source_target_pairs={{0,1},{1,0},{2,3},{3,2},{4,5},{5,4},{6,7},{7,6},{8,9},{9,8},{10,11... | collective-permute-start | bytes 1966088 | tf_op jit(solution)/shard_map/ppermute | solution.py:373
  14.8 4.7 %collective-permute-start.4 = (bf16[1280,128]{1,0:T(8,128)(2,1)S(1)}, bf16[1280,128]{1,0:T(8,128)(2,1)S(1)}, u32[]{:S(2)}, u32[]{:S(2)}) collective-permute-start(bf16[1280,128]{1,0:T(8,128)(2,1)S(1)} %collective-permute-done.3.refs_0_), channel_id=1, source_target_pairs={{0,1},{1,0},{2,3},{3,2},{4,5},{5,4},{6,7},{7,6},{8,9},{9,8},{10,11... | collective-permute-start | bytes 983048 | tf_op jit(solution)/shard_map/ppermute | solution.py:373
  15.4 9.4 %collective-permute-start.1 = (bf16[2,64,1280]{2,1,0:T(8,128)(2,1)S(1)}, bf16[2,64,1280]{2,1,0:T(8,128)(2,1)S(1)}, u32[]{:S(2)}, u32[]{:S(2)}) collective-permute-start(bf16[2,64,1280]{2,1,0:T(8,128)(2,1)S(1)} %shard_map.93), channel_id=1, source_target_pairs={{0,2},{1,3},{2,0},{3,1},{4,6},{5,7},{6,4},{7,5},{8,10},{9,11},{10,... | collective-permute-start | bytes 983048 | tf_op jit(solution)/shard_map/ppermute | solution.py:373
  16.9 38.1 %collective-permute-start.19 = (bf16[1024,640]{1,0:T(8,128)(2,1)S(1)}, bf16[1024,640]{1,0:T(8,128)(2,1)S(1)}, u32[]{:S(2)}, u32[]{:S(2)}) collective-permute-start(bf16[1024,640]{1,0:T(8,128)(2,1)S(1)} %shard_map.94), channel_id=1, source_target_pairs={{0,4},{4,0},{8,12},{12,8},{1,5},{5,1},{9,13},{13,9},{2,6},{6,2},{1... | collective-permute-start | bytes 3932168 | tf_op jit(solution)/shard_map/ppermute | solution.py:373
  18.2 9.9 %collective-permute-start.7 = (bf16[1280,128]{1,0:T(8,128)(2,1)S(1)}, bf16[1280,128]{1,0:T(8,128)(2,1)S(1)}, u32[]{:S(2)}, u32[]{:S(2)}) collective-permute-start(bf16[1280,128]{1,0:T(8,128)(2,1)S(1)} %collective-permute-done.3.refs_0_), channel_id=1, source_target_pairs={{0,16},{16,0},{1,17},{17,1},{2,18},{18,2},{3,19},{19,3},{4,20},{20... | collective-permute-start | bytes 983048 | tf_op jit(solution)/shard_map/ppermute | solution.py:373
  27.2 2.4 %collective-permute-start.5 = (f32[128,1024]{1,0:T(8,128)S(1)}, f32[128,1024]{1,0:T(8,128)S(1)}, u32[]{:S(2)}, u32[]{:S(2)}) collective-permute-start(f32[128,1024]{1,0:T(8,128)S(1)} %get-tuple-element.36), channel_id=1, source_target_pairs={{0,1},{1,0},{2,3},{3,2},{4,5},{5,4},{6,7},{7,6},{8,9},{9,8},{10,11... | collective-permute-start | bytes 1572872 | tf_op jit(solution)/shard_map/ppermute | solution.py:373
  28.1 3.6 %collective-permute-start.8 = (bf16[1280,128]{1,0:T(8,128)(2,1)S(1)}, bf16[1280,128]{1,0:T(8,128)(2,1)S(1)}, u32[]{:S(2)}, u32[]{:S(2)}) collective-permute-start(bf16[1280,128]{1,0:T(8,128)(2,1)S(1)} %collective-permute-done.7.refs_1_), channel_id=1, source_target_pairs={{0,1},{1,0},{2,3},{3,2},{4,5},{5,4},{6,7},{7,6},{8,9},{9,8},{10,11... | collective-permute-start | bytes 983048 | tf_op jit(solution)/shard_map/ppermute | solution.py:373
  30.2 11.8 %collective-permute-start.6 = (f32[64,1024]{1,0:T(8,128)S(1)}, f32[64,1024]{1,0:T(8,128)S(1)}, u32[]{:S(2)}, u32[]{:S(2)}) collective-permute-start(f32[64,1024]{1,0:T(8,128)S(1)} %shard_map.98), channel_id=1, source_target_pairs={{0,2},{1,3},{2,0},{3,1},{4,6},{5,7},{6,4},{7,5},{8,10},{9,11},{10,... | collective-permute-start | bytes 786440 | tf_op jit(solution)/shard_map/ppermute | solution.py:373
  32.9 7.0 %collective-permute-start.10 = (bf16[192,256]{1,0:T(8,128)(2,1)S(1)}, bf16[192,256]{1,0:T(8,128)(2,1)S(1)}, u32[]{:S(2)}, u32[]{:S(2)}) collective-permute-start(bf16[192,256]{1,0:T(8,128)(2,1)S(1)} %shard_map.99.refs_0_), channel_id=1, source_target_pairs={{0,2},{1,3},{2,0},{3,1},{4,6},{5,7},{6,4},{7,5},{8,10},{9,11},{10,... | collective-permute-start | bytes 294920 | tf_op jit(solution)/shard_map/ppermute | solution.py:373
  33.0 8.1 %collective-permute-start.9 = (bf16[192,256]{1,0:T(8,128)(2,1)S(1)}, bf16[192,256]{1,0:T(8,128)(2,1)S(1)}, u32[]{:S(2)}, u32[]{:S(2)}) collective-permute-start(bf16[192,256]{1,0:T(8,128)(2,1)S(1)} %shard_map.99.refs_0_), channel_id=1, source_target_pairs={{0,1},{1,0},{2,3},{3,2},{4,5},{5,4},{6,7},{7,6},{8,9},{9,8},{10,11... | collective-permute-start | bytes 294920 | tf_op jit(solution)/shard_map/ppermute | solution.py:373
  39.9 2.1 %collective-permute-start.11 = (bf16[192,256]{1,0:T(8,128)(2,1)S(1)}, bf16[192,256]{1,0:T(8,128)(2,1)S(1)}, u32[]{:S(2)}, u32[]{:S(2)}) collective-permute-start(bf16[192,256]{1,0:T(8,128)(2,1)S(1)} %collective-permute-done.10.refs_2_), channel_id=1, source_target_pairs={{0,1},{1,0},{2,3},{3,2},{4,5},{5,4},{6,7},{7,6},{8,9},{9,8},{10,11... | collective-permute-start | bytes 294920 | tf_op jit(solution)/shard_map/ppermute | solution.py:373
  45.0 4.8 %collective-permute-start.13 = (bf16[64,1024]{1,0:T(8,128)(2,1)S(1)}, bf16[64,1024]{1,0:T(8,128)(2,1)S(1)}, u32[]{:S(2)}, u32[]{:S(2)}) collective-permute-start(bf16[64,1024]{1,0:T(8,128)(2,1)S(1)} %shard_map.100.refs_0_), channel_id=1, source_target_pairs={{0,2},{1,3},{2,0},{3,1},{4,6},{5,7},{6,4},{7,5},{8,10},{9,11},{10,... | collective-permute-start | bytes 393224 | tf_op jit(solution)/shard_map/ppermute | solution.py:373
  46.5 4.5 %collective-permute-start.15 = (bf16[64,1024]{1,0:T(8,128)(2,1)S(1)}, bf16[64,1024]{1,0:T(8,128)(2,1)S(1)}, u32[]{:S(2)}, u32[]{:S(2)}) collective-permute-start(bf16[64,1024]{1,0:T(8,128)(2,1)S(1)} %shard_map.100.refs_0_), channel_id=1, source_target_pairs={{0,4},{1,5},{2,6},{3,7},{4,0},{5,1},{6,2},{7,3},{8,12},{9,13},{10,... | collective-permute-start | bytes 393224 | tf_op jit(solution)/shard_map/ppermute | solution.py:382
  47.8 5.8 %collective-permute-start.17 = (bf16[64,1024]{1,0:T(8,128)(2,1)S(1)}, bf16[64,1024]{1,0:T(8,128)(2,1)S(1)}, u32[]{:S(2)}, u32[]{:S(2)}) collective-permute-start(bf16[64,1024]{1,0:T(8,128)(2,1)S(1)} %shard_map.100.refs_0_), channel_id=1, source_target_pairs={{0,6},{1,7},{2,4},{3,5},{4,2},{5,3},{6,0},{7,1},{8,14},{9,15},{10,... | collective-permute-start | bytes 393224 | tf_op jit(solution)/shard_map/ppermute | solution.py:382
  47.8 7.2 %collective-permute-start.12 = (bf16[64,1024]{1,0:T(8,128)(2,1)S(1)}, bf16[64,1024]{1,0:T(8,128)(2,1)S(1)}, u32[]{:S(2)}, u32[]{:S(2)}) collective-permute-start(bf16[64,1024]{1,0:T(8,128)(2,1)S(1)} %shard_map.100.refs_0_), channel_id=1, source_target_pairs={{0,1},{1,0},{2,3},{3,2},{4,5},{5,4},{6,7},{7,6},{8,9},{9,8},{10,11... | collective-permute-start | bytes 393224 | tf_op jit(solution)/shard_map/ppermute | solution.py:373
  49.8 5.3 %collective-permute-start.14 = (bf16[64,1024]{1,0:T(8,128)(2,1)S(1)}, bf16[64,1024]{1,0:T(8,128)(2,1)S(1)}, u32[]{:S(2)}, u32[]{:S(2)}) collective-permute-start(bf16[64,1024]{1,0:T(8,128)(2,1)S(1)} %collective-permute-done.13.refs_2_), channel_id=1, source_target_pairs={{0,1},{1,0},{2,3},{3,2},{4,5},{5,4},{6,7},{7,6},{8,9},{9,8},{10,11... | collective-permute-start | bytes 393224 | tf_op jit(solution)/shard_map/ppermute | solution.py:373
  51.0 4.1 %collective-permute-start.16 = (bf16[64,1024]{1,0:T(8,128)(2,1)S(1)}, bf16[64,1024]{1,0:T(8,128)(2,1)S(1)}, u32[]{:S(2)}, u32[]{:S(2)}) collective-permute-start(bf16[64,1024]{1,0:T(8,128)(2,1)S(1)} %collective-permute-done.15.refs_4_), channel_id=1, source_target_pairs={{0,1},{1,0},{2,3},{3,2},{4,5},{5,4},{6,7},{7,6},{8,9},{9,8},{10,11... | collective-permute-start | bytes 393224 | tf_op jit(solution)/shard_map/ppermute | solution.py:373
  53.6 2.4 %collective-permute-start.18 = (bf16[64,1024]{1,0:T(8,128)(2,1)S(1)}, bf16[64,1024]{1,0:T(8,128)(2,1)S(1)}, u32[]{:S(2)}, u32[]{:S(2)}) collective-permute-start(bf16[64,1024]{1,0:T(8,128)(2,1)S(1)} %collective-permute-done.17.refs_6_), channel_id=1, source_target_pairs={{0,1},{1,0},{2,3},{3,2},{4,5},{5,4},{6,7},{7,6},{8,9},{9,8},{10,11... | collective-permute-start | bytes 393224 | tf_op jit(solution)/shard_map/ppermute | solution.py:373
  57.6 7.8 %collective-permute-start.20 = (bf16[64,640]{1,0:T(8,128)(2,1)S(1)}, bf16[64,640]{1,0:T(8,128)(2,1)S(1)}, u32[]{:S(2)}, u32[]{:S(2)}) collective-permute-start(bf16[64,640]{1,0:T(8,128)(2,1)S(1)} %get-tuple-element.39), channel_id=1, source_target_pairs={{0,0},{1,4},{2,8},{3,12},{4,1},{5,5},{6,9},{7,13},{8,2},{9,6},{10,... | collective-permute-start | bytes 245768 | tf_op jit(solution)/shard_map/ppermute | solution.py:579
  61.3 4.2 %collective-permute-start.21 = (bf16[64,640]{1,0:T(8,128)(2,1)S(1)}, bf16[64,640]{1,0:T(8,128)(2,1)S(1)}, u32[]{:S(2)}, u32[]{:S(2)}) collective-permute-start(bf16[64,640]{1,0:T(8,128)(2,1)S(1)} %get-tuple-element.40), channel_id=1, source_target_pairs={{0,1},{1,5},{2,9},{3,13},{4,0},{5,4},{6,8},{7,12},{8,3},{9,7},{10,... | collective-permute-start | bytes 245768 | tf_op jit(solution)/shard_map/ppermute | solution.py:579
  61.4 9.5 %collective-permute-start.22 = (bf16[64,640]{1,0:T(8,128)(2,1)S(1)}, bf16[64,640]{1,0:T(8,128)(2,1)S(1)}, u32[]{:S(2)}, u32[]{:S(2)}) collective-permute-start(bf16[64,640]{1,0:T(8,128)(2,1)S(1)} %get-tuple-element.41), channel_id=1, source_target_pairs={{0,2},{1,6},{2,10},{3,14},{4,3},{5,7},{6,11},{7,15},{8,0},{9,4},{1... | collective-permute-start | bytes 245768 | tf_op jit(solution)/shard_map/ppermute | solution.py:579
  65.1 13.4 %collective-permute-start.23 = (bf16[64,640]{1,0:T(8,128)(2,1)S(1)}, bf16[64,640]{1,0:T(8,128)(2,1)S(1)}, u32[]{:S(2)}, u32[]{:S(2)}) collective-permute-start(bf16[64,640]{1,0:T(8,128)(2,1)S(1)} %get-tuple-element.42), channel_id=1, source_target_pairs={{0,3},{1,7},{2,11},{3,15},{4,2},{5,6},{6,10},{7,14},{8,1},{9,5},{1... | collective-permute-start | bytes 245768 | tf_op jit(solution)/shard_map/ppermute | solution.py:579
  (9 other events, 51.7 us)

commit v9 on v8

--- a/solution.py
+++ b/solution.py
@@ -411,8 +411,7 @@
     return {**held, **{d ^ 1: swap(held[d], axis, 1) for d in sorted(held)}}
 
 
-def sum_blocks(place, keep, send, axis, count):
-    near = swap(send, axis, 1)
+def sum_over_chips(place, keep, near, axis, count):
     rows = keep.shape[0] // (count // 2)
     held = {d: add_rows(place, keep, near, d // 2 * rows, rows) for d in range(2, count, 2)}
     far = 0.0
@@ -421,7 +420,7 @@
         got = {d ^ bit: swap(held[d], axis, bit) for d in sent}
         far = far + got.pop(0)
         held = {d: held[d] + got[d] for d in got}
-    return keep, near, far
+    return far
 
 
 def table_kernel(prompt_rows, prompt_total, place, lengths, cosine, sine):
@@ -552,14 +551,15 @@
     others = both_cores(others, "sp")
 
     keep, send = query_parts(place, cont, [other] + got, query_weight)
-    mine, near, far = sum_blocks(place, keep, send, "sp", sp_count)
+    near = swap(send, "sp", 1)
     weights = [held[d] for d in range(2, sp_count) for held in (halves, others)]
     pair = keyval_rows(place, prompt, cont, cosine, sine, key_gain, near_pair, weights)
     pairs = gather_blocks(pair, "sp", sp_count)
+    far = sum_over_chips(place, keep, after(near, pair), "sp", sp_count)
     heads = attend(
         place,
         sample_lengths,
-        mine,
+        keep,
         near,
         far,
         cosine,

time: 79.9 us -> 81.5 us (1.020)
  waiting for transfers between devices: 31.5 us -> 33.2 us
    ppermute x18, waiting for transfers between devices: 18.4 us -> 20.1 us  [swap(): lax.ppermute(array, axis, [(i, i ^ bits) for i in range(lax.axis_size(axi...]
  transfers between devices with their start and end apart: 24 -> 24, of which waited for: 10 -> 10; matrix products, arithmetic and copies ran while one was open for 0% -> 0% of each run, Pallas kernels for 15% -> 14%
where the time goes in v9:
time: 81.5 us; the launch traced here: 81.4 us
  waiting for transfers between devices  33.2 us (41%)
  starting transfers between devices  29.5 us (36%)
  Pallas kernels  16.5 us (20%)
  local copies, waits for them, and re-layouts  1.92 us (2%)
    ppermute x18, starting transfers between devices, swap(): lax.ppermute(array, axis, [(i, i ^ bits) for i in range(lax.axis_size(axi...  20.4 us
    ppermute x18, waiting for transfers between devices, swap(): lax.ppermute(array, axis, [(i, i ^ bits) for i in range(lax.axis_size(axi...  20.1 us
    pallas_call x12, Pallas kernels, call(): pl.pallas_call(kernel, out_shape=out_shape, grid_spec=pltpu.PrefetchScala...  16.5 us
    ppermute x4, waiting for transfers between devices, on_device(): lax.ppermute(part, ('tp', 'sp'), [(t * sp_count + s, s * sp_count + (t ^...  13 us
    ppermute x4, starting transfers between devices, on_device(): lax.ppermute(part, ('tp', 'sp'), [(t * sp_count + s, s * sp_count + (t ^...  7.79 us
    unnamed x18, local copies, waits for them, and re-layouts  1.92 us
  transfers between devices with their start and end apart: 24, of which 10 were waited for; matrix products, arithmetic and copies ran while one was open for 0% of the time, Pallas kernels for 14%

profile of v9, /device:TPU:1, one launch (start us, length us, event | category | flops | bytes accessed | tf_op | source)
XLA Modules:
  0.0 81.4 jit_solution(8201813170926083617)
XLA Ops:
  0.1 1.7 %copy-done = bf16[1280,1024]{1,0:T(8,128)(2,1)S(1)} copy-done((bf16[1280,1024]{1,0:T(8,128)(2,1)S(1)}, bf16[1280,1024]{1,0:T(8,128)(2,1)}, u32[]{:S(2)}) %copy-start) | copy-done | bytes 2621464
  4.1 2.7 %collective-permute-start.3 = (bf16[1280,128]{1,0:T(8,128)(2,1)S(1)}, bf16[1280,128]{1,0:T(8,128)(2,1)S(1)}, u32[]{:S(2)}, u32[]{:S(2)}) collective-permute-start(bf16[1280,128]{1,0:T(8,128)(2,1)S(1)} %get-tuple-element.25), channel_id=1, source_target_pairs={{0,2},{1,3},{2,0},{3,1},{4,6},{5,7},{6,4},{7,5},{8,10},{9,11},{10,... | collective-permute-start | bytes 983048 | tf_op jit(solution)/shard_map/ppermute | solution.py:373
  7.1 1.5 %shard_map.95 = (f32[192,128]{1,0:T(8,128)S(1)}, f32[192,128]{1,0:T(8,128)S(1)}) custom-call(s32[4]{0:T(128)S(1)} %pad_add_fusion.place, s32[8]{0:T(128)S(1)} %copy-done.7), custom_call_target="tpu_custom_call" | custom-call | flops 2457600 | bytes 196608 | tf_op jit(solution)/shard_map/pallas_call | solution.py:21
  10.1 4.6 %collective-permute-done.3.refs_0_ = bf16[1280,128]{1,0:T(8,128)(2,1)S(1)} collective-permute-done((bf16[1280,128]{1,0:T(8,128)(2,1)S(1)}, bf16[1280,128]{1,0:T(8,128)(2,1)S(1)}, u32[]{:S(2)}, u32[]{:S(2)}) %collective-permute-start.3) | collective-permute-done | bytes 327712 | tf_op jit(solution)/shard_map/ppermute | solution.py:373
  15.4 1.5 %collective-permute-start.1 = (bf16[2,64,1280]{2,1,0:T(8,128)(2,1)S(1)}, bf16[2,64,1280]{2,1,0:T(8,128)(2,1)S(1)}, u32[]{:S(2)}, u32[]{:S(2)}) collective-permute-start(bf16[2,64,1280]{2,1,0:T(8,128)(2,1)S(1)} %shard_map.93), channel_id=1, source_target_pairs={{0,2},{1,3},{2,0},{3,1},{4,6},{5,7},{6,4},{7,5},{8,10},{9,11},{10,... | collective-permute-start | bytes 983048 | tf_op jit(solution)/shard_map/ppermute | solution.py:373
  16.9 1.3 %collective-permute-start.19 = (bf16[1024,640]{1,0:T(8,128)(2,1)S(1)}, bf16[1024,640]{1,0:T(8,128)(2,1)S(1)}, u32[]{:S(2)}, u32[]{:S(2)}) collective-permute-start(bf16[1024,640]{1,0:T(8,128)(2,1)S(1)} %shard_map.94), channel_id=1, source_target_pairs={{0,4},{4,0},{8,12},{12,8},{1,5},{5,1},{9,13},{13,9},{2,6},{6,2},{1... | collective-permute-start | bytes 3932168 | tf_op jit(solution)/shard_map/ppermute | solution.py:373
  18.2 1.2 %collective-permute-start.6 = (bf16[1280,128]{1,0:T(8,128)(2,1)S(1)}, bf16[1280,128]{1,0:T(8,128)(2,1)S(1)}, u32[]{:S(2)}, u32[]{:S(2)}) collective-permute-start(bf16[1280,128]{1,0:T(8,128)(2,1)S(1)} %collective-permute-done.3.refs_0_), channel_id=1, source_target_pairs={{0,16},{16,0},{1,17},{17,1},{2,18},{18,2},{3,19},{19,3},{4,20},{20... | collective-permute-start | bytes 983048 | tf_op jit(solution)/shard_map/ppermute | solution.py:373
  19.5 1.6 %shard_map.96 = (bf16[4,128,1280]{2,1,0:T(8,128)(2,1)S(1)}, f32[192,256]{1,0:T(8,128)S(1)}) custom-call(s32[4]{0:T(128)S(1)} %pad_add_fusion.place, bf16[128,5120]{1,0:T(8,128)(2,1)S(1)} %copy-done.4, f32[1,5120]{1,0:T(1,128)S(1)} %bitcast.8, bf16[4,64,1280]{2,1,0:T(8,128)(2,1)S(1)} %get-tuple-element.27.cont.refs_0_, ...), custom_call_target="tpu_custom_call" | custom-call | flops 251658240 | bytes 5242880 | tf_op jit(solution)/shard_map/pallas_call | solution.py:21
  21.1 3.7 %collective-permute-done.1.refs_2_ = bf16[2,64,1280]{2,1,0:T(8,128)(2,1)S(1)} collective-permute-done((bf16[2,64,1280]{2,1,0:T(8,128)(2,1)S(1)}, bf16[2,64,1280]{2,1,0:T(8,128)(2,1)S(1)}, u32[]{:S(2)}, u32[]{:S(2)}) %collective-permute-start.1) | collective-permute-done | bytes 327712 | tf_op jit(solution)/shard_map/ppermute | solution.py:373
  24.8 2.4 %shard_map.97 = (f32[128,1024]{1,0:T(8,128)S(1)}, f32[128,1024]{1,0:T(8,128)S(1)}) custom-call(s32[4]{0:T(128)S(1)} %pad_add_fusion.place, bf16[4,64,1280]{2,1,0:T(8,128)(2,1)S(1)} %get-tuple-element.27.cont.refs_0_, bf16[2,64,1280]{2,1,0:T(8,128)(2,1)S(1)} %collective-permute-done.other.refs_1_, bf16[2,64,1280]{2,1,0:T(8,128)(2,1)S(1)} %collective-permute-done.1.refs_2_, ...), custom_call_target="tpu_custom_call" | custom-call | flops 671088640 | bytes 2621440 | tf_op jit(solution)/shard_map/pallas_call | solution.py:21
  28.3 1.7 %collective-permute-done.7.refs_3_ = bf16[1280,128]{1,0:T(8,128)(2,1)S(1)} collective-permute-done((bf16[1280,128]{1,0:T(8,128)(2,1)S(1)}, bf16[1280,128]{1,0:T(8,128)(2,1)S(1)}, u32[]{:S(2)}, u32[]{:S(2)}) %collective-permute-start.7) | collective-permute-done | bytes 327712 | tf_op jit(solution)/shard_map/ppermute | solution.py:373
  31.8 1.5 %collective-permute-start.8 = (f32[64,1024]{1,0:T(8,128)S(1)}, f32[64,1024]{1,0:T(8,128)S(1)}, u32[]{:S(2)}, u32[]{:S(2)}) collective-permute-start(f32[64,1024]{1,0:T(8,128)S(1)} %shard_map.99), channel_id=1, source_target_pairs={{0,2},{1,3},{2,0},{3,1},{4,6},{5,7},{6,4},{7,5},{8,10},{9,11},{10,... | collective-permute-start | bytes 786440 | tf_op jit(solution)/shard_map/ppermute | solution.py:373
  34.3 7.2 %collective-permute-done.10.refs_2_ = bf16[192,256]{1,0:T(8,128)(2,1)S(1)} collective-permute-done((bf16[192,256]{1,0:T(8,128)(2,1)S(1)}, bf16[192,256]{1,0:T(8,128)(2,1)S(1)}, u32[]{:S(2)}, u32[]{:S(2)}) %collective-permute-start.10) | collective-permute-done | bytes 98336 | tf_op jit(solution)/shard_map/ppermute | solution.py:373
  43.6 3.0 %shard_map.100.refs_0_ = bf16[64,1024]{1,0:T(8,128)(2,1)S(1)} custom-call(s32[4]{0:T(128)S(1)} %pad_add_fusion.place, s32[8]{0:T(128)S(1)} %copy-done.7, f32[128,1024]{1,0:T(8,128)S(1)} %get-tuple-element.36.left.mine, f32[128,1024]{1,0:T(8,128)S(1)} %collective-permute-done.5.right.near, f32[64,1024]{1,0:T(8,128)S(1)} %collective-permute-done.8.far, ...), custom_call_target="tpu_custom_call" | custom-call | flops 201326592 | bytes 1048576 | tf_op jit(solution)/shard_map/pallas_call | solution.py:21
  46.6 1.5 %collective-permute-start.13 = (bf16[64,1024]{1,0:T(8,128)(2,1)S(1)}, bf16[64,1024]{1,0:T(8,128)(2,1)S(1)}, u32[]{:S(2)}, u32[]{:S(2)}) collective-permute-start(bf16[64,1024]{1,0:T(8,128)(2,1)S(1)} %shard_map.100.refs_0_), channel_id=1, source_target_pairs={{0,2},{1,3},{2,0},{3,1},{4,6},{5,7},{6,4},{7,5},{8,10},{9,11},{10,... | collective-permute-start | bytes 393224 | tf_op jit(solution)/shard_map/ppermute | solution.py:373
  48.2 1.3 %collective-permute-start.15 = (bf16[64,1024]{1,0:T(8,128)(2,1)S(1)}, bf16[64,1024]{1,0:T(8,128)(2,1)S(1)}, u32[]{:S(2)}, u32[]{:S(2)}) collective-permute-start(bf16[64,1024]{1,0:T(8,128)(2,1)S(1)} %shard_map.100.refs_0_), channel_id=1, source_target_pairs={{0,4},{1,5},{2,6},{3,7},{4,0},{5,1},{6,2},{7,3},{8,12},{9,13},{10,... | collective-permute-start | bytes 393224 | tf_op jit(solution)/shard_map/ppermute | solution.py:382
  52.6 2.6 %collective-permute-start.16 = (bf16[64,1024]{1,0:T(8,128)(2,1)S(1)}, bf16[64,1024]{1,0:T(8,128)(2,1)S(1)}, u32[]{:S(2)}, u32[]{:S(2)}) collective-permute-start(bf16[64,1024]{1,0:T(8,128)(2,1)S(1)} %collective-permute-done.15.refs_4_), channel_id=1, source_target_pairs={{0,1},{1,0},{2,3},{3,2},{4,5},{5,4},{6,7},{7,6},{8,9},{9,8},{10,11... | collective-permute-start | bytes 393224 | tf_op jit(solution)/shard_map/ppermute | solution.py:373
  55.3 1.4 %collective-permute-start.18 = (bf16[64,1024]{1,0:T(8,128)(2,1)S(1)}, bf16[64,1024]{1,0:T(8,128)(2,1)S(1)}, u32[]{:S(2)}, u32[]{:S(2)}) collective-permute-start(bf16[64,1024]{1,0:T(8,128)(2,1)S(1)} %collective-permute-done.17.refs_6_), channel_id=1, source_target_pairs={{0,1},{1,0},{2,3},{3,2},{4,5},{5,4},{6,7},{7,6},{8,9},{9,8},{10,11... | collective-permute-start | bytes 393224 | tf_op jit(solution)/shard_map/ppermute | solution.py:373
  57.7 1.6 %shard_map.101 = (bf16[64,640]{1,0:T(8,128)(2,1)S(1)}, bf16[64,640]{1,0:T(8,128)(2,1)S(1)}, bf16[64,640]{1,0:T(8,128)(2,1)S(1)}, bf16[64,640]{1,0:T(8,128)(2,1)S(1)}) custom-call(s32[4]{0:T(128)S(1)} %pad_add_fusion.place, bf16[64,1024]{1,0:T(8,128)(2,1)S(1)} %shard_map.100.refs_0_, bf16[64,1024]{1,0:T(8,128)(2,1)S(1)} %collective-permute-done.12.refs_1_, ...), custom_call_target="tpu_custom_call" | custom-call | flops 671088640 | bytes 2621440 | tf_op jit(solution)/shard_map/pallas_call | solution.py:21
  59.3 3.6 %collective-permute-start.20 = (bf16[64,640]{1,0:T(8,128)(2,1)S(1)}, bf16[64,640]{1,0:T(8,128)(2,1)S(1)}, u32[]{:S(2)}, u32[]{:S(2)}) collective-permute-start(bf16[64,640]{1,0:T(8,128)(2,1)S(1)} %get-tuple-element.41), channel_id=1, source_target_pairs={{0,0},{1,4},{2,8},{3,12},{4,1},{5,5},{6,9},{7,13},{8,2},{9,6},{10,... | collective-permute-start | bytes 245768 | tf_op jit(solution)/shard_map/ppermute | solution.py:579
  63.0 3.7 %collective-permute-start.22 = (bf16[64,640]{1,0:T(8,128)(2,1)S(1)}, bf16[64,640]{1,0:T(8,128)(2,1)S(1)}, u32[]{:S(2)}, u32[]{:S(2)}) collective-permute-start(bf16[64,640]{1,0:T(8,128)(2,1)S(1)} %get-tuple-element.43), channel_id=1, source_target_pairs={{0,2},{1,6},{2,10},{3,14},{4,3},{5,7},{6,11},{7,15},{8,0},{9,4},{1... | collective-permute-start | bytes 245768 | tf_op jit(solution)/shard_map/ppermute | solution.py:579
  67.1 5.4 %collective-permute-done.22.refs_2_ = bf16[64,640]{1,0:T(8,128)(2,1)S(1)} collective-permute-done((bf16[64,640]{1,0:T(8,128)(2,1)S(1)}, bf16[64,640]{1,0:T(8,128)(2,1)S(1)}, u32[]{:S(2)}, u32[]{:S(2)}) %collective-permute-start.22) | collective-permute-done | bytes 81952 | tf_op jit(solution)/shard_map/ppermute | solution.py:579
  72.5 7.6 %collective-permute-done.23.refs_3_ = bf16[64,640]{1,0:T(8,128)(2,1)S(1)} collective-permute-done((bf16[64,640]{1,0:T(8,128)(2,1)S(1)}, bf16[64,640]{1,0:T(8,128)(2,1)S(1)}, u32[]{:S(2)}, u32[]{:S(2)}) %collective-permute-start.23) | collective-permute-done | bytes 81952 | tf_op jit(solution)/shard_map/ppermute | solution.py:579
  80.1 1.3 %shard_map.102 = bf16[64,1280]{1,0:T(8,128)(2,1)} custom-call(s32[4]{0:T(128)S(1)} %pad_add_fusion.place, bf16[64,5120]{1,0:T(8,128)(2,1)S(1)} %copy-done.2, bf16[64,640]{1,0:T(8,128)(2,1)S(1)} %collective-permute-done.20.refs_0_, bf16[64,640]{1,0:T(8,128)(2,1)S(1)} %collective-permute-done.21.refs_1_, bf16[64,640]{1,0:T(8,128)(2,1)S(1)} %collective-permute-done.22.refs_2_, ...), custom_call_target="tpu_custom_call" | custom-call | flops 327680 | bytes 983040 | tf_op jit(solution)/shard_map/pallas_call | solution.py:21
  (55 shorter events, 15.4 us)
Async XLA Ops:
  4.0 4.6 %collective-permute-start = (bf16[2,64,1280]{2,1,0:T(8,128)(2,1)S(1)}, bf16[2,64,1280]{2,1,0:T(8,128)(2,1)S(1)}, u32[]{:S(2)}, u32[]{:S(2)}) collective-permute-start(bf16[2,64,1280]{2,1,0:T(8,128)(2,1)S(1)} %get-tuple-element.28), channel_id=1, source_target_pairs={{0,1},{1,0},{2,3},{3,2},{4,5},{5,4},{6,7},{7,6},{8,9},{9,8},{10,11... | collective-permute-start | bytes 983048 | tf_op jit(solution)/shard_map/ppermute | solution.py:373
  4.1 10.7 %collective-permute-start.3 = (bf16[1280,128]{1,0:T(8,128)(2,1)S(1)}, bf16[1280,128]{1,0:T(8,128)(2,1)S(1)}, u32[]{:S(2)}, u32[]{:S(2)}) collective-permute-start(bf16[1280,128]{1,0:T(8,128)(2,1)S(1)} %get-tuple-element.25), channel_id=1, source_target_pairs={{0,2},{1,3},{2,0},{3,1},{4,6},{5,7},{6,4},{7,5},{8,10},{9,11},{10,... | collective-permute-start | bytes 983048 | tf_op jit(solution)/shard_map/ppermute | solution.py:373
  6.8 12.7 %collective-permute-start.2 = (bf16[1280,256]{1,0:T(8,128)(2,1)S(1)}, bf16[1280,256]{1,0:T(8,128)(2,1)S(1)}, u32[]{:S(2)}, u32[]{:S(2)}) collective-permute-start(bf16[1280,256]{1,0:T(8,128)(2,1)S(1)} %get-tuple-element.29.own), channel_id=1, source_target_pairs={{0,1},{1,0},{2,3},{3,2},{4,5},{5,4},{6,7},{7,6},{8,9},{9,8},{10,11... | collective-permute-start | bytes 1966088 | tf_op jit(solution)/shard_map/ppermute | solution.py:373
  14.8 4.7 %collective-permute-start.4 = (bf16[1280,128]{1,0:T(8,128)(2,1)S(1)}, bf16[1280,128]{1,0:T(8,128)(2,1)S(1)}, u32[]{:S(2)}, u32[]{:S(2)}) collective-permute-start(bf16[1280,128]{1,0:T(8,128)(2,1)S(1)} %collective-permute-done.3.refs_0_), channel_id=1, source_target_pairs={{0,1},{1,0},{2,3},{3,2},{4,5},{5,4},{6,7},{7,6},{8,9},{9,8},{10,11... | collective-permute-start | bytes 983048 | tf_op jit(solution)/shard_map/ppermute | solution.py:373
  15.4 9.4 %collective-permute-start.1 = (bf16[2,64,1280]{2,1,0:T(8,128)(2,1)S(1)}, bf16[2,64,1280]{2,1,0:T(8,128)(2,1)S(1)}, u32[]{:S(2)}, u32[]{:S(2)}) collective-permute-start(bf16[2,64,1280]{2,1,0:T(8,128)(2,1)S(1)} %shard_map.93), channel_id=1, source_target_pairs={{0,2},{1,3},{2,0},{3,1},{4,6},{5,7},{6,4},{7,5},{8,10},{9,11},{10,... | collective-permute-start | bytes 983048 | tf_op jit(solution)/shard_map/ppermute | solution.py:373
  16.9 39.8 %collective-permute-start.19 = (bf16[1024,640]{1,0:T(8,128)(2,1)S(1)}, bf16[1024,640]{1,0:T(8,128)(2,1)S(1)}, u32[]{:S(2)}, u32[]{:S(2)}) collective-permute-start(bf16[1024,640]{1,0:T(8,128)(2,1)S(1)} %shard_map.94), channel_id=1, source_target_pairs={{0,4},{4,0},{8,12},{12,8},{1,5},{5,1},{9,13},{13,9},{2,6},{6,2},{1... | collective-permute-start | bytes 3932168 | tf_op jit(solution)/shard_map/ppermute | solution.py:373
  18.2 9.8 %collective-permute-start.6 = (bf16[1280,128]{1,0:T(8,128)(2,1)S(1)}, bf16[1280,128]{1,0:T(8,128)(2,1)S(1)}, u32[]{:S(2)}, u32[]{:S(2)}) collective-permute-start(bf16[1280,128]{1,0:T(8,128)(2,1)S(1)} %collective-permute-done.3.refs_0_), channel_id=1, source_target_pairs={{0,16},{16,0},{1,17},{17,1},{2,18},{18,2},{3,19},{19,3},{4,20},{20... | collective-permute-start | bytes 983048 | tf_op jit(solution)/shard_map/ppermute | solution.py:373
  27.2 4.0 %collective-permute-start.5 = (f32[128,1024]{1,0:T(8,128)S(1)}, f32[128,1024]{1,0:T(8,128)S(1)}, u32[]{:S(2)}, u32[]{:S(2)}) collective-permute-start(f32[128,1024]{1,0:T(8,128)S(1)} %get-tuple-element.37), channel_id=1, source_target_pairs={{0,1},{1,0},{2,3},{3,2},{4,5},{5,4},{6,7},{7,6},{8,9},{9,8},{10,11... | collective-permute-start | bytes 1572872 | tf_op jit(solution)/shard_map/ppermute | solution.py:373
  28.1 2.0 %collective-permute-start.7 = (bf16[1280,128]{1,0:T(8,128)(2,1)S(1)}, bf16[1280,128]{1,0:T(8,128)(2,1)S(1)}, u32[]{:S(2)}, u32[]{:S(2)}) collective-permute-start(bf16[1280,128]{1,0:T(8,128)(2,1)S(1)} %collective-permute-done.6.refs_1_), channel_id=1, source_target_pairs={{0,1},{1,0},{2,3},{3,2},{4,5},{5,4},{6,7},{7,6},{8,9},{9,8},{10,11... | collective-permute-start | bytes 983048 | tf_op jit(solution)/shard_map/ppermute | solution.py:373
  31.8 11.8 %collective-permute-start.8 = (f32[64,1024]{1,0:T(8,128)S(1)}, f32[64,1024]{1,0:T(8,128)S(1)}, u32[]{:S(2)}, u32[]{:S(2)}) collective-permute-start(f32[64,1024]{1,0:T(8,128)S(1)} %shard_map.99), channel_id=1, source_target_pairs={{0,2},{1,3},{2,0},{3,1},{4,6},{5,7},{6,4},{7,5},{8,10},{9,11},{10,... | collective-permute-start | bytes 786440 | tf_op jit(solution)/shard_map/ppermute | solution.py:373
  33.3 8.2 %collective-permute-start.10 = (bf16[192,256]{1,0:T(8,128)(2,1)S(1)}, bf16[192,256]{1,0:T(8,128)(2,1)S(1)}, u32[]{:S(2)}, u32[]{:S(2)}) collective-permute-start(bf16[192,256]{1,0:T(8,128)(2,1)S(1)} %shard_map.98.refs_0_), channel_id=1, source_target_pairs={{0,2},{1,3},{2,0},{3,1},{4,6},{5,7},{6,4},{7,5},{8,10},{9,11},{10,... | collective-permute-start | bytes 294920 | tf_op jit(solution)/shard_map/ppermute | solution.py:373
  33.4 9.3 %collective-permute-start.9 = (bf16[192,256]{1,0:T(8,128)(2,1)S(1)}, bf16[192,256]{1,0:T(8,128)(2,1)S(1)}, u32[]{:S(2)}, u32[]{:S(2)}) collective-permute-start(bf16[192,256]{1,0:T(8,128)(2,1)S(1)} %shard_map.98.refs_0_), channel_id=1, source_target_pairs={{0,1},{1,0},{2,3},{3,2},{4,5},{5,4},{6,7},{7,6},{8,9},{9,8},{10,11... | collective-permute-start | bytes 294920 | tf_op jit(solution)/shard_map/ppermute | solution.py:373
  41.5 2.2 %collective-permute-start.11 = (bf16[192,256]{1,0:T(8,128)(2,1)S(1)}, bf16[192,256]{1,0:T(8,128)(2,1)S(1)}, u32[]{:S(2)}, u32[]{:S(2)}) collective-permute-start(bf16[192,256]{1,0:T(8,128)(2,1)S(1)} %collective-permute-done.10.refs_2_), channel_id=1, source_target_pairs={{0,1},{1,0},{2,3},{3,2},{4,5},{5,4},{6,7},{7,6},{8,9},{9,8},{10,11... | collective-permute-start | bytes 294920 | tf_op jit(solution)/shard_map/ppermute | solution.py:373
  46.6 4.8 %collective-permute-start.13 = (bf16[64,1024]{1,0:T(8,128)(2,1)S(1)}, bf16[64,1024]{1,0:T(8,128)(2,1)S(1)}, u32[]{:S(2)}, u32[]{:S(2)}) collective-permute-start(bf16[64,1024]{1,0:T(8,128)(2,1)S(1)} %shard_map.100.refs_0_), channel_id=1, source_target_pairs={{0,2},{1,3},{2,0},{3,1},{4,6},{5,7},{6,4},{7,5},{8,10},{9,11},{10,... | collective-permute-start | bytes 393224 | tf_op jit(solution)/shard_map/ppermute | solution.py:373
  48.2 4.5 %collective-permute-start.15 = (bf16[64,1024]{1,0:T(8,128)(2,1)S(1)}, bf16[64,1024]{1,0:T(8,128)(2,1)S(1)}, u32[]{:S(2)}, u32[]{:S(2)}) collective-permute-start(bf16[64,1024]{1,0:T(8,128)(2,1)S(1)} %shard_map.100.refs_0_), channel_id=1, source_target_pairs={{0,4},{1,5},{2,6},{3,7},{4,0},{5,1},{6,2},{7,3},{8,12},{9,13},{10,... | collective-permute-start | bytes 393224 | tf_op jit(solution)/shard_map/ppermute | solution.py:382
  49.5 5.8 %collective-permute-start.17 = (bf16[64,1024]{1,0:T(8,128)(2,1)S(1)}, bf16[64,1024]{1,0:T(8,128)(2,1)S(1)}, u32[]{:S(2)}, u32[]{:S(2)}) collective-permute-start(bf16[64,1024]{1,0:T(8,128)(2,1)S(1)} %shard_map.100.refs_0_), channel_id=1, source_target_pairs={{0,6},{1,7},{2,4},{3,5},{4,2},{5,3},{6,0},{7,1},{8,14},{9,15},{10,... | collective-permute-start | bytes 393224 | tf_op jit(solution)/shard_map/ppermute | solution.py:382
  49.5 7.2 %collective-permute-start.12 = (bf16[64,1024]{1,0:T(8,128)(2,1)S(1)}, bf16[64,1024]{1,0:T(8,128)(2,1)S(1)}, u32[]{:S(2)}, u32[]{:S(2)}) collective-permute-start(bf16[64,1024]{1,0:T(8,128)(2,1)S(1)} %shard_map.100.refs_0_), channel_id=1, source_target_pairs={{0,1},{1,0},{2,3},{3,2},{4,5},{5,4},{6,7},{7,6},{8,9},{9,8},{10,11... | collective-permute-start | bytes 393224 | tf_op jit(solution)/shard_map/ppermute | solution.py:373
  51.4 5.3 %collective-permute-start.14 = (bf16[64,1024]{1,0:T(8,128)(2,1)S(1)}, bf16[64,1024]{1,0:T(8,128)(2,1)S(1)}, u32[]{:S(2)}, u32[]{:S(2)}) collective-permute-start(bf16[64,1024]{1,0:T(8,128)(2,1)S(1)} %collective-permute-done.13.refs_2_), channel_id=1, source_target_pairs={{0,1},{1,0},{2,3},{3,2},{4,5},{5,4},{6,7},{7,6},{8,9},{9,8},{10,11... | collective-permute-start | bytes 393224 | tf_op jit(solution)/shard_map/ppermute | solution.py:373
  52.6 4.1 %collective-permute-start.16 = (bf16[64,1024]{1,0:T(8,128)(2,1)S(1)}, bf16[64,1024]{1,0:T(8,128)(2,1)S(1)}, u32[]{:S(2)}, u32[]{:S(2)}) collective-permute-start(bf16[64,1024]{1,0:T(8,128)(2,1)S(1)} %collective-permute-done.15.refs_4_), channel_id=1, source_target_pairs={{0,1},{1,0},{2,3},{3,2},{4,5},{5,4},{6,7},{7,6},{8,9},{9,8},{10,11... | collective-permute-start | bytes 393224 | tf_op jit(solution)/shard_map/ppermute | solution.py:373
  55.3 2.4 %collective-permute-start.18 = (bf16[64,1024]{1,0:T(8,128)(2,1)S(1)}, bf16[64,1024]{1,0:T(8,128)(2,1)S(1)}, u32[]{:S(2)}, u32[]{:S(2)}) collective-permute-start(bf16[64,1024]{1,0:T(8,128)(2,1)S(1)} %collective-permute-done.17.refs_6_), channel_id=1, source_target_pairs={{0,1},{1,0},{2,3},{3,2},{4,5},{5,4},{6,7},{7,6},{8,9},{9,8},{10,11... | collective-permute-start | bytes 393224 | tf_op jit(solution)/shard_map/ppermute | solution.py:373
  59.3 7.8 %collective-permute-start.20 = (bf16[64,640]{1,0:T(8,128)(2,1)S(1)}, bf16[64,640]{1,0:T(8,128)(2,1)S(1)}, u32[]{:S(2)}, u32[]{:S(2)}) collective-permute-start(bf16[64,640]{1,0:T(8,128)(2,1)S(1)} %get-tuple-element.41), channel_id=1, source_target_pairs={{0,0},{1,4},{2,8},{3,12},{4,1},{5,5},{6,9},{7,13},{8,2},{9,6},{10,... | collective-permute-start | bytes 245768 | tf_op jit(solution)/shard_map/ppermute | solution.py:579
  62.9 4.2 %collective-permute-start.21 = (bf16[64,640]{1,0:T(8,128)(2,1)S(1)}, bf16[64,640]{1,0:T(8,128)(2,1)S(1)}, u32[]{:S(2)}, u32[]{:S(2)}) collective-permute-start(bf16[64,640]{1,0:T(8,128)(2,1)S(1)} %get-tuple-element.42), channel_id=1, source_target_pairs={{0,1},{1,5},{2,9},{3,13},{4,0},{5,4},{6,8},{7,12},{8,3},{9,7},{10,... | collective-permute-start | bytes 245768 | tf_op jit(solution)/shard_map/ppermute | solution.py:579
  63.0 9.5 %collective-permute-start.22 = (bf16[64,640]{1,0:T(8,128)(2,1)S(1)}, bf16[64,640]{1,0:T(8,128)(2,1)S(1)}, u32[]{:S(2)}, u32[]{:S(2)}) collective-permute-start(bf16[64,640]{1,0:T(8,128)(2,1)S(1)} %get-tuple-element.43), channel_id=1, source_target_pairs={{0,2},{1,6},{2,10},{3,14},{4,3},{5,7},{6,11},{7,15},{8,0},{9,4},{1... | collective-permute-start | bytes 245768 | tf_op jit(solution)/shard_map/ppermute | solution.py:579
  66.7 13.4 %collective-permute-start.23 = (bf16[64,640]{1,0:T(8,128)(2,1)S(1)}, bf16[64,640]{1,0:T(8,128)(2,1)S(1)}, u32[]{:S(2)}, u32[]{:S(2)}) collective-permute-start(bf16[64,640]{1,0:T(8,128)(2,1)S(1)} %get-tuple-element.44), channel_id=1, source_target_pairs={{0,3},{1,7},{2,11},{3,15},{4,2},{5,6},{6,10},{7,14},{8,1},{9,5},{1... | collective-permute-start | bytes 245768 | tf_op jit(solution)/shard_map/ppermute | solution.py:579
  (9 other events, 54.6 us)

commit v10 on v8

--- a/solution.py
+++ b/solution.py
@@ -142,15 +142,14 @@
 def query_parts(place, cont, got, weight):
     count, block, depth = cont.shape
     width = weight.shape[1]
-    step = min(width, 256)
     half = count // 2 * block
     return call(
         functools.partial(query_kernel, count),
         place,
-        (width // step,),
+        (1,),
         [whole(a) for a in (cont, *got)]
-        + [pl.BlockSpec((depth, step), lambda i, place: (0, i))],
-        [pl.BlockSpec((half, step), lambda i, place: (0, i))] * 2,
+        + [whole(weight)],
+        [pl.BlockSpec((half, width), lambda i, place: (0, 0))] * 2,
         [shape_of((half, width), F32)] * 2,
         (cont, *got, weight),
         (2 * count * block * depth * width, 2 * depth * width),

time: 79.9 us -> 78.9 us (0.987)
  Pallas kernels: 16.5 us -> 15.5 us
  starting transfers between devices: 29.5 us -> 30.5 us
  waiting for transfers between devices: 31.5 us -> 30.5 us
    ppermute x18, waiting for transfers between devices: 18.4 us -> 17.4 us  [swap(): lax.ppermute(array, axis, [(i, i ^ bits) for i in range(lax.axis_size(axi...]
    pallas_call x12, Pallas kernels: 16.5 us -> 15.5 us  [call(): pl.pallas_call(kernel, out_shape=out_shape, grid_spec=pltpu.PrefetchScala...]
    ppermute x18, starting transfers between devices: 20.4 us -> 21.4 us  [swap(): lax.ppermute(array, axis, [(i, i ^ bits) for i in range(lax.axis_size(axi...]
  transfers between devices with their start and end apart: 24 -> 24, of which waited for: 10 -> 10; matrix products, arithmetic and copies ran while one was open for 0% -> 0% of each run, Pallas kernels for 15% -> 14%
where the time goes in v10:
time: 78.9 us; the launch traced here: 78.7 us
  starting transfers between devices  30.5 us (39%)
  waiting for transfers between devices  30.5 us (39%)
  Pallas kernels  15.5 us (20%)
  local copies, waits for them, and re-layouts  1.92 us (2%)
    ppermute x18, starting transfers between devices, swap(): lax.ppermute(array, axis, [(i, i ^ bits) for i in range(lax.axis_size(axi...  21.4 us
    ppermute x18, waiting for transfers between devices, swap(): lax.ppermute(array, axis, [(i, i ^ bits) for i in range(lax.axis_size(axi...  17.4 us
    pallas_call x12, Pallas kernels, call(): pl.pallas_call(kernel, out_shape=out_shape, grid_spec=pltpu.PrefetchScala...  15.5 us
    ppermute x4, waiting for transfers between devices, on_device(): lax.ppermute(part, ('tp', 'sp'), [(t * sp_count + s, s * sp_count + (t ^...  13 us
    ppermute x4, starting transfers between devices, on_device(): lax.ppermute(part, ('tp', 'sp'), [(t * sp_count + s, s * sp_count + (t ^...  7.8 us
    unnamed x18, local copies, waits for them, and re-layouts  1.92 us
  transfers between devices with their start and end apart: 24, of which 10 were waited for; matrix products, arithmetic and copies ran while one was open for 0% of the time, Pallas kernels for 14%

profile of v10, /device:TPU:1, one launch (start us, length us, event | category | flops | bytes accessed | tf_op | source)
XLA Modules:
  0.0 78.7 jit_solution(7651961690122725120)
XLA Ops:
  0.1 1.7 %copy-done = bf16[1280,1024]{1,0:T(8,128)(2,1)S(1)} copy-done((bf16[1280,1024]{1,0:T(8,128)(2,1)S(1)}, bf16[1280,1024]{1,0:T(8,128)(2,1)}, u32[]{:S(2)}) %copy-start) | copy-done | bytes 2621464
  4.1 2.7 %collective-permute-start.3 = (bf16[1280,128]{1,0:T(8,128)(2,1)S(1)}, bf16[1280,128]{1,0:T(8,128)(2,1)S(1)}, u32[]{:S(2)}, u32[]{:S(2)}) collective-permute-start(bf16[1280,128]{1,0:T(8,128)(2,1)S(1)} %get-tuple-element.24), channel_id=1, source_target_pairs={{0,2},{1,3},{2,0},{3,1},{4,6},{5,7},{6,4},{7,5},{8,10},{9,11},{10,... | collective-permute-start | bytes 983048 | tf_op jit(solution)/shard_map/ppermute | solution.py:372
  7.1 1.5 %shard_map.95 = (f32[192,128]{1,0:T(8,128)S(1)}, f32[192,128]{1,0:T(8,128)S(1)}) custom-call(s32[4]{0:T(128)S(1)} %pad_add_fusion.place, s32[8]{0:T(128)S(1)} %copy-done.7), custom_call_target="tpu_custom_call" | custom-call | flops 2457600 | bytes 196608 | tf_op jit(solution)/shard_map/pallas_call | solution.py:21
  10.1 4.6 %collective-permute-done.3.refs_0_ = bf16[1280,128]{1,0:T(8,128)(2,1)S(1)} collective-permute-done((bf16[1280,128]{1,0:T(8,128)(2,1)S(1)}, bf16[1280,128]{1,0:T(8,128)(2,1)S(1)}, u32[]{:S(2)}, u32[]{:S(2)}) %collective-permute-start.3) | collective-permute-done | bytes 327712 | tf_op jit(solution)/shard_map/ppermute | solution.py:372
  15.4 1.5 %collective-permute-start.1 = (bf16[2,64,1280]{2,1,0:T(8,128)(2,1)S(1)}, bf16[2,64,1280]{2,1,0:T(8,128)(2,1)S(1)}, u32[]{:S(2)}, u32[]{:S(2)}) collective-permute-start(bf16[2,64,1280]{2,1,0:T(8,128)(2,1)S(1)} %shard_map.93), channel_id=1, source_target_pairs={{0,2},{1,3},{2,0},{3,1},{4,6},{5,7},{6,4},{7,5},{8,10},{9,11},{10,... | collective-permute-start | bytes 983048 | tf_op jit(solution)/shard_map/ppermute | solution.py:372
  16.9 1.3 %collective-permute-start.19 = (bf16[1024,640]{1,0:T(8,128)(2,1)S(1)}, bf16[1024,640]{1,0:T(8,128)(2,1)S(1)}, u32[]{:S(2)}, u32[]{:S(2)}) collective-permute-start(bf16[1024,640]{1,0:T(8,128)(2,1)S(1)} %shard_map.94), channel_id=1, source_target_pairs={{0,4},{4,0},{8,12},{12,8},{1,5},{5,1},{9,13},{13,9},{2,6},{6,2},{1... | collective-permute-start | bytes 3932168 | tf_op jit(solution)/shard_map/ppermute | solution.py:372
  18.2 1.2 %collective-permute-start.7 = (bf16[1280,128]{1,0:T(8,128)(2,1)S(1)}, bf16[1280,128]{1,0:T(8,128)(2,1)S(1)}, u32[]{:S(2)}, u32[]{:S(2)}) collective-permute-start(bf16[1280,128]{1,0:T(8,128)(2,1)S(1)} %collective-permute-done.3.refs_0_), channel_id=1, source_target_pairs={{0,16},{16,0},{1,17},{17,1},{2,18},{18,2},{3,19},{19,3},{4,20},{20... | collective-permute-start | bytes 983048 | tf_op jit(solution)/shard_map/ppermute | solution.py:372
  19.5 1.6 %shard_map.96 = (bf16[4,128,1280]{2,1,0:T(8,128)(2,1)S(1)}, f32[192,256]{1,0:T(8,128)S(1)}) custom-call(s32[4]{0:T(128)S(1)} %pad_add_fusion.place, bf16[128,5120]{1,0:T(8,128)(2,1)S(1)} %copy-done.4, f32[1,5120]{1,0:T(1,128)S(1)} %bitcast.8, bf16[4,64,1280]{2,1,0:T(8,128)(2,1)S(1)} %get-tuple-element.26.cont.refs_0_, ...), custom_call_target="tpu_custom_call" | custom-call | flops 251658240 | bytes 5242880 | tf_op jit(solution)/shard_map/pallas_call | solution.py:21
  21.1 3.7 %collective-permute-done.1.refs_2_ = bf16[2,64,1280]{2,1,0:T(8,128)(2,1)S(1)} collective-permute-done((bf16[2,64,1280]{2,1,0:T(8,128)(2,1)S(1)}, bf16[2,64,1280]{2,1,0:T(8,128)(2,1)S(1)}, u32[]{:S(2)}, u32[]{:S(2)}) %collective-permute-start.1) | collective-permute-done | bytes 327712 | tf_op jit(solution)/shard_map/ppermute | solution.py:372
  24.8 1.4 %shard_map.97 = (f32[128,1024]{1,0:T(8,128)S(1)}, f32[128,1024]{1,0:T(8,128)S(1)}) custom-call(s32[4]{0:T(128)S(1)} %pad_add_fusion.place, bf16[4,64,1280]{2,1,0:T(8,128)(2,1)S(1)} %get-tuple-element.26.cont.refs_0_, bf16[2,64,1280]{2,1,0:T(8,128)(2,1)S(1)} %collective-permute-done.other.refs_1_, bf16[2,64,1280]{2,1,0:T(8,128)(2,1)S(1)} %collective-permute-done.1.refs_2_, ...), custom_call_target="tpu_custom_call" | custom-call | flops 671088640 | bytes 2621440 | tf_op jit(solution)/shard_map/pallas_call | solution.py:21
  27.1 1.3 %collective-permute-start.8 = (bf16[1280,128]{1,0:T(8,128)(2,1)S(1)}, bf16[1280,128]{1,0:T(8,128)(2,1)S(1)}, u32[]{:S(2)}, u32[]{:S(2)}) collective-permute-start(bf16[1280,128]{1,0:T(8,128)(2,1)S(1)} %collective-permute-done.7.refs_1_), channel_id=1, source_target_pairs={{0,1},{1,0},{2,3},{3,2},{4,5},{5,4},{6,7},{7,6},{8,9},{9,8},{10,11... | collective-permute-start | bytes 983048 | tf_op jit(solution)/shard_map/ppermute | solution.py:372
  29.2 1.5 %collective-permute-start.6 = (f32[64,1024]{1,0:T(8,128)S(1)}, f32[64,1024]{1,0:T(8,128)S(1)}, u32[]{:S(2)}, u32[]{:S(2)}) collective-permute-start(f32[64,1024]{1,0:T(8,128)S(1)} %shard_map.98), channel_id=1, source_target_pairs={{0,2},{1,3},{2,0},{3,1},{4,6},{5,7},{6,4},{7,5},{8,10},{9,11},{10,... | collective-permute-start | bytes 786440 | tf_op jit(solution)/shard_map/ppermute | solution.py:372
  32.9 6.0 %collective-permute-done.10.refs_2_ = bf16[192,256]{1,0:T(8,128)(2,1)S(1)} collective-permute-done((bf16[192,256]{1,0:T(8,128)(2,1)S(1)}, bf16[192,256]{1,0:T(8,128)(2,1)S(1)}, u32[]{:S(2)}, u32[]{:S(2)}) %collective-permute-start.10) | collective-permute-done | bytes 98336 | tf_op jit(solution)/shard_map/ppermute | solution.py:372
  41.0 3.0 %shard_map.100.refs_0_ = bf16[64,1024]{1,0:T(8,128)(2,1)S(1)} custom-call(s32[4]{0:T(128)S(1)} %pad_add_fusion.place, s32[8]{0:T(128)S(1)} %copy-done.7, f32[128,1024]{1,0:T(8,128)S(1)} %get-tuple-element.35.left.mine, f32[128,1024]{1,0:T(8,128)S(1)} %collective-permute-done.5.right.near, f32[64,1024]{1,0:T(8,128)S(1)} %collective-permute-done.6.far, ...), custom_call_target="tpu_custom_call" | custom-call | flops 201326592 | bytes 1048576 | tf_op jit(solution)/shard_map/pallas_call | solution.py:21
  44.0 1.5 %collective-permute-start.13 = (bf16[64,1024]{1,0:T(8,128)(2,1)S(1)}, bf16[64,1024]{1,0:T(8,128)(2,1)S(1)}, u32[]{:S(2)}, u32[]{:S(2)}) collective-permute-start(bf16[64,1024]{1,0:T(8,128)(2,1)S(1)} %shard_map.100.refs_0_), channel_id=1, source_target_pairs={{0,2},{1,3},{2,0},{3,1},{4,6},{5,7},{6,4},{7,5},{8,10},{9,11},{10,... | collective-permute-start | bytes 393224 | tf_op jit(solution)/shard_map/ppermute | solution.py:372
  45.5 1.3 %collective-permute-start.15 = (bf16[64,1024]{1,0:T(8,128)(2,1)S(1)}, bf16[64,1024]{1,0:T(8,128)(2,1)S(1)}, u32[]{:S(2)}, u32[]{:S(2)}) collective-permute-start(bf16[64,1024]{1,0:T(8,128)(2,1)S(1)} %shard_map.100.refs_0_), channel_id=1, source_target_pairs={{0,4},{1,5},{2,6},{3,7},{4,0},{5,1},{6,2},{7,3},{8,12},{9,13},{10,... | collective-permute-start | bytes 393224 | tf_op jit(solution)/shard_map/ppermute | solution.py:381
  50.0 2.5 %collective-permute-start.16 = (bf16[64,1024]{1,0:T(8,128)(2,1)S(1)}, bf16[64,1024]{1,0:T(8,128)(2,1)S(1)}, u32[]{:S(2)}, u32[]{:S(2)}) collective-permute-start(bf16[64,1024]{1,0:T(8,128)(2,1)S(1)} %collective-permute-done.15.refs_4_), channel_id=1, source_target_pairs={{0,1},{1,0},{2,3},{3,2},{4,5},{5,4},{6,7},{7,6},{8,9},{9,8},{10,11... | collective-permute-start | bytes 393224 | tf_op jit(solution)/shard_map/ppermute | solution.py:372
  52.6 1.4 %collective-permute-start.18 = (bf16[64,1024]{1,0:T(8,128)(2,1)S(1)}, bf16[64,1024]{1,0:T(8,128)(2,1)S(1)}, u32[]{:S(2)}, u32[]{:S(2)}) collective-permute-start(bf16[64,1024]{1,0:T(8,128)(2,1)S(1)} %collective-permute-done.17.refs_6_), channel_id=1, source_target_pairs={{0,1},{1,0},{2,3},{3,2},{4,5},{5,4},{6,7},{7,6},{8,9},{9,8},{10,11... | collective-permute-start | bytes 393224 | tf_op jit(solution)/shard_map/ppermute | solution.py:372
  55.0 1.6 %shard_map.101 = (bf16[64,640]{1,0:T(8,128)(2,1)S(1)}, bf16[64,640]{1,0:T(8,128)(2,1)S(1)}, bf16[64,640]{1,0:T(8,128)(2,1)S(1)}, bf16[64,640]{1,0:T(8,128)(2,1)S(1)}) custom-call(s32[4]{0:T(128)S(1)} %pad_add_fusion.place, bf16[64,1024]{1,0:T(8,128)(2,1)S(1)} %shard_map.100.refs_0_, bf16[64,1024]{1,0:T(8,128)(2,1)S(1)} %collective-permute-done.12.refs_1_, ...), custom_call_target="tpu_custom_call" | custom-call | flops 671088640 | bytes 2621440 | tf_op jit(solution)/shard_map/pallas_call | solution.py:21
  56.6 3.6 %collective-permute-start.20 = (bf16[64,640]{1,0:T(8,128)(2,1)S(1)}, bf16[64,640]{1,0:T(8,128)(2,1)S(1)}, u32[]{:S(2)}, u32[]{:S(2)}) collective-permute-start(bf16[64,640]{1,0:T(8,128)(2,1)S(1)} %get-tuple-element.39), channel_id=1, source_target_pairs={{0,0},{1,4},{2,8},{3,12},{4,1},{5,5},{6,9},{7,13},{8,2},{9,6},{10,... | collective-permute-start | bytes 245768 | tf_op jit(solution)/shard_map/ppermute | solution.py:578
  60.3 3.7 %collective-permute-start.22 = (bf16[64,640]{1,0:T(8,128)(2,1)S(1)}, bf16[64,640]{1,0:T(8,128)(2,1)S(1)}, u32[]{:S(2)}, u32[]{:S(2)}) collective-permute-start(bf16[64,640]{1,0:T(8,128)(2,1)S(1)} %get-tuple-element.41), channel_id=1, source_target_pairs={{0,2},{1,6},{2,10},{3,14},{4,3},{5,7},{6,11},{7,15},{8,0},{9,4},{1... | collective-permute-start | bytes 245768 | tf_op jit(solution)/shard_map/ppermute | solution.py:578
  64.4 5.4 %collective-permute-done.22.refs_2_ = bf16[64,640]{1,0:T(8,128)(2,1)S(1)} collective-permute-done((bf16[64,640]{1,0:T(8,128)(2,1)S(1)}, bf16[64,640]{1,0:T(8,128)(2,1)S(1)}, u32[]{:S(2)}, u32[]{:S(2)}) %collective-permute-start.22) | collective-permute-done | bytes 81952 | tf_op jit(solution)/shard_map/ppermute | solution.py:578
  69.8 7.6 %collective-permute-done.23.refs_3_ = bf16[64,640]{1,0:T(8,128)(2,1)S(1)} collective-permute-done((bf16[64,640]{1,0:T(8,128)(2,1)S(1)}, bf16[64,640]{1,0:T(8,128)(2,1)S(1)}, u32[]{:S(2)}, u32[]{:S(2)}) %collective-permute-start.23) | collective-permute-done | bytes 81952 | tf_op jit(solution)/shard_map/ppermute | solution.py:578
  77.4 1.3 %shard_map.102 = bf16[64,1280]{1,0:T(8,128)(2,1)} custom-call(s32[4]{0:T(128)S(1)} %pad_add_fusion.place, bf16[64,5120]{1,0:T(8,128)(2,1)S(1)} %copy-done.2, bf16[64,640]{1,0:T(8,128)(2,1)S(1)} %collective-permute-done.20.refs_0_, bf16[64,640]{1,0:T(8,128)(2,1)S(1)} %collective-permute-done.21.refs_1_, bf16[64,640]{1,0:T(8,128)(2,1)S(1)} %collective-permute-done.22.refs_2_, ...), custom_call_target="tpu_custom_call" | custom-call | flops 327680 | bytes 983040 | tf_op jit(solution)/shard_map/pallas_call | solution.py:21
  (55 shorter events, 15.5 us)
Async XLA Ops:
  4.0 4.6 %collective-permute-start = (bf16[2,64,1280]{2,1,0:T(8,128)(2,1)S(1)}, bf16[2,64,1280]{2,1,0:T(8,128)(2,1)S(1)}, u32[]{:S(2)}, u32[]{:S(2)}) collective-permute-start(bf16[2,64,1280]{2,1,0:T(8,128)(2,1)S(1)} %get-tuple-element.27), channel_id=1, source_target_pairs={{0,1},{1,0},{2,3},{3,2},{4,5},{5,4},{6,7},{7,6},{8,9},{9,8},{10,11... | collective-permute-start | bytes 983048 | tf_op jit(solution)/shard_map/ppermute | solution.py:372
  4.1 10.7 %collective-permute-start.3 = (bf16[1280,128]{1,0:T(8,128)(2,1)S(1)}, bf16[1280,128]{1,0:T(8,128)(2,1)S(1)}, u32[]{:S(2)}, u32[]{:S(2)}) collective-permute-start(bf16[1280,128]{1,0:T(8,128)(2,1)S(1)} %get-tuple-element.24), channel_id=1, source_target_pairs={{0,2},{1,3},{2,0},{3,1},{4,6},{5,7},{6,4},{7,5},{8,10},{9,11},{10,... | collective-permute-start | bytes 983048 | tf_op jit(solution)/shard_map/ppermute | solution.py:372
  6.8 12.7 %collective-permute-start.2 = (bf16[1280,256]{1,0:T(8,128)(2,1)S(1)}, bf16[1280,256]{1,0:T(8,128)(2,1)S(1)}, u32[]{:S(2)}, u32[]{:S(2)}) collective-permute-start(bf16[1280,256]{1,0:T(8,128)(2,1)S(1)} %get-tuple-element.28.own), channel_id=1, source_target_pairs={{0,1},{1,0},{2,3},{3,2},{4,5},{5,4},{6,7},{7,6},{8,9},{9,8},{10,11... | collective-permute-start | bytes 1966088 | tf_op jit(solution)/shard_map/ppermute | solution.py:372
  14.8 4.7 %collective-permute-start.4 = (bf16[1280,128]{1,0:T(8,128)(2,1)S(1)}, bf16[1280,128]{1,0:T(8,128)(2,1)S(1)}, u32[]{:S(2)}, u32[]{:S(2)}) collective-permute-start(bf16[1280,128]{1,0:T(8,128)(2,1)S(1)} %collective-permute-done.3.refs_0_), channel_id=1, source_target_pairs={{0,1},{1,0},{2,3},{3,2},{4,5},{5,4},{6,7},{7,6},{8,9},{9,8},{10,11... | collective-permute-start | bytes 983048 | tf_op jit(solution)/shard_map/ppermute | solution.py:372
  15.4 9.4 %collective-permute-start.1 = (bf16[2,64,1280]{2,1,0:T(8,128)(2,1)S(1)}, bf16[2,64,1280]{2,1,0:T(8,128)(2,1)S(1)}, u32[]{:S(2)}, u32[]{:S(2)}) collective-permute-start(bf16[2,64,1280]{2,1,0:T(8,128)(2,1)S(1)} %shard_map.93), channel_id=1, source_target_pairs={{0,2},{1,3},{2,0},{3,1},{4,6},{5,7},{6,4},{7,5},{8,10},{9,11},{10,... | collective-permute-start | bytes 983048 | tf_op jit(solution)/shard_map/ppermute | solution.py:372
  16.9 37.1 %collective-permute-start.19 = (bf16[1024,640]{1,0:T(8,128)(2,1)S(1)}, bf16[1024,640]{1,0:T(8,128)(2,1)S(1)}, u32[]{:S(2)}, u32[]{:S(2)}) collective-permute-start(bf16[1024,640]{1,0:T(8,128)(2,1)S(1)} %shard_map.94), channel_id=1, source_target_pairs={{0,4},{4,0},{8,12},{12,8},{1,5},{5,1},{9,13},{13,9},{2,6},{6,2},{1... | collective-permute-start | bytes 3932168 | tf_op jit(solution)/shard_map/ppermute | solution.py:372
  18.2 8.9 %collective-permute-start.7 = (bf16[1280,128]{1,0:T(8,128)(2,1)S(1)}, bf16[1280,128]{1,0:T(8,128)(2,1)S(1)}, u32[]{:S(2)}, u32[]{:S(2)}) collective-permute-start(bf16[1280,128]{1,0:T(8,128)(2,1)S(1)} %collective-permute-done.3.refs_0_), channel_id=1, source_target_pairs={{0,16},{16,0},{1,17},{17,1},{2,18},{18,2},{3,19},{19,3},{4,20},{20... | collective-permute-start | bytes 983048 | tf_op jit(solution)/shard_map/ppermute | solution.py:372
  26.2 2.4 %collective-permute-start.5 = (f32[128,1024]{1,0:T(8,128)S(1)}, f32[128,1024]{1,0:T(8,128)S(1)}, u32[]{:S(2)}, u32[]{:S(2)}) collective-permute-start(f32[128,1024]{1,0:T(8,128)S(1)} %get-tuple-element.36), channel_id=1, source_target_pairs={{0,1},{1,0},{2,3},{3,2},{4,5},{5,4},{6,7},{7,6},{8,9},{9,8},{10,11... | collective-permute-start | bytes 1572872 | tf_op jit(solution)/shard_map/ppermute | solution.py:372
  27.1 3.6 %collective-permute-start.8 = (bf16[1280,128]{1,0:T(8,128)(2,1)S(1)}, bf16[1280,128]{1,0:T(8,128)(2,1)S(1)}, u32[]{:S(2)}, u32[]{:S(2)}) collective-permute-start(bf16[1280,128]{1,0:T(8,128)(2,1)S(1)} %collective-permute-done.7.refs_1_), channel_id=1, source_target_pairs={{0,1},{1,0},{2,3},{3,2},{4,5},{5,4},{6,7},{7,6},{8,9},{9,8},{10,11... | collective-permute-start | bytes 983048 | tf_op jit(solution)/shard_map/ppermute | solution.py:372
  29.2 11.8 %collective-permute-start.6 = (f32[64,1024]{1,0:T(8,128)S(1)}, f32[64,1024]{1,0:T(8,128)S(1)}, u32[]{:S(2)}, u32[]{:S(2)}) collective-permute-start(f32[64,1024]{1,0:T(8,128)S(1)} %shard_map.98), channel_id=1, source_target_pairs={{0,2},{1,3},{2,0},{3,1},{4,6},{5,7},{6,4},{7,5},{8,10},{9,11},{10,... | collective-permute-start | bytes 786440 | tf_op jit(solution)/shard_map/ppermute | solution.py:372
  31.8 7.0 %collective-permute-start.10 = (bf16[192,256]{1,0:T(8,128)(2,1)S(1)}, bf16[192,256]{1,0:T(8,128)(2,1)S(1)}, u32[]{:S(2)}, u32[]{:S(2)}) collective-permute-start(bf16[192,256]{1,0:T(8,128)(2,1)S(1)} %shard_map.99.refs_0_), channel_id=1, source_target_pairs={{0,2},{1,3},{2,0},{3,1},{4,6},{5,7},{6,4},{7,5},{8,10},{9,11},{10,... | collective-permute-start | bytes 294920 | tf_op jit(solution)/shard_map/ppermute | solution.py:372
  31.9 8.1 %collective-permute-start.9 = (bf16[192,256]{1,0:T(8,128)(2,1)S(1)}, bf16[192,256]{1,0:T(8,128)(2,1)S(1)}, u32[]{:S(2)}, u32[]{:S(2)}) collective-permute-start(bf16[192,256]{1,0:T(8,128)(2,1)S(1)} %shard_map.99.refs_0_), channel_id=1, source_target_pairs={{0,1},{1,0},{2,3},{3,2},{4,5},{5,4},{6,7},{7,6},{8,9},{9,8},{10,11... | collective-permute-start | bytes 294920 | tf_op jit(solution)/shard_map/ppermute | solution.py:372
  38.9 2.1 %collective-permute-start.11 = (bf16[192,256]{1,0:T(8,128)(2,1)S(1)}, bf16[192,256]{1,0:T(8,128)(2,1)S(1)}, u32[]{:S(2)}, u32[]{:S(2)}) collective-permute-start(bf16[192,256]{1,0:T(8,128)(2,1)S(1)} %collective-permute-done.10.refs_2_), channel_id=1, source_target_pairs={{0,1},{1,0},{2,3},{3,2},{4,5},{5,4},{6,7},{7,6},{8,9},{9,8},{10,11... | collective-permute-start | bytes 294920 | tf_op jit(solution)/shard_map/ppermute | solution.py:372
  44.0 4.8 %collective-permute-start.13 = (bf16[64,1024]{1,0:T(8,128)(2,1)S(1)}, bf16[64,1024]{1,0:T(8,128)(2,1)S(1)}, u32[]{:S(2)}, u32[]{:S(2)}) collective-permute-start(bf16[64,1024]{1,0:T(8,128)(2,1)S(1)} %shard_map.100.refs_0_), channel_id=1, source_target_pairs={{0,2},{1,3},{2,0},{3,1},{4,6},{5,7},{6,4},{7,5},{8,10},{9,11},{10,... | collective-permute-start | bytes 393224 | tf_op jit(solution)/shard_map/ppermute | solution.py:372
  45.5 4.5 %collective-permute-start.15 = (bf16[64,1024]{1,0:T(8,128)(2,1)S(1)}, bf16[64,1024]{1,0:T(8,128)(2,1)S(1)}, u32[]{:S(2)}, u32[]{:S(2)}) collective-permute-start(bf16[64,1024]{1,0:T(8,128)(2,1)S(1)} %shard_map.100.refs_0_), channel_id=1, source_target_pairs={{0,4},{1,5},{2,6},{3,7},{4,0},{5,1},{6,2},{7,3},{8,12},{9,13},{10,... | collective-permute-start | bytes 393224 | tf_op jit(solution)/shard_map/ppermute | solution.py:381
  46.8 5.8 %collective-permute-start.17 = (bf16[64,1024]{1,0:T(8,128)(2,1)S(1)}, bf16[64,1024]{1,0:T(8,128)(2,1)S(1)}, u32[]{:S(2)}, u32[]{:S(2)}) collective-permute-start(bf16[64,1024]{1,0:T(8,128)(2,1)S(1)} %shard_map.100.refs_0_), channel_id=1, source_target_pairs={{0,6},{1,7},{2,4},{3,5},{4,2},{5,3},{6,0},{7,1},{8,14},{9,15},{10,... | collective-permute-start | bytes 393224 | tf_op jit(solution)/shard_map/ppermute | solution.py:381
  46.8 7.2 %collective-permute-start.12 = (bf16[64,1024]{1,0:T(8,128)(2,1)S(1)}, bf16[64,1024]{1,0:T(8,128)(2,1)S(1)}, u32[]{:S(2)}, u32[]{:S(2)}) collective-permute-start(bf16[64,1024]{1,0:T(8,128)(2,1)S(1)} %shard_map.100.refs_0_), channel_id=1, source_target_pairs={{0,1},{1,0},{2,3},{3,2},{4,5},{5,4},{6,7},{7,6},{8,9},{9,8},{10,11... | collective-permute-start | bytes 393224 | tf_op jit(solution)/shard_map/ppermute | solution.py:372
  48.8 5.3 %collective-permute-start.14 = (bf16[64,1024]{1,0:T(8,128)(2,1)S(1)}, bf16[64,1024]{1,0:T(8,128)(2,1)S(1)}, u32[]{:S(2)}, u32[]{:S(2)}) collective-permute-start(bf16[64,1024]{1,0:T(8,128)(2,1)S(1)} %collective-permute-done.13.refs_2_), channel_id=1, source_target_pairs={{0,1},{1,0},{2,3},{3,2},{4,5},{5,4},{6,7},{7,6},{8,9},{9,8},{10,11... | collective-permute-start | bytes 393224 | tf_op jit(solution)/shard_map/ppermute | solution.py:372
  50.0 4.1 %collective-permute-start.16 = (bf16[64,1024]{1,0:T(8,128)(2,1)S(1)}, bf16[64,1024]{1,0:T(8,128)(2,1)S(1)}, u32[]{:S(2)}, u32[]{:S(2)}) collective-permute-start(bf16[64,1024]{1,0:T(8,128)(2,1)S(1)} %collective-permute-done.15.refs_4_), channel_id=1, source_target_pairs={{0,1},{1,0},{2,3},{3,2},{4,5},{5,4},{6,7},{7,6},{8,9},{9,8},{10,11... | collective-permute-start | bytes 393224 | tf_op jit(solution)/shard_map/ppermute | solution.py:372
  52.6 2.4 %collective-permute-start.18 = (bf16[64,1024]{1,0:T(8,128)(2,1)S(1)}, bf16[64,1024]{1,0:T(8,128)(2,1)S(1)}, u32[]{:S(2)}, u32[]{:S(2)}) collective-permute-start(bf16[64,1024]{1,0:T(8,128)(2,1)S(1)} %collective-permute-done.17.refs_6_), channel_id=1, source_target_pairs={{0,1},{1,0},{2,3},{3,2},{4,5},{5,4},{6,7},{7,6},{8,9},{9,8},{10,11... | collective-permute-start | bytes 393224 | tf_op jit(solution)/shard_map/ppermute | solution.py:372
  56.6 7.8 %collective-permute-start.20 = (bf16[64,640]{1,0:T(8,128)(2,1)S(1)}, bf16[64,640]{1,0:T(8,128)(2,1)S(1)}, u32[]{:S(2)}, u32[]{:S(2)}) collective-permute-start(bf16[64,640]{1,0:T(8,128)(2,1)S(1)} %get-tuple-element.39), channel_id=1, source_target_pairs={{0,0},{1,4},{2,8},{3,12},{4,1},{5,5},{6,9},{7,13},{8,2},{9,6},{10,... | collective-permute-start | bytes 245768 | tf_op jit(solution)/shard_map/ppermute | solution.py:578
  60.3 4.2 %collective-permute-start.21 = (bf16[64,640]{1,0:T(8,128)(2,1)S(1)}, bf16[64,640]{1,0:T(8,128)(2,1)S(1)}, u32[]{:S(2)}, u32[]{:S(2)}) collective-permute-start(bf16[64,640]{1,0:T(8,128)(2,1)S(1)} %get-tuple-element.40), channel_id=1, source_target_pairs={{0,1},{1,5},{2,9},{3,13},{4,0},{5,4},{6,8},{7,12},{8,3},{9,7},{10,... | collective-permute-start | bytes 245768 | tf_op jit(solution)/shard_map/ppermute | solution.py:578
  60.3 9.5 %collective-permute-start.22 = (bf16[64,640]{1,0:T(8,128)(2,1)S(1)}, bf16[64,640]{1,0:T(8,128)(2,1)S(1)}, u32[]{:S(2)}, u32[]{:S(2)}) collective-permute-start(bf16[64,640]{1,0:T(8,128)(2,1)S(1)} %get-tuple-element.41), channel_id=1, source_target_pairs={{0,2},{1,6},{2,10},{3,14},{4,3},{5,7},{6,11},{7,15},{8,0},{9,4},{1... | collective-permute-start | bytes 245768 | tf_op jit(solution)/shard_map/ppermute | solution.py:578
  64.1 13.4 %collective-permute-start.23 = (bf16[64,640]{1,0:T(8,128)(2,1)S(1)}, bf16[64,640]{1,0:T(8,128)(2,1)S(1)}, u32[]{:S(2)}, u32[]{:S(2)}) collective-permute-start(bf16[64,640]{1,0:T(8,128)(2,1)S(1)} %get-tuple-element.42), channel_id=1, source_target_pairs={{0,3},{1,7},{2,11},{3,15},{4,2},{5,6},{6,10},{7,14},{8,1},{9,5},{1... | collective-permute-start | bytes 245768 | tf_op jit(solution)/shard_map/ppermute | solution.py:578
  (9 other events, 51.7 us)

commit v11 on v10

--- a/solution.py
+++ b/solution.py
@@ -245,14 +245,12 @@
     queries = jnp.concatenate(queries, axis=0)
     prompt = jnp.concatenate([pair[:prompt_rows] for pair in pairs], axis=0)
     cont = jnp.concatenate([pair[prompt_rows:] for pair in pairs], axis=0)
-    scale = 1.0 / math.sqrt(size)
+    scale = 1.0 / (math.sqrt(size) * math.log(2.0))
     by_rows = (((1,), (1,)), ((), ()))
-    to_prompt = (
-        lax.dot_general(queries, prompt[:, :size], by_rows, preferred_element_type=F32) * scale
-    )
-    to_cont = (
-        lax.dot_general(queries, cont[:, :size], by_rows, preferred_element_type=F32) * scale
-    )
+    to_prompt = lax.dot_general(
+        queries, prompt[:, :size], by_rows, preferred_element_type=F32
+    )
+    to_cont = lax.dot_general(queries, cont[:, :size], by_rows, preferred_element_type=F32)
     shape = (rows, cont.shape[0])
     own = place[SP] * rows + lax.broadcasted_iota(jnp.int32, shape, 0)
     at = lax.broadcasted_iota(jnp.int32, shape, 1)
@@ -265,12 +263,14 @@
     peak = jnp.maximum(
         jnp.max(to_prompt, axis=1, keepdims=True), jnp.max(to_cont, axis=1, keepdims=True)
     )
-    to_prompt = jnp.exp(to_prompt - peak)
-    to_cont = jnp.exp(to_cont - peak)
-    divisor = jnp.sum(to_prompt, axis=1, keepdims=True) + jnp.sum(to_cont, axis=1, keepdims=True)
+    to_prompt = jnp.exp2((to_prompt - peak) * scale)
+    to_cont = jnp.exp2((to_cont - peak) * scale)
+    factor = 1.0 / (
+        jnp.sum(to_prompt, axis=1, keepdims=True) + jnp.sum(to_cont, axis=1, keepdims=True)
+    )
     result = jnp.dot(
-        (to_prompt / divisor).astype(BF16), prompt[:, size:], preferred_element_type=F32
-    ) + jnp.dot((to_cont / divisor).astype(BF16), cont[:, size:], preferred_element_type=F32)
+        (to_prompt * factor).astype(BF16), prompt[:, size:], preferred_element_type=F32
+    ) + jnp.dot((to_cont * factor).astype(BF16), cont[:, size:], preferred_element_type=F32)
     for h in range(heads):
         out[:, h * size : (h + 1) * size] = result[h * rows : (h + 1) * rows].astype(BF16)
 

time: 78.9 us -> 78.8 us (level)
  transfers between devices with their start and end apart: 24 -> 24, of which waited for: 10 -> 10; matrix products, arithmetic and copies ran while one was open for 0% -> 0% of each run, Pallas kernels for 14% -> 13%
where the time goes in v11:
time: 78.8 us; the launch traced here: 78.7 us
  starting transfers between devices  30.5 us (39%)
  waiting for transfers between devices  30.5 us (39%)
  Pallas kernels  15.5 us (20%)
  local copies, waits for them, and re-layouts  1.92 us (2%)
    ppermute x18, starting transfers between devices, swap(): lax.ppermute(array, axis, [(i, i ^ bits) for i in range(lax.axis_size(axi...  21.4 us
    ppermute x18, waiting for transfers between devices, swap(): lax.ppermute(array, axis, [(i, i ^ bits) for i in range(lax.axis_size(axi...  17.4 us
    pallas_call x12, Pallas kernels, call(): pl.pallas_call(kernel, out_shape=out_shape, grid_spec=pltpu.PrefetchScala...  15.5 us
    ppermute x4, waiting for transfers between devices, on_device(): lax.ppermute(part, ('tp', 'sp'), [(t * sp_count + s, s * sp_count + (t ^...  13 us
    ppermute x4, starting transfers between devices, on_device(): lax.ppermute(part, ('tp', 'sp'), [(t * sp_count + s, s * sp_count + (t ^...  7.79 us
    unnamed x18, local copies, waits for them, and re-layouts  1.92 us
  transfers between devices with their start and end apart: 24, of which 10 were waited for; matrix products, arithmetic and copies ran while one was open for 0% of the time, Pallas kernels for 13%

profile of v11, /device:TPU:1, one launch (start us, length us, event | category | flops | bytes accessed | tf_op | source)
XLA Modules:
  0.0 78.7 jit_solution(7069423787570559343)
XLA Ops:
  0.1 1.7 %copy-done = bf16[1280,1024]{1,0:T(8,128)(2,1)S(1)} copy-done((bf16[1280,1024]{1,0:T(8,128)(2,1)S(1)}, bf16[1280,1024]{1,0:T(8,128)(2,1)}, u32[]{:S(2)}) %copy-start) | copy-done | bytes 2621464
  4.1 2.7 %collective-permute-start.3 = (bf16[1280,128]{1,0:T(8,128)(2,1)S(1)}, bf16[1280,128]{1,0:T(8,128)(2,1)S(1)}, u32[]{:S(2)}, u32[]{:S(2)}) collective-permute-start(bf16[1280,128]{1,0:T(8,128)(2,1)S(1)} %get-tuple-element.24), channel_id=1, source_target_pairs={{0,2},{1,3},{2,0},{3,1},{4,6},{5,7},{6,4},{7,5},{8,10},{9,11},{10,... | collective-permute-start | bytes 983048 | tf_op jit(solution)/shard_map/ppermute | solution.py:372
  7.1 1.5 %shard_map.95 = (f32[192,128]{1,0:T(8,128)S(1)}, f32[192,128]{1,0:T(8,128)S(1)}) custom-call(s32[4]{0:T(128)S(1)} %pad_add_fusion.place, s32[8]{0:T(128)S(1)} %copy-done.7), custom_call_target="tpu_custom_call" | custom-call | flops 2457600 | bytes 196608 | tf_op jit(solution)/shard_map/pallas_call | solution.py:21
  10.1 4.6 %collective-permute-done.3.refs_0_ = bf16[1280,128]{1,0:T(8,128)(2,1)S(1)} collective-permute-done((bf16[1280,128]{1,0:T(8,128)(2,1)S(1)}, bf16[1280,128]{1,0:T(8,128)(2,1)S(1)}, u32[]{:S(2)}, u32[]{:S(2)}) %collective-permute-start.3) | collective-permute-done | bytes 327712 | tf_op jit(solution)/shard_map/ppermute | solution.py:372
  15.4 1.5 %collective-permute-start.1 = (bf16[2,64,1280]{2,1,0:T(8,128)(2,1)S(1)}, bf16[2,64,1280]{2,1,0:T(8,128)(2,1)S(1)}, u32[]{:S(2)}, u32[]{:S(2)}) collective-permute-start(bf16[2,64,1280]{2,1,0:T(8,128)(2,1)S(1)} %shard_map.93), channel_id=1, source_target_pairs={{0,2},{1,3},{2,0},{3,1},{4,6},{5,7},{6,4},{7,5},{8,10},{9,11},{10,... | collective-permute-start | bytes 983048 | tf_op jit(solution)/shard_map/ppermute | solution.py:372
  16.9 1.3 %collective-permute-start.19 = (bf16[1024,640]{1,0:T(8,128)(2,1)S(1)}, bf16[1024,640]{1,0:T(8,128)(2,1)S(1)}, u32[]{:S(2)}, u32[]{:S(2)}) collective-permute-start(bf16[1024,640]{1,0:T(8,128)(2,1)S(1)} %shard_map.94), channel_id=1, source_target_pairs={{0,4},{4,0},{8,12},{12,8},{1,5},{5,1},{9,13},{13,9},{2,6},{6,2},{1... | collective-permute-start | bytes 3932168 | tf_op jit(solution)/shard_map/ppermute | solution.py:372
  18.2 1.2 %collective-permute-start.7 = (bf16[1280,128]{1,0:T(8,128)(2,1)S(1)}, bf16[1280,128]{1,0:T(8,128)(2,1)S(1)}, u32[]{:S(2)}, u32[]{:S(2)}) collective-permute-start(bf16[1280,128]{1,0:T(8,128)(2,1)S(1)} %collective-permute-done.3.refs_0_), channel_id=1, source_target_pairs={{0,16},{16,0},{1,17},{17,1},{2,18},{18,2},{3,19},{19,3},{4,20},{20... | collective-permute-start | bytes 983048 | tf_op jit(solution)/shard_map/ppermute | solution.py:372
  19.5 1.6 %shard_map.96 = (bf16[4,128,1280]{2,1,0:T(8,128)(2,1)S(1)}, f32[192,256]{1,0:T(8,128)S(1)}) custom-call(s32[4]{0:T(128)S(1)} %pad_add_fusion.place, bf16[128,5120]{1,0:T(8,128)(2,1)S(1)} %copy-done.4, f32[1,5120]{1,0:T(1,128)S(1)} %bitcast.8, bf16[4,64,1280]{2,1,0:T(8,128)(2,1)S(1)} %get-tuple-element.26.cont.refs_0_, ...), custom_call_target="tpu_custom_call" | custom-call | flops 251658240 | bytes 5242880 | tf_op jit(solution)/shard_map/pallas_call | solution.py:21
  21.1 3.7 %collective-permute-done.1.refs_2_ = bf16[2,64,1280]{2,1,0:T(8,128)(2,1)S(1)} collective-permute-done((bf16[2,64,1280]{2,1,0:T(8,128)(2,1)S(1)}, bf16[2,64,1280]{2,1,0:T(8,128)(2,1)S(1)}, u32[]{:S(2)}, u32[]{:S(2)}) %collective-permute-start.1) | collective-permute-done | bytes 327712 | tf_op jit(solution)/shard_map/ppermute | solution.py:372
  24.8 1.4 %shard_map.97 = (f32[128,1024]{1,0:T(8,128)S(1)}, f32[128,1024]{1,0:T(8,128)S(1)}) custom-call(s32[4]{0:T(128)S(1)} %pad_add_fusion.place, bf16[4,64,1280]{2,1,0:T(8,128)(2,1)S(1)} %get-tuple-element.26.cont.refs_0_, bf16[2,64,1280]{2,1,0:T(8,128)(2,1)S(1)} %collective-permute-done.other.refs_1_, bf16[2,64,1280]{2,1,0:T(8,128)(2,1)S(1)} %collective-permute-done.1.refs_2_, ...), custom_call_target="tpu_custom_call" | custom-call | flops 671088640 | bytes 2621440 | tf_op jit(solution)/shard_map/pallas_call | solution.py:21
  27.1 1.3 %collective-permute-start.8 = (bf16[1280,128]{1,0:T(8,128)(2,1)S(1)}, bf16[1280,128]{1,0:T(8,128)(2,1)S(1)}, u32[]{:S(2)}, u32[]{:S(2)}) collective-permute-start(bf16[1280,128]{1,0:T(8,128)(2,1)S(1)} %collective-permute-done.7.refs_1_), channel_id=1, source_target_pairs={{0,1},{1,0},{2,3},{3,2},{4,5},{5,4},{6,7},{7,6},{8,9},{9,8},{10,11... | collective-permute-start | bytes 983048 | tf_op jit(solution)/shard_map/ppermute | solution.py:372
  29.2 1.5 %collective-permute-start.6 = (f32[64,1024]{1,0:T(8,128)S(1)}, f32[64,1024]{1,0:T(8,128)S(1)}, u32[]{:S(2)}, u32[]{:S(2)}) collective-permute-start(f32[64,1024]{1,0:T(8,128)S(1)} %shard_map.98), channel_id=1, source_target_pairs={{0,2},{1,3},{2,0},{3,1},{4,6},{5,7},{6,4},{7,5},{8,10},{9,11},{10,... | collective-permute-start | bytes 786440 | tf_op jit(solution)/shard_map/ppermute | solution.py:372
  32.9 6.0 %collective-permute-done.10.refs_2_ = bf16[192,256]{1,0:T(8,128)(2,1)S(1)} collective-permute-done((bf16[192,256]{1,0:T(8,128)(2,1)S(1)}, bf16[192,256]{1,0:T(8,128)(2,1)S(1)}, u32[]{:S(2)}, u32[]{:S(2)}) %collective-permute-start.10) | collective-permute-done | bytes 98336 | tf_op jit(solution)/shard_map/ppermute | solution.py:372
  41.0 2.9 %shard_map.100.refs_0_ = bf16[64,1024]{1,0:T(8,128)(2,1)S(1)} custom-call(s32[4]{0:T(128)S(1)} %pad_add_fusion.place, s32[8]{0:T(128)S(1)} %copy-done.7, f32[128,1024]{1,0:T(8,128)S(1)} %get-tuple-element.35.left.mine, f32[128,1024]{1,0:T(8,128)S(1)} %collective-permute-done.5.right.near, f32[64,1024]{1,0:T(8,128)S(1)} %collective-permute-done.6.far, ...), custom_call_target="tpu_custom_call" | custom-call | flops 201326592 | bytes 1048576 | tf_op jit(solution)/shard_map/pallas_call | solution.py:21
  44.0 1.5 %collective-permute-start.13 = (bf16[64,1024]{1,0:T(8,128)(2,1)S(1)}, bf16[64,1024]{1,0:T(8,128)(2,1)S(1)}, u32[]{:S(2)}, u32[]{:S(2)}) collective-permute-start(bf16[64,1024]{1,0:T(8,128)(2,1)S(1)} %shard_map.100.refs_0_), channel_id=1, source_target_pairs={{0,2},{1,3},{2,0},{3,1},{4,6},{5,7},{6,4},{7,5},{8,10},{9,11},{10,... | collective-permute-start | bytes 393224 | tf_op jit(solution)/shard_map/ppermute | solution.py:372
  45.5 1.3 %collective-permute-start.15 = (bf16[64,1024]{1,0:T(8,128)(2,1)S(1)}, bf16[64,1024]{1,0:T(8,128)(2,1)S(1)}, u32[]{:S(2)}, u32[]{:S(2)}) collective-permute-start(bf16[64,1024]{1,0:T(8,128)(2,1)S(1)} %shard_map.100.refs_0_), channel_id=1, source_target_pairs={{0,4},{1,5},{2,6},{3,7},{4,0},{5,1},{6,2},{7,3},{8,12},{9,13},{10,... | collective-permute-start | bytes 393224 | tf_op jit(solution)/shard_map/ppermute | solution.py:381
  49.9 2.5 %collective-permute-start.16 = (bf16[64,1024]{1,0:T(8,128)(2,1)S(1)}, bf16[64,1024]{1,0:T(8,128)(2,1)S(1)}, u32[]{:S(2)}, u32[]{:S(2)}) collective-permute-start(bf16[64,1024]{1,0:T(8,128)(2,1)S(1)} %collective-permute-done.15.refs_4_), channel_id=1, source_target_pairs={{0,1},{1,0},{2,3},{3,2},{4,5},{5,4},{6,7},{7,6},{8,9},{9,8},{10,11... | collective-permute-start | bytes 393224 | tf_op jit(solution)/shard_map/ppermute | solution.py:372
  52.6 1.4 %collective-permute-start.18 = (bf16[64,1024]{1,0:T(8,128)(2,1)S(1)}, bf16[64,1024]{1,0:T(8,128)(2,1)S(1)}, u32[]{:S(2)}, u32[]{:S(2)}) collective-permute-start(bf16[64,1024]{1,0:T(8,128)(2,1)S(1)} %collective-permute-done.17.refs_6_), channel_id=1, source_target_pairs={{0,1},{1,0},{2,3},{3,2},{4,5},{5,4},{6,7},{7,6},{8,9},{9,8},{10,11... | collective-permute-start | bytes 393224 | tf_op jit(solution)/shard_map/ppermute | solution.py:372
  55.0 1.6 %shard_map.101 = (bf16[64,640]{1,0:T(8,128)(2,1)S(1)}, bf16[64,640]{1,0:T(8,128)(2,1)S(1)}, bf16[64,640]{1,0:T(8,128)(2,1)S(1)}, bf16[64,640]{1,0:T(8,128)(2,1)S(1)}) custom-call(s32[4]{0:T(128)S(1)} %pad_add_fusion.place, bf16[64,1024]{1,0:T(8,128)(2,1)S(1)} %shard_map.100.refs_0_, bf16[64,1024]{1,0:T(8,128)(2,1)S(1)} %collective-permute-done.12.refs_1_, ...), custom_call_target="tpu_custom_call" | custom-call | flops 671088640 | bytes 2621440 | tf_op jit(solution)/shard_map/pallas_call | solution.py:21
  56.6 3.6 %collective-permute-start.20 = (bf16[64,640]{1,0:T(8,128)(2,1)S(1)}, bf16[64,640]{1,0:T(8,128)(2,1)S(1)}, u32[]{:S(2)}, u32[]{:S(2)}) collective-permute-start(bf16[64,640]{1,0:T(8,128)(2,1)S(1)} %get-tuple-element.39), channel_id=1, source_target_pairs={{0,0},{1,4},{2,8},{3,12},{4,1},{5,5},{6,9},{7,13},{8,2},{9,6},{10,... | collective-permute-start | bytes 245768 | tf_op jit(solution)/shard_map/ppermute | solution.py:578
  60.3 3.7 %collective-permute-start.22 = (bf16[64,640]{1,0:T(8,128)(2,1)S(1)}, bf16[64,640]{1,0:T(8,128)(2,1)S(1)}, u32[]{:S(2)}, u32[]{:S(2)}) collective-permute-start(bf16[64,640]{1,0:T(8,128)(2,1)S(1)} %get-tuple-element.41), channel_id=1, source_target_pairs={{0,2},{1,6},{2,10},{3,14},{4,3},{5,7},{6,11},{7,15},{8,0},{9,4},{1... | collective-permute-start | bytes 245768 | tf_op jit(solution)/shard_map/ppermute | solution.py:578
  64.4 5.4 %collective-permute-done.22.refs_2_ = bf16[64,640]{1,0:T(8,128)(2,1)S(1)} collective-permute-done((bf16[64,640]{1,0:T(8,128)(2,1)S(1)}, bf16[64,640]{1,0:T(8,128)(2,1)S(1)}, u32[]{:S(2)}, u32[]{:S(2)}) %collective-permute-start.22) | collective-permute-done | bytes 81952 | tf_op jit(solution)/shard_map/ppermute | solution.py:578
  69.8 7.6 %collective-permute-done.23.refs_3_ = bf16[64,640]{1,0:T(8,128)(2,1)S(1)} collective-permute-done((bf16[64,640]{1,0:T(8,128)(2,1)S(1)}, bf16[64,640]{1,0:T(8,128)(2,1)S(1)}, u32[]{:S(2)}, u32[]{:S(2)}) %collective-permute-start.23) | collective-permute-done | bytes 81952 | tf_op jit(solution)/shard_map/ppermute | solution.py:578
  77.4 1.3 %shard_map.102 = bf16[64,1280]{1,0:T(8,128)(2,1)} custom-call(s32[4]{0:T(128)S(1)} %pad_add_fusion.place, bf16[64,5120]{1,0:T(8,128)(2,1)S(1)} %copy-done.2, bf16[64,640]{1,0:T(8,128)(2,1)S(1)} %collective-permute-done.20.refs_0_, bf16[64,640]{1,0:T(8,128)(2,1)S(1)} %collective-permute-done.21.refs_1_, bf16[64,640]{1,0:T(8,128)(2,1)S(1)} %collective-permute-done.22.refs_2_, ...), custom_call_target="tpu_custom_call" | custom-call | flops 327680 | bytes 983040 | tf_op jit(solution)/shard_map/pallas_call | solution.py:21
  (55 shorter events, 15.5 us)
Async XLA Ops:
  4.0 4.6 %collective-permute-start = (bf16[2,64,1280]{2,1,0:T(8,128)(2,1)S(1)}, bf16[2,64,1280]{2,1,0:T(8,128)(2,1)S(1)}, u32[]{:S(2)}, u32[]{:S(2)}) collective-permute-start(bf16[2,64,1280]{2,1,0:T(8,128)(2,1)S(1)} %get-tuple-element.27), channel_id=1, source_target_pairs={{0,1},{1,0},{2,3},{3,2},{4,5},{5,4},{6,7},{7,6},{8,9},{9,8},{10,11... | collective-permute-start | bytes 983048 | tf_op jit(solution)/shard_map/ppermute | solution.py:372
  4.1 10.7 %collective-permute-start.3 = (bf16[1280,128]{1,0:T(8,128)(2,1)S(1)}, bf16[1280,128]{1,0:T(8,128)(2,1)S(1)}, u32[]{:S(2)}, u32[]{:S(2)}) collective-permute-start(bf16[1280,128]{1,0:T(8,128)(2,1)S(1)} %get-tuple-element.24), channel_id=1, source_target_pairs={{0,2},{1,3},{2,0},{3,1},{4,6},{5,7},{6,4},{7,5},{8,10},{9,11},{10,... | collective-permute-start | bytes 983048 | tf_op jit(solution)/shard_map/ppermute | solution.py:372
  6.8 12.7 %collective-permute-start.2 = (bf16[1280,256]{1,0:T(8,128)(2,1)S(1)}, bf16[1280,256]{1,0:T(8,128)(2,1)S(1)}, u32[]{:S(2)}, u32[]{:S(2)}) collective-permute-start(bf16[1280,256]{1,0:T(8,128)(2,1)S(1)} %get-tuple-element.28.own), channel_id=1, source_target_pairs={{0,1},{1,0},{2,3},{3,2},{4,5},{5,4},{6,7},{7,6},{8,9},{9,8},{10,11... | collective-permute-start | bytes 1966088 | tf_op jit(solution)/shard_map/ppermute | solution.py:372
  14.8 4.7 %collective-permute-start.4 = (bf16[1280,128]{1,0:T(8,128)(2,1)S(1)}, bf16[1280,128]{1,0:T(8,128)(2,1)S(1)}, u32[]{:S(2)}, u32[]{:S(2)}) collective-permute-start(bf16[1280,128]{1,0:T(8,128)(2,1)S(1)} %collective-permute-done.3.refs_0_), channel_id=1, source_target_pairs={{0,1},{1,0},{2,3},{3,2},{4,5},{5,4},{6,7},{7,6},{8,9},{9,8},{10,11... | collective-permute-start | bytes 983048 | tf_op jit(solution)/shard_map/ppermute | solution.py:372
  15.4 9.4 %collective-permute-start.1 = (bf16[2,64,1280]{2,1,0:T(8,128)(2,1)S(1)}, bf16[2,64,1280]{2,1,0:T(8,128)(2,1)S(1)}, u32[]{:S(2)}, u32[]{:S(2)}) collective-permute-start(bf16[2,64,1280]{2,1,0:T(8,128)(2,1)S(1)} %shard_map.93), channel_id=1, source_target_pairs={{0,2},{1,3},{2,0},{3,1},{4,6},{5,7},{6,4},{7,5},{8,10},{9,11},{10,... | collective-permute-start | bytes 983048 | tf_op jit(solution)/shard_map/ppermute | solution.py:372
  16.9 37.1 %collective-permute-start.19 = (bf16[1024,640]{1,0:T(8,128)(2,1)S(1)}, bf16[1024,640]{1,0:T(8,128)(2,1)S(1)}, u32[]{:S(2)}, u32[]{:S(2)}) collective-permute-start(bf16[1024,640]{1,0:T(8,128)(2,1)S(1)} %shard_map.94), channel_id=1, source_target_pairs={{0,4},{4,0},{8,12},{12,8},{1,5},{5,1},{9,13},{13,9},{2,6},{6,2},{1... | collective-permute-start | bytes 3932168 | tf_op jit(solution)/shard_map/ppermute | solution.py:372
  18.2 8.9 %collective-permute-start.7 = (bf16[1280,128]{1,0:T(8,128)(2,1)S(1)}, bf16[1280,128]{1,0:T(8,128)(2,1)S(1)}, u32[]{:S(2)}, u32[]{:S(2)}) collective-permute-start(bf16[1280,128]{1,0:T(8,128)(2,1)S(1)} %collective-permute-done.3.refs_0_), channel_id=1, source_target_pairs={{0,16},{16,0},{1,17},{17,1},{2,18},{18,2},{3,19},{19,3},{4,20},{20... | collective-permute-start | bytes 983048 | tf_op jit(solution)/shard_map/ppermute | solution.py:372
  26.2 2.4 %collective-permute-start.5 = (f32[128,1024]{1,0:T(8,128)S(1)}, f32[128,1024]{1,0:T(8,128)S(1)}, u32[]{:S(2)}, u32[]{:S(2)}) collective-permute-start(f32[128,1024]{1,0:T(8,128)S(1)} %get-tuple-element.36), channel_id=1, source_target_pairs={{0,1},{1,0},{2,3},{3,2},{4,5},{5,4},{6,7},{7,6},{8,9},{9,8},{10,11... | collective-permute-start | bytes 1572872 | tf_op jit(solution)/shard_map/ppermute | solution.py:372
  27.1 3.6 %collective-permute-start.8 = (bf16[1280,128]{1,0:T(8,128)(2,1)S(1)}, bf16[1280,128]{1,0:T(8,128)(2,1)S(1)}, u32[]{:S(2)}, u32[]{:S(2)}) collective-permute-start(bf16[1280,128]{1,0:T(8,128)(2,1)S(1)} %collective-permute-done.7.refs_1_), channel_id=1, source_target_pairs={{0,1},{1,0},{2,3},{3,2},{4,5},{5,4},{6,7},{7,6},{8,9},{9,8},{10,11... | collective-permute-start | bytes 983048 | tf_op jit(solution)/shard_map/ppermute | solution.py:372
  29.2 11.8 %collective-permute-start.6 = (f32[64,1024]{1,0:T(8,128)S(1)}, f32[64,1024]{1,0:T(8,128)S(1)}, u32[]{:S(2)}, u32[]{:S(2)}) collective-permute-start(f32[64,1024]{1,0:T(8,128)S(1)} %shard_map.98), channel_id=1, source_target_pairs={{0,2},{1,3},{2,0},{3,1},{4,6},{5,7},{6,4},{7,5},{8,10},{9,11},{10,... | collective-permute-start | bytes 786440 | tf_op jit(solution)/shard_map/ppermute | solution.py:372
  31.8 7.0 %collective-permute-start.10 = (bf16[192,256]{1,0:T(8,128)(2,1)S(1)}, bf16[192,256]{1,0:T(8,128)(2,1)S(1)}, u32[]{:S(2)}, u32[]{:S(2)}) collective-permute-start(bf16[192,256]{1,0:T(8,128)(2,1)S(1)} %shard_map.99.refs_0_), channel_id=1, source_target_pairs={{0,2},{1,3},{2,0},{3,1},{4,6},{5,7},{6,4},{7,5},{8,10},{9,11},{10,... | collective-permute-start | bytes 294920 | tf_op jit(solution)/shard_map/ppermute | solution.py:372
  31.9 8.1 %collective-permute-start.9 = (bf16[192,256]{1,0:T(8,128)(2,1)S(1)}, bf16[192,256]{1,0:T(8,128)(2,1)S(1)}, u32[]{:S(2)}, u32[]{:S(2)}) collective-permute-start(bf16[192,256]{1,0:T(8,128)(2,1)S(1)} %shard_map.99.refs_0_), channel_id=1, source_target_pairs={{0,1},{1,0},{2,3},{3,2},{4,5},{5,4},{6,7},{7,6},{8,9},{9,8},{10,11... | collective-permute-start | bytes 294920 | tf_op jit(solution)/shard_map/ppermute | solution.py:372
  38.9 2.1 %collective-permute-start.11 = (bf16[192,256]{1,0:T(8,128)(2,1)S(1)}, bf16[192,256]{1,0:T(8,128)(2,1)S(1)}, u32[]{:S(2)}, u32[]{:S(2)}) collective-permute-start(bf16[192,256]{1,0:T(8,128)(2,1)S(1)} %collective-permute-done.10.refs_2_), channel_id=1, source_target_pairs={{0,1},{1,0},{2,3},{3,2},{4,5},{5,4},{6,7},{7,6},{8,9},{9,8},{10,11... | collective-permute-start | bytes 294920 | tf_op jit(solution)/shard_map/ppermute | solution.py:372
  44.0 4.8 %collective-permute-start.13 = (bf16[64,1024]{1,0:T(8,128)(2,1)S(1)}, bf16[64,1024]{1,0:T(8,128)(2,1)S(1)}, u32[]{:S(2)}, u32[]{:S(2)}) collective-permute-start(bf16[64,1024]{1,0:T(8,128)(2,1)S(1)} %shard_map.100.refs_0_), channel_id=1, source_target_pairs={{0,2},{1,3},{2,0},{3,1},{4,6},{5,7},{6,4},{7,5},{8,10},{9,11},{10,... | collective-permute-start | bytes 393224 | tf_op jit(solution)/shard_map/ppermute | solution.py:372
  45.5 4.5 %collective-permute-start.15 = (bf16[64,1024]{1,0:T(8,128)(2,1)S(1)}, bf16[64,1024]{1,0:T(8,128)(2,1)S(1)}, u32[]{:S(2)}, u32[]{:S(2)}) collective-permute-start(bf16[64,1024]{1,0:T(8,128)(2,1)S(1)} %shard_map.100.refs_0_), channel_id=1, source_target_pairs={{0,4},{1,5},{2,6},{3,7},{4,0},{5,1},{6,2},{7,3},{8,12},{9,13},{10,... | collective-permute-start | bytes 393224 | tf_op jit(solution)/shard_map/ppermute | solution.py:381
  46.8 5.8 %collective-permute-start.17 = (bf16[64,1024]{1,0:T(8,128)(2,1)S(1)}, bf16[64,1024]{1,0:T(8,128)(2,1)S(1)}, u32[]{:S(2)}, u32[]{:S(2)}) collective-permute-start(bf16[64,1024]{1,0:T(8,128)(2,1)S(1)} %shard_map.100.refs_0_), channel_id=1, source_target_pairs={{0,6},{1,7},{2,4},{3,5},{4,2},{5,3},{6,0},{7,1},{8,14},{9,15},{10,... | collective-permute-start | bytes 393224 | tf_op jit(solution)/shard_map/ppermute | solution.py:381
  46.8 7.2 %collective-permute-start.12 = (bf16[64,1024]{1,0:T(8,128)(2,1)S(1)}, bf16[64,1024]{1,0:T(8,128)(2,1)S(1)}, u32[]{:S(2)}, u32[]{:S(2)}) collective-permute-start(bf16[64,1024]{1,0:T(8,128)(2,1)S(1)} %shard_map.100.refs_0_), channel_id=1, source_target_pairs={{0,1},{1,0},{2,3},{3,2},{4,5},{5,4},{6,7},{7,6},{8,9},{9,8},{10,11... | collective-permute-start | bytes 393224 | tf_op jit(solution)/shard_map/ppermute | solution.py:372
  48.7 5.3 %collective-permute-start.14 = (bf16[64,1024]{1,0:T(8,128)(2,1)S(1)}, bf16[64,1024]{1,0:T(8,128)(2,1)S(1)}, u32[]{:S(2)}, u32[]{:S(2)}) collective-permute-start(bf16[64,1024]{1,0:T(8,128)(2,1)S(1)} %collective-permute-done.13.refs_2_), channel_id=1, source_target_pairs={{0,1},{1,0},{2,3},{3,2},{4,5},{5,4},{6,7},{7,6},{8,9},{9,8},{10,11... | collective-permute-start | bytes 393224 | tf_op jit(solution)/shard_map/ppermute | solution.py:372
  49.9 4.1 %collective-permute-start.16 = (bf16[64,1024]{1,0:T(8,128)(2,1)S(1)}, bf16[64,1024]{1,0:T(8,128)(2,1)S(1)}, u32[]{:S(2)}, u32[]{:S(2)}) collective-permute-start(bf16[64,1024]{1,0:T(8,128)(2,1)S(1)} %collective-permute-done.15.refs_4_), channel_id=1, source_target_pairs={{0,1},{1,0},{2,3},{3,2},{4,5},{5,4},{6,7},{7,6},{8,9},{9,8},{10,11... | collective-permute-start | bytes 393224 | tf_op jit(solution)/shard_map/ppermute | solution.py:372
  52.6 2.4 %collective-permute-start.18 = (bf16[64,1024]{1,0:T(8,128)(2,1)S(1)}, bf16[64,1024]{1,0:T(8,128)(2,1)S(1)}, u32[]{:S(2)}, u32[]{:S(2)}) collective-permute-start(bf16[64,1024]{1,0:T(8,128)(2,1)S(1)} %collective-permute-done.17.refs_6_), channel_id=1, source_target_pairs={{0,1},{1,0},{2,3},{3,2},{4,5},{5,4},{6,7},{7,6},{8,9},{9,8},{10,11... | collective-permute-start | bytes 393224 | tf_op jit(solution)/shard_map/ppermute | solution.py:372
  56.6 7.8 %collective-permute-start.20 = (bf16[64,640]{1,0:T(8,128)(2,1)S(1)}, bf16[64,640]{1,0:T(8,128)(2,1)S(1)}, u32[]{:S(2)}, u32[]{:S(2)}) collective-permute-start(bf16[64,640]{1,0:T(8,128)(2,1)S(1)} %get-tuple-element.39), channel_id=1, source_target_pairs={{0,0},{1,4},{2,8},{3,12},{4,1},{5,5},{6,9},{7,13},{8,2},{9,6},{10,... | collective-permute-start | bytes 245768 | tf_op jit(solution)/shard_map/ppermute | solution.py:578
  60.2 4.2 %collective-permute-start.21 = (bf16[64,640]{1,0:T(8,128)(2,1)S(1)}, bf16[64,640]{1,0:T(8,128)(2,1)S(1)}, u32[]{:S(2)}, u32[]{:S(2)}) collective-permute-start(bf16[64,640]{1,0:T(8,128)(2,1)S(1)} %get-tuple-element.40), channel_id=1, source_target_pairs={{0,1},{1,5},{2,9},{3,13},{4,0},{5,4},{6,8},{7,12},{8,3},{9,7},{10,... | collective-permute-start | bytes 245768 | tf_op jit(solution)/shard_map/ppermute | solution.py:578
  60.3 9.5 %collective-permute-start.22 = (bf16[64,640]{1,0:T(8,128)(2,1)S(1)}, bf16[64,640]{1,0:T(8,128)(2,1)S(1)}, u32[]{:S(2)}, u32[]{:S(2)}) collective-permute-start(bf16[64,640]{1,0:T(8,128)(2,1)S(1)} %get-tuple-element.41), channel_id=1, source_target_pairs={{0,2},{1,6},{2,10},{3,14},{4,3},{5,7},{6,11},{7,15},{8,0},{9,4},{1... | collective-permute-start | bytes 245768 | tf_op jit(solution)/shard_map/ppermute | solution.py:578
  64.0 13.4 %collective-permute-start.23 = (bf16[64,640]{1,0:T(8,128)(2,1)S(1)}, bf16[64,640]{1,0:T(8,128)(2,1)S(1)}, u32[]{:S(2)}, u32[]{:S(2)}) collective-permute-start(bf16[64,640]{1,0:T(8,128)(2,1)S(1)} %get-tuple-element.42), channel_id=1, source_target_pairs={{0,3},{1,7},{2,11},{3,15},{4,2},{5,6},{6,10},{7,14},{8,1},{9,5},{1... | collective-permute-start | bytes 245768 | tf_op jit(solution)/shard_map/ppermute | solution.py:578
  (9 other events, 51.7 us)

commit v12 on v11

--- a/solution.py
+++ b/solution.py
@@ -100,30 +100,24 @@
     )
 
 
-def pick_kernel(place, first, key, value, half, both):
+def pick_kernel(place, columns, half, both):
     size = half.shape[1]
-    half[...] = first[...]
-    both[:, :size] = key[...]
-    both[:, size:] = value[...]
+    both[...] = columns[...]
+    half[...] = jnp.where(place[GROUP] == 1, columns[:, size:], columns[:, :size])
 
 
 def pick_columns(place, weight, size):
     depth = weight.shape[0]
-    block = (depth, size)
-    outs = [shape_of(block, BF16), shape_of((depth, 2 * size), BF16)]
+    outs = [shape_of((depth, n * size), BF16) for n in (1, 2)]
     return call(
         pick_kernel,
         place,
         (1,),
-        [
-            pl.BlockSpec(block, lambda i, place: (0, 2 * place[HEAD] + place[GROUP])),
-            pl.BlockSpec(block, lambda i, place: (0, 2 * place[HEAD])),
-            pl.BlockSpec(block, lambda i, place: (0, 2 * place[HEAD] + 1)),
-        ],
+        [pl.BlockSpec((depth, 2 * size), lambda i, place: (0, place[HEAD]))],
         [whole(out) for out in outs],
         outs,
-        (weight, weight, weight),
-        (0, 12 * depth * size),
+        (weight,),
+        (0, 10 * depth * size),
     )
 
 

time: 78.8 us -> 79.6 us (1.010)
  local copies, waits for them, and re-layouts: 1.92 us -> 2.93 us
    unnamed x18 -> x20, local copies, waits for them, and re-layouts: 1.92 us -> 2.93 us
where the time goes in v12:
time: 79.6 us; the launch traced here: 79.5 us
  starting transfers between devices  30.5 us (38%)
  waiting for transfers between devices  30.5 us (38%)
  Pallas kernels  15.2 us (19%)
  local copies, waits for them, and re-layouts  2.93 us (4%)
    ppermute x18, starting transfers between devices, swap(): lax.ppermute(array, axis, [(i, i ^ bits) for i in range(lax.axis_size(axi...  21.4 us
    ppermute x18, waiting for transfers between devices, swap(): lax.ppermute(array, axis, [(i, i ^ bits) for i in range(lax.axis_size(axi...  17.4 us
    pallas_call x12, Pallas kernels, call(): pl.pallas_call(kernel, out_shape=out_shape, grid_spec=pltpu.PrefetchScala...  15.2 us
    ppermute x4, waiting for transfers between devices, on_device(): lax.ppermute(part, ('tp', 'sp'), [(t * sp_count + s, s * sp_count + (t ^...  13 us
    ppermute x4, starting transfers between devices, on_device(): lax.ppermute(part, ('tp', 'sp'), [(t * sp_count + s, s * sp_count + (t ^...  7.8 us
    unnamed x20, local copies, waits for them, and re-layouts  2.93 us
  transfers between devices with their start and end apart: 24, of which 10 were waited for; matrix products, arithmetic and copies ran while one was open for 0% of the time, Pallas kernels for 13%

profile of v12, /device:TPU:1, one launch (start us, length us, event | category | flops | bytes accessed | tf_op | source)
XLA Modules:
  0.0 79.5 jit_solution(16409627369560040484)
XLA Ops:
  0.1 1.7 %copy-done.1 = bf16[1280,1024]{1,0:T(8,128)(2,1)S(1)} copy-done((bf16[1280,1024]{1,0:T(8,128)(2,1)S(1)}, bf16[1280,1024]{1,0:T(8,128)(2,1)}, u32[]{:S(2)}) %copy-start.1) | copy-done | bytes 2621464
  4.9 2.7 %collective-permute-start.3 = (bf16[1280,128]{1,0:T(8,128)(2,1)S(1)}, bf16[1280,128]{1,0:T(8,128)(2,1)S(1)}, u32[]{:S(2)}, u32[]{:S(2)}) collective-permute-start(bf16[1280,128]{1,0:T(8,128)(2,1)S(1)} %get-tuple-element.24), channel_id=1, source_target_pairs={{0,2},{1,3},{2,0},{3,1},{4,6},{5,7},{6,4},{7,5},{8,10},{9,11},{10,... | collective-permute-start | bytes 983048 | tf_op jit(solution)/shard_map/ppermute | solution.py:366
  7.9 1.5 %shard_map.95 = (f32[192,128]{1,0:T(8,128)S(1)}, f32[192,128]{1,0:T(8,128)S(1)}) custom-call(s32[4]{0:T(128)S(1)} %pad_add_fusion.place, s32[8]{0:T(128)S(1)} %copy-done.8), custom_call_target="tpu_custom_call" | custom-call | flops 2457600 | bytes 196608 | tf_op jit(solution)/shard_map/pallas_call | solution.py:21
  10.9 4.6 %collective-permute-done.3.refs_0_ = bf16[1280,128]{1,0:T(8,128)(2,1)S(1)} collective-permute-done((bf16[1280,128]{1,0:T(8,128)(2,1)S(1)}, bf16[1280,128]{1,0:T(8,128)(2,1)S(1)}, u32[]{:S(2)}, u32[]{:S(2)}) %collective-permute-start.3) | collective-permute-done | bytes 327712 | tf_op jit(solution)/shard_map/ppermute | solution.py:366
  16.3 1.5 %collective-permute-start.1 = (bf16[2,64,1280]{2,1,0:T(8,128)(2,1)S(1)}, bf16[2,64,1280]{2,1,0:T(8,128)(2,1)S(1)}, u32[]{:S(2)}, u32[]{:S(2)}) collective-permute-start(bf16[2,64,1280]{2,1,0:T(8,128)(2,1)S(1)} %shard_map.93), channel_id=1, source_target_pairs={{0,2},{1,3},{2,0},{3,1},{4,6},{5,7},{6,4},{7,5},{8,10},{9,11},{10,... | collective-permute-start | bytes 983048 | tf_op jit(solution)/shard_map/ppermute | solution.py:366
  17.7 1.3 %collective-permute-start.19 = (bf16[1024,640]{1,0:T(8,128)(2,1)S(1)}, bf16[1024,640]{1,0:T(8,128)(2,1)S(1)}, u32[]{:S(2)}, u32[]{:S(2)}) collective-permute-start(bf16[1024,640]{1,0:T(8,128)(2,1)S(1)} %shard_map.94), channel_id=1, source_target_pairs={{0,4},{4,0},{8,12},{12,8},{1,5},{5,1},{9,13},{13,9},{2,6},{6,2},{1... | collective-permute-start | bytes 3932168 | tf_op jit(solution)/shard_map/ppermute | solution.py:366
  19.0 1.2 %collective-permute-start.7 = (bf16[1280,128]{1,0:T(8,128)(2,1)S(1)}, bf16[1280,128]{1,0:T(8,128)(2,1)S(1)}, u32[]{:S(2)}, u32[]{:S(2)}) collective-permute-start(bf16[1280,128]{1,0:T(8,128)(2,1)S(1)} %collective-permute-done.3.refs_0_), channel_id=1, source_target_pairs={{0,16},{16,0},{1,17},{17,1},{2,18},{18,2},{3,19},{19,3},{4,20},{20... | collective-permute-start | bytes 983048 | tf_op jit(solution)/shard_map/ppermute | solution.py:366
  20.3 1.6 %shard_map.96 = (bf16[4,128,1280]{2,1,0:T(8,128)(2,1)S(1)}, f32[192,256]{1,0:T(8,128)S(1)}) custom-call(s32[4]{0:T(128)S(1)} %pad_add_fusion.place, bf16[128,5120]{1,0:T(8,128)(2,1)S(1)} %copy-done.5, f32[1,5120]{1,0:T(1,128)S(1)} %bitcast.8, bf16[4,64,1280]{2,1,0:T(8,128)(2,1)S(1)} %get-tuple-element.26.cont.refs_0_, ...), custom_call_target="tpu_custom_call" | custom-call | flops 251658240 | bytes 5242880 | tf_op jit(solution)/shard_map/pallas_call | solution.py:21
  21.9 3.7 %collective-permute-done.1.refs_2_ = bf16[2,64,1280]{2,1,0:T(8,128)(2,1)S(1)} collective-permute-done((bf16[2,64,1280]{2,1,0:T(8,128)(2,1)S(1)}, bf16[2,64,1280]{2,1,0:T(8,128)(2,1)S(1)}, u32[]{:S(2)}, u32[]{:S(2)}) %collective-permute-start.1) | collective-permute-done | bytes 327712 | tf_op jit(solution)/shard_map/ppermute | solution.py:366
  25.6 1.4 %shard_map.97 = (f32[128,1024]{1,0:T(8,128)S(1)}, f32[128,1024]{1,0:T(8,128)S(1)}) custom-call(s32[4]{0:T(128)S(1)} %pad_add_fusion.place, bf16[4,64,1280]{2,1,0:T(8,128)(2,1)S(1)} %get-tuple-element.26.cont.refs_0_, bf16[2,64,1280]{2,1,0:T(8,128)(2,1)S(1)} %collective-permute-done.other.refs_1_, bf16[2,64,1280]{2,1,0:T(8,128)(2,1)S(1)} %collective-permute-done.1.refs_2_, ...), custom_call_target="tpu_custom_call" | custom-call | flops 671088640 | bytes 2621440 | tf_op jit(solution)/shard_map/pallas_call | solution.py:21
  27.9 1.3 %collective-permute-start.8 = (bf16[1280,128]{1,0:T(8,128)(2,1)S(1)}, bf16[1280,128]{1,0:T(8,128)(2,1)S(1)}, u32[]{:S(2)}, u32[]{:S(2)}) collective-permute-start(bf16[1280,128]{1,0:T(8,128)(2,1)S(1)} %collective-permute-done.7.refs_1_), channel_id=1, source_target_pairs={{0,1},{1,0},{2,3},{3,2},{4,5},{5,4},{6,7},{7,6},{8,9},{9,8},{10,11... | collective-permute-start | bytes 983048 | tf_op jit(solution)/shard_map/ppermute | solution.py:366
  30.0 1.5 %collective-permute-start.6 = (f32[64,1024]{1,0:T(8,128)S(1)}, f32[64,1024]{1,0:T(8,128)S(1)}, u32[]{:S(2)}, u32[]{:S(2)}) collective-permute-start(f32[64,1024]{1,0:T(8,128)S(1)} %shard_map.98), channel_id=1, source_target_pairs={{0,2},{1,3},{2,0},{3,1},{4,6},{5,7},{6,4},{7,5},{8,10},{9,11},{10,... | collective-permute-start | bytes 786440 | tf_op jit(solution)/shard_map/ppermute | solution.py:366
  33.6 6.0 %collective-permute-done.10.refs_2_ = bf16[192,256]{1,0:T(8,128)(2,1)S(1)} collective-permute-done((bf16[192,256]{1,0:T(8,128)(2,1)S(1)}, bf16[192,256]{1,0:T(8,128)(2,1)S(1)}, u32[]{:S(2)}, u32[]{:S(2)}) %collective-permute-start.10) | collective-permute-done | bytes 98336 | tf_op jit(solution)/shard_map/ppermute | solution.py:366
  41.8 2.9 %shard_map.100.refs_0_ = bf16[64,1024]{1,0:T(8,128)(2,1)S(1)} custom-call(s32[4]{0:T(128)S(1)} %pad_add_fusion.place, s32[8]{0:T(128)S(1)} %copy-done.8, f32[128,1024]{1,0:T(8,128)S(1)} %get-tuple-element.35.left.mine, f32[128,1024]{1,0:T(8,128)S(1)} %collective-permute-done.5.right.near, f32[64,1024]{1,0:T(8,128)S(1)} %collective-permute-done.6.far, ...), custom_call_target="tpu_custom_call" | custom-call | flops 201326592 | bytes 1048576 | tf_op jit(solution)/shard_map/pallas_call | solution.py:21
  44.8 1.5 %collective-permute-start.13 = (bf16[64,1024]{1,0:T(8,128)(2,1)S(1)}, bf16[64,1024]{1,0:T(8,128)(2,1)S(1)}, u32[]{:S(2)}, u32[]{:S(2)}) collective-permute-start(bf16[64,1024]{1,0:T(8,128)(2,1)S(1)} %shard_map.100.refs_0_), channel_id=1, source_target_pairs={{0,2},{1,3},{2,0},{3,1},{4,6},{5,7},{6,4},{7,5},{8,10},{9,11},{10,... | collective-permute-start | bytes 393224 | tf_op jit(solution)/shard_map/ppermute | solution.py:366
  46.3 1.3 %collective-permute-start.15 = (bf16[64,1024]{1,0:T(8,128)(2,1)S(1)}, bf16[64,1024]{1,0:T(8,128)(2,1)S(1)}, u32[]{:S(2)}, u32[]{:S(2)}) collective-permute-start(bf16[64,1024]{1,0:T(8,128)(2,1)S(1)} %shard_map.100.refs_0_), channel_id=1, source_target_pairs={{0,4},{1,5},{2,6},{3,7},{4,0},{5,1},{6,2},{7,3},{8,12},{9,13},{10,... | collective-permute-start | bytes 393224 | tf_op jit(solution)/shard_map/ppermute | solution.py:375
  50.7 2.6 %collective-permute-start.16 = (bf16[64,1024]{1,0:T(8,128)(2,1)S(1)}, bf16[64,1024]{1,0:T(8,128)(2,1)S(1)}, u32[]{:S(2)}, u32[]{:S(2)}) collective-permute-start(bf16[64,1024]{1,0:T(8,128)(2,1)S(1)} %collective-permute-done.15.refs_4_), channel_id=1, source_target_pairs={{0,1},{1,0},{2,3},{3,2},{4,5},{5,4},{6,7},{7,6},{8,9},{9,8},{10,11... | collective-permute-start | bytes 393224 | tf_op jit(solution)/shard_map/ppermute | solution.py:366
  53.4 1.4 %collective-permute-start.18 = (bf16[64,1024]{1,0:T(8,128)(2,1)S(1)}, bf16[64,1024]{1,0:T(8,128)(2,1)S(1)}, u32[]{:S(2)}, u32[]{:S(2)}) collective-permute-start(bf16[64,1024]{1,0:T(8,128)(2,1)S(1)} %collective-permute-done.17.refs_6_), channel_id=1, source_target_pairs={{0,1},{1,0},{2,3},{3,2},{4,5},{5,4},{6,7},{7,6},{8,9},{9,8},{10,11... | collective-permute-start | bytes 393224 | tf_op jit(solution)/shard_map/ppermute | solution.py:366
  55.8 1.6 %shard_map.101 = (bf16[64,640]{1,0:T(8,128)(2,1)S(1)}, bf16[64,640]{1,0:T(8,128)(2,1)S(1)}, bf16[64,640]{1,0:T(8,128)(2,1)S(1)}, bf16[64,640]{1,0:T(8,128)(2,1)S(1)}) custom-call(s32[4]{0:T(128)S(1)} %pad_add_fusion.place, bf16[64,1024]{1,0:T(8,128)(2,1)S(1)} %shard_map.100.refs_0_, bf16[64,1024]{1,0:T(8,128)(2,1)S(1)} %collective-permute-done.12.refs_1_, ...), custom_call_target="tpu_custom_call" | custom-call | flops 671088640 | bytes 2621440 | tf_op jit(solution)/shard_map/pallas_call | solution.py:21
  57.4 3.6 %collective-permute-start.20 = (bf16[64,640]{1,0:T(8,128)(2,1)S(1)}, bf16[64,640]{1,0:T(8,128)(2,1)S(1)}, u32[]{:S(2)}, u32[]{:S(2)}) collective-permute-start(bf16[64,640]{1,0:T(8,128)(2,1)S(1)} %get-tuple-element.39), channel_id=1, source_target_pairs={{0,0},{1,4},{2,8},{3,12},{4,1},{5,5},{6,9},{7,13},{8,2},{9,6},{10,... | collective-permute-start | bytes 245768 | tf_op jit(solution)/shard_map/ppermute | solution.py:572
  61.1 3.7 %collective-permute-start.22 = (bf16[64,640]{1,0:T(8,128)(2,1)S(1)}, bf16[64,640]{1,0:T(8,128)(2,1)S(1)}, u32[]{:S(2)}, u32[]{:S(2)}) collective-permute-start(bf16[64,640]{1,0:T(8,128)(2,1)S(1)} %get-tuple-element.41), channel_id=1, source_target_pairs={{0,2},{1,6},{2,10},{3,14},{4,3},{5,7},{6,11},{7,15},{8,0},{9,4},{1... | collective-permute-start | bytes 245768 | tf_op jit(solution)/shard_map/ppermute | solution.py:572
  65.2 5.4 %collective-permute-done.22.refs_2_ = bf16[64,640]{1,0:T(8,128)(2,1)S(1)} collective-permute-done((bf16[64,640]{1,0:T(8,128)(2,1)S(1)}, bf16[64,640]{1,0:T(8,128)(2,1)S(1)}, u32[]{:S(2)}, u32[]{:S(2)}) %collective-permute-start.22) | collective-permute-done | bytes 81952 | tf_op jit(solution)/shard_map/ppermute | solution.py:572
  70.6 7.6 %collective-permute-done.23.refs_3_ = bf16[64,640]{1,0:T(8,128)(2,1)S(1)} collective-permute-done((bf16[64,640]{1,0:T(8,128)(2,1)S(1)}, bf16[64,640]{1,0:T(8,128)(2,1)S(1)}, u32[]{:S(2)}, u32[]{:S(2)}) %collective-permute-start.23) | collective-permute-done | bytes 81952 | tf_op jit(solution)/shard_map/ppermute | solution.py:572
  78.2 1.3 %shard_map.102 = bf16[64,1280]{1,0:T(8,128)(2,1)} custom-call(s32[4]{0:T(128)S(1)} %pad_add_fusion.place, bf16[64,5120]{1,0:T(8,128)(2,1)S(1)} %copy-done.3, bf16[64,640]{1,0:T(8,128)(2,1)S(1)} %collective-permute-done.20.refs_0_, bf16[64,640]{1,0:T(8,128)(2,1)S(1)} %collective-permute-done.21.refs_1_, bf16[64,640]{1,0:T(8,128)(2,1)S(1)} %collective-permute-done.22.refs_2_, ...), custom_call_target="tpu_custom_call" | custom-call | flops 327680 | bytes 983040 | tf_op jit(solution)/shard_map/pallas_call | solution.py:21
  (57 shorter events, 16.2 us)
Async XLA Ops:
  4.8 4.6 %collective-permute-start = (bf16[2,64,1280]{2,1,0:T(8,128)(2,1)S(1)}, bf16[2,64,1280]{2,1,0:T(8,128)(2,1)S(1)}, u32[]{:S(2)}, u32[]{:S(2)}) collective-permute-start(bf16[2,64,1280]{2,1,0:T(8,128)(2,1)S(1)} %get-tuple-element.27), channel_id=1, source_target_pairs={{0,1},{1,0},{2,3},{3,2},{4,5},{5,4},{6,7},{7,6},{8,9},{9,8},{10,11... | collective-permute-start | bytes 983048 | tf_op jit(solution)/shard_map/ppermute | solution.py:366
  4.9 10.7 %collective-permute-start.3 = (bf16[1280,128]{1,0:T(8,128)(2,1)S(1)}, bf16[1280,128]{1,0:T(8,128)(2,1)S(1)}, u32[]{:S(2)}, u32[]{:S(2)}) collective-permute-start(bf16[1280,128]{1,0:T(8,128)(2,1)S(1)} %get-tuple-element.24), channel_id=1, source_target_pairs={{0,2},{1,3},{2,0},{3,1},{4,6},{5,7},{6,4},{7,5},{8,10},{9,11},{10,... | collective-permute-start | bytes 983048 | tf_op jit(solution)/shard_map/ppermute | solution.py:366
  7.6 12.7 %collective-permute-start.2 = (bf16[1280,256]{1,0:T(8,128)(2,1)S(1)}, bf16[1280,256]{1,0:T(8,128)(2,1)S(1)}, u32[]{:S(2)}, u32[]{:S(2)}) collective-permute-start(bf16[1280,256]{1,0:T(8,128)(2,1)S(1)} %get-tuple-element.28.own), channel_id=1, source_target_pairs={{0,1},{1,0},{2,3},{3,2},{4,5},{5,4},{6,7},{7,6},{8,9},{9,8},{10,11... | collective-permute-start | bytes 1966088 | tf_op jit(solution)/shard_map/ppermute | solution.py:366
  15.6 4.7 %collective-permute-start.4 = (bf16[1280,128]{1,0:T(8,128)(2,1)S(1)}, bf16[1280,128]{1,0:T(8,128)(2,1)S(1)}, u32[]{:S(2)}, u32[]{:S(2)}) collective-permute-start(bf16[1280,128]{1,0:T(8,128)(2,1)S(1)} %collective-permute-done.3.refs_0_), channel_id=1, source_target_pairs={{0,1},{1,0},{2,3},{3,2},{4,5},{5,4},{6,7},{7,6},{8,9},{9,8},{10,11... | collective-permute-start | bytes 983048 | tf_op jit(solution)/shard_map/ppermute | solution.py:366
  16.3 9.4 %collective-permute-start.1 = (bf16[2,64,1280]{2,1,0:T(8,128)(2,1)S(1)}, bf16[2,64,1280]{2,1,0:T(8,128)(2,1)S(1)}, u32[]{:S(2)}, u32[]{:S(2)}) collective-permute-start(bf16[2,64,1280]{2,1,0:T(8,128)(2,1)S(1)} %shard_map.93), channel_id=1, source_target_pairs={{0,2},{1,3},{2,0},{3,1},{4,6},{5,7},{6,4},{7,5},{8,10},{9,11},{10,... | collective-permute-start | bytes 983048 | tf_op jit(solution)/shard_map/ppermute | solution.py:366
  17.7 37.1 %collective-permute-start.19 = (bf16[1024,640]{1,0:T(8,128)(2,1)S(1)}, bf16[1024,640]{1,0:T(8,128)(2,1)S(1)}, u32[]{:S(2)}, u32[]{:S(2)}) collective-permute-start(bf16[1024,640]{1,0:T(8,128)(2,1)S(1)} %shard_map.94), channel_id=1, source_target_pairs={{0,4},{4,0},{8,12},{12,8},{1,5},{5,1},{9,13},{13,9},{2,6},{6,2},{1... | collective-permute-start | bytes 3932168 | tf_op jit(solution)/shard_map/ppermute | solution.py:366
  19.0 8.8 %collective-permute-start.7 = (bf16[1280,128]{1,0:T(8,128)(2,1)S(1)}, bf16[1280,128]{1,0:T(8,128)(2,1)S(1)}, u32[]{:S(2)}, u32[]{:S(2)}) collective-permute-start(bf16[1280,128]{1,0:T(8,128)(2,1)S(1)} %collective-permute-done.3.refs_0_), channel_id=1, source_target_pairs={{0,16},{16,0},{1,17},{17,1},{2,18},{18,2},{3,19},{19,3},{4,20},{20... | collective-permute-start | bytes 983048 | tf_op jit(solution)/shard_map/ppermute | solution.py:366
  27.0 2.4 %collective-permute-start.5 = (f32[128,1024]{1,0:T(8,128)S(1)}, f32[128,1024]{1,0:T(8,128)S(1)}, u32[]{:S(2)}, u32[]{:S(2)}) collective-permute-start(f32[128,1024]{1,0:T(8,128)S(1)} %get-tuple-element.36), channel_id=1, source_target_pairs={{0,1},{1,0},{2,3},{3,2},{4,5},{5,4},{6,7},{7,6},{8,9},{9,8},{10,11... | collective-permute-start | bytes 1572872 | tf_op jit(solution)/shard_map/ppermute | solution.py:366
  27.9 3.6 %collective-permute-start.8 = (bf16[1280,128]{1,0:T(8,128)(2,1)S(1)}, bf16[1280,128]{1,0:T(8,128)(2,1)S(1)}, u32[]{:S(2)}, u32[]{:S(2)}) collective-permute-start(bf16[1280,128]{1,0:T(8,128)(2,1)S(1)} %collective-permute-done.7.refs_1_), channel_id=1, source_target_pairs={{0,1},{1,0},{2,3},{3,2},{4,5},{5,4},{6,7},{7,6},{8,9},{9,8},{10,11... | collective-permute-start | bytes 983048 | tf_op jit(solution)/shard_map/ppermute | solution.py:366
  30.0 11.9 %collective-permute-start.6 = (f32[64,1024]{1,0:T(8,128)S(1)}, f32[64,1024]{1,0:T(8,128)S(1)}, u32[]{:S(2)}, u32[]{:S(2)}) collective-permute-start(f32[64,1024]{1,0:T(8,128)S(1)} %shard_map.98), channel_id=1, source_target_pairs={{0,2},{1,3},{2,0},{3,1},{4,6},{5,7},{6,4},{7,5},{8,10},{9,11},{10,... | collective-permute-start | bytes 786440 | tf_op jit(solution)/shard_map/ppermute | solution.py:366
  32.6 7.0 %collective-permute-start.10 = (bf16[192,256]{1,0:T(8,128)(2,1)S(1)}, bf16[192,256]{1,0:T(8,128)(2,1)S(1)}, u32[]{:S(2)}, u32[]{:S(2)}) collective-permute-start(bf16[192,256]{1,0:T(8,128)(2,1)S(1)} %shard_map.99.refs_0_), channel_id=1, source_target_pairs={{0,2},{1,3},{2,0},{3,1},{4,6},{5,7},{6,4},{7,5},{8,10},{9,11},{10,... | collective-permute-start | bytes 294920 | tf_op jit(solution)/shard_map/ppermute | solution.py:366
  32.8 8.1 %collective-permute-start.9 = (bf16[192,256]{1,0:T(8,128)(2,1)S(1)}, bf16[192,256]{1,0:T(8,128)(2,1)S(1)}, u32[]{:S(2)}, u32[]{:S(2)}) collective-permute-start(bf16[192,256]{1,0:T(8,128)(2,1)S(1)} %shard_map.99.refs_0_), channel_id=1, source_target_pairs={{0,1},{1,0},{2,3},{3,2},{4,5},{5,4},{6,7},{7,6},{8,9},{9,8},{10,11... | collective-permute-start | bytes 294920 | tf_op jit(solution)/shard_map/ppermute | solution.py:366
  39.7 2.1 %collective-permute-start.11 = (bf16[192,256]{1,0:T(8,128)(2,1)S(1)}, bf16[192,256]{1,0:T(8,128)(2,1)S(1)}, u32[]{:S(2)}, u32[]{:S(2)}) collective-permute-start(bf16[192,256]{1,0:T(8,128)(2,1)S(1)} %collective-permute-done.10.refs_2_), channel_id=1, source_target_pairs={{0,1},{1,0},{2,3},{3,2},{4,5},{5,4},{6,7},{7,6},{8,9},{9,8},{10,11... | collective-permute-start | bytes 294920 | tf_op jit(solution)/shard_map/ppermute | solution.py:366
  44.8 4.8 %collective-permute-start.13 = (bf16[64,1024]{1,0:T(8,128)(2,1)S(1)}, bf16[64,1024]{1,0:T(8,128)(2,1)S(1)}, u32[]{:S(2)}, u32[]{:S(2)}) collective-permute-start(bf16[64,1024]{1,0:T(8,128)(2,1)S(1)} %shard_map.100.refs_0_), channel_id=1, source_target_pairs={{0,2},{1,3},{2,0},{3,1},{4,6},{5,7},{6,4},{7,5},{8,10},{9,11},{10,... | collective-permute-start | bytes 393224 | tf_op jit(solution)/shard_map/ppermute | solution.py:366
  46.3 4.5 %collective-permute-start.15 = (bf16[64,1024]{1,0:T(8,128)(2,1)S(1)}, bf16[64,1024]{1,0:T(8,128)(2,1)S(1)}, u32[]{:S(2)}, u32[]{:S(2)}) collective-permute-start(bf16[64,1024]{1,0:T(8,128)(2,1)S(1)} %shard_map.100.refs_0_), channel_id=1, source_target_pairs={{0,4},{1,5},{2,6},{3,7},{4,0},{5,1},{6,2},{7,3},{8,12},{9,13},{10,... | collective-permute-start | bytes 393224 | tf_op jit(solution)/shard_map/ppermute | solution.py:375
  47.6 5.8 %collective-permute-start.17 = (bf16[64,1024]{1,0:T(8,128)(2,1)S(1)}, bf16[64,1024]{1,0:T(8,128)(2,1)S(1)}, u32[]{:S(2)}, u32[]{:S(2)}) collective-permute-start(bf16[64,1024]{1,0:T(8,128)(2,1)S(1)} %shard_map.100.refs_0_), channel_id=1, source_target_pairs={{0,6},{1,7},{2,4},{3,5},{4,2},{5,3},{6,0},{7,1},{8,14},{9,15},{10,... | collective-permute-start | bytes 393224 | tf_op jit(solution)/shard_map/ppermute | solution.py:375
  47.6 7.2 %collective-permute-start.12 = (bf16[64,1024]{1,0:T(8,128)(2,1)S(1)}, bf16[64,1024]{1,0:T(8,128)(2,1)S(1)}, u32[]{:S(2)}, u32[]{:S(2)}) collective-permute-start(bf16[64,1024]{1,0:T(8,128)(2,1)S(1)} %shard_map.100.refs_0_), channel_id=1, source_target_pairs={{0,1},{1,0},{2,3},{3,2},{4,5},{5,4},{6,7},{7,6},{8,9},{9,8},{10,11... | collective-permute-start | bytes 393224 | tf_op jit(solution)/shard_map/ppermute | solution.py:366
  49.6 5.3 %collective-permute-start.14 = (bf16[64,1024]{1,0:T(8,128)(2,1)S(1)}, bf16[64,1024]{1,0:T(8,128)(2,1)S(1)}, u32[]{:S(2)}, u32[]{:S(2)}) collective-permute-start(bf16[64,1024]{1,0:T(8,128)(2,1)S(1)} %collective-permute-done.13.refs_2_), channel_id=1, source_target_pairs={{0,1},{1,0},{2,3},{3,2},{4,5},{5,4},{6,7},{7,6},{8,9},{9,8},{10,11... | collective-permute-start | bytes 393224 | tf_op jit(solution)/shard_map/ppermute | solution.py:366
  50.7 4.1 %collective-permute-start.16 = (bf16[64,1024]{1,0:T(8,128)(2,1)S(1)}, bf16[64,1024]{1,0:T(8,128)(2,1)S(1)}, u32[]{:S(2)}, u32[]{:S(2)}) collective-permute-start(bf16[64,1024]{1,0:T(8,128)(2,1)S(1)} %collective-permute-done.15.refs_4_), channel_id=1, source_target_pairs={{0,1},{1,0},{2,3},{3,2},{4,5},{5,4},{6,7},{7,6},{8,9},{9,8},{10,11... | collective-permute-start | bytes 393224 | tf_op jit(solution)/shard_map/ppermute | solution.py:366
  53.4 2.4 %collective-permute-start.18 = (bf16[64,1024]{1,0:T(8,128)(2,1)S(1)}, bf16[64,1024]{1,0:T(8,128)(2,1)S(1)}, u32[]{:S(2)}, u32[]{:S(2)}) collective-permute-start(bf16[64,1024]{1,0:T(8,128)(2,1)S(1)} %collective-permute-done.17.refs_6_), channel_id=1, source_target_pairs={{0,1},{1,0},{2,3},{3,2},{4,5},{5,4},{6,7},{7,6},{8,9},{9,8},{10,11... | collective-permute-start | bytes 393224 | tf_op jit(solution)/shard_map/ppermute | solution.py:366
  57.4 7.8 %collective-permute-start.20 = (bf16[64,640]{1,0:T(8,128)(2,1)S(1)}, bf16[64,640]{1,0:T(8,128)(2,1)S(1)}, u32[]{:S(2)}, u32[]{:S(2)}) collective-permute-start(bf16[64,640]{1,0:T(8,128)(2,1)S(1)} %get-tuple-element.39), channel_id=1, source_target_pairs={{0,0},{1,4},{2,8},{3,12},{4,1},{5,5},{6,9},{7,13},{8,2},{9,6},{10,... | collective-permute-start | bytes 245768 | tf_op jit(solution)/shard_map/ppermute | solution.py:572
  61.0 4.2 %collective-permute-start.21 = (bf16[64,640]{1,0:T(8,128)(2,1)S(1)}, bf16[64,640]{1,0:T(8,128)(2,1)S(1)}, u32[]{:S(2)}, u32[]{:S(2)}) collective-permute-start(bf16[64,640]{1,0:T(8,128)(2,1)S(1)} %get-tuple-element.40), channel_id=1, source_target_pairs={{0,1},{1,5},{2,9},{3,13},{4,0},{5,4},{6,8},{7,12},{8,3},{9,7},{10,... | collective-permute-start | bytes 245768 | tf_op jit(solution)/shard_map/ppermute | solution.py:572
  61.1 9.5 %collective-permute-start.22 = (bf16[64,640]{1,0:T(8,128)(2,1)S(1)}, bf16[64,640]{1,0:T(8,128)(2,1)S(1)}, u32[]{:S(2)}, u32[]{:S(2)}) collective-permute-start(bf16[64,640]{1,0:T(8,128)(2,1)S(1)} %get-tuple-element.41), channel_id=1, source_target_pairs={{0,2},{1,6},{2,10},{3,14},{4,3},{5,7},{6,11},{7,15},{8,0},{9,4},{1... | collective-permute-start | bytes 245768 | tf_op jit(solution)/shard_map/ppermute | solution.py:572
  64.8 13.4 %collective-permute-start.23 = (bf16[64,640]{1,0:T(8,128)(2,1)S(1)}, bf16[64,640]{1,0:T(8,128)(2,1)S(1)}, u32[]{:S(2)}, u32[]{:S(2)}) collective-permute-start(bf16[64,640]{1,0:T(8,128)(2,1)S(1)} %get-tuple-element.42), channel_id=1, source_target_pairs={{0,3},{1,7},{2,11},{3,15},{4,2},{5,6},{6,10},{7,14},{8,1},{9,5},{1... | collective-permute-start | bytes 245768 | tf_op jit(solution)/shard_map/ppermute | solution.py:572
  (10 other events, 88.3 us)
